TPU v7x, 32 devices: a whole 2x2x4 slice. The times are simulated.
32 devices in a mesh: dp: 4 (over z), row: 4 (over y, core), col: 2 (over x).
Axes of the slice: x: 2, y: 2, z: 4, core: 2. Of those that a mesh axis runs over, the one named last changes fastest.
Arguments:
- grad_wi: bfloat16 [4, 4096, 16384], P('dp', 'row', 'col'), may hold values from -100 to 100
- grad_wo: bfloat16 [4, 16384, 4096], P('dp', 'row', 'col'), may hold values from -100 to 100
- row_wi: float32 [4096], P('row'), may hold values from 0.01 to 1
- col_wi: float32 [16384], P('col'), may hold values from 0.01 to 1
- row_wo: float32 [16384], P('row'), may hold values from 0.01 to 1
- col_wo: float32 [4096], P('col'), may hold values from 0.01 to 1
Outputs:
- update_wi: bfloat16 [4096, 16384], P('row', 'col')
- row_wi_new: float32 [4096], P('row')
- col_wi_new: float32 [16384], P('col')
- update_wo: bfloat16 [16384, 4096], P('row', 'col')
- row_wo_new: float32 [16384], P('row')
- col_wo_new: float32 [4096], P('col')
All inputs are finite; a program needn't handle non-finite values.
Results may differ from a plain program's by a relative error of at most 0.015.
Values may be sent and summed in bfloat16 or wider, within the bound.
No kernel may reach another device: no remote copies, remote signals or barrier semaphores. Data moves between devices by JAX's collectives and lax.ppermute only.
A program may use at most 192 MiB of HBM per device.

v0:
```python
import jax
import jax.numpy as jnp
from jax import lax
from jax.sharding import PartitionSpec as P

D = 4096
FF = 16384


BETA = 0.8
EPS_SQUARE = 1e-30


def column_totals(square_wi, square_wo):
    return lax.psum((jnp.sum(square_wi, axis=0), jnp.sum(square_wo, axis=0)), "row")


def local(grad_wi, grad_wo, row_wi, col_wi, row_wo, col_wo):
    terms = (grad_wi[0].astype(jnp.float32), grad_wo[0].astype(jnp.float32))
    total_wi, total_wo = (
        lax.psum(terms[0].astype(jnp.bfloat16), "dp").astype(jnp.float32),
        lax.psum(terms[1].astype(jnp.bfloat16), "dp").astype(jnp.float32),
    )
    square_wi = total_wi * total_wi + EPS_SQUARE
    square_wo = total_wo * total_wo + EPS_SQUARE
    row_sum_wi, row_sum_wo = lax.psum(
        (jnp.sum(square_wi, axis=1), jnp.sum(square_wo, axis=1)), "col"
    )
    col_sum_wi, col_sum_wo = column_totals(square_wi, square_wo)
    row_new_wi = BETA * row_wi + (1.0 - BETA) * (row_sum_wi / FF)
    row_new_wo = BETA * row_wo + (1.0 - BETA) * (row_sum_wo / D)
    col_new_wi = BETA * col_wi + (1.0 - BETA) * (col_sum_wi / D)
    col_new_wo = BETA * col_wo + (1.0 - BETA) * (col_sum_wo / FF)
    raw_wi = total_wi / jnp.sqrt(row_new_wi[:, None] * col_new_wi[None, :])
    raw_wo = total_wo / jnp.sqrt(row_new_wo[:, None] * col_new_wo[None, :])
    local_squares = (jnp.sum(raw_wi * raw_wi), jnp.sum(raw_wo * raw_wo))
    energy_wi, energy_wo = lax.psum((local_squares[0], local_squares[1]), ("row", "col"))
    update_wi = (raw_wi / jnp.maximum(1.0, jnp.sqrt(energy_wi / (D * FF)))).astype(jnp.bfloat16)
    update_wo = (raw_wo / jnp.maximum(1.0, jnp.sqrt(energy_wo / (D * FF)))).astype(jnp.bfloat16)
    return (update_wi, row_new_wi, col_new_wi, update_wo, row_new_wo, col_new_wo)


def solution(mesh):
    return jax.shard_map(
        local,
        mesh=mesh,
        in_specs=(
            P("dp", "row", "col"),
            P("dp", "row", "col"),
            P("row"),
            P("col"),
            P("row"),
            P("col"),
        ),
        out_specs=(P("row", "col"), P("row"), P("col"), P("row", "col"), P("row"), P("col")),
        check_vma=False,
    )
```

profile of v0, /device:TPU:0, one launch (start us, length us, event | category | flops | bytes accessed | tf_op | source)
XLA Modules:
  0.0 1239.4 jit_solution(17220952272279389015)
XLA Ops:
  7.2 0.0 all-reduce.6.cloned.1.call-start
  7.2 0.7 all-reduce.6.cloned.1.call-update
  7.9 1111.1 %all-reduce.6.cloned.1.call-done = (bf16[1024,8192]{1,0:T(8,128)(2,1)}, bf16[4096,2048]{1,0:T(8,128)(2,1)}) async-done(((bf16[1024,8192]{1,0:T(8,128)(2,1)}, bf16[4096,2048]{1,0:T(8,128)(2,1)}), (bf16[1024,8192]{1,0:T(8,128)(2,1)}, bf16[4096,2048]{1,0:T(8,128)(2,1)})) %all-reduce.6.cloned.1.call-update) | async-done | bytes 33554448 | tf_op jit(solution)/shard_map/psum | solution.py:21
  1119.0 0.0 copy-start
  1119.0 0.0 copy-start.8
  1119.0 0.0 copy-start.6
  1119.0 0.0 copy-start.5
  1119.0 0.0 copy-start.7
  1119.0 10.5 fusion.5
  1129.5 0.2 copy-done
  1129.7 7.9 fusion.2
  1137.6 8.2 all-reduce.2
  1145.9 0.0 copy-done.8
  1145.9 0.0 copy-start.4
  1145.9 0.0 copy-done.6
  1145.9 0.0 copy-start.2
  1145.9 10.5 all-reduce.1
  1156.5 0.0 copy-done.5
  1156.5 0.0 copy-start.1
  1156.5 0.0 copy-done.7
  1156.5 0.0 copy-start.3
  1156.5 16.3 %multiply_reduce_fusion = f32[]{:T(128)} fusion(bf16[4096,2048]{1,0:T(8,128)(2,1)} %get-tuple-element.17, f32[2048]{0:T(1024)S(1)} %multiply_add_fusion.2, f32[4096]{0:T(1024)S(1)} %multiply_add_fusion.1), kind=kLoop, calls=%fused_computation.11 | loop fusion | flops 41943040 | bytes 16801796 | tf_op jit(solution)/shard_map/reduce_sum | solution.py:36
  1172.9 11.8 multiply_reduce_fusion.1
  1184.6 13.2 %all-reduce = (f32[]{:T(128)}, f32[]{:T(128)}) all-reduce(f32[]{:T(128)} %multiply_reduce_fusion.1, f32[]{:T(128)} %multiply_reduce_fusion), channel_id=1, replica_groups=mesh['dp'=4,'row'=4,'col'=2] {'row','col'}, use_global_device_ids=true, to_apply=%region_6.0 | all-reduce | flops 2 | bytes 16 | tf_op jit(solution)/shard_map/psum | solution.py:37
  1199.3 0.0 copy-done.4
  1199.3 0.0 copy-done.1
  1199.3 16.4 %divide_convert_fusion.1 = bf16[1024,8192]{1,0:T(8,128)(2,1)} fusion(bf16[1024,8192]{1,0:T(8,128)(2,1)} %get-tuple-element.16, f32[]{:T(128)S(6)} %max.6, f32[8192]{0:T(1024)S(1)} %multiply_add_fusion, f32[1024]{0:T(1024)S(1)} %multiply_add_fusion.3), kind=kLoop, calls=%fused_computation.12 | loop fusion | flops 41943040 | bytes 33591300 | tf_op jit(solution)/shard_map/convert_element_type | solution.py:38
  1215.7 0.0 copy-done.2
  1215.7 0.0 copy-done.3
  1215.7 16.8 %divide_convert_fusion = bf16[4096,2048]{1,0:T(8,128)(2,1)} fusion(bf16[4096,2048]{1,0:T(8,128)(2,1)} %get-tuple-element.17, f32[]{:T(128)S(6)} %max.7, f32[2048]{0:T(1024)S(1)} %multiply_add_fusion.2, f32[4096]{0:T(1024)S(1)} %multiply_add_fusion.1), kind=kLoop, calls=%fused_computation.10 | loop fusion | flops 41943040 | bytes 33579012 | tf_op jit(solution)/shard_map/convert_element_type | solution.py:39
  (4 shorter events, 0.0 us)
Async XLA Ops:
  7.2 1111.8 %all-reduce.6.cloned.1.call-start = ((), (), s32[]{:S(2)}) async-start(), calls=%async_computation | async-start | bytes 67108864 | tf_op jit(solution)/shard_map/psum | solution.py:21
  1119.0 10.7 copy-start
  1119.0 26.9 %copy-start.8 = (f32[1024]{0:T(1024)S(1)}, f32[1024]{0:T(1024)}, u32[]{:S(2)}) copy-start(f32[1024]{0:T(1024)} %param.8) | copy-start | bytes 12292
  1119.0 26.9 %copy-start.6 = (f32[4096]{0:T(1024)S(1)}, f32[4096]{0:T(1024)}, u32[]{:S(2)}) copy-start(f32[4096]{0:T(1024)} %param.10) | copy-start | bytes 49156
  1119.0 37.5 %copy-start.5 = (f32[8192]{0:T(1024)S(1)}, f32[8192]{0:T(1024)}, u32[]{:S(2)}) copy-start(f32[8192]{0:T(1024)} %param.9) | copy-start | bytes 98308
  1119.0 37.5 %copy-start.7 = (f32[2048]{0:T(1024)S(1)}, f32[2048]{0:T(1024)}, u32[]{:S(2)}) copy-start(f32[2048]{0:T(1024)} %param.11) | copy-start | bytes 24580
  1145.9 53.4 %copy-start.4 = (f32[1024]{0:T(1024)}, f32[1024]{0:T(1024)S(1)}, u32[]{:S(2)}) copy-start(f32[1024]{0:T(1024)S(1)} %multiply_add_fusion.3) | copy-start | bytes 12292
  1145.9 69.8 %copy-start.2 = (f32[4096]{0:T(1024)}, f32[4096]{0:T(1024)S(1)}, u32[]{:S(2)}) copy-start(f32[4096]{0:T(1024)S(1)} %multiply_add_fusion.1) | copy-start | bytes 49156
  1156.5 42.8 %copy-start.1 = (f32[8192]{0:T(1024)}, f32[8192]{0:T(1024)S(1)}, u32[]{:S(2)}) copy-start(f32[8192]{0:T(1024)S(1)} %multiply_add_fusion) | copy-start | bytes 98308
  1156.5 59.2 %copy-start.3 = (f32[2048]{0:T(1024)}, f32[2048]{0:T(1024)S(1)}, u32[]{:S(2)}) copy-start(f32[2048]{0:T(1024)S(1)} %multiply_add_fusion.2) | copy-start | bytes 24580
Sparse Core Ops, SparseCore 0:
  10.7 1108.2 all-reduce.5
where the time goes:
time: 1240 us
  waiting for transfers between devices  1110 us (90%)
  other arithmetic  79.8 us (6%)
  blocking collectives  32 us (3%)
  between operations  15.5 us (1%)
    psum x1, waiting for transfers between devices, local(): lax.psum(terms[0].astype(jnp.bfloat16), 'dp').astype(jnp.float32)  1110 us
    reduce_sum x2, other arithmetic, local(): local_squares = (jnp.sum(raw_wi * raw_wi), jnp.sum(raw_wo * raw_wo))  28.1 us
  transfers between devices with their start and end apart: 1, of which 1 were waited for; matrix products, arithmetic and copies ran while one was open for 0% of the time, Pallas kernels for 0%

commit v1 on v0

v1 whole, which is shorter than its diff:
```python
import jax
import jax.numpy as jnp
from jax import lax
from jax.sharding import PartitionSpec as P

BETA = 0.8
EPS_SQUARE = 1e-30
CHUNKS = 16
LAG = 2


def chunk_count(rows):
    half = rows // 2
    count = CHUNKS
    while half % count or (half // count) % 8:
        count //= 2
    return count


def make_local(n_dp, n_row, n_col):
    last = n_dp - 1

    def local(grad_wi, grad_wo, row_wi, col_wi, row_wo, col_wo):
        f32, bf16 = jnp.float32, jnp.bfloat16
        place = lax.axis_index("dp")
        grads = (grad_wi[0], grad_wo[0])
        prevs = ((row_wi, col_wi), (row_wo, col_wo))
        shapes = [g.shape for g in grads]
        counts = [chunk_count(rows) for rows, _ in shapes]
        sizes = [rows // 2 // count for (rows, _), count in zip(shapes, counts)]

        position = (place, last - place)
        at_end = (place == last) | (place == 0)

        segments = []
        start = 0
        for kind in ("sum", "spread"):
            for m in range(2):
                segments.append((kind, m, start))
                start += counts[m]
        steps = start + LAG * last

        def hop(value, direction, senders):
            pairs = []
            for p in senders:
                if p < last:
                    pairs.append((p, p + 1) if direction == 0 else (last - p, last - p - 1))
            return lax.ppermute(value, "dp", pairs) if pairs else None

        inflight = {}
        finals = {(m, d): [] for m in range(2) for d in range(2)}
        latest = {}
        updates = {}
        outs = [jnp.zeros(shape, bf16) for shape in shapes]
        results = {}

        def statistics(m):
            rows, cols = shapes[m]
            half = rows // 2
            total = jnp.concatenate(
                [jnp.where(place == 0, low, high) for high, low in zip(finals[m, 0], finals[m, 1])]
            )
            if updates:
                total, _ = lax.optimization_barrier((total, updates[m - 1][3]))
            wide = total.astype(f32)
            square = wide * wide + EPS_SQUARE
            row_part = jnp.sum(square, axis=1)
            col_part = jnp.sum(square, axis=0)
            row_all = jnp.concatenate(
                [jnp.where(place == last, row_part, 0.0), jnp.where(place == 0, row_part, 0.0)]
            )
            row_sum = lax.psum(row_all, ("dp", "col"))
            col_sum = lax.psum(jnp.where(at_end, col_part, 0.0), ("dp", "row"))
            row_new = BETA * prevs[m][0] + (1.0 - BETA) * (row_sum / (cols * n_col))
            col_new = BETA * prevs[m][1] + (1.0 - BETA) * (col_sum / (rows * n_row))
            row_half = jnp.where(place == 0, row_new[half:], row_new[:half])
            row_scale = lax.rsqrt(row_half)
            col_scale = lax.rsqrt(col_new)
            raw = wide * row_scale[:, None] * col_scale[None, :]
            energy = lax.psum(jnp.where(at_end, jnp.sum(raw * raw), 0.0), ("dp", "row", "col"))
            rms = jnp.sqrt(energy / (rows * n_row * cols * n_col))
            row_final = row_scale / jnp.maximum(1.0, rms)
            updates[m] = (raw_update(total, row_final, col_scale), row_new, col_new, energy)

        def raw_update(total, row_final, col_scale):
            wide = total.astype(f32)
            return (wide * row_final[:, None] * col_scale[None, :]).astype(bf16)

        arrived = {}
        tied = {}
        for s in range(steps):
            batch = []
            for index, (kind, m, begin) in enumerate(segments):
                members = [p for p in range(n_dp) if 0 <= s - LAG * p - begin < counts[m]]
                if not members:
                    continue
                size = sizes[m]
                half = shapes[m][0] // 2
                cols = shapes[m][1]
                if kind == "spread" and m not in updates:
                    statistics(m)
                for d in range(2):
                    got = inflight.pop((index, d, s - LAG), None)
                    at = jnp.clip(s - begin - LAG * position[d], 0, counts[m] - 1) * size
                    if kind == "sum":
                        own = lax.dynamic_slice(grads[m], (d * half + at, 0), (size, cols))
                        value = own
                        if got is not None:
                            value = (got.astype(f32) + own.astype(f32)).astype(bf16)
                        if last in members:
                            finals[m, d].append(value)
                    else:
                        value = got
                        if 0 in members:
                            k = s - begin
                            mine = updates[m][0][k * size : (k + 1) * size]
                            value = mine if got is None else jnp.where(position[d] == 0, mine, got)
                        elif got is not None:
                            done = s - LAG * position[d] - begin >= counts[m]
                            value = jnp.where(done, latest[m, d], got)
                        latest[m, d] = value
                        outs[m] = lax.dynamic_update_slice(
                            outs[m], value, ((1 - d) * half + at, 0)
                        )
                    if min(members) < last:
                        batch.append((index, d, members, value))
            values = [value for _, _, _, value in batch]
            after = arrived.get(s - LAG, []) + tied.get(s - 1, [])
            if values:
                values, _ = lax.optimization_barrier((values, after))
            tied[s] = values
            arrived[s] = []
            for (index, d, members, _), value in zip(batch, values):
                inflight[index, d, s] = hop(value, d, members)
                arrived[s].append(inflight[index, d, s])
        return (outs[0], updates[0][1], updates[0][2], outs[1], updates[1][1], updates[1][2])

    return local


def solution(mesh):
    sizes = mesh.shape
    return jax.shard_map(
        make_local(sizes["dp"], sizes["row"], sizes["col"]),
        mesh=mesh,
        in_specs=(
            P("dp", "row", "col"),
            P("dp", "row", "col"),
            P("row"),
            P("col"),
            P("row"),
            P("col"),
        ),
        out_specs=(P("row", "col"), P("row"), P("col"), P("row", "col"), P("row"), P("col")),
        check_vma=False,
    )
```

time: 1240 us -> 1120 us (0.903)
  waiting for transfers between devices: 1110 us -> 280 us
  starting transfers between devices: 0.04 us -> 422 us
  blocking collectives: 32 us -> 218 us
  other arithmetic: 79.8 us -> 154 us
  local copies, waits for them, and re-layouts: 0.22 us -> 27.3 us
    psum x1 -> x0, waiting for transfers between devices: 1110 us -> none  [local(): lax.psum(terms[0].astype(jnp.bfloat16), 'dp').astype(jnp.float32)]
    ppermute x0 -> x160, starting transfers between devices: none -> 422 us  [hop(): return lax.ppermute(value, 'dp', pairs) if pairs else None]
    ppermute x0 -> x160, waiting for transfers between devices: none -> 280 us  [hop(): return lax.ppermute(value, 'dp', pairs) if pairs else None]
    psum x3 -> x6, blocking collectives: 32 us -> 218 us  [the longest x2 87.7 us: statistics(): col_sum = lax.psum(jnp.where(at_end, col_part, 0.0), ('dp', 'row'))]
    unnamed x0 -> x34, other arithmetic: none -> 45.6 us
    dynamic_update_slice x0 -> x80, other arithmetic: none -> 44.9 us  [local(): outs[m] = lax.dynamic_update_slice(outs[m], value, ((1 - d) * half + at, 0))]
    unnamed x18 -> x46, local copies, waits for them, and re-layouts: 0.22 us -> 18.9 us
    reduce_sum x4, other arithmetic: 46.5 us -> 32.1 us  [the longest x2 17.8 us: statistics(): jnp.sum(raw * raw)]
  transfers between devices with their start and end apart: 1 -> 160, of which waited for: 1 -> 81; matrix products, arithmetic and copies ran while one was open for 0% -> 14% of each run, Pallas kernels for 0% -> 0%
where the time goes in v1:
time: 1120 us; the launch traced here: 1110 us
  starting transfers between devices  422 us (38%)
  waiting for transfers between devices  280 us (25%)
  blocking collectives  218 us (19%)
  other arithmetic  154 us (14%)
  local copies, waits for them, and re-layouts  27.3 us (2%)
    ppermute x160, starting transfers between devices, hop(): return lax.ppermute(value, 'dp', pairs) if pairs else None  422 us
    ppermute x160, waiting for transfers between devices, hop(): return lax.ppermute(value, 'dp', pairs) if pairs else None  280 us
    psum x2, blocking collectives, statistics(): col_sum = lax.psum(jnp.where(at_end, col_part, 0.0), ('dp', 'row'))  87.7 us
    psum x2, blocking collectives, statistics(): lax.psum(jnp.where(at_end, jnp.sum(raw * raw), 0.0), ('dp', 'row', 'col'))  77.5 us
    psum x2, blocking collectives, statistics(): row_sum = lax.psum(row_all, ('dp', 'col'))  52.6 us
    unnamed x34, other arithmetic  45.6 us
    dynamic_update_slice x80, other arithmetic, local(): outs[m] = lax.dynamic_update_slice(outs[m], value, ((1 - d) * half + at, 0))  44.9 us
  transfers between devices with their start and end apart: 160, of which 81 were waited for; matrix products, arithmetic and copies ran while one was open for 14% of the time, Pallas kernels for 0%

profile of v1, /device:TPU:0, one launch (start us, length us, event | category | flops | bytes accessed | tf_op | source)
XLA Modules:
  0.0 1108.2 jit_solution(2158243930082207463)
XLA Ops:
  11.7 9.5 collective-permute-done.4
  21.2 10.1 collective-permute-done
  40.7 5.9 collective-permute-start.2
  46.7 5.7 collective-permute-done.8
  53.2 8.4 collective-permute-done.2
  201.3 7.3 collective-permute-start.36
  210.8 6.3 collective-permute-done.32
  222.3 6.2 collective-permute-done.40
  240.6 7.0 collective-permute-done.38
  250.1 5.4 collective-permute-done.42
  261.4 7.3 fusion.1
  268.8 18.6 %psum.42 = f32[1024]{0:T(1024)S(1)} all-reduce(f32[1024]{0:T(1024)S(1)} %pad_maximum_fusion.1), channel_id=1, replica_groups=mesh['dp'=4,'row'=4,'col'=2] {'dp','col'}, use_global_device_ids=true, to_apply=%region_1.2 | all-reduce | flops 1024 | bytes 8192 | tf_op jit(solution)/shard_map/psum | solution.py:72
  287.4 57.7 %psum.43 = f32[8192]{0:T(1024)S(1)} all-reduce(f32[8192]{0:T(1024)S(1)} %broadcast_select_fusion.76), channel_id=1, replica_groups=mesh['dp'=4,'row'=4,'col'=2] {'dp','row'}, use_global_device_ids=true, to_apply=%region_3.4 | all-reduce | flops 8192 | bytes 65536 | tf_op jit(solution)/shard_map/psum | solution.py:73
  349.2 5.5 collective-permute-start.46
  355.3 8.4 fusion.5
  364.4 37.0 %psum.44 = f32[]{:T(128)} all-reduce(f32[]{:T(128)S(6)} %select_n.1173), channel_id=1, replica_groups=mesh['dp'=4,'row'=4,'col'=2] {'dp','row','col'}, use_global_device_ids=true, to_apply=%region_5.6 | all-reduce | flops 1 | bytes 8 | tf_op jit(solution)/shard_map/psum | solution.py:80
  403.3 6.2 collective-permute-start.52
  441.0 10.0 fusion.7
  538.4 7.6 collective-permute-start.74
  555.5 9.1 collective-permute-start.78
  581.0 8.9 collective-permute-start.86
  593.1 6.2 copy-done.2
  599.3 8.6 collective-permute-start.90
  610.1 6.9 fusion.9
  617.0 30.0 %psum.46 = f32[2048]{0:T(1024)S(1)} all-reduce(f32[2048]{0:T(1024)S(1)} %broadcast_select_fusion.77), channel_id=1, replica_groups=mesh['dp'=4,'row'=4,'col'=2] {'dp','row'}, use_global_device_ids=true, to_apply=%region_9.10 | all-reduce | flops 2048 | bytes 16384 | tf_op jit(solution)/shard_map/psum | solution.py:73
  647.1 34.0 %psum.45 = f32[4096]{0:T(1024)S(1)} all-reduce(f32[4096]{0:T(1024)S(1)} %pad_maximum_fusion), channel_id=1, replica_groups=mesh['dp'=4,'row'=4,'col'=2] {'dp','col'}, use_global_device_ids=true, to_apply=%region_7.8 | all-reduce | flops 4096 | bytes 32768 | tf_op jit(solution)/shard_map/psum | solution.py:72
  681.7 9.4 fusion.13
  693.1 40.6 %psum.47 = f32[]{:T(128)} all-reduce(f32[]{:T(128)S(6)} %select_n.1308), channel_id=1, replica_groups=mesh['dp'=4,'row'=4,'col'=2] {'dp','row','col'}, use_global_device_ids=true, to_apply=%region_11.12 | all-reduce | flops 1 | bytes 8 | tf_op jit(solution)/shard_map/psum | solution.py:80
  734.4 8.7 fusion.15
  757.8 5.6 collective-permute-start.94
  863.0 5.6 collective-permute-start.116
  879.0 9.6 collective-permute-start.120
  908.2 6.3 collective-permute-start.126
  919.8 7.1 collective-permute-done.126
  939.1 9.2 collective-permute-start.132
  951.9 7.5 collective-permute-start.134
  965.0 5.7 collective-permute-start.136
  976.2 5.7 collective-permute-start.138
  987.5 5.7 collective-permute-start.140
  998.7 5.7 collective-permute-start.142
  1010.0 5.7 collective-permute-start.144
  1021.2 5.7 collective-permute-start.146
  1032.4 5.7 collective-permute-start.148
  1043.7 5.7 collective-permute-start.150
  1057.2 8.9 collective-permute-done.151
  1068.4 8.9 collective-permute-done.153
  1079.7 8.9 collective-permute-done.155
  1101.6 6.2 copy-done.3
  (476 shorter events, 579.7 us)
Async XLA Ops:
  9.6 21.7 %collective-permute-start = (bf16[32,8192]{1,0:T(8,128)(2,1)S(1)}, bf16[32,8192]{1,0:T(8,128)(2,1)}, u32[]{:S(2)}, u32[]{:S(2)}) collective-permute-start(bf16[32,8192]{1,0:T(8,128)(2,1)S(1)} %get-tuple-element.167), channel_id=1, source_target_pairs={{0,8},{1,9},{2,10},{3,11},{4,12},{5,13},{6,14},{7,15}} | collective-permute-start | bytes 1572872 | tf_op jit(solution)/shard_map/ppermute | solution.py:48
  40.7 20.8 %collective-permute-start.2 = (bf16[32,8192]{1,0:T(8,128)(2,1)S(1)}, bf16[32,8192]{1,0:T(8,128)(2,1)}, u32[]{:S(2)}, u32[]{:S(2)}) collective-permute-start(bf16[32,8192]{1,0:T(8,128)(2,1)S(1)} %get-tuple-element.171), channel_id=1, source_target_pairs={{0,8},{8,16},{1,9},{9,17},{2,10},{10,18},{3,11},{11,19},{4,12},{12... | collective-permute-start | bytes 1572872 | tf_op jit(solution)/shard_map/ppermute | solution.py:48
  71.8 20.4 %collective-permute-start.11 = (bf16[32,8192]{1,0:T(8,128)(2,1)S(1)}, bf16[32,8192]{1,0:T(8,128)(2,1)S(1)}, u32[]{:S(2)}, u32[]{:S(2)}) collective-permute-start(bf16[32,8192]{1,0:T(8,128)(2,1)S(1)} %get-tuple-element.178), channel_id=1, source_target_pairs={{0,8},{8,16},{16,24},{1,9},{9,17},{17,25},{2,10},{10,18},{18,26},{... | collective-permute-start | bytes 1572872 | tf_op jit(solution)/shard_map/ppermute | solution.py:48
  76.8 19.9 %collective-permute-start.10 = (bf16[32,8192]{1,0:T(8,128)(2,1)S(1)}, bf16[32,8192]{1,0:T(8,128)(2,1)S(1)}, u32[]{:S(2)}, u32[]{:S(2)}) collective-permute-start(bf16[32,8192]{1,0:T(8,128)(2,1)S(1)} %get-tuple-element.177), channel_id=1, source_target_pairs={{24,16},{16,8},{8,0},{25,17},{17,9},{9,1},{26,18},{18,10},{10,2},{... | collective-permute-start | bytes 1572872 | tf_op jit(solution)/shard_map/ppermute | solution.py:48
  200.1 28.4 %collective-permute-start.37 = (bf16[128,2048]{1,0:T(8,128)(2,1)S(1)}, bf16[128,2048]{1,0:T(8,128)(2,1)S(1)}, u32[]{:S(2)}, u32[]{:S(2)}) collective-permute-start(bf16[128,2048]{1,0:T(8,128)(2,1)S(1)} %get-tuple-element.202), channel_id=1, source_target_pairs={{24,16},{25,17},{26,18},{27,19},{28,20},{29,21},{30,22},{31,23}} | collective-permute-start | bytes 1572872 | tf_op jit(solution)/shard_map/ppermute | solution.py:48
  201.3 27.2 %collective-permute-start.36 = (bf16[128,2048]{1,0:T(8,128)(2,1)S(1)}, bf16[128,2048]{1,0:T(8,128)(2,1)S(1)}, u32[]{:S(2)}, u32[]{:S(2)}) collective-permute-start(bf16[128,2048]{1,0:T(8,128)(2,1)S(1)} %get-tuple-element.201), channel_id=1, source_target_pairs={{0,8},{1,9},{2,10},{3,11},{4,12},{5,13},{6,14},{7,15}} | collective-permute-start | bytes 1572872 | tf_op jit(solution)/shard_map/ppermute | solution.py:48
  209.4 24.4 %collective-permute-start.35 = (bf16[32,8192]{1,0:T(8,128)(2,1)S(1)}, bf16[32,8192]{1,0:T(8,128)(2,1)S(1)}, u32[]{:S(2)}, u32[]{:S(2)}) collective-permute-start(bf16[32,8192]{1,0:T(8,128)(2,1)S(1)} %get-tuple-element.204), channel_id=1, source_target_pairs={{8,16},{16,24},{9,17},{17,25},{10,18},{18,26},{11,19},{19,27},{12,... | collective-permute-start | bytes 1572872 | tf_op jit(solution)/shard_map/ppermute | solution.py:48
  233.1 112.1 %collective-permute-start.45 = (bf16[128,2048]{1,0:T(8,128)(2,1)S(1)}, bf16[128,2048]{1,0:T(8,128)(2,1)S(1)}, u32[]{:S(2)}, u32[]{:S(2)}) collective-permute-start(bf16[128,2048]{1,0:T(8,128)(2,1)S(1)} %get-tuple-element.210), channel_id=1, source_target_pairs={{24,16},{16,8},{25,17},{17,9},{26,18},{18,10},{27,19},{19,11},{28,... | collective-permute-start | bytes 1572872 | tf_op jit(solution)/shard_map/ppermute | solution.py:48
  233.8 111.4 %collective-permute-start.44 = (bf16[128,2048]{1,0:T(8,128)(2,1)S(1)}, bf16[128,2048]{1,0:T(8,128)(2,1)S(1)}, u32[]{:S(2)}, u32[]{:S(2)}) collective-permute-start(bf16[128,2048]{1,0:T(8,128)(2,1)S(1)} %get-tuple-element.209), channel_id=1, source_target_pairs={{0,8},{8,16},{1,9},{9,17},{2,10},{10,18},{3,11},{11,19},{4,12},{12... | collective-permute-start | bytes 1572872 | tf_op jit(solution)/shard_map/ppermute | solution.py:48
  248.4 96.8 %collective-permute-start.49 = (bf16[128,2048]{1,0:T(8,128)(2,1)S(1)}, bf16[128,2048]{1,0:T(8,128)(2,1)}, u32[]{:S(2)}, u32[]{:S(2)}) collective-permute-start(bf16[128,2048]{1,0:T(8,128)(2,1)S(1)} %get-tuple-element.214), channel_id=1, source_target_pairs={{24,16},{16,8},{25,17},{17,9},{26,18},{18,10},{27,19},{19,11},{28,... | collective-permute-start | bytes 1572872 | tf_op jit(solution)/shard_map/ppermute | solution.py:48
  255.5 89.7 %collective-permute-start.48 = (bf16[128,2048]{1,0:T(8,128)(2,1)S(1)}, bf16[128,2048]{1,0:T(8,128)(2,1)}, u32[]{:S(2)}, u32[]{:S(2)}) collective-permute-start(bf16[128,2048]{1,0:T(8,128)(2,1)S(1)} %get-tuple-element.213), channel_id=1, source_target_pairs={{0,8},{8,16},{1,9},{9,17},{2,10},{10,18},{3,11},{11,19},{4,12},{12... | collective-permute-start | bytes 1572872 | tf_op jit(solution)/shard_map/ppermute | solution.py:48
  347.9 61.7 %collective-permute-start.47 = (bf16[128,2048]{1,0:T(8,128)(2,1)S(1)}, bf16[128,2048]{1,0:T(8,128)(2,1)S(1)}, u32[]{:S(2)}, u32[]{:S(2)}) collective-permute-start(bf16[128,2048]{1,0:T(8,128)(2,1)S(1)} %get-tuple-element.216), channel_id=1, source_target_pairs={{24,16},{16,8},{8,0},{25,17},{17,9},{9,1},{26,18},{18,10},{10,2},{... | collective-permute-start | bytes 1572872 | tf_op jit(solution)/shard_map/ppermute | solution.py:48
  349.2 60.4 %collective-permute-start.46 = (bf16[128,2048]{1,0:T(8,128)(2,1)S(1)}, bf16[128,2048]{1,0:T(8,128)(2,1)}, u32[]{:S(2)}, u32[]{:S(2)}) collective-permute-start(bf16[128,2048]{1,0:T(8,128)(2,1)S(1)} %get-tuple-element.215), channel_id=1, source_target_pairs={{0,8},{8,16},{16,24},{1,9},{9,17},{17,25},{2,10},{10,18},{18,26},{... | collective-permute-start | bytes 1572872 | tf_op jit(solution)/shard_map/ppermute | solution.py:48
  423.8 27.3 %collective-permute-start.57 = (bf16[128,2048]{1,0:T(8,128)(2,1)}, bf16[128,2048]{1,0:T(8,128)(2,1)S(1)}, u32[]{:S(2)}, u32[]{:S(2)}) collective-permute-start(bf16[128,2048]{1,0:T(8,128)(2,1)} %get-tuple-element.222), channel_id=1, source_target_pairs={{24,16},{16,8},{8,0},{25,17},{17,9},{9,1},{26,18},{18,10},{10,2},{... | collective-permute-start | bytes 1572872 | tf_op jit(solution)/shard_map/ppermute | solution.py:48
  425.1 26.0 %collective-permute-start.56 = (bf16[128,2048]{1,0:T(8,128)(2,1)S(1)}, bf16[128,2048]{1,0:T(8,128)(2,1)S(1)}, u32[]{:S(2)}, u32[]{:S(2)}) collective-permute-start(bf16[128,2048]{1,0:T(8,128)(2,1)S(1)} %get-tuple-element.221), channel_id=1, source_target_pairs={{0,8},{8,16},{16,24},{1,9},{9,17},{17,25},{2,10},{10,18},{18,26},{... | collective-permute-start | bytes 1572872 | tf_op jit(solution)/shard_map/ppermute | solution.py:48
  434.7 24.8 %collective-permute-start.55 = (bf16[128,2048]{1,0:T(8,128)(2,1)S(1)}, bf16[128,2048]{1,0:T(8,128)(2,1)S(1)}, u32[]{:S(2)}, u32[]{:S(2)}) collective-permute-start(bf16[128,2048]{1,0:T(8,128)(2,1)S(1)} %get-tuple-element.224), channel_id=1, source_target_pairs={{24,16},{16,8},{8,0},{25,17},{17,9},{9,1},{26,18},{18,10},{10,2},{... | collective-permute-start | bytes 1572872 | tf_op jit(solution)/shard_map/ppermute | solution.py:48
  436.0 23.6 %collective-permute-start.54 = (bf16[128,2048]{1,0:T(8,128)(2,1)S(1)}, bf16[128,2048]{1,0:T(8,128)(2,1)S(1)}, u32[]{:S(2)}, u32[]{:S(2)}) collective-permute-start(bf16[128,2048]{1,0:T(8,128)(2,1)S(1)} %get-tuple-element.223), channel_id=1, source_target_pairs={{0,8},{8,16},{16,24},{1,9},{9,17},{17,25},{2,10},{10,18},{18,26},{... | collective-permute-start | bytes 1572872 | tf_op jit(solution)/shard_map/ppermute | solution.py:48
  504.9 19.7 %collective-permute-start.67 = (bf16[128,2048]{1,0:T(8,128)(2,1)}, bf16[128,2048]{1,0:T(8,128)(2,1)S(1)}, u32[]{:S(2)}, u32[]{:S(2)}) collective-permute-start(bf16[128,2048]{1,0:T(8,128)(2,1)} %get-tuple-element.236), channel_id=1, source_target_pairs={{24,16},{16,8},{8,0},{25,17},{17,9},{9,1},{26,18},{18,10},{10,2},{... | collective-permute-start | bytes 1572872 | tf_op jit(solution)/shard_map/ppermute | solution.py:48
  506.2 19.7 %collective-permute-start.66 = (bf16[128,2048]{1,0:T(8,128)(2,1)S(1)}, bf16[128,2048]{1,0:T(8,128)(2,1)S(1)}, u32[]{:S(2)}, u32[]{:S(2)}) collective-permute-start(bf16[128,2048]{1,0:T(8,128)(2,1)S(1)} %get-tuple-element.235), channel_id=1, source_target_pairs={{0,8},{8,16},{16,24},{1,9},{9,17},{17,25},{2,10},{10,18},{18,26},{... | collective-permute-start | bytes 1572872 | tf_op jit(solution)/shard_map/ppermute | solution.py:48
  517.2 19.9 %collective-permute-start.72 = (bf16[128,2048]{1,0:T(8,128)(2,1)S(1)}, bf16[128,2048]{1,0:T(8,128)(2,1)S(1)}, u32[]{:S(2)}, u32[]{:S(2)}) collective-permute-start(bf16[128,2048]{1,0:T(8,128)(2,1)S(1)} %get-tuple-element.237), channel_id=1, source_target_pairs={{0,8},{8,16},{16,24},{1,9},{9,17},{17,25},{2,10},{10,18},{18,26},{... | collective-permute-start | bytes 1572872 | tf_op jit(solution)/shard_map/ppermute | solution.py:48
  527.2 21.2 %collective-permute-start.70 = (bf16[32,8192]{1,0:T(8,128)(2,1)S(1)}, bf16[32,8192]{1,0:T(8,128)(2,1)S(1)}, u32[]{:S(2)}, u32[]{:S(2)}) collective-permute-start(bf16[32,8192]{1,0:T(8,128)(2,1)S(1)} %get-tuple-element.240), channel_id=1, source_target_pairs={{0,8},{1,9},{2,10},{3,11},{4,12},{5,13},{6,14},{7,15}} | collective-permute-start | bytes 1572872 | tf_op jit(solution)/shard_map/ppermute | solution.py:48
  538.4 26.2 %collective-permute-start.74 = (bf16[32,8192]{1,0:T(8,128)(2,1)S(1)}, bf16[32,8192]{1,0:T(8,128)(2,1)}, u32[]{:S(2)}, u32[]{:S(2)}) collective-permute-start(bf16[32,8192]{1,0:T(8,128)(2,1)S(1)} %get-tuple-element.244), channel_id=1, source_target_pairs={{0,8},{1,9},{2,10},{3,11},{4,12},{5,13},{6,14},{7,15}} | collective-permute-start | bytes 1572872 | tf_op jit(solution)/shard_map/ppermute | solution.py:48
  555.5 20.5 %collective-permute-start.78 = (bf16[32,8192]{1,0:T(8,128)(2,1)S(1)}, bf16[32,8192]{1,0:T(8,128)(2,1)}, u32[]{:S(2)}, u32[]{:S(2)}) collective-permute-start(bf16[32,8192]{1,0:T(8,128)(2,1)S(1)} %get-tuple-element.247), channel_id=1, source_target_pairs={{0,8},{8,16},{1,9},{9,17},{2,10},{10,18},{3,11},{11,19},{4,12},{12... | collective-permute-start | bytes 1572872 | tf_op jit(solution)/shard_map/ppermute | solution.py:48
  576.9 22.4 %collective-permute-start.88 = (bf16[128,2048]{1,0:T(8,128)(2,1)S(1)}, bf16[128,2048]{1,0:T(8,128)(2,1)S(1)}, u32[]{:S(2)}, u32[]{:S(2)}) collective-permute-start(bf16[128,2048]{1,0:T(8,128)(2,1)S(1)} %get-tuple-element.253), channel_id=1, source_target_pairs={{16,24},{17,25},{18,26},{19,27},{20,28},{21,29},{22,30},{23,31}} | collective-permute-start | bytes 1572872 | tf_op jit(solution)/shard_map/ppermute | solution.py:48
  579.5 19.7 %collective-permute-start.89 = (bf16[128,2048]{1,0:T(8,128)(2,1)S(1)}, bf16[128,2048]{1,0:T(8,128)(2,1)S(1)}, u32[]{:S(2)}, u32[]{:S(2)}) collective-permute-start(bf16[128,2048]{1,0:T(8,128)(2,1)S(1)} %get-tuple-element.254), channel_id=1, source_target_pairs={{8,0},{9,1},{10,2},{11,3},{12,4},{13,5},{14,6},{15,7}} | collective-permute-start | bytes 1572872 | tf_op jit(solution)/shard_map/ppermute | solution.py:48
  581.0 165.8 %collective-permute-start.86 = (bf16[32,8192]{1,0:T(8,128)(2,1)S(1)}, bf16[32,8192]{1,0:T(8,128)(2,1)}, u32[]{:S(2)}, u32[]{:S(2)}) collective-permute-start(bf16[32,8192]{1,0:T(8,128)(2,1)S(1)} %get-tuple-element.255), channel_id=1, source_target_pairs={{0,8},{8,16},{16,24},{1,9},{9,17},{17,25},{2,10},{10,18},{18,26},{... | collective-permute-start | bytes 1572872 | tf_op jit(solution)/shard_map/ppermute | solution.py:48
  589.9 158.8 %collective-permute-start.87 = (bf16[32,8192]{1,0:T(8,128)(2,1)}, bf16[32,8192]{1,0:T(8,128)(2,1)}, u32[]{:S(2)}, u32[]{:S(2)}) collective-permute-start(bf16[32,8192]{1,0:T(8,128)(2,1)} %get-tuple-element.256), channel_id=1, source_target_pairs={{24,16},{16,8},{8,0},{25,17},{17,9},{9,1},{26,18},{18,10},{10,2},{... | collective-permute-start | bytes 1572872 | tf_op jit(solution)/shard_map/ppermute | solution.py:48
  599.3 155.6 %collective-permute-start.90 = (bf16[32,8192]{1,0:T(8,128)(2,1)}, bf16[32,8192]{1,0:T(8,128)(2,1)}, u32[]{:S(2)}, u32[]{:S(2)}) collective-permute-start(bf16[32,8192]{1,0:T(8,128)(2,1)} %get-tuple-element.257), channel_id=1, source_target_pairs={{0,8},{8,16},{16,24},{1,9},{9,17},{17,25},{2,10},{10,18},{18,26},{... | collective-permute-start | bytes 1572872 | tf_op jit(solution)/shard_map/ppermute | solution.py:48
  691.8 64.1 %collective-permute-start.91 = (bf16[32,8192]{1,0:T(8,128)(2,1)}, bf16[32,8192]{1,0:T(8,128)(2,1)}, u32[]{:S(2)}, u32[]{:S(2)}) collective-permute-start(bf16[32,8192]{1,0:T(8,128)(2,1)} %get-tuple-element.258), channel_id=1, source_target_pairs={{24,16},{16,8},{8,0},{25,17},{17,9},{9,1},{26,18},{18,10},{10,2},{... | collective-permute-start | bytes 1572872 | tf_op jit(solution)/shard_map/ppermute | solution.py:48
  757.8 19.4 %collective-permute-start.94 = (bf16[32,8192]{1,0:T(8,128)(2,1)S(1)}, bf16[32,8192]{1,0:T(8,128)(2,1)S(1)}, u32[]{:S(2)}, u32[]{:S(2)}) collective-permute-start(bf16[32,8192]{1,0:T(8,128)(2,1)S(1)} %get-tuple-element.261), channel_id=1, source_target_pairs={{0,8},{8,16},{16,24},{1,9},{9,17},{17,25},{2,10},{10,18},{18,26},{... | collective-permute-start | bytes 1572872 | tf_op jit(solution)/shard_map/ppermute | solution.py:48
  773.7 19.0 %collective-permute-start.97 = (bf16[32,8192]{1,0:T(8,128)(2,1)S(1)}, bf16[32,8192]{1,0:T(8,128)(2,1)S(1)}, u32[]{:S(2)}, u32[]{:S(2)}) collective-permute-start(bf16[32,8192]{1,0:T(8,128)(2,1)S(1)} %get-tuple-element.264), channel_id=1, source_target_pairs={{24,16},{16,8},{8,0},{25,17},{17,9},{9,1},{26,18},{18,10},{10,2},{... | collective-permute-start | bytes 1572872 | tf_op jit(solution)/shard_map/ppermute | solution.py:48
  796.2 19.0 %collective-permute-start.101 = (bf16[32,8192]{1,0:T(8,128)(2,1)S(1)}, bf16[32,8192]{1,0:T(8,128)(2,1)S(1)}, u32[]{:S(2)}, u32[]{:S(2)}) collective-permute-start(bf16[32,8192]{1,0:T(8,128)(2,1)S(1)} %get-tuple-element.268), channel_id=1, source_target_pairs={{24,16},{16,8},{8,0},{25,17},{17,9},{9,1},{26,18},{18,10},{10,2},{... | collective-permute-start | bytes 1572872 | tf_op jit(solution)/shard_map/ppermute | solution.py:48
  818.7 19.0 %collective-permute-start.105 = (bf16[32,8192]{1,0:T(8,128)(2,1)S(1)}, bf16[32,8192]{1,0:T(8,128)(2,1)S(1)}, u32[]{:S(2)}, u32[]{:S(2)}) collective-permute-start(bf16[32,8192]{1,0:T(8,128)(2,1)S(1)} %get-tuple-element.272), channel_id=1, source_target_pairs={{24,16},{16,8},{8,0},{25,17},{17,9},{9,1},{26,18},{18,10},{10,2},{... | collective-permute-start | bytes 1572872 | tf_op jit(solution)/shard_map/ppermute | solution.py:48
  852.4 19.0 %collective-permute-start.111 = (bf16[32,8192]{1,0:T(8,128)(2,1)S(1)}, bf16[32,8192]{1,0:T(8,128)(2,1)S(1)}, u32[]{:S(2)}, u32[]{:S(2)}) collective-permute-start(bf16[32,8192]{1,0:T(8,128)(2,1)S(1)} %get-tuple-element.278), channel_id=1, source_target_pairs={{24,16},{16,8},{8,0},{25,17},{17,9},{9,1},{26,18},{18,10},{10,2},{... | collective-permute-start | bytes 1572872 | tf_op jit(solution)/shard_map/ppermute | solution.py:48
  861.0 27.6 %collective-permute-start.112 = (bf16[32,8192]{1,0:T(8,128)(2,1)S(1)}, bf16[32,8192]{1,0:T(8,128)(2,1)S(1)}, u32[]{:S(2)}, u32[]{:S(2)}) collective-permute-start(bf16[32,8192]{1,0:T(8,128)(2,1)S(1)} %get-tuple-element.280), channel_id=1, source_target_pairs={{8,16},{16,24},{9,17},{17,25},{10,18},{18,26},{11,19},{19,27},{12,... | collective-permute-start | bytes 1572872 | tf_op jit(solution)/shard_map/ppermute | solution.py:48
  861.7 28.5 %collective-permute-start.113 = (bf16[32,8192]{1,0:T(8,128)(2,1)S(1)}, bf16[32,8192]{1,0:T(8,128)(2,1)S(1)}, u32[]{:S(2)}, u32[]{:S(2)}) collective-permute-start(bf16[32,8192]{1,0:T(8,128)(2,1)S(1)} %get-tuple-element.281), channel_id=1, source_target_pairs={{16,8},{8,0},{17,9},{9,1},{18,10},{10,2},{19,11},{11,3},{20,12},{1... | collective-permute-start | bytes 1572872 | tf_op jit(solution)/shard_map/ppermute | solution.py:48
  877.7 19.0 %collective-permute-start.115 = (bf16[32,8192]{1,0:T(8,128)(2,1)S(1)}, bf16[32,8192]{1,0:T(8,128)(2,1)S(1)}, u32[]{:S(2)}, u32[]{:S(2)}) collective-permute-start(bf16[32,8192]{1,0:T(8,128)(2,1)S(1)} %get-tuple-element.285), channel_id=1, source_target_pairs={{16,8},{8,0},{17,9},{9,1},{18,10},{10,2},{19,11},{11,3},{20,12},{1... | collective-permute-start | bytes 1572872 | tf_op jit(solution)/shard_map/ppermute | solution.py:48
  879.0 20.6 %collective-permute-start.120 = (bf16[128,2048]{1,0:T(8,128)(2,1)S(1)}, bf16[128,2048]{1,0:T(8,128)(2,1)S(1)}, u32[]{:S(2)}, u32[]{:S(2)}) collective-permute-start(bf16[128,2048]{1,0:T(8,128)(2,1)S(1)} %get-tuple-element.287), channel_id=1, source_target_pairs={{0,8},{1,9},{2,10},{3,11},{4,12},{5,13},{6,14},{7,15}} | collective-permute-start | bytes 1572872 | tf_op jit(solution)/shard_map/ppermute | solution.py:48
  891.1 23.7 %collective-permute-start.118 = (bf16[32,8192]{1,0:T(8,128)(2,1)S(1)}, bf16[32,8192]{1,0:T(8,128)(2,1)S(1)}, u32[]{:S(2)}, u32[]{:S(2)}) collective-permute-start(bf16[32,8192]{1,0:T(8,128)(2,1)S(1)} %get-tuple-element.288), channel_id=1, source_target_pairs={{16,24},{17,25},{18,26},{19,27},{20,28},{21,29},{22,30},{23,31}} | collective-permute-start | bytes 1572872 | tf_op jit(solution)/shard_map/ppermute | solution.py:48
  891.8 23.7 %collective-permute-start.119 = (bf16[32,8192]{1,0:T(8,128)(2,1)S(1)}, bf16[32,8192]{1,0:T(8,128)(2,1)S(1)}, u32[]{:S(2)}, u32[]{:S(2)}) collective-permute-start(bf16[32,8192]{1,0:T(8,128)(2,1)S(1)} %get-tuple-element.289), channel_id=1, source_target_pairs={{8,0},{9,1},{10,2},{11,3},{12,4},{13,5},{14,6},{15,7}} | collective-permute-start | bytes 1572872 | tf_op jit(solution)/shard_map/ppermute | solution.py:48
  900.6 27.9 %collective-permute-start.122 = (bf16[32,8192]{1,0:T(8,128)(2,1)S(1)}, bf16[32,8192]{1,0:T(8,128)(2,1)S(1)}, u32[]{:S(2)}, u32[]{:S(2)}) collective-permute-start(bf16[32,8192]{1,0:T(8,128)(2,1)S(1)} %get-tuple-element.292), channel_id=1, source_target_pairs={{16,24},{17,25},{18,26},{19,27},{20,28},{21,29},{22,30},{23,31}} | collective-permute-start | bytes 1572872 | tf_op jit(solution)/shard_map/ppermute | solution.py:48
  906.5 22.1 %collective-permute-start.123 = (bf16[32,8192]{1,0:T(8,128)(2,1)S(1)}, bf16[32,8192]{1,0:T(8,128)(2,1)S(1)}, u32[]{:S(2)}, u32[]{:S(2)}) collective-permute-start(bf16[32,8192]{1,0:T(8,128)(2,1)S(1)} %get-tuple-element.293), channel_id=1, source_target_pairs={{8,0},{9,1},{10,2},{11,3},{12,4},{13,5},{14,6},{15,7}} | collective-permute-start | bytes 1572872 | tf_op jit(solution)/shard_map/ppermute | solution.py:48
  915.5 22.7 %collective-permute-start.128 = (bf16[128,2048]{1,0:T(8,128)(2,1)S(1)}, bf16[128,2048]{1,0:T(8,128)(2,1)S(1)}, u32[]{:S(2)}, u32[]{:S(2)}) collective-permute-start(bf16[128,2048]{1,0:T(8,128)(2,1)S(1)} %get-tuple-element.296), channel_id=1, source_target_pairs={{0,8},{8,16},{16,24},{1,9},{9,17},{17,25},{2,10},{10,18},{18,26},{... | collective-permute-start | bytes 1572872 | tf_op jit(solution)/shard_map/ppermute | solution.py:48
  928.6 23.0 %collective-permute-start.130 = (bf16[128,2048]{1,0:T(8,128)(2,1)S(1)}, bf16[128,2048]{1,0:T(8,128)(2,1)S(1)}, u32[]{:S(2)}, u32[]{:S(2)}) collective-permute-start(bf16[128,2048]{1,0:T(8,128)(2,1)S(1)} %get-tuple-element.298), channel_id=1, source_target_pairs={{0,8},{8,16},{16,24},{1,9},{9,17},{17,25},{2,10},{10,18},{18,26},{... | collective-permute-start | bytes 1572872 | tf_op jit(solution)/shard_map/ppermute | solution.py:48
  939.1 21.7 %collective-permute-start.132 = (bf16[128,2048]{1,0:T(8,128)(2,1)S(1)}, bf16[128,2048]{1,0:T(8,128)(2,1)S(1)}, u32[]{:S(2)}, u32[]{:S(2)}) collective-permute-start(bf16[128,2048]{1,0:T(8,128)(2,1)S(1)} %get-tuple-element.300), channel_id=1, source_target_pairs={{0,8},{8,16},{16,24},{1,9},{9,17},{17,25},{2,10},{10,18},{18,26},{... | collective-permute-start | bytes 1572872 | tf_op jit(solution)/shard_map/ppermute | solution.py:48
  951.9 20.1 %collective-permute-start.134 = (bf16[128,2048]{1,0:T(8,128)(2,1)S(1)}, bf16[128,2048]{1,0:T(8,128)(2,1)S(1)}, u32[]{:S(2)}, u32[]{:S(2)}) collective-permute-start(bf16[128,2048]{1,0:T(8,128)(2,1)S(1)} %get-tuple-element.302), channel_id=1, source_target_pairs={{0,8},{8,16},{16,24},{1,9},{9,17},{17,25},{2,10},{10,18},{18,26},{... | collective-permute-start | bytes 1572872 | tf_op jit(solution)/shard_map/ppermute | solution.py:48
  1055.7 21.6 %collective-permute-start.153 = (bf16[128,2048]{1,0:T(8,128)(2,1)S(1)}, bf16[128,2048]{1,0:T(8,128)(2,1)S(1)}, u32[]{:S(2)}, u32[]{:S(2)}) collective-permute-start(bf16[128,2048]{1,0:T(8,128)(2,1)S(1)} %get-tuple-element.321), channel_id=1, source_target_pairs={{16,8},{8,0},{17,9},{9,1},{18,10},{10,2},{19,11},{11,3},{20,12},{1... | collective-permute-start | bytes 1572872 | tf_op jit(solution)/shard_map/ppermute | solution.py:48
  1067.0 21.6 %collective-permute-start.155 = (bf16[128,2048]{1,0:T(8,128)(2,1)S(1)}, bf16[128,2048]{1,0:T(8,128)(2,1)S(1)}, u32[]{:S(2)}, u32[]{:S(2)}) collective-permute-start(bf16[128,2048]{1,0:T(8,128)(2,1)S(1)} %get-tuple-element.323), channel_id=1, source_target_pairs={{16,8},{8,0},{17,9},{9,1},{18,10},{10,2},{19,11},{11,3},{20,12},{1... | collective-permute-start | bytes 1572872 | tf_op jit(solution)/shard_map/ppermute | solution.py:48
  (135 other events, 3014.8 us)

commit v2 on v1

v2 whole, which is shorter than its diff:
```python
import jax
import jax.numpy as jnp
from jax import lax
from jax.sharding import PartitionSpec as P

BETA = 0.8
EPS_SQUARE = 1e-30
CHUNKS = 32
LAG = 2
GROUPS = 4
FAR = 3


def chunk_count(rows):
    half = rows // 2
    count = CHUNKS
    while half % count or (half // count) % 8:
        count //= 2
    return count


def make_local(axis_sizes):
    n_dp, n_row, n_col = axis_sizes["dp"], axis_sizes["row"], axis_sizes["col"]
    last = n_dp - 1

    def spread_ends(value):
        total = value
        for j in range(1, n_dp):
            pairs = [[(0, j)], [(last, last - j)]]
            if j != last - j:
                pairs = [pairs[0] + pairs[1]]
            for some in pairs:
                total = total + lax.ppermute(value, "dp", some)
        return total

    def butterfly(value, axis, distance):
        n = axis_sizes[axis]
        return value + lax.ppermute(value, axis, [(i, i ^ distance) for i in range(n)])

    def distances(axis):
        out, d = [], 1
        while d < axis_sizes[axis]:
            out.append(d)
            d *= 2
        return out

    def local(grad_wi, grad_wo, row_wi, col_wi, row_wo, col_wo):
        f32, bf16 = jnp.float32, jnp.bfloat16
        place = lax.axis_index("dp")
        grads = (grad_wi[0], grad_wo[0])
        prevs = ((row_wi, col_wi), (row_wo, col_wo))
        shapes = [g.shape for g in grads]
        counts = [chunk_count(rows) for rows, _ in shapes]
        sizes = [rows // 2 // count for (rows, _), count in zip(shapes, counts)]

        at_end = (place == last) | (place == 0)

        segments = []
        start = 0
        for kind in ("sum", "spread"):
            for m in range(2):
                segments.append((kind, m, start))
                start += counts[m]
        steps = start + LAG * last

        def hop(value, direction, senders):
            pairs = []
            for p in senders:
                if p < last:
                    pairs.append((p, p + 1) if direction == 0 else (last - p, last - p - 1))
            return lax.ppermute(value, "dp", pairs)

        held = {0: [], 1: []}
        scales = {}
        results = {}
        cell = [None]

        def settle(value):
            value, _ = lax.optimization_barrier((value, cell[0]))
            return value

        def group_of(m, g):
            per = counts[m] // GROUPS
            return jnp.concatenate(held[m][g * per : (g + 1) * per])

        def statistics(m):
            rows, cols = shapes[m]
            half = rows // 2
            per = counts[m] // GROUPS
            row_parts, col_part = [], None
            for g in range(GROUPS):
                while len(held[m]) < (g + 1) * per:
                    yield [], 1
                wide = settle(group_of(m, g)).astype(f32)
                square = wide * wide + EPS_SQUARE
                row_parts.append(jnp.sum(square, axis=1))
                part = jnp.sum(square, axis=0)
                col_part = part if col_part is None else col_part + part
                yield [row_parts[-1], col_part], 1
            row_part = jnp.concatenate(row_parts)
            levels = max(len(distances("row")), len(distances("col")))
            for level in range(levels):
                row_part, col_part = settle((row_part, col_part))
                if level < len(distances("col")):
                    row_part = butterfly(row_part, "col", distances("col")[level])
                if level < len(distances("row")):
                    col_part = butterfly(col_part, "row", distances("row")[level])
                yield [], 1
            row_part, col_part = settle((row_part, col_part))
            packed = jnp.concatenate(
                [
                    jnp.where(place == last, row_part, 0.0),
                    jnp.where(place == 0, row_part, 0.0),
                    jnp.where(at_end, col_part, 0.0),
                ]
            )
            packed = spread_ends(packed)
            yield [], FAR
            packed = settle(packed)
            row_new = BETA * prevs[m][0] + (1.0 - BETA) * (packed[:rows] / (cols * n_col))
            col_new = BETA * prevs[m][1] + (1.0 - BETA) * (packed[rows:] / (rows * n_row))
            row_scale = lax.rsqrt(jnp.where(place == 0, row_new[half:], row_new[:half]))
            col_scale = lax.rsqrt(col_new)
            yield [row_scale, col_scale], 1
            energy = None
            for g in range(GROUPS):
                own_rows = row_scale[g * half // GROUPS : (g + 1) * half // GROUPS]
                wide = settle(group_of(m, g)).astype(f32)
                raw = wide * own_rows[:, None] * col_scale[None, :]
                part = jnp.sum(raw * raw)
                energy = part if energy is None else energy + part
                yield [energy], 1
            energy = jnp.broadcast_to(energy, (8, 128))
            for axis in ("col", "row"):
                for distance in distances(axis):
                    energy = butterfly(settle(energy), axis, distance)
                    yield [], 1
            energy = settle(energy)
            energy = energy + lax.ppermute(energy, "dp", [(0, last), (last, 0)])
            yield [], FAR
            energy = settle(energy)[0, 0]
            rms = jnp.sqrt(energy / (rows * n_row * cols * n_col))
            row_final = row_scale / jnp.maximum(1.0, rms)
            scales[m] = (row_final, col_scale)
            results[m] = (row_new, col_new)
            yield [row_final], 1

        workers = [statistics(0), statistics(1)]
        wakes = [0, 0]

        def advance(m):
            try:
                ties, wait = next(workers[m])
            except StopIteration:
                return [], steps
            return ties, wait

        outs = [jnp.zeros(shape, bf16) for shape in shapes]
        inflight = {}
        latest = {}
        arrived = {}
        tied = []
        for s in range(steps):
            active = []
            for index, (kind, m, begin) in enumerate(segments):
                members = [p for p in range(n_dp) if 0 <= s - LAG * p - begin < counts[m]]
                if members:
                    active.append((index, kind, m, begin, members))
                if members and kind == "spread" and m not in scales:
                    while m not in scales:
                        advance(m)
                    wakes[m] = steps
            gots = [
                inflight.pop((index, d, s - LAG), None)
                for index, _, _, _, _ in active
                for d in range(2)
            ]
            here = place
            position = (here, last - here)
            before, tied = tied, []
            batch = []
            turn = 0
            for index, kind, m, begin, members in active:
                size = sizes[m]
                half = shapes[m][0] // 2
                cols = shapes[m][1]
                ending = {}
                for d in range(2):
                    got = gots[turn]
                    turn += 1
                    at = jnp.clip(s - begin - LAG * position[d], 0, counts[m] - 1) * size
                    if kind == "sum":
                        own = lax.dynamic_slice(grads[m], (d * half + at, 0), (size, cols))
                        value = own
                        if got is not None:
                            value = (got.astype(f32) + own.astype(f32)).astype(bf16)
                        ending[d] = value
                    else:
                        value = got
                        if 0 in members:
                            k = s - begin
                            per = counts[m] // GROUPS
                            low = (k % per) * size
                            row_final, col_scale = scales[m]
                            wide = group_of(m, k // per)[low : low + size].astype(f32)
                            rows_here = row_final[k * size : (k + 1) * size]
                            mine = (wide * rows_here[:, None] * col_scale[None, :]).astype(bf16)
                            value = mine if got is None else jnp.where(position[d] == 0, mine, got)
                        elif got is not None:
                            done = s - LAG * position[d] - begin >= counts[m]
                            value = jnp.where(done, latest[m, d], got)
                        latest[m, d] = value
                        outs[m] = lax.dynamic_update_slice(
                            outs[m], value, ((1 - d) * half + at, 0)
                        )
                    if min(members) < last:
                        batch.append((index, d, members, value))
                        tied.append(value)
                if kind == "sum" and last in members:
                    held[m].append(jnp.where(here == 0, ending[1], ending[0]))
            if batch:
                values, _ = lax.optimization_barrier(([b[3] for b in batch], (before, arrived.get(s - LAG, []))))
                tied = list(values)
            arrived[s] = []
            for (index, d, members, _), value in zip(batch, tied):
                inflight[index, d, s] = hop(value, d, members)
                arrived[s].append(inflight[index, d, s])
            cell[0] = list(tied)
            for m in range(2):
                if s >= wakes[m]:
                    ties, wait = advance(m)
                    tied = tied + ties
                    wakes[m] = s + wait
        return (outs[0], *results[0], outs[1], *results[1])

    return local


def solution(mesh):
    return jax.shard_map(
        make_local(dict(mesh.shape)),
        mesh=mesh,
        in_specs=(
            P("dp", "row", "col"),
            P("dp", "row", "col"),
            P("row"),
            P("col"),
            P("row"),
            P("col"),
        ),
        out_specs=(P("row", "col"), P("row"), P("col"), P("row", "col"), P("row"), P("col")),
        check_vma=False,
    )
```

time: 1120 us -> 1200 us (1.071)
  starting transfers between devices: 422 us -> 767 us
  blocking collectives: 218 us -> 0 us
  waiting for transfers between devices: 280 us -> 126 us
  other arithmetic: 154 us -> 247 us
    ppermute x160 -> x308, starting transfers between devices: 422 us -> 767 us  [the longest x288 737 us: hop(): return lax.ppermute(value, 'dp', pairs)]
    psum x6 -> x0, blocking collectives: 218 us -> none  [the longest x2 87.7 us: statistics(): col_sum = lax.psum(jnp.where(at_end, col_part, 0.0), ('dp', 'row'))]
    ppermute x160 -> x308, waiting for transfers between devices: 280 us -> 126 us  [the longest x288 117 us: hop(): return lax.ppermute(value, 'dp', pairs)]
    dynamic_update_slice x80 -> x148, other arithmetic: 44.9 us -> 107 us  [local(): outs[m] = lax.dynamic_update_slice(outs[m], value, ((1 - d) * half + at, 0))]
    unnamed x34 -> x51, other arithmetic: 45.6 us -> 78.9 us
    convert_element_type x2 -> x0, other arithmetic: 18.8 us -> none  [raw_update(): return (wide * row_final[:, None] * col_scale[None, :]).astype(bf16)]
    concatenate x2 -> x9, other arithmetic: 1.39 us -> 14.6 us  [the longest x7 14.5 us: group_of(): return jnp.concatenate(held[m][g * per:(g + 1) * per])]
    reduce_sum x4 -> x16, other arithmetic: 32.1 us -> 38 us  [the longest x8 24.7 us: statistics(): part = jnp.sum(raw * raw)]
  transfers between devices with their start and end apart: 160 -> 308, of which waited for: 81 -> 60; matrix products, arithmetic and copies ran while one was open for 14% -> 21% of each run, Pallas kernels for 0% -> 0%
where the time goes in v2:
time: 1200 us; the launch traced here: 1180 us
  starting transfers between devices  767 us (64%)
  other arithmetic  247 us (21%)
  waiting for transfers between devices  126 us (10%)
  local copies, waits for them, and re-layouts  21.8 us (2%)
  between operations  14.7 us (1%)
    ppermute x288, starting transfers between devices, hop(): return lax.ppermute(value, 'dp', pairs)  737 us
    ppermute x288, waiting for transfers between devices, hop(): return lax.ppermute(value, 'dp', pairs)  117 us
    dynamic_update_slice x148, other arithmetic, local(): outs[m] = lax.dynamic_update_slice(outs[m], value, ((1 - d) * half + at, 0))  107 us
    unnamed x51, other arithmetic  78.9 us
    reduce_sum x8, other arithmetic, statistics(): part = jnp.sum(raw * raw)  24.7 us
  transfers between devices with their start and end apart: 308, of which 60 were waited for; matrix products, arithmetic and copies ran while one was open for 21% of the time, Pallas kernels for 0%

profile of v2, /device:TPU:0, one launch (start us, length us, event | category | flops | bytes accessed | tf_op | source)
XLA Modules:
  0.0 1176.8 jit_solution(13620863611332415631)
XLA Ops:
  2.6 4.9 collective-permute-start.4
  9.6 4.6 collective-permute-done.4
  20.9 5.0 collective-permute-start.8
  26.5 5.2 collective-permute-start.2
  38.9 5.0 collective-permute-start.7
  45.2 4.9 collective-permute-start.11
  59.8 4.6 collective-permute-start.15
  81.1 4.6 collective-permute-start.21
  88.2 5.3 collective-permute-start.23
  101.8 6.2 collective-permute-done.24
  134.0 4.6 collective-permute-start.33
  157.4 5.3 collective-permute-start.39
  170.9 5.2 collective-permute-done.40
  223.6 5.4 collective-permute-start.55
  270.5 6.4 collective-permute-start.68
  292.4 5.0 collective-permute-start.78
  336.7 5.3 collective-permute-start.87
  390.5 5.2 collective-permute-start.102
  403.3 5.9 collective-permute-start.104
  417.7 5.3 collective-permute-start.106
  430.5 5.3 collective-permute-start.109
  464.8 5.3 collective-permute-start.122
  485.9 6.1 collective-permute-start.117
  512.4 6.1 broadcast_in_dim.22
  565.1 5.9 collective-permute-done.137
  601.5 5.2 collective-permute-start.148
  612.4 5.3 collective-permute-start.152
  623.4 4.6 collective-permute-start.156
  632.4 4.6 collective-permute-start.160
  641.4 5.2 collective-permute-start.164
  730.1 5.3 collective-permute-start.186
  743.0 5.3 collective-permute-start.188
  756.1 5.3 collective-permute-start.190
  808.3 5.1 collective-permute-start.209
  821.6 4.7 collective-permute-start.202
  829.3 4.7 collective-permute-start.204
  849.5 4.8 collective-permute-start.212
  857.3 4.7 collective-permute-start.214
  865.1 4.7 collective-permute-start.216
  913.2 7.0 collective-permute-start.232
  925.3 5.2 collective-permute-start.236
  935.1 4.6 collective-permute-start.240
  946.8 8.5 collective-permute-start.242
  963.0 5.1 collective-permute-start.246
  1007.0 4.6 collective-permute-start.258
  1030.1 4.6 collective-permute-start.264
  1164.2 5.9 collective-permute-done.307
  1170.2 6.2 copy-done
  (1261 shorter events, 908.8 us)
Async XLA Ops:
  269.8 17.0 %collective-permute-start.69 = (bf16[64,2048]{1,0:T(8,128)(2,1)S(1)}, bf16[64,2048]{1,0:T(8,128)(2,1)S(1)}, u32[]{:S(2)}, u32[]{:S(2)}) collective-permute-start(bf16[64,2048]{1,0:T(8,128)(2,1)S(1)} %get-tuple-element.404), channel_id=1, source_target_pairs={{24,16},{25,17},{26,18},{27,19},{28,20},{29,21},{30,22},{31,23}} | collective-permute-start | bytes 786440 | tf_op jit(solution)/shard_map/ppermute | solution.py:71
  270.5 17.6 %collective-permute-start.68 = (bf16[64,2048]{1,0:T(8,128)(2,1)S(1)}, bf16[64,2048]{1,0:T(8,128)(2,1)S(1)}, u32[]{:S(2)}, u32[]{:S(2)}) collective-permute-start(bf16[64,2048]{1,0:T(8,128)(2,1)S(1)} %get-tuple-element.403), channel_id=1, source_target_pairs={{0,8},{1,9},{2,10},{3,11},{4,12},{5,13},{6,14},{7,15}} | collective-permute-start | bytes 786440 | tf_op jit(solution)/shard_map/ppermute | solution.py:71
  278.8 18.6 %collective-permute-start.67 = (bf16[16,8192]{1,0:T(8,128)(2,1)S(1)}, bf16[16,8192]{1,0:T(8,128)(2,1)S(1)}, u32[]{:S(2)}, u32[]{:S(2)}) collective-permute-start(bf16[16,8192]{1,0:T(8,128)(2,1)S(1)} %get-tuple-element.406), channel_id=1, source_target_pairs={{8,16},{16,24},{9,17},{17,25},{10,18},{18,26},{11,19},{19,27},{12,... | collective-permute-start | bytes 786440 | tf_op jit(solution)/shard_map/ppermute | solution.py:71
  315.4 17.9 %collective-permute-start.81 = (bf16[64,2048]{1,0:T(8,128)(2,1)S(1)}, bf16[64,2048]{1,0:T(8,128)(2,1)S(1)}, u32[]{:S(2)}, u32[]{:S(2)}) collective-permute-start(bf16[64,2048]{1,0:T(8,128)(2,1)S(1)} %get-tuple-element.418), channel_id=1, source_target_pairs={{24,16},{16,8},{8,0},{25,17},{17,9},{9,1},{26,18},{18,10},{10,2},{... | collective-permute-start | bytes 786440 | tf_op jit(solution)/shard_map/ppermute | solution.py:71
  316.7 16.6 %collective-permute-start.80 = (bf16[64,2048]{1,0:T(8,128)(2,1)S(1)}, bf16[64,2048]{1,0:T(8,128)(2,1)S(1)}, u32[]{:S(2)}, u32[]{:S(2)}) collective-permute-start(bf16[64,2048]{1,0:T(8,128)(2,1)S(1)} %get-tuple-element.417), channel_id=1, source_target_pairs={{0,8},{8,16},{16,24},{1,9},{9,17},{17,25},{2,10},{10,18},{18,26},{... | collective-permute-start | bytes 786440 | tf_op jit(solution)/shard_map/ppermute | solution.py:71
  321.3 22.1 %collective-permute-start.85 = (bf16[64,2048]{1,0:T(8,128)(2,1)S(1)}, bf16[64,2048]{1,0:T(8,128)(2,1)S(1)}, u32[]{:S(2)}, u32[]{:S(2)}) collective-permute-start(bf16[64,2048]{1,0:T(8,128)(2,1)S(1)} %get-tuple-element.420), channel_id=1, source_target_pairs={{24,16},{16,8},{8,0},{25,17},{17,9},{9,1},{26,18},{18,10},{10,2},{... | collective-permute-start | bytes 786440 | tf_op jit(solution)/shard_map/ppermute | solution.py:71
  322.6 20.8 %collective-permute-start.84 = (bf16[64,2048]{1,0:T(8,128)(2,1)S(1)}, bf16[64,2048]{1,0:T(8,128)(2,1)S(1)}, u32[]{:S(2)}, u32[]{:S(2)}) collective-permute-start(bf16[64,2048]{1,0:T(8,128)(2,1)S(1)} %get-tuple-element.419), channel_id=1, source_target_pairs={{0,8},{8,16},{16,24},{1,9},{9,17},{17,25},{2,10},{10,18},{18,26},{... | collective-permute-start | bytes 786440 | tf_op jit(solution)/shard_map/ppermute | solution.py:71
  335.4 17.6 %collective-permute-start.88 = (bf16[64,2048]{1,0:T(8,128)(2,1)}, bf16[64,2048]{1,0:T(8,128)(2,1)}, u32[]{:S(2)}, u32[]{:S(2)}) collective-permute-start(bf16[64,2048]{1,0:T(8,128)(2,1)} %get-tuple-element.423), channel_id=1, source_target_pairs={{24,16},{16,8},{8,0},{25,17},{17,9},{9,1},{26,18},{18,10},{10,2},{... | collective-permute-start | bytes 786440 | tf_op jit(solution)/shard_map/ppermute | solution.py:71
  336.7 16.3 %collective-permute-start.87 = (bf16[64,2048]{1,0:T(8,128)(2,1)}, bf16[64,2048]{1,0:T(8,128)(2,1)}, u32[]{:S(2)}, u32[]{:S(2)}) collective-permute-start(bf16[64,2048]{1,0:T(8,128)(2,1)} %get-tuple-element.422), channel_id=1, source_target_pairs={{0,8},{8,16},{16,24},{1,9},{9,17},{17,25},{2,10},{10,18},{18,26},{... | collective-permute-start | bytes 786440 | tf_op jit(solution)/shard_map/ppermute | solution.py:71
  383.1 16.0 %collective-permute-start.100 = (bf16[64,2048]{1,0:T(8,128)(2,1)S(1)}, bf16[64,2048]{1,0:T(8,128)(2,1)S(1)}, u32[]{:S(2)}, u32[]{:S(2)}) collective-permute-start(bf16[64,2048]{1,0:T(8,128)(2,1)S(1)} %get-tuple-element.438), channel_id=1, source_target_pairs={{0,8},{8,16},{16,24},{1,9},{9,17},{17,25},{2,10},{10,18},{18,26},{... | collective-permute-start | bytes 786440 | tf_op jit(solution)/shard_map/ppermute | solution.py:71
  402.0 25.0 %collective-permute-start.105 = (bf16[64,2048]{1,0:T(8,128)(2,1)}, bf16[64,2048]{1,0:T(8,128)(2,1)}, u32[]{:S(2)}, u32[]{:S(2)}) collective-permute-start(bf16[64,2048]{1,0:T(8,128)(2,1)} %get-tuple-element.445), channel_id=1, source_target_pairs={{24,16},{16,8},{8,0},{25,17},{17,9},{9,1},{26,18},{18,10},{10,2},{... | collective-permute-start | bytes 786440 | tf_op jit(solution)/shard_map/ppermute | solution.py:71
  403.3 23.7 %collective-permute-start.104 = (bf16[64,2048]{1,0:T(8,128)(2,1)S(1)}, bf16[64,2048]{1,0:T(8,128)(2,1)}, u32[]{:S(2)}, u32[]{:S(2)}) collective-permute-start(bf16[64,2048]{1,0:T(8,128)(2,1)S(1)} %get-tuple-element.444), channel_id=1, source_target_pairs={{0,8},{8,16},{16,24},{1,9},{9,17},{17,25},{2,10},{10,18},{18,26},{... | collective-permute-start | bytes 786440 | tf_op jit(solution)/shard_map/ppermute | solution.py:71
  416.5 23.3 %collective-permute-start.107 = (bf16[64,2048]{1,0:T(8,128)(2,1)S(1)}, bf16[64,2048]{1,0:T(8,128)(2,1)}, u32[]{:S(2)}, u32[]{:S(2)}) collective-permute-start(bf16[64,2048]{1,0:T(8,128)(2,1)S(1)} %get-tuple-element.449), channel_id=1, source_target_pairs={{24,16},{16,8},{8,0},{25,17},{17,9},{9,1},{26,18},{18,10},{10,2},{... | collective-permute-start | bytes 786440 | tf_op jit(solution)/shard_map/ppermute | solution.py:71
  417.7 22.0 %collective-permute-start.106 = (bf16[64,2048]{1,0:T(8,128)(2,1)S(1)}, bf16[64,2048]{1,0:T(8,128)(2,1)}, u32[]{:S(2)}, u32[]{:S(2)}) collective-permute-start(bf16[64,2048]{1,0:T(8,128)(2,1)S(1)} %get-tuple-element.448), channel_id=1, source_target_pairs={{0,8},{8,16},{16,24},{1,9},{9,17},{17,25},{2,10},{10,18},{18,26},{... | collective-permute-start | bytes 786440 | tf_op jit(solution)/shard_map/ppermute | solution.py:71
  429.2 17.8 %collective-permute-start.110 = (bf16[64,2048]{1,0:T(8,128)(2,1)}, bf16[64,2048]{1,0:T(8,128)(2,1)}, u32[]{:S(2)}, u32[]{:S(2)}) collective-permute-start(bf16[64,2048]{1,0:T(8,128)(2,1)} %get-tuple-element.452), channel_id=1, source_target_pairs={{24,16},{16,8},{8,0},{25,17},{17,9},{9,1},{26,18},{18,10},{10,2},{... | collective-permute-start | bytes 786440 | tf_op jit(solution)/shard_map/ppermute | solution.py:71
  430.5 16.5 %collective-permute-start.109 = (bf16[64,2048]{1,0:T(8,128)(2,1)}, bf16[64,2048]{1,0:T(8,128)(2,1)}, u32[]{:S(2)}, u32[]{:S(2)}) collective-permute-start(bf16[64,2048]{1,0:T(8,128)(2,1)} %get-tuple-element.451), channel_id=1, source_target_pairs={{0,8},{8,16},{16,24},{1,9},{9,17},{17,25},{2,10},{10,18},{18,26},{... | collective-permute-start | bytes 786440 | tf_op jit(solution)/shard_map/ppermute | solution.py:71
  463.5 30.0 %collective-permute-start.123 = (bf16[64,2048]{1,0:T(8,128)(2,1)}, bf16[64,2048]{1,0:T(8,128)(2,1)}, u32[]{:S(2)}, u32[]{:S(2)}) collective-permute-start(bf16[64,2048]{1,0:T(8,128)(2,1)} %get-tuple-element.464), channel_id=1, source_target_pairs={{24,16},{16,8},{8,0},{25,17},{17,9},{9,1},{26,18},{18,10},{10,2},{... | collective-permute-start | bytes 786440 | tf_op jit(solution)/shard_map/ppermute | solution.py:71
  464.8 28.7 %collective-permute-start.122 = (bf16[64,2048]{1,0:T(8,128)(2,1)}, bf16[64,2048]{1,0:T(8,128)(2,1)}, u32[]{:S(2)}, u32[]{:S(2)}) collective-permute-start(bf16[64,2048]{1,0:T(8,128)(2,1)} %get-tuple-element.463), channel_id=1, source_target_pairs={{0,8},{8,16},{16,24},{1,9},{9,17},{17,25},{2,10},{10,18},{18,26},{... | collective-permute-start | bytes 786440 | tf_op jit(solution)/shard_map/ppermute | solution.py:71
  472.1 21.4 %collective-permute-start.120 = (bf16[64,2048]{1,0:T(8,128)(2,1)}, bf16[64,2048]{1,0:T(8,128)(2,1)}, u32[]{:S(2)}, u32[]{:S(2)}) collective-permute-start(bf16[64,2048]{1,0:T(8,128)(2,1)} %get-tuple-element.466), channel_id=1, source_target_pairs={{0,8},{8,16},{16,24},{1,9},{9,17},{17,25},{2,10},{10,18},{18,26},{... | collective-permute-start | bytes 786440 | tf_op jit(solution)/shard_map/ppermute | solution.py:71
  476.1 17.5 %collective-permute-start.121 = (bf16[64,2048]{1,0:T(8,128)(2,1)}, bf16[64,2048]{1,0:T(8,128)(2,1)}, u32[]{:S(2)}, u32[]{:S(2)}) collective-permute-start(bf16[64,2048]{1,0:T(8,128)(2,1)} %get-tuple-element.467), channel_id=1, source_target_pairs={{24,16},{16,8},{8,0},{25,17},{17,9},{9,1},{26,18},{18,10},{10,2},{... | collective-permute-start | bytes 786440 | tf_op jit(solution)/shard_map/ppermute | solution.py:71
  496.2 24.6 %collective-permute-start.127 = (bf16[64,2048]{1,0:T(8,128)(2,1)S(1)}, bf16[64,2048]{1,0:T(8,128)(2,1)S(1)}, u32[]{:S(2)}, u32[]{:S(2)}) collective-permute-start(bf16[64,2048]{1,0:T(8,128)(2,1)S(1)} %get-tuple-element.469), channel_id=1, source_target_pairs={{24,16},{16,8},{8,0},{25,17},{17,9},{9,1},{26,18},{18,10},{10,2},{... | collective-permute-start | bytes 786440 | tf_op jit(solution)/shard_map/ppermute | solution.py:71
  497.5 23.3 %collective-permute-start.126 = (bf16[64,2048]{1,0:T(8,128)(2,1)S(1)}, bf16[64,2048]{1,0:T(8,128)(2,1)S(1)}, u32[]{:S(2)}, u32[]{:S(2)}) collective-permute-start(bf16[64,2048]{1,0:T(8,128)(2,1)S(1)} %get-tuple-element.468), channel_id=1, source_target_pairs={{0,8},{8,16},{16,24},{1,9},{9,17},{17,25},{2,10},{10,18},{18,26},{... | collective-permute-start | bytes 786440 | tf_op jit(solution)/shard_map/ppermute | solution.py:71
  504.7 23.3 %collective-permute-start.125 = (bf16[64,2048]{1,0:T(8,128)(2,1)S(1)}, bf16[64,2048]{1,0:T(8,128)(2,1)S(1)}, u32[]{:S(2)}, u32[]{:S(2)}) collective-permute-start(bf16[64,2048]{1,0:T(8,128)(2,1)S(1)} %get-tuple-element.472), channel_id=1, source_target_pairs={{24,16},{16,8},{8,0},{25,17},{17,9},{9,1},{26,18},{18,10},{10,2},{... | collective-permute-start | bytes 786440 | tf_op jit(solution)/shard_map/ppermute | solution.py:71
  506.0 22.0 %collective-permute-start.124 = (bf16[64,2048]{1,0:T(8,128)(2,1)S(1)}, bf16[64,2048]{1,0:T(8,128)(2,1)S(1)}, u32[]{:S(2)}, u32[]{:S(2)}) collective-permute-start(bf16[64,2048]{1,0:T(8,128)(2,1)S(1)} %get-tuple-element.471), channel_id=1, source_target_pairs={{0,8},{8,16},{16,24},{1,9},{9,17},{17,25},{2,10},{10,18},{18,26},{... | collective-permute-start | bytes 786440 | tf_op jit(solution)/shard_map/ppermute | solution.py:71
  601.5 16.2 %collective-permute-start.148 = (bf16[16,8192]{1,0:T(8,128)(2,1)S(1)}, bf16[16,8192]{1,0:T(8,128)(2,1)S(1)}, u32[]{:S(2)}, u32[]{:S(2)}) collective-permute-start(bf16[16,8192]{1,0:T(8,128)(2,1)S(1)} %get-tuple-element.498), channel_id=1, source_target_pairs={{0,8},{1,9},{2,10},{3,11},{4,12},{5,13},{6,14},{7,15}} | collective-permute-start | bytes 786440 | tf_op jit(solution)/shard_map/ppermute | solution.py:71
  612.4 15.6 %collective-permute-start.152 = (bf16[16,8192]{1,0:T(8,128)(2,1)S(1)}, bf16[16,8192]{1,0:T(8,128)(2,1)S(1)}, u32[]{:S(2)}, u32[]{:S(2)}) collective-permute-start(bf16[16,8192]{1,0:T(8,128)(2,1)S(1)} %get-tuple-element.501), channel_id=1, source_target_pairs={{0,8},{8,16},{1,9},{9,17},{2,10},{10,18},{3,11},{11,19},{4,12},{12... | collective-permute-start | bytes 786440 | tf_op jit(solution)/shard_map/ppermute | solution.py:71
  641.4 19.5 %collective-permute-start.164 = (bf16[16,8192]{1,0:T(8,128)(2,1)}, bf16[16,8192]{1,0:T(8,128)(2,1)}, u32[]{:S(2)}, u32[]{:S(2)}) collective-permute-start(bf16[16,8192]{1,0:T(8,128)(2,1)} %get-tuple-element.511), channel_id=1, source_target_pairs={{0,8},{8,16},{16,24},{1,9},{9,17},{17,25},{2,10},{10,18},{18,26},{... | collective-permute-start | bytes 786440 | tf_op jit(solution)/shard_map/ppermute | solution.py:71
  666.6 19.2 %collective-permute-start.168 = (bf16[16,8192]{1,0:T(8,128)(2,1)S(1)}, bf16[16,8192]{1,0:T(8,128)(2,1)S(1)}, u32[]{:S(2)}, u32[]{:S(2)}) collective-permute-start(bf16[16,8192]{1,0:T(8,128)(2,1)S(1)} %get-tuple-element.516), channel_id=1, source_target_pairs={{0,8},{8,16},{16,24},{1,9},{9,17},{17,25},{2,10},{10,18},{18,26},{... | collective-permute-start | bytes 786440 | tf_op jit(solution)/shard_map/ppermute | solution.py:71
  708.5 19.8 %collective-permute-start.176 = (bf16[16,8192]{1,0:T(8,128)(2,1)S(1)}, bf16[16,8192]{1,0:T(8,128)(2,1)S(1)}, u32[]{:S(2)}, u32[]{:S(2)}) collective-permute-start(bf16[16,8192]{1,0:T(8,128)(2,1)S(1)} %get-tuple-element.524), channel_id=1, source_target_pairs={{0,8},{8,16},{16,24},{1,9},{9,17},{17,25},{2,10},{10,18},{18,26},{... | collective-permute-start | bytes 786440 | tf_op jit(solution)/shard_map/ppermute | solution.py:71
  713.0 16.2 %collective-permute-start.177 = (bf16[16,8192]{1,0:T(8,128)(2,1)S(1)}, bf16[16,8192]{1,0:T(8,128)(2,1)S(1)}, u32[]{:S(2)}, u32[]{:S(2)}) collective-permute-start(bf16[16,8192]{1,0:T(8,128)(2,1)S(1)} %get-tuple-element.525), channel_id=1, source_target_pairs={{24,16},{16,8},{8,0},{25,17},{17,9},{9,1},{26,18},{18,10},{10,2},{... | collective-permute-start | bytes 786440 | tf_op jit(solution)/shard_map/ppermute | solution.py:71
  718.7 18.0 %collective-permute-start.184 = (bf16[16,8192]{1,0:T(8,128)(2,1)S(1)}, bf16[16,8192]{1,0:T(8,128)(2,1)S(1)}, u32[]{:S(2)}, u32[]{:S(2)}) collective-permute-start(bf16[16,8192]{1,0:T(8,128)(2,1)S(1)} %get-tuple-element.533), channel_id=1, source_target_pairs={{0,8},{8,16},{16,24},{1,9},{9,17},{17,25},{2,10},{10,18},{18,26},{... | collective-permute-start | bytes 786440 | tf_op jit(solution)/shard_map/ppermute | solution.py:71
  723.3 17.7 %collective-permute-start.185 = (bf16[16,8192]{1,0:T(8,128)(2,1)}, bf16[16,8192]{1,0:T(8,128)(2,1)}, u32[]{:S(2)}, u32[]{:S(2)}) collective-permute-start(bf16[16,8192]{1,0:T(8,128)(2,1)} %get-tuple-element.534), channel_id=1, source_target_pairs={{24,16},{16,8},{8,0},{25,17},{17,9},{9,1},{26,18},{18,10},{10,2},{... | collective-permute-start | bytes 786440 | tf_op jit(solution)/shard_map/ppermute | solution.py:71
  730.1 22.2 %collective-permute-start.186 = (bf16[16,8192]{1,0:T(8,128)(2,1)}, bf16[16,8192]{1,0:T(8,128)(2,1)}, u32[]{:S(2)}, u32[]{:S(2)}) collective-permute-start(bf16[16,8192]{1,0:T(8,128)(2,1)} %get-tuple-element.536), channel_id=1, source_target_pairs={{0,8},{8,16},{16,24},{1,9},{9,17},{17,25},{2,10},{10,18},{18,26},{... | collective-permute-start | bytes 786440 | tf_op jit(solution)/shard_map/ppermute | solution.py:71
  735.4 18.8 %collective-permute-start.187 = (bf16[16,8192]{1,0:T(8,128)(2,1)}, bf16[16,8192]{1,0:T(8,128)(2,1)}, u32[]{:S(2)}, u32[]{:S(2)}) collective-permute-start(bf16[16,8192]{1,0:T(8,128)(2,1)} %get-tuple-element.537), channel_id=1, source_target_pairs={{24,16},{16,8},{8,0},{25,17},{17,9},{9,1},{26,18},{18,10},{10,2},{... | collective-permute-start | bytes 786440 | tf_op jit(solution)/shard_map/ppermute | solution.py:71
  743.0 18.4 %collective-permute-start.188 = (bf16[16,8192]{1,0:T(8,128)(2,1)}, bf16[16,8192]{1,0:T(8,128)(2,1)}, u32[]{:S(2)}, u32[]{:S(2)}) collective-permute-start(bf16[16,8192]{1,0:T(8,128)(2,1)} %get-tuple-element.539), channel_id=1, source_target_pairs={{0,8},{8,16},{16,24},{1,9},{9,17},{17,25},{2,10},{10,18},{18,26},{... | collective-permute-start | bytes 786440 | tf_op jit(solution)/shard_map/ppermute | solution.py:71
  756.1 20.6 %collective-permute-start.190 = (bf16[16,8192]{1,0:T(8,128)(2,1)S(1)}, bf16[16,8192]{1,0:T(8,128)(2,1)}, u32[]{:S(2)}, u32[]{:S(2)}) collective-permute-start(bf16[16,8192]{1,0:T(8,128)(2,1)S(1)} %get-tuple-element.542), channel_id=1, source_target_pairs={{0,8},{8,16},{16,24},{1,9},{9,17},{17,25},{2,10},{10,18},{18,26},{... | collective-permute-start | bytes 786440 | tf_op jit(solution)/shard_map/ppermute | solution.py:71
  781.3 17.3 %collective-permute-start.194 = (bf16[16,8192]{1,0:T(8,128)(2,1)}, bf16[16,8192]{1,0:T(8,128)(2,1)}, u32[]{:S(2)}, u32[]{:S(2)}) collective-permute-start(bf16[16,8192]{1,0:T(8,128)(2,1)} %get-tuple-element.547), channel_id=1, source_target_pairs={{0,8},{8,16},{16,24},{1,9},{9,17},{17,25},{2,10},{10,18},{18,26},{... | collective-permute-start | bytes 786440 | tf_op jit(solution)/shard_map/ppermute | solution.py:71
  792.7 20.7 %collective-permute-start.196 = (bf16[16,8192]{1,0:T(8,128)(2,1)}, bf16[16,8192]{1,0:T(8,128)(2,1)S(1)}, u32[]{:S(2)}, u32[]{:S(2)}) collective-permute-start(bf16[16,8192]{1,0:T(8,128)(2,1)} %get-tuple-element.549), channel_id=1, source_target_pairs={{0,8},{8,16},{16,24},{1,9},{9,17},{17,25},{2,10},{10,18},{18,26},{... | collective-permute-start | bytes 786440 | tf_op jit(solution)/shard_map/ppermute | solution.py:71
  797.3 18.0 %collective-permute-start.197 = (bf16[16,8192]{1,0:T(8,128)(2,1)}, bf16[16,8192]{1,0:T(8,128)(2,1)S(1)}, u32[]{:S(2)}, u32[]{:S(2)}) collective-permute-start(bf16[16,8192]{1,0:T(8,128)(2,1)} %get-tuple-element.550), channel_id=1, source_target_pairs={{24,16},{16,8},{8,0},{25,17},{17,9},{9,1},{26,18},{18,10},{10,2},{... | collective-permute-start | bytes 786440 | tf_op jit(solution)/shard_map/ppermute | solution.py:71
  804.0 15.8 %collective-permute-start.198 = (bf16[16,8192]{1,0:T(8,128)(2,1)S(1)}, bf16[16,8192]{1,0:T(8,128)(2,1)S(1)}, u32[]{:S(2)}, u32[]{:S(2)}) collective-permute-start(bf16[16,8192]{1,0:T(8,128)(2,1)S(1)} %get-tuple-element.551), channel_id=1, source_target_pairs={{0,8},{8,16},{16,24},{1,9},{9,17},{17,25},{2,10},{10,18},{18,26},{... | collective-permute-start | bytes 786440 | tf_op jit(solution)/shard_map/ppermute | solution.py:71
  821.6 18.6 %collective-permute-start.202 = (bf16[16,8192]{1,0:T(8,128)(2,1)S(1)}, bf16[16,8192]{1,0:T(8,128)(2,1)S(1)}, u32[]{:S(2)}, u32[]{:S(2)}) collective-permute-start(bf16[16,8192]{1,0:T(8,128)(2,1)S(1)} %get-tuple-element.555), channel_id=1, source_target_pairs={{0,8},{8,16},{16,24},{1,9},{9,17},{17,25},{2,10},{10,18},{18,26},{... | collective-permute-start | bytes 786440 | tf_op jit(solution)/shard_map/ppermute | solution.py:71
  829.3 18.4 %collective-permute-start.204 = (bf16[16,8192]{1,0:T(8,128)(2,1)S(1)}, bf16[16,8192]{1,0:T(8,128)(2,1)S(1)}, u32[]{:S(2)}, u32[]{:S(2)}) collective-permute-start(bf16[16,8192]{1,0:T(8,128)(2,1)S(1)} %get-tuple-element.557), channel_id=1, source_target_pairs={{0,8},{8,16},{16,24},{1,9},{9,17},{17,25},{2,10},{10,18},{18,26},{... | collective-permute-start | bytes 786440 | tf_op jit(solution)/shard_map/ppermute | solution.py:71
  904.1 16.0 %collective-permute-start.226 = (bf16[16,8192]{1,0:T(8,128)(2,1)S(1)}, bf16[16,8192]{1,0:T(8,128)(2,1)S(1)}, u32[]{:S(2)}, u32[]{:S(2)}) collective-permute-start(bf16[16,8192]{1,0:T(8,128)(2,1)S(1)} %get-tuple-element.580), channel_id=1, source_target_pairs={{0,8},{8,16},{16,24},{1,9},{9,17},{17,25},{2,10},{10,18},{18,26},{... | collective-permute-start | bytes 786440 | tf_op jit(solution)/shard_map/ppermute | solution.py:71
  913.2 18.1 %collective-permute-start.232 = (bf16[64,2048]{1,0:T(8,128)(2,1)S(1)}, bf16[64,2048]{1,0:T(8,128)(2,1)S(1)}, u32[]{:S(2)}, u32[]{:S(2)}) collective-permute-start(bf16[64,2048]{1,0:T(8,128)(2,1)S(1)} %get-tuple-element.585), channel_id=1, source_target_pairs={{0,8},{1,9},{2,10},{3,11},{4,12},{5,13},{6,14},{7,15}} | collective-permute-start | bytes 786440 | tf_op jit(solution)/shard_map/ppermute | solution.py:71
  932.3 23.3 %collective-permute-start.234 = (bf16[16,8192]{1,0:T(8,128)(2,1)S(1)}, bf16[16,8192]{1,0:T(8,128)(2,1)S(1)}, u32[]{:S(2)}, u32[]{:S(2)}) collective-permute-start(bf16[16,8192]{1,0:T(8,128)(2,1)S(1)} %get-tuple-element.590), channel_id=1, source_target_pairs={{16,24},{17,25},{18,26},{19,27},{20,28},{21,29},{22,30},{23,31}} | collective-permute-start | bytes 786440 | tf_op jit(solution)/shard_map/ppermute | solution.py:71
  933.0 23.3 %collective-permute-start.235 = (bf16[16,8192]{1,0:T(8,128)(2,1)S(1)}, bf16[16,8192]{1,0:T(8,128)(2,1)S(1)}, u32[]{:S(2)}, u32[]{:S(2)}) collective-permute-start(bf16[16,8192]{1,0:T(8,128)(2,1)S(1)} %get-tuple-element.591), channel_id=1, source_target_pairs={{8,0},{9,1},{10,2},{11,3},{12,4},{13,5},{14,6},{15,7}} | collective-permute-start | bytes 786440 | tf_op jit(solution)/shard_map/ppermute | solution.py:71
  941.5 21.6 %collective-permute-start.238 = (bf16[16,8192]{1,0:T(8,128)(2,1)S(1)}, bf16[16,8192]{1,0:T(8,128)(2,1)S(1)}, u32[]{:S(2)}, u32[]{:S(2)}) collective-permute-start(bf16[16,8192]{1,0:T(8,128)(2,1)S(1)} %get-tuple-element.594), channel_id=1, source_target_pairs={{16,24},{17,25},{18,26},{19,27},{20,28},{21,29},{22,30},{23,31}} | collective-permute-start | bytes 786440 | tf_op jit(solution)/shard_map/ppermute | solution.py:71
  945.4 17.7 %collective-permute-start.239 = (bf16[16,8192]{1,0:T(8,128)(2,1)S(1)}, bf16[16,8192]{1,0:T(8,128)(2,1)S(1)}, u32[]{:S(2)}, u32[]{:S(2)}) collective-permute-start(bf16[16,8192]{1,0:T(8,128)(2,1)S(1)} %get-tuple-element.595), channel_id=1, source_target_pairs={{8,0},{9,1},{10,2},{11,3},{12,4},{13,5},{14,6},{15,7}} | collective-permute-start | bytes 786440 | tf_op jit(solution)/shard_map/ppermute | solution.py:71
  (466 other events, 14760.2 us)

commit v3 on v2

v3 whole, which is shorter than its diff:
```python
import functools

import jax
import jax.numpy as jnp
from jax import lax
from jax.experimental import pallas as pl
from jax.experimental.pallas import tpu as pltpu
from jax.sharding import PartitionSpec as P

BETA = 0.8
EPS_SQUARE = 1e-30
CHUNKS = 16
LAG = 2
GROUPS = 4
FAR = 2
LANES = 128

F32 = jnp.float32
BF16 = jnp.bfloat16
ANY = pl.BlockSpec(memory_space=pl.ANY)


def chunk_count(rows):
    half = rows // 2
    count = CHUNKS
    while half % count or (half // count) % 16:
        count //= 2
    return count


def block_rows(size, cols):
    rows = size
    while rows % 32 == 0 and rows * cols > 16 * 8192:
        rows //= 2
    return rows


def sum_kernel(with_got, with_total, first_total, at_ref, *refs):
    refs = list(refs)
    gots = [refs.pop(0), refs.pop(0)] if with_got else [None, None]
    owns = [refs.pop(0), refs.pop(0)]
    if with_total and not first_total:
        refs.pop(0)
        refs.pop(0)
        col_in = refs.pop(0)
    sends = [refs.pop(0), refs.pop(0)]
    rows, cols = sends[0].shape
    low_end = at_ref[2] == 0
    if with_total:
        total_ref, row_ref, col_ref = refs

        @pl.when(pl.program_id(0) == 0)
        def _():
            col_ref[...] = jnp.zeros(col_ref.shape, F32) if first_total else col_in[...]

    row_part = jnp.zeros((rows, LANES), F32)
    for j in range(cols // LANES):
        lanes = pl.ds(j * LANES, LANES)
        values = []
        for got, own, send in zip(gots, owns, sends):
            value = own[:, lanes]
            if got is not None:
                value = (got[:, lanes].astype(F32) + value.astype(F32)).astype(BF16)
            send[:, lanes] = value
            values.append(value)
        if with_total:
            total = jnp.where(low_end, values[1], values[0])
            total_ref[:, lanes] = total
            wide = total.astype(F32)
            square = wide * wide + EPS_SQUARE
            row_part = row_part + square
            col_part = square[0:8]
            for r in range(8, rows, 8):
                col_part = col_part + square[r : r + 8]
            col_ref[:, lanes] += col_part
    if with_total:
        row_ref[...] = row_part


def sum_step(at, gots, grad, size, chunk, count, state):
    rows, cols = grad.shape
    half = rows // 2
    block = block_rows(size, cols)
    per = size // block

    def from_grad(d):
        return pl.BlockSpec((block, cols), lambda i, at: (at[d] // block + i, 0))

    piece = pl.BlockSpec((block, cols), lambda i, at: (i, 0))
    operands, in_specs = [], []
    if gots[0] is not None:
        operands += gots
        in_specs += [piece, piece]
    operands += [grad, grad]
    in_specs += [from_grad(0), from_grad(1)]
    out_shape = [jax.ShapeDtypeStruct((size, cols), BF16)] * 2
    out_specs = [piece, piece]
    aliases = {}
    if chunk is not None:
        whole = pl.BlockSpec((8, cols), lambda i, at: (0, 0))
        if state is not None:
            base = len(operands) + 1
            operands += state
            in_specs += [ANY, ANY, whole]
            aliases = {base: 2, base + 1: 3, base + 2: 4}
        out_shape += [
            jax.ShapeDtypeStruct((half, cols), BF16),
            jax.ShapeDtypeStruct((half, LANES), F32),
            jax.ShapeDtypeStruct((8, cols), F32),
        ]
        out_specs += [
            pl.BlockSpec((block, cols), lambda i, at: (chunk * per + i, 0)),
            pl.BlockSpec((block, LANES), lambda i, at: (chunk * per + i, 0)),
            whole,
        ]
    out = pl.pallas_call(
        functools.partial(sum_kernel, gots[0] is not None, chunk is not None, state is None),
        grid_spec=pltpu.PrefetchScalarGridSpec(
            num_scalar_prefetch=1, grid=(per,), in_specs=in_specs, out_specs=out_specs
        ),
        out_shape=out_shape,
        input_output_aliases=aliases,
        compiler_params=pltpu.CompilerParams(vmem_limit_bytes=16 * 1024 * 1024),
        cost_estimate=pl.CostEstimate(
            flops=4 * size * cols, bytes_accessed=12 * size * cols, transcendentals=0
        ),
        name="sum_step",
    )(at, *operands)
    return out[:2], list(out[2:])


def spread_kernel(size, chunk, with_got, with_out, sending, at_ref, *refs):
    refs = list(refs)
    gots = [refs.pop(0), refs.pop(0)] if with_got else [None, None]
    if chunk is not None:
        total_ref, row_ref, col_ref = refs.pop(0), refs.pop(0), refs.pop(0)
    if with_out:
        refs.pop(0)
    out_ref = refs.pop(0)
    sends = [refs.pop(0), refs.pop(0)] if sending else [None, None]
    update, sems = refs
    cols = update.shape[1]

    def copies(source, d):
        row = pl.multiple_of(at_ref[d], 16)
        keep = pltpu.make_async_copy(source, out_ref.at[pl.ds(row, size), :], sems.at[d, 0])
        give = pltpu.make_async_copy(source, sends[d], sems.at[d, 1]) if sending else None
        return keep, give

    for d in range(2):
        valid = at_ref[2 + d] == 1
        source = at_ref[4 + d] == 1
        if with_got:

            @pl.when(valid & jnp.logical_not(source))
            def _():
                keep, give = copies(gots[d], d)
                keep.start()
                if sending:
                    give.start()

        if chunk is not None:

            @pl.when(source)
            def _():
                for j in range(cols // LANES):
                    lanes = pl.ds(j * LANES, LANES)
                    wide = total_ref[:, lanes].astype(F32)
                    update[:, lanes] = (wide * row_ref[...] * col_ref[0:1, lanes]).astype(BF16)
                keep, give = copies(update, d)
                keep.start()
                if sending:
                    give.start()

    for d in range(2):

        @pl.when(at_ref[2 + d] == 1)
        def _():
            keep, give = copies(update, d)
            keep.wait()
            if sending:
                give.wait()


def spread_step(at, gots, parts, chunk, out, shape, size, sending):
    rows, cols = shape
    operands, in_specs, aliases = [], [], {}
    if gots[0] is not None:
        operands += gots
        in_specs += [ANY, ANY]
    if chunk is not None:
        operands += parts
        in_specs += [
            pl.BlockSpec((size, cols), lambda i, at: (chunk, 0)),
            pl.BlockSpec((size, LANES), lambda i, at: (chunk, 0)),
            pl.BlockSpec((8, cols), lambda i, at: (0, 0)),
        ]
    if out is not None:
        aliases = {len(operands) + 1: 0}
        operands.append(out)
        in_specs.append(ANY)
    out_shape = [jax.ShapeDtypeStruct(shape, BF16)]
    if sending:
        out_shape += [jax.ShapeDtypeStruct((size, cols), BF16)] * 2
    return pl.pallas_call(
        functools.partial(
            spread_kernel, size, chunk, gots[0] is not None, out is not None, sending
        ),
        grid_spec=pltpu.PrefetchScalarGridSpec(
            num_scalar_prefetch=1,
            grid=(1,),
            in_specs=in_specs,
            out_specs=[ANY] * len(out_shape),
            scratch_shapes=[pltpu.VMEM((size, cols), BF16), pltpu.SemaphoreType.DMA((2, 2))],
        ),
        out_shape=out_shape,
        input_output_aliases=aliases,
        compiler_params=pltpu.CompilerParams(vmem_limit_bytes=16 * 1024 * 1024),
        cost_estimate=pl.CostEstimate(
            flops=2 * size * cols, bytes_accessed=12 * size * cols, transcendentals=0
        ),
        name="spread_step",
    )(at, *operands)


def make_local(axis_sizes):
    n_dp, n_row, n_col = axis_sizes["dp"], axis_sizes["row"], axis_sizes["col"]
    last = n_dp - 1

    def spread_ends(value):
        total = value
        for j in range(1, n_dp):
            pairs = [[(0, j)], [(last, last - j)]]
            if j != last - j:
                pairs = [pairs[0] + pairs[1]]
            for some in pairs:
                total = total + lax.ppermute(value, "dp", some)
        return total

    def butterfly(value, axis, distance):
        n = axis_sizes[axis]
        return value + lax.ppermute(value, axis, [(i, i ^ distance) for i in range(n)])

    def distances(axis):
        out, d = [], 1
        while d < axis_sizes[axis]:
            out.append(d)
            d *= 2
        return out

    def local(grad_wi, grad_wo, row_wi, col_wi, row_wo, col_wo):
        place = lax.axis_index("dp")
        grads = (grad_wi[0], grad_wo[0])
        prevs = ((row_wi, col_wi), (row_wo, col_wo))
        shapes = [g.shape for g in grads]
        counts = [chunk_count(rows) for rows, _ in shapes]
        sizes = [rows // 2 // count for (rows, _), count in zip(shapes, counts)]

        position = jnp.stack([place, last - place])
        at_end = (place == last) | (place == 0)

        segments = []
        start = 0
        for kind in ("sum", "spread"):
            for m in range(2):
                segments.append((kind, m, start))
                start += counts[m]
        steps = start + LAG * last

        def hop(value, direction, senders):
            pairs = []
            for p in senders:
                if p < last:
                    pairs.append((p, p + 1) if direction == 0 else (last - p, last - p - 1))
            return lax.ppermute(value, "dp", pairs)

        states = {}
        finished = [0, 0]
        scales = {}
        results = {}
        cell = [None]

        def settle(value):
            value, _ = lax.optimization_barrier((value, cell[0]))
            return value

        def statistics(m):
            rows, cols = shapes[m]
            half = rows // 2
            while finished[m] < counts[m]:
                yield [], 1
            total, row_lanes, col_rows = states[m]
            row_part = jnp.sum(row_lanes, axis=1)
            col_part = jnp.sum(col_rows, axis=0)
            levels = max(len(distances("row")), len(distances("col")))
            for level in range(levels):
                if level < len(distances("col")):
                    row_part = butterfly(row_part, "col", distances("col")[level])
                if level < len(distances("row")):
                    col_part = butterfly(col_part, "row", distances("row")[level])
                yield [], 1
                row_part, col_part = settle((row_part, col_part))
            packed = jnp.concatenate(
                [
                    jnp.where(place == last, row_part, 0.0),
                    jnp.where(place == 0, row_part, 0.0),
                    jnp.where(at_end, col_part, 0.0),
                ]
            )
            packed = spread_ends(packed)
            yield [], FAR
            packed = settle(packed)
            row_new = BETA * prevs[m][0] + (1.0 - BETA) * (packed[:rows] / (cols * n_col))
            col_new = BETA * prevs[m][1] + (1.0 - BETA) * (packed[rows:] / (rows * n_row))
            row_scale = lax.rsqrt(jnp.where(place == 0, row_new[half:], row_new[:half]))
            col_scale = lax.rsqrt(col_new)
            energy = None
            for g in range(GROUPS):
                low, high = g * half // GROUPS, (g + 1) * half // GROUPS
                wide = settle(total)[low:high].astype(F32)
                raw = wide * row_scale[low:high, None] * col_scale[None, :]
                part = jnp.sum(raw * raw)
                energy = part if energy is None else energy + part
                if g == GROUPS // 2 - 1:
                    yield [energy], 1
            energy = jnp.broadcast_to(energy, (8, LANES))
            for axis in ("col", "row"):
                for distance in distances(axis):
                    energy = butterfly(energy, axis, distance)
                    yield [], 1
                    energy = settle(energy)
            energy = energy + lax.ppermute(energy, "dp", [(0, last), (last, 0)])
            yield [], FAR
            energy = settle(energy)[0, 0]
            rms = jnp.sqrt(energy / (rows * n_row * cols * n_col))
            row_final = row_scale / jnp.maximum(1.0, rms)
            scales[m] = [
                total,
                jnp.broadcast_to(row_final[:, None], (half, LANES)),
                jnp.broadcast_to(col_scale[None, :], (8, cols)),
            ]
            results[m] = (row_new, col_new)
            yield [scales[m][1], scales[m][2]], 1

        workers = [statistics(0), statistics(1)]
        wakes = [0, 0]

        def advance(m):
            try:
                return next(workers[m])
            except StopIteration:
                return [], steps

        outs = [None, None]
        inflight = {}
        arrived = {}
        tied = []
        for s in range(steps):
            before, tied = tied, []
            batch = []
            for index, (kind, m, begin) in enumerate(segments):
                members = [p for p in range(n_dp) if 0 <= s - LAG * p - begin < counts[m]]
                if not members:
                    continue
                while kind == "spread" and m not in scales:
                    advance(m)
                    wakes[m] = steps
                size = sizes[m]
                half = shapes[m][0] // 2
                gots = [inflight.pop((index, d, s - LAG), None) for d in range(2)]
                sending = min(members) < last
                number = s - begin - LAG * position
                at = jnp.clip(number, 0, counts[m] - 1) * size
                if kind == "sum":
                    at = jnp.concatenate([at + jnp.array([0, half]), place[None]])
                    chunk = s - begin - LAG * last if last in members else None
                    values, state = sum_step(
                        at.astype(jnp.int32), gots, grads[m], size, chunk, counts[m], states.get(m)
                    )
                    if chunk is not None:
                        states[m] = state
                        finished[m] += 1
                else:
                    valid = (number >= 0) & (number < counts[m])
                    source = valid & (position == 0)
                    at = jnp.concatenate([at + jnp.array([half, 0]), valid, source])
                    chunk = s - begin if 0 in members else None
                    outs[m], *values = spread_step(
                        at.astype(jnp.int32),
                        gots,
                        scales[m],
                        chunk,
                        outs[m],
                        shapes[m],
                        size,
                        sending,
                    )
                if sending:
                    for d in range(2):
                        batch.append((index, d, members, values[d]))
            if batch:
                values, _ = lax.optimization_barrier(
                    ([b[3] for b in batch], (before, arrived.get(s - LAG, [])))
                )
                tied = list(values)
            arrived[s] = []
            for (index, d, members, _), value in zip(batch, tied):
                inflight[index, d, s] = hop(value, d, members)
                arrived[s].append(inflight[index, d, s])
            cell[0] = list(tied)
            for m in range(2):
                if s >= wakes[m]:
                    ties, wait = advance(m)
                    tied = tied + ties
                    wakes[m] = s + wait
        return (outs[0], *results[0], outs[1], *results[1])

    return local


def solution(mesh):
    return jax.shard_map(
        make_local(dict(mesh.shape)),
        mesh=mesh,
        in_specs=(
            P("dp", "row", "col"),
            P("dp", "row", "col"),
            P("row"),
            P("col"),
            P("row"),
            P("col"),
        ),
        out_specs=(P("row", "col"), P("row"), P("col"), P("row", "col"), P("row"), P("col")),
        check_vma=False,
    )
```

time: 1200 us -> 961 us (0.80)
  starting transfers between devices: 767 us -> 395 us
  other arithmetic: 247 us -> 21.7 us
  Pallas kernels: 0 us -> 147 us
  waiting for transfers between devices: 126 us -> 252 us
  local copies, waits for them, and re-layouts: 21.8 us -> 122 us
    ppermute x288 -> x160, starting transfers between devices: 737 us -> 353 us  [hop(): return lax.ppermute(value, 'dp', pairs)]
    pallas_call x0 -> x88, Pallas kernels: none -> 147 us  [the longest x44 86.9 us: spread_step(): pl.pallas_call(functools.partial(spread_kernel, size, chunk, gots[0] is n...]
    unnamed x412 -> x340, local copies, waits for them, and re-layouts: 7.27 us -> 120 us
    dynamic_update_slice x148 -> x0, other arithmetic: 107 us -> none  [local(): outs[m] = lax.dynamic_update_slice(outs[m], value, ((1 - d) * half + at, 0))]
    ppermute x288 -> x160, waiting for transfers between devices: 117 us -> 211 us  [hop(): return lax.ppermute(value, 'dp', pairs)]
    unnamed x51 -> x8, other arithmetic: 78.9 us -> 0.01 us
    ppermute x6, starting transfers between devices: 9.01 us -> 27 us  [spread_ends(): total = total + lax.ppermute(value, 'dp', some)]
    ppermute x6, waiting for transfers between devices: 1.11 us -> 17.3 us  [spread_ends(): total = total + lax.ppermute(value, 'dp', some)]
  transfers between devices with their start and end apart: 308 -> 180, of which waited for: 60 -> 65; matrix products, arithmetic and copies ran while one was open for 21% -> 2% of each run, Pallas kernels for 0% -> 15%
where the time goes in v3:
time: 961 us; the launch traced here: 949 us
  starting transfers between devices  395 us (41%)
  waiting for transfers between devices  252 us (26%)
  Pallas kernels  147 us (15%)
  local copies, waits for them, and re-layouts  122 us (13%)
  other arithmetic  21.7 us (2%)
  between operations  11.8 us (1%)
    ppermute x160, starting transfers between devices, hop(): return lax.ppermute(value, 'dp', pairs)  353 us
    ppermute x160, waiting for transfers between devices, hop(): return lax.ppermute(value, 'dp', pairs)  211 us
    unnamed x340, local copies, waits for them, and re-layouts  120 us
    pallas_call x44, Pallas kernels, spread_step(): pl.pallas_call(functools.partial(spread_kernel, size, chunk, gots[0] is n...  86.9 us
    pallas_call x44, Pallas kernels, sum_step(): pl.pallas_call(functools.partial(sum_kernel, gots[0] is not None, chunk i...  59.7 us
    ppermute x6, starting transfers between devices, spread_ends(): total = total + lax.ppermute(value, 'dp', some)  27 us
  transfers between devices with their start and end apart: 180, of which 65 were waited for; matrix products, arithmetic and copies ran while one was open for 2% of the time, Pallas kernels for 15%

profile of v3, /device:TPU:0, one launch (start us, length us, event | category | flops | bytes accessed | tf_op | source)
XLA Modules:
  0.0 948.6 jit_solution(2999862589242042318)
XLA Ops:
  3.5 5.8 copy-done
  10.0 5.2 collective-permute-start.2
  21.5 6.0 collective-permute-done.2.refs_0_
  33.5 5.1 collective-permute-done.refs_0_
  44.8 5.1 collective-permute-done.6.refs_0_
  171.3 4.7 collective-permute-start.30
  182.9 5.1 collective-permute-start.28
  196.1 6.8 collective-permute-start.38
  203.6 5.8 copy-done.2
  221.8 4.8 collective-permute-start.36
  257.1 4.6 collective-permute-start.40
  266.5 4.6 collective-permute-start.50
  297.3 5.8 copy-done.3
  310.9 5.8 copy-done.4
  321.4 6.0 collective-permute-start.64
  333.0 4.6 collective-permute-start.52
  338.9 5.2 collective-permute-start.63
  344.1 10.8 %collective-permute-done.63 = f32[9216]{0:T(1024)S(1)} collective-permute-done((f32[9216]{0:T(1024)S(1)}, f32[9216]{0:T(1024)S(1)}, u32[]{:S(2)}, u32[]{:S(2)}) %collective-permute-start.63) | collective-permute-done | bytes 36896 | tf_op jit(solution)/shard_map/ppermute | solution.py:237
  368.2 8.2 collective-permute-start.56
  382.2 5.8 copy-done.5
  428.2 5.8 copy-done.6
  445.8 4.6 collective-permute-start.76
  459.3 6.6 collective-permute-done.81
  478.6 5.1 collective-permute-start.88
  514.3 4.6 collective-permute-start.90
  566.3 17.8 %spread_step.51 = (bf16[1024,8192]{1,0:T(8,128)(2,1)}, bf16[32,8192]{1,0:T(8,128)(2,1)S(1)}, bf16[32,8192]{1,0:T(8,128)(2,1)S(1)}) custom-call(s32[6]{0:T(128)S(1)} %get-tuple-element.1028.at_ref, bf16[32,8192]{1,0:T(8,128)(2,1)S(1)} %collective-permute-done.98.refs_0_, ...), custom_call_target="tpu_custom_call", output_to_operand_aliasing={{0}: (6, {})} | custom-call | flops 524288 | bytes 3145728 | tf_op jit(solution)/shard_map/spread_step/pallas_call | solution.py:205
  589.9 5.5 collective-permute-start.114
  598.9 6.2 collective-permute-start.115
  619.5 5.4 collective-permute-start.106
  652.1 4.7 collective-permute-done.119.refs_1_
  711.1 6.0 collective-permute-start.138
  721.7 7.7 collective-permute-done.135.refs_1_
  758.8 4.6 collective-permute-start.150
  777.7 6.0 collective-permute-done.151.refs_1_
  789.0 6.0 collective-permute-done.149.refs_1_
  800.2 6.0 collective-permute-done.155.refs_1_
  811.5 6.0 collective-permute-done.153.refs_1_
  822.7 6.0 collective-permute-done.159.refs_1_
  833.9 6.0 collective-permute-done.157.refs_1_
  845.2 6.0 collective-permute-done.163.refs_1_
  856.4 6.0 collective-permute-done.161.refs_1_
  867.6 6.0 collective-permute-done.167.refs_1_
  878.9 6.0 collective-permute-done.165.refs_1_
  890.1 6.0 collective-permute-done.171.refs_1_
  899.5 7.8 collective-permute-done.169.refs_1_
  910.7 7.8 collective-permute-done.175.refs_1_
  921.9 7.8 collective-permute-done.173.refs_1_
  936.2 4.8 collective-permute-done.179.refs_1_
  (863 shorter events, 642.7 us)
Async XLA Ops:
  16.6 22.1 %collective-permute-start = (bf16[32,8192]{1,0:T(8,128)(2,1)S(1)}, bf16[32,8192]{1,0:T(8,128)(2,1)S(1)}, u32[]{:S(2)}, u32[]{:S(2)}) collective-permute-start(bf16[32,8192]{1,0:T(8,128)(2,1)S(1)} %get-tuple-element.486), channel_id=1, source_target_pairs={{0,8},{1,9},{2,10},{3,11},{4,12},{5,13},{6,14},{7,15}} | collective-permute-start | bytes 1572872 | tf_op jit(solution)/shard_map/ppermute | solution.py:275
  28.3 21.6 %collective-permute-start.6 = (bf16[32,8192]{1,0:T(8,128)(2,1)S(1)}, bf16[32,8192]{1,0:T(8,128)(2,1)S(1)}, u32[]{:S(2)}, u32[]{:S(2)}) collective-permute-start(bf16[32,8192]{1,0:T(8,128)(2,1)S(1)} %get-tuple-element.492), channel_id=1, source_target_pairs={{0,8},{8,16},{1,9},{9,17},{2,10},{10,18},{3,11},{11,19},{4,12},{12... | collective-permute-start | bytes 1572872 | tf_op jit(solution)/shard_map/ppermute | solution.py:275
  39.6 21.6 %collective-permute-start.4 = (bf16[32,8192]{1,0:T(8,128)(2,1)S(1)}, bf16[32,8192]{1,0:T(8,128)(2,1)S(1)}, u32[]{:S(2)}, u32[]{:S(2)}) collective-permute-start(bf16[32,8192]{1,0:T(8,128)(2,1)S(1)} %get-tuple-element.494), channel_id=1, source_target_pairs={{0,8},{8,16},{1,9},{9,17},{2,10},{10,18},{3,11},{11,19},{4,12},{12... | collective-permute-start | bytes 1572872 | tf_op jit(solution)/shard_map/ppermute | solution.py:275
  50.8 21.6 %collective-permute-start.10 = (bf16[32,8192]{1,0:T(8,128)(2,1)S(1)}, bf16[32,8192]{1,0:T(8,128)(2,1)S(1)}, u32[]{:S(2)}, u32[]{:S(2)}) collective-permute-start(bf16[32,8192]{1,0:T(8,128)(2,1)S(1)} %get-tuple-element.500), channel_id=1, source_target_pairs={{0,8},{8,16},{16,24},{1,9},{9,17},{17,25},{2,10},{10,18},{18,26},{... | collective-permute-start | bytes 1572872 | tf_op jit(solution)/shard_map/ppermute | solution.py:275
  62.0 21.6 %collective-permute-start.8 = (bf16[32,8192]{1,0:T(8,128)(2,1)S(1)}, bf16[32,8192]{1,0:T(8,128)(2,1)S(1)}, u32[]{:S(2)}, u32[]{:S(2)}) collective-permute-start(bf16[32,8192]{1,0:T(8,128)(2,1)S(1)} %get-tuple-element.502), channel_id=1, source_target_pairs={{0,8},{8,16},{16,24},{1,9},{9,17},{17,25},{2,10},{10,18},{18,26},{... | collective-permute-start | bytes 1572872 | tf_op jit(solution)/shard_map/ppermute | solution.py:275
  73.6 21.3 %collective-permute-start.14 = (bf16[32,8192]{1,0:T(8,128)(2,1)S(1)}, bf16[32,8192]{1,0:T(8,128)(2,1)S(1)}, u32[]{:S(2)}, u32[]{:S(2)}) collective-permute-start(bf16[32,8192]{1,0:T(8,128)(2,1)S(1)} %get-tuple-element.511), channel_id=1, source_target_pairs={{0,8},{8,16},{16,24},{1,9},{9,17},{17,25},{2,10},{10,18},{18,26},{... | collective-permute-start | bytes 1572872 | tf_op jit(solution)/shard_map/ppermute | solution.py:275
  96.1 21.3 %collective-permute-start.18 = (bf16[32,8192]{1,0:T(8,128)(2,1)S(1)}, bf16[32,8192]{1,0:T(8,128)(2,1)S(1)}, u32[]{:S(2)}, u32[]{:S(2)}) collective-permute-start(bf16[32,8192]{1,0:T(8,128)(2,1)S(1)} %get-tuple-element.525), channel_id=1, source_target_pairs={{0,8},{8,16},{16,24},{1,9},{9,17},{17,25},{2,10},{10,18},{18,26},{... | collective-permute-start | bytes 1572872 | tf_op jit(solution)/shard_map/ppermute | solution.py:275
  155.6 22.6 %collective-permute-start.24 = (bf16[32,8192]{1,0:T(8,128)(2,1)S(1)}, bf16[32,8192]{1,0:T(8,128)(2,1)S(1)}, u32[]{:S(2)}, u32[]{:S(2)}) collective-permute-start(bf16[32,8192]{1,0:T(8,128)(2,1)S(1)} %get-tuple-element.555), channel_id=1, source_target_pairs={{0,8},{8,16},{16,24},{1,9},{9,17},{17,25},{2,10},{10,18},{18,26},{... | collective-permute-start | bytes 1572872 | tf_op jit(solution)/shard_map/ppermute | solution.py:275
  182.9 28.1 %collective-permute-start.28 = (bf16[32,8192]{1,0:T(8,128)(2,1)S(1)}, bf16[32,8192]{1,0:T(8,128)(2,1)S(1)}, u32[]{:S(2)}, u32[]{:S(2)}) collective-permute-start(bf16[32,8192]{1,0:T(8,128)(2,1)S(1)} %get-tuple-element.569), channel_id=1, source_target_pairs={{0,8},{8,16},{16,24},{1,9},{9,17},{17,25},{2,10},{10,18},{18,26},{... | collective-permute-start | bytes 1572872 | tf_op jit(solution)/shard_map/ppermute | solution.py:275
  188.0 24.3 %collective-permute-start.29 = (bf16[32,8192]{1,0:T(8,128)(2,1)S(1)}, bf16[32,8192]{1,0:T(8,128)(2,1)S(1)}, u32[]{:S(2)}, u32[]{:S(2)}) collective-permute-start(bf16[32,8192]{1,0:T(8,128)(2,1)S(1)} %get-tuple-element.570), channel_id=1, source_target_pairs={{24,16},{16,8},{8,0},{25,17},{17,9},{9,1},{26,18},{18,10},{10,2},{... | collective-permute-start | bytes 1572872 | tf_op jit(solution)/shard_map/ppermute | solution.py:275
  195.4 31.2 %collective-permute-start.34 = (bf16[32,8192]{1,0:T(8,128)(2,1)S(1)}, bf16[32,8192]{1,0:T(8,128)(2,1)S(1)}, u32[]{:S(2)}, u32[]{:S(2)}) collective-permute-start(bf16[32,8192]{1,0:T(8,128)(2,1)S(1)} %get-tuple-element.585), channel_id=1, source_target_pairs={{8,16},{16,24},{9,17},{17,25},{10,18},{18,26},{11,19},{19,27},{12,... | collective-permute-start | bytes 1572872 | tf_op jit(solution)/shard_map/ppermute | solution.py:275
  196.1 31.3 %collective-permute-start.38 = (bf16[128,2048]{1,0:T(8,128)(2,1)S(1)}, bf16[128,2048]{1,0:T(8,128)(2,1)S(1)}, u32[]{:S(2)}, u32[]{:S(2)}) collective-permute-start(bf16[128,2048]{1,0:T(8,128)(2,1)S(1)} %get-tuple-element.587), channel_id=1, source_target_pairs={{0,8},{1,9},{2,10},{3,11},{4,12},{5,13},{6,14},{7,15}} | collective-permute-start | bytes 1572872 | tf_op jit(solution)/shard_map/ppermute | solution.py:275
  202.9 25.2 %collective-permute-start.39 = (bf16[128,2048]{1,0:T(8,128)(2,1)S(1)}, bf16[128,2048]{1,0:T(8,128)(2,1)S(1)}, u32[]{:S(2)}, u32[]{:S(2)}) collective-permute-start(bf16[128,2048]{1,0:T(8,128)(2,1)S(1)} %get-tuple-element.588), channel_id=1, source_target_pairs={{24,16},{25,17},{26,18},{27,19},{28,20},{29,21},{30,22},{31,23}} | collective-permute-start | bytes 1572872 | tf_op jit(solution)/shard_map/ppermute | solution.py:275
  239.6 22.1 %collective-permute-start.44 = (bf16[32,8192]{1,0:T(8,128)(2,1)}, bf16[32,8192]{1,0:T(8,128)(2,1)S(1)}, u32[]{:S(2)}, u32[]{:S(2)}) collective-permute-start(bf16[32,8192]{1,0:T(8,128)(2,1)} %get-tuple-element.607), channel_id=1, source_target_pairs={{16,24},{17,25},{18,26},{19,27},{20,28},{21,29},{22,30},{23,31}} | collective-permute-start | bytes 1572872 | tf_op jit(solution)/shard_map/ppermute | solution.py:275
  240.8 21.6 %collective-permute-start.42 = (bf16[128,2048]{1,0:T(8,128)(2,1)}, bf16[128,2048]{1,0:T(8,128)(2,1)S(1)}, u32[]{:S(2)}, u32[]{:S(2)}) collective-permute-start(bf16[128,2048]{1,0:T(8,128)(2,1)} %get-tuple-element.609), channel_id=1, source_target_pairs={{0,8},{8,16},{1,9},{9,17},{2,10},{10,18},{3,11},{11,19},{4,12},{12... | collective-permute-start | bytes 1572872 | tf_op jit(solution)/shard_map/ppermute | solution.py:275
  266.5 30.8 %collective-permute-start.50 = (bf16[128,2048]{1,0:T(8,128)(2,1)}, bf16[128,2048]{1,0:T(8,128)(2,1)S(1)}, u32[]{:S(2)}, u32[]{:S(2)}) collective-permute-start(bf16[128,2048]{1,0:T(8,128)(2,1)} %get-tuple-element.619), channel_id=1, source_target_pairs={{0,8},{8,16},{16,24},{1,9},{9,17},{17,25},{2,10},{10,18},{18,26},{... | collective-permute-start | bytes 1572872 | tf_op jit(solution)/shard_map/ppermute | solution.py:275
  271.1 26.1 %collective-permute-start.51 = (bf16[128,2048]{1,0:T(8,128)(2,1)}, bf16[128,2048]{1,0:T(8,128)(2,1)S(1)}, u32[]{:S(2)}, u32[]{:S(2)}) collective-permute-start(bf16[128,2048]{1,0:T(8,128)(2,1)} %get-tuple-element.620), channel_id=1, source_target_pairs={{24,16},{16,8},{8,0},{25,17},{17,9},{9,1},{26,18},{18,10},{10,2},{... | collective-permute-start | bytes 1572872 | tf_op jit(solution)/shard_map/ppermute | solution.py:275
  278.7 32.2 %collective-permute-start.48 = (bf16[128,2048]{1,0:T(8,128)(2,1)}, bf16[128,2048]{1,0:T(8,128)(2,1)S(1)}, u32[]{:S(2)}, u32[]{:S(2)}) collective-permute-start(bf16[128,2048]{1,0:T(8,128)(2,1)} %get-tuple-element.621), channel_id=1, source_target_pairs={{0,8},{8,16},{16,24},{1,9},{9,17},{17,25},{2,10},{10,18},{18,26},{... | collective-permute-start | bytes 1572872 | tf_op jit(solution)/shard_map/ppermute | solution.py:275
  280.2 30.7 %collective-permute-start.49 = (bf16[128,2048]{1,0:T(8,128)(2,1)}, bf16[128,2048]{1,0:T(8,128)(2,1)S(1)}, u32[]{:S(2)}, u32[]{:S(2)}) collective-permute-start(bf16[128,2048]{1,0:T(8,128)(2,1)} %get-tuple-element.622), channel_id=1, source_target_pairs={{24,16},{16,8},{8,0},{25,17},{17,9},{9,1},{26,18},{18,10},{10,2},{... | collective-permute-start | bytes 1572872 | tf_op jit(solution)/shard_map/ppermute | solution.py:275
  330.3 24.6 %collective-permute-start.54 = (bf16[128,2048]{1,0:T(8,128)(2,1)S(1)}, bf16[128,2048]{1,0:T(8,128)(2,1)S(1)}, u32[]{:S(2)}, u32[]{:S(2)}) collective-permute-start(bf16[128,2048]{1,0:T(8,128)(2,1)S(1)} %copy-done.34), channel_id=1, source_target_pairs={{0,8},{8,16},{16,24},{1,9},{9,17},{17,25},{2,10},{10,18},{18,26},{... | collective-permute-start | bytes 1572872 | tf_op jit(solution)/shard_map/ppermute | solution.py:275
  331.7 23.3 %collective-permute-start.55 = (bf16[128,2048]{1,0:T(8,128)(2,1)S(1)}, bf16[128,2048]{1,0:T(8,128)(2,1)S(1)}, u32[]{:S(2)}, u32[]{:S(2)}) collective-permute-start(bf16[128,2048]{1,0:T(8,128)(2,1)S(1)} %copy-done.32), channel_id=1, source_target_pairs={{24,16},{16,8},{8,0},{25,17},{17,9},{9,1},{26,18},{18,10},{10,2},{... | collective-permute-start | bytes 1572872 | tf_op jit(solution)/shard_map/ppermute | solution.py:275
  333.0 29.8 %collective-permute-start.52 = (bf16[128,2048]{1,0:T(8,128)(2,1)S(1)}, bf16[128,2048]{1,0:T(8,128)(2,1)S(1)}, u32[]{:S(2)}, u32[]{:S(2)}) collective-permute-start(bf16[128,2048]{1,0:T(8,128)(2,1)S(1)} %get-tuple-element.632), channel_id=1, source_target_pairs={{0,8},{8,16},{16,24},{1,9},{9,17},{17,25},{2,10},{10,18},{18,26},{... | collective-permute-start | bytes 1572872 | tf_op jit(solution)/shard_map/ppermute | solution.py:275
  337.6 25.2 %collective-permute-start.53 = (bf16[128,2048]{1,0:T(8,128)(2,1)S(1)}, bf16[128,2048]{1,0:T(8,128)(2,1)S(1)}, u32[]{:S(2)}, u32[]{:S(2)}) collective-permute-start(bf16[128,2048]{1,0:T(8,128)(2,1)S(1)} %get-tuple-element.633), channel_id=1, source_target_pairs={{24,16},{16,8},{8,0},{25,17},{17,9},{9,1},{26,18},{18,10},{10,2},{... | collective-permute-start | bytes 1572872 | tf_op jit(solution)/shard_map/ppermute | solution.py:275
  357.0 25.2 %collective-permute-start.58 = (bf16[128,2048]{1,0:T(8,128)(2,1)}, bf16[128,2048]{1,0:T(8,128)(2,1)S(1)}, u32[]{:S(2)}, u32[]{:S(2)}) collective-permute-start(bf16[128,2048]{1,0:T(8,128)(2,1)} %get-tuple-element.644), channel_id=1, source_target_pairs={{0,8},{8,16},{16,24},{1,9},{9,17},{17,25},{2,10},{10,18},{18,26},{... | collective-permute-start | bytes 1572872 | tf_op jit(solution)/shard_map/ppermute | solution.py:275
  368.2 31.8 %collective-permute-start.56 = (bf16[128,2048]{1,0:T(8,128)(2,1)}, bf16[128,2048]{1,0:T(8,128)(2,1)S(1)}, u32[]{:S(2)}, u32[]{:S(2)}) collective-permute-start(bf16[128,2048]{1,0:T(8,128)(2,1)} %get-tuple-element.646), channel_id=1, source_target_pairs={{0,8},{8,16},{16,24},{1,9},{9,17},{17,25},{2,10},{10,18},{18,26},{... | collective-permute-start | bytes 1572872 | tf_op jit(solution)/shard_map/ppermute | solution.py:275
  376.4 23.6 %collective-permute-start.57 = (bf16[128,2048]{1,0:T(8,128)(2,1)}, bf16[128,2048]{1,0:T(8,128)(2,1)S(1)}, u32[]{:S(2)}, u32[]{:S(2)}) collective-permute-start(bf16[128,2048]{1,0:T(8,128)(2,1)} %get-tuple-element.647), channel_id=1, source_target_pairs={{24,16},{16,8},{8,0},{25,17},{17,9},{9,1},{26,18},{18,10},{10,2},{... | collective-permute-start | bytes 1572872 | tf_op jit(solution)/shard_map/ppermute | solution.py:275
  402.0 26.1 %collective-permute-start.66 = (bf16[128,2048]{1,0:T(8,128)(2,1)}, bf16[128,2048]{1,0:T(8,128)(2,1)S(1)}, u32[]{:S(2)}, u32[]{:S(2)}) collective-permute-start(bf16[128,2048]{1,0:T(8,128)(2,1)} %get-tuple-element.675), channel_id=1, source_target_pairs={{0,8},{8,16},{16,24},{1,9},{9,17},{17,25},{2,10},{10,18},{18,26},{... | collective-permute-start | bytes 1572872 | tf_op jit(solution)/shard_map/ppermute | solution.py:275
  406.6 21.6 %collective-permute-start.67 = (bf16[128,2048]{1,0:T(8,128)(2,1)}, bf16[128,2048]{1,0:T(8,128)(2,1)S(1)}, u32[]{:S(2)}, u32[]{:S(2)}) collective-permute-start(bf16[128,2048]{1,0:T(8,128)(2,1)} %get-tuple-element.676), channel_id=1, source_target_pairs={{24,16},{16,8},{8,0},{25,17},{17,9},{9,1},{26,18},{18,10},{10,2},{... | collective-permute-start | bytes 1572872 | tf_op jit(solution)/shard_map/ppermute | solution.py:275
  417.4 27.1 %collective-permute-start.72 = (bf16[128,2048]{1,0:T(8,128)(2,1)}, bf16[128,2048]{1,0:T(8,128)(2,1)S(1)}, u32[]{:S(2)}, u32[]{:S(2)}) collective-permute-start(bf16[128,2048]{1,0:T(8,128)(2,1)} %get-tuple-element.687), channel_id=1, source_target_pairs={{0,8},{8,16},{16,24},{1,9},{9,17},{17,25},{2,10},{10,18},{18,26},{... | collective-permute-start | bytes 1572872 | tf_op jit(solution)/shard_map/ppermute | solution.py:275
  421.1 23.4 %collective-permute-start.73 = (bf16[128,2048]{1,0:T(8,128)(2,1)}, bf16[128,2048]{1,0:T(8,128)(2,1)S(1)}, u32[]{:S(2)}, u32[]{:S(2)}) collective-permute-start(bf16[128,2048]{1,0:T(8,128)(2,1)} %get-tuple-element.688), channel_id=1, source_target_pairs={{24,16},{16,8},{8,0},{25,17},{17,9},{9,1},{26,18},{18,10},{10,2},{... | collective-permute-start | bytes 1572872 | tf_op jit(solution)/shard_map/ppermute | solution.py:275
  438.5 27.4 %collective-permute-start.70 = (bf16[128,2048]{1,0:T(8,128)(2,1)S(1)}, bf16[128,2048]{1,0:T(8,128)(2,1)S(1)}, u32[]{:S(2)}, u32[]{:S(2)}) collective-permute-start(bf16[128,2048]{1,0:T(8,128)(2,1)S(1)} %get-tuple-element.689), channel_id=1, source_target_pairs={{0,8},{8,16},{16,24},{1,9},{9,17},{17,25},{2,10},{10,18},{18,26},{... | collective-permute-start | bytes 1572872 | tf_op jit(solution)/shard_map/ppermute | solution.py:275
  443.1 22.8 %collective-permute-start.71 = (bf16[128,2048]{1,0:T(8,128)(2,1)S(1)}, bf16[128,2048]{1,0:T(8,128)(2,1)S(1)}, u32[]{:S(2)}, u32[]{:S(2)}) collective-permute-start(bf16[128,2048]{1,0:T(8,128)(2,1)S(1)} %get-tuple-element.690), channel_id=1, source_target_pairs={{24,16},{16,8},{8,0},{25,17},{17,9},{9,1},{26,18},{18,10},{10,2},{... | collective-permute-start | bytes 1572872 | tf_op jit(solution)/shard_map/ppermute | solution.py:275
  445.8 30.8 %collective-permute-start.76 = (bf16[128,2048]{1,0:T(8,128)(2,1)S(1)}, bf16[128,2048]{1,0:T(8,128)(2,1)S(1)}, u32[]{:S(2)}, u32[]{:S(2)}) collective-permute-start(bf16[128,2048]{1,0:T(8,128)(2,1)S(1)} %get-tuple-element.701), channel_id=1, source_target_pairs={{0,8},{8,16},{16,24},{1,9},{9,17},{17,25},{2,10},{10,18},{18,26},{... | collective-permute-start | bytes 1572872 | tf_op jit(solution)/shard_map/ppermute | solution.py:275
  450.4 26.2 %collective-permute-start.77 = (bf16[128,2048]{1,0:T(8,128)(2,1)S(1)}, bf16[128,2048]{1,0:T(8,128)(2,1)S(1)}, u32[]{:S(2)}, u32[]{:S(2)}) collective-permute-start(bf16[128,2048]{1,0:T(8,128)(2,1)S(1)} %get-tuple-element.702), channel_id=1, source_target_pairs={{24,16},{16,8},{8,0},{25,17},{17,9},{9,1},{26,18},{18,10},{10,2},{... | collective-permute-start | bytes 1572872 | tf_op jit(solution)/shard_map/ppermute | solution.py:275
  528.2 26.4 %collective-permute-start.100 = (bf16[32,8192]{1,0:T(8,128)(2,1)}, bf16[32,8192]{1,0:T(8,128)(2,1)S(1)}, u32[]{:S(2)}, u32[]{:S(2)}) collective-permute-start(bf16[32,8192]{1,0:T(8,128)(2,1)} %get-tuple-element.763), channel_id=1, source_target_pairs={{0,8},{8,16},{16,24},{1,9},{9,17},{17,25},{2,10},{10,18},{18,26},{... | collective-permute-start | bytes 1572872 | tf_op jit(solution)/shard_map/ppermute | solution.py:275
  531.9 22.7 %collective-permute-start.101 = (bf16[32,8192]{1,0:T(8,128)(2,1)}, bf16[32,8192]{1,0:T(8,128)(2,1)S(1)}, u32[]{:S(2)}, u32[]{:S(2)}) collective-permute-start(bf16[32,8192]{1,0:T(8,128)(2,1)} %get-tuple-element.764), channel_id=1, source_target_pairs={{24,16},{16,8},{8,0},{25,17},{17,9},{9,1},{26,18},{18,10},{10,2},{... | collective-permute-start | bytes 1572872 | tf_op jit(solution)/shard_map/ppermute | solution.py:275
  539.4 26.8 %collective-permute-start.98 = (bf16[32,8192]{1,0:T(8,128)(2,1)}, bf16[32,8192]{1,0:T(8,128)(2,1)S(1)}, u32[]{:S(2)}, u32[]{:S(2)}) collective-permute-start(bf16[32,8192]{1,0:T(8,128)(2,1)} %get-tuple-element.765), channel_id=1, source_target_pairs={{0,8},{8,16},{16,24},{1,9},{9,17},{17,25},{2,10},{10,18},{18,26},{... | collective-permute-start | bytes 1572872 | tf_op jit(solution)/shard_map/ppermute | solution.py:275
  540.9 25.3 %collective-permute-start.99 = (bf16[32,8192]{1,0:T(8,128)(2,1)}, bf16[32,8192]{1,0:T(8,128)(2,1)}, u32[]{:S(2)}, u32[]{:S(2)}) collective-permute-start(bf16[32,8192]{1,0:T(8,128)(2,1)} %get-tuple-element.766), channel_id=1, source_target_pairs={{24,16},{16,8},{8,0},{25,17},{17,9},{9,1},{26,18},{18,10},{10,2},{... | collective-permute-start | bytes 1572872 | tf_op jit(solution)/shard_map/ppermute | solution.py:275
  559.9 29.9 %collective-permute-start.112 = (f32[2048]{0:T(1024)S(1)}, f32[2048]{0:T(1024)S(1)}, u32[]{:S(2)}, u32[]{:S(2)}) collective-permute-start(f32[2048]{0:T(1024)S(1)} %add.431), channel_id=1, source_target_pairs={{0,4},{2,6},{4,0},{6,2},{1,5},{3,7},{5,1},{7,3},{8,12},{10,14},{12... | collective-permute-start | bytes 24584 | tf_op jit(solution)/shard_map/ppermute | solution.py:242
  560.6 49.2 %collective-permute-start.104 = (bf16[32,8192]{1,0:T(8,128)(2,1)S(1)}, bf16[32,8192]{1,0:T(8,128)(2,1)S(1)}, u32[]{:S(2)}, u32[]{:S(2)}) collective-permute-start(bf16[32,8192]{1,0:T(8,128)(2,1)S(1)} %get-tuple-element.773), channel_id=1, source_target_pairs={{0,8},{8,16},{16,24},{1,9},{9,17},{17,25},{2,10},{10,18},{18,26},{... | collective-permute-start | bytes 1572872 | tf_op jit(solution)/shard_map/ppermute | solution.py:275
  564.9 44.9 %collective-permute-start.105 = (bf16[32,8192]{1,0:T(8,128)(2,1)S(1)}, bf16[32,8192]{1,0:T(8,128)(2,1)S(1)}, u32[]{:S(2)}, u32[]{:S(2)}) collective-permute-start(bf16[32,8192]{1,0:T(8,128)(2,1)S(1)} %get-tuple-element.774), channel_id=1, source_target_pairs={{24,16},{16,8},{8,0},{25,17},{17,9},{9,1},{26,18},{18,10},{10,2},{... | collective-permute-start | bytes 1572872 | tf_op jit(solution)/shard_map/ppermute | solution.py:275
  584.1 33.3 %collective-permute-start.102 = (bf16[32,8192]{1,0:T(8,128)(2,1)S(1)}, bf16[32,8192]{1,0:T(8,128)(2,1)S(1)}, u32[]{:S(2)}, u32[]{:S(2)}) collective-permute-start(bf16[32,8192]{1,0:T(8,128)(2,1)S(1)} %get-tuple-element.775), channel_id=1, source_target_pairs={{0,8},{8,16},{16,24},{1,9},{9,17},{17,25},{2,10},{10,18},{18,26},{... | collective-permute-start | bytes 1572872 | tf_op jit(solution)/shard_map/ppermute | solution.py:275
  588.5 28.8 %collective-permute-start.103 = (bf16[32,8192]{1,0:T(8,128)(2,1)S(1)}, bf16[32,8192]{1,0:T(8,128)(2,1)S(1)}, u32[]{:S(2)}, u32[]{:S(2)}) collective-permute-start(bf16[32,8192]{1,0:T(8,128)(2,1)S(1)} %get-tuple-element.776), channel_id=1, source_target_pairs={{24,16},{16,8},{8,0},{25,17},{17,9},{9,1},{26,18},{18,10},{10,2},{... | collective-permute-start | bytes 1572872 | tf_op jit(solution)/shard_map/ppermute | solution.py:275
  619.5 23.0 %collective-permute-start.106 = (bf16[32,8192]{1,0:T(8,128)(2,1)}, bf16[32,8192]{1,0:T(8,128)(2,1)S(1)}, u32[]{:S(2)}, u32[]{:S(2)}) collective-permute-start(bf16[32,8192]{1,0:T(8,128)(2,1)} %get-tuple-element.785), channel_id=1, source_target_pairs={{0,8},{8,16},{16,24},{1,9},{9,17},{17,25},{2,10},{10,18},{18,26},{... | collective-permute-start | bytes 1572872 | tf_op jit(solution)/shard_map/ppermute | solution.py:275
  644.6 23.1 %collective-permute-start.116 = (bf16[32,8192]{1,0:T(8,128)(2,1)}, bf16[32,8192]{1,0:T(8,128)(2,1)S(1)}, u32[]{:S(2)}, u32[]{:S(2)}) collective-permute-start(bf16[32,8192]{1,0:T(8,128)(2,1)} %get-tuple-element.810), channel_id=1, source_target_pairs={{0,8},{8,16},{16,24},{1,9},{9,17},{17,25},{2,10},{10,18},{18,26},{... | collective-permute-start | bytes 1572872 | tf_op jit(solution)/shard_map/ppermute | solution.py:275
  673.2 25.3 %collective-permute-start.120 = (bf16[32,8192]{1,0:T(8,128)(2,1)S(1)}, bf16[32,8192]{1,0:T(8,128)(2,1)S(1)}, u32[]{:S(2)}, u32[]{:S(2)}) collective-permute-start(bf16[32,8192]{1,0:T(8,128)(2,1)S(1)} %get-tuple-element.820), channel_id=1, source_target_pairs={{0,8},{8,16},{16,24},{1,9},{9,17},{17,25},{2,10},{10,18},{18,26},{... | collective-permute-start | bytes 1572872 | tf_op jit(solution)/shard_map/ppermute | solution.py:275
  680.5 25.5 %collective-permute-start.126 = (bf16[32,8192]{1,0:T(8,128)(2,1)S(1)}, bf16[32,8192]{1,0:T(8,128)(2,1)S(1)}, u32[]{:S(2)}, u32[]{:S(2)}) collective-permute-start(bf16[32,8192]{1,0:T(8,128)(2,1)S(1)} %get-tuple-element.828), channel_id=1, source_target_pairs={{0,8},{8,16},{16,24},{1,9},{9,17},{17,25},{2,10},{10,18},{18,26},{... | collective-permute-start | bytes 1572872 | tf_op jit(solution)/shard_map/ppermute | solution.py:275
  711.1 22.0 %collective-permute-start.138 = (bf16[128,2048]{1,0:T(8,128)(2,1)S(1)}, bf16[128,2048]{1,0:T(8,128)(2,1)S(1)}, u32[]{:S(2)}, u32[]{:S(2)}) collective-permute-start(bf16[128,2048]{1,0:T(8,128)(2,1)S(1)} %get-tuple-element.850), channel_id=1, source_target_pairs={{0,8},{1,9},{2,10},{3,11},{4,12},{5,13},{6,14},{7,15}} | collective-permute-start | bytes 1572872 | tf_op jit(solution)/shard_map/ppermute | solution.py:275
  (302 other events, 3926.4 us)

commit v4 on v3

--- a/solution.py
+++ b/solution.py
@@ -14,6 +14,7 @@
 GROUPS = 4
 FAR = 2
 LANES = 128
+VMEM_BYTES = 48 * 1024 * 1024
 
 F32 = jnp.float32
 BF16 = jnp.bfloat16
@@ -35,7 +36,7 @@
     return rows
 
 
-def sum_kernel(with_got, with_total, first_total, at_ref, *refs):
+def sum_kernel(with_got, with_total, first_total, place_ref, *refs):
     refs = list(refs)
     gots = [refs.pop(0), refs.pop(0)] if with_got else [None, None]
     owns = [refs.pop(0), refs.pop(0)]
@@ -45,7 +46,7 @@
         col_in = refs.pop(0)
     sends = [refs.pop(0), refs.pop(0)]
     rows, cols = sends[0].shape
-    low_end = at_ref[2] == 0
+    low_end = place_ref[0] == 0
     if with_total:
         total_ref, row_ref, col_ref = refs
 
@@ -77,14 +78,22 @@
         row_ref[...] = row_part
 
 
-def sum_step(at, gots, grad, size, chunk, count, state):
+def number_of(place, d, turn, last):
+    return turn - LAG * (place if d == 0 else last - place)
+
+
+def sum_step(place, gots, grad, size, turn, count, last, chunk, state):
     rows, cols = grad.shape
     half = rows // 2
     block = block_rows(size, cols)
     per = size // block
 
     def from_grad(d):
-        return pl.BlockSpec((block, cols), lambda i, at: (at[d] // block + i, 0))
+        def index(i, at):
+            number = jnp.clip(number_of(at[0], d, turn, last), 0, count - 1)
+            return ((d * count + number) * per + i, 0)
+
+        return pl.BlockSpec((block, cols), index)
 
     piece = pl.BlockSpec((block, cols), lambda i, at: (i, 0))
     operands, in_specs = [], []
@@ -120,16 +129,16 @@
         ),
         out_shape=out_shape,
         input_output_aliases=aliases,
-        compiler_params=pltpu.CompilerParams(vmem_limit_bytes=16 * 1024 * 1024),
+        compiler_params=pltpu.CompilerParams(vmem_limit_bytes=VMEM_BYTES),
         cost_estimate=pl.CostEstimate(
             flops=4 * size * cols, bytes_accessed=12 * size * cols, transcendentals=0
         ),
         name="sum_step",
-    )(at, *operands)
+    )(place, *operands)
     return out[:2], list(out[2:])
 
 
-def spread_kernel(size, chunk, with_got, with_out, sending, at_ref, *refs):
+def spread_kernel(turn, count, last, chunk, with_got, with_out, sending, place_ref, *refs):
     refs = list(refs)
     gots = [refs.pop(0), refs.pop(0)] if with_got else [None, None]
     if chunk is not None:
@@ -139,20 +148,21 @@
     out_ref = refs.pop(0)
     sends = [refs.pop(0), refs.pop(0)] if sending else [None, None]
     update, sems = refs
-    cols = update.shape[1]
+    size, cols = update.shape
+    numbers = [number_of(place_ref[0], d, turn, last) for d in range(2)]
+    valids = [(number >= 0) & (number < count) for number in numbers]
+    sources = [valids[0] & (place_ref[0] == 0), valids[1] & (place_ref[0] == last)]
 
     def copies(source, d):
-        row = pl.multiple_of(at_ref[d], 16)
+        row = pl.multiple_of(((1 - d) * count + jnp.clip(numbers[d], 0, count - 1)) * size, 16)
         keep = pltpu.make_async_copy(source, out_ref.at[pl.ds(row, size), :], sems.at[d, 0])
         give = pltpu.make_async_copy(source, sends[d], sems.at[d, 1]) if sending else None
         return keep, give
 
     for d in range(2):
-        valid = at_ref[2 + d] == 1
-        source = at_ref[4 + d] == 1
         if with_got:
 
-            @pl.when(valid & jnp.logical_not(source))
+            @pl.when(valids[d] & jnp.logical_not(sources[d]))
             def _():
                 keep, give = copies(gots[d], d)
                 keep.start()
@@ -161,7 +171,7 @@
 
         if chunk is not None:
 
-            @pl.when(source)
+            @pl.when(sources[d])
             def _():
                 for j in range(cols // LANES):
                     lanes = pl.ds(j * LANES, LANES)
@@ -174,7 +184,7 @@
 
     for d in range(2):
 
-        @pl.when(at_ref[2 + d] == 1)
+        @pl.when(valids[d])
         def _():
             keep, give = copies(update, d)
             keep.wait()
@@ -182,7 +192,7 @@
                 give.wait()
 
 
-def spread_step(at, gots, parts, chunk, out, shape, size, sending):
+def spread_step(place, gots, parts, size, turn, count, last, chunk, out, shape, sending):
     rows, cols = shape
     operands, in_specs, aliases = [], [], {}
     if gots[0] is not None:
@@ -204,7 +214,7 @@
         out_shape += [jax.ShapeDtypeStruct((size, cols), BF16)] * 2
     return pl.pallas_call(
         functools.partial(
-            spread_kernel, size, chunk, gots[0] is not None, out is not None, sending
+            spread_kernel, turn, count, last, chunk, gots[0] is not None, out is not None, sending
         ),
         grid_spec=pltpu.PrefetchScalarGridSpec(
             num_scalar_prefetch=1,
@@ -215,12 +225,12 @@
         ),
         out_shape=out_shape,
         input_output_aliases=aliases,
-        compiler_params=pltpu.CompilerParams(vmem_limit_bytes=16 * 1024 * 1024),
+        compiler_params=pltpu.CompilerParams(vmem_limit_bytes=VMEM_BYTES),
         cost_estimate=pl.CostEstimate(
             flops=2 * size * cols, bytes_accessed=12 * size * cols, transcendentals=0
         ),
         name="spread_step",
-    )(at, *operands)
+    )(place, *operands)
 
 
 def make_local(axis_sizes):
@@ -256,7 +266,7 @@
         counts = [chunk_count(rows) for rows, _ in shapes]
         sizes = [rows // 2 // count for (rows, _), count in zip(shapes, counts)]
 
-        position = jnp.stack([place, last - place])
+        here = place[None].astype(jnp.int32)
         at_end = (place == last) | (place == 0)
 
         segments = []
@@ -366,33 +376,30 @@
                     advance(m)
                     wakes[m] = steps
                 size = sizes[m]
-                half = shapes[m][0] // 2
                 gots = [inflight.pop((index, d, s - LAG), None) for d in range(2)]
                 sending = min(members) < last
-                number = s - begin - LAG * position
-                at = jnp.clip(number, 0, counts[m] - 1) * size
+                turn = s - begin
                 if kind == "sum":
-                    at = jnp.concatenate([at + jnp.array([0, half]), place[None]])
-                    chunk = s - begin - LAG * last if last in members else None
+                    chunk = turn - LAG * last if last in members else None
                     values, state = sum_step(
-                        at.astype(jnp.int32), gots, grads[m], size, chunk, counts[m], states.get(m)
+                        here, gots, grads[m], size, turn, counts[m], last, chunk, states.get(m)
                     )
                     if chunk is not None:
                         states[m] = state
                         finished[m] += 1
                 else:
-                    valid = (number >= 0) & (number < counts[m])
-                    source = valid & (position == 0)
-                    at = jnp.concatenate([at + jnp.array([half, 0]), valid, source])
-                    chunk = s - begin if 0 in members else None
+                    chunk = turn if 0 in members else None
                     outs[m], *values = spread_step(
-                        at.astype(jnp.int32),
+                        here,
                         gots,
                         scales[m],
+                        size,
+                        turn,
+                        counts[m],
+                        last,
                         chunk,
                         outs[m],
                         shapes[m],
-                        size,
                         sending,
                     )
                 if sending:

time: 961 us -> 895 us (0.931)
  local copies, waits for them, and re-layouts: 122 us -> 3.19 us
  Pallas kernels: 147 us -> 190 us
  waiting for transfers between devices: 252 us -> 279 us
  starting transfers between devices: 395 us -> 385 us
    unnamed x340 -> x36, local copies, waits for them, and re-layouts: 120 us -> 1.67 us
    pallas_call x44, Pallas kernels: 59.7 us -> 93.8 us  [sum_step(): pl.pallas_call(functools.partial(sum_kernel, gots[0] is not None, chunk i...]
    ppermute x160, waiting for transfers between devices: 211 us -> 236 us  [hop(): return lax.ppermute(value, 'dp', pairs)]
    ppermute x160, starting transfers between devices: 353 us -> 342 us  [hop(): return lax.ppermute(value, 'dp', pairs)]
    pallas_call x44, Pallas kernels: 86.9 us -> 96.5 us  [spread_step(): pl.pallas_call(functools.partial(spread_kernel, turn, count, last, chunk,...]
  transfers between devices with their start and end apart: 180 -> 180, of which waited for: 65 -> 75; matrix products, arithmetic and copies ran while one was open for 2% -> 2% of each run, Pallas kernels for 15% -> 21%
where the time goes in v4:
time: 895 us; the launch traced here: 881 us
  starting transfers between devices  385 us (43%)
  waiting for transfers between devices  279 us (31%)
  Pallas kernels  190 us (21%)
  other arithmetic  12.6 us (1%)
  between operations  10.5 us (1%)
    ppermute x160, starting transfers between devices, hop(): return lax.ppermute(value, 'dp', pairs)  342 us
    ppermute x160, waiting for transfers between devices, hop(): return lax.ppermute(value, 'dp', pairs)  236 us
    pallas_call x44, Pallas kernels, spread_step(): pl.pallas_call(functools.partial(spread_kernel, turn, count, last, chunk,...  96.5 us
    pallas_call x44, Pallas kernels, sum_step(): pl.pallas_call(functools.partial(sum_kernel, gots[0] is not None, chunk i...  93.8 us
    ppermute x6, starting transfers between devices, spread_ends(): total = total + lax.ppermute(value, 'dp', some)  26.2 us
    ppermute x12, waiting for transfers between devices, butterfly(): lax.ppermute(value, axis, [(i, i ^ distance) for i in range(n)])  18 us
  transfers between devices with their start and end apart: 180, of which 75 were waited for; matrix products, arithmetic and copies ran while one was open for 2% of the time, Pallas kernels for 21%

profile of v4, /device:TPU:0, one launch (start us, length us, event | category | flops | bytes accessed | tf_op | source)
XLA Modules:
  0.0 880.7 jit_solution(15465505864288594038)
XLA Ops:
  1.9 5.0 collective-permute-start.2
  10.9 8.3 collective-permute-done.2.refs_0_
  20.6 4.4 collective-permute-start.6
  25.7 4.7 collective-permute-done.refs_0_
  31.8 4.4 collective-permute-start.4
  36.9 4.7 collective-permute-done.6.refs_0_
  179.4 7.9 collective-permute-start.38
  193.0 4.6 collective-permute-start.36
  219.6 4.6 collective-permute-start.40
  275.8 4.6 collective-permute-start.52
  281.8 5.1 collective-permute-start.63
  286.9 11.0 %collective-permute-done.63 = f32[9216]{0:T(1024)S(1)} collective-permute-done((f32[9216]{0:T(1024)S(1)}, f32[9216]{0:T(1024)S(1)}, u32[]{:S(2)}, u32[]{:S(2)}) %collective-permute-start.63) | collective-permute-done | bytes 36896 | tf_op jit(solution)/shard_map/ppermute | solution.py:247
  309.0 8.1 collective-permute-start.56
  343.5 5.1 collective-permute-done.69.refs_1_
  354.7 4.8 collective-permute-done.67.refs_1_
  408.8 6.4 collective-permute-start.88
  421.6 4.6 collective-permute-start.86
  445.9 5.0 collective-permute-start.90
  456.2 4.6 collective-permute-start.100
  464.6 4.7 collective-permute-done.97.refs_1_
  485.3 4.4 collective-permute-start.104
  491.1 18.2 %spread_step.51 = (bf16[1024,8192]{1,0:T(8,128)(2,1)}, bf16[32,8192]{1,0:T(8,128)(2,1)S(1)}, bf16[32,8192]{1,0:T(8,128)(2,1)S(1)}) custom-call(s32[1]{0:T(128)} %bitcast.place_ref, bf16[32,8192]{1,0:T(8,128)(2,1)S(1)} %collective-permute-done.98.refs_0_, bf16[32,8192]{1,0:T(8,128)(2,1)} %collective-permute-done.99.refs_1_, ...), custom_call_target="tpu_custom_call", output_to_operand_aliasing={{0}: (6, {})} | custom-call | flops 524288 | bytes 3145728 | tf_op jit(solution)/shard_map/spread_step/pallas_call | solution.py:215
  509.3 4.4 collective-permute-start.102
  515.1 6.1 collective-permute-start.114
  524.4 6.5 collective-permute-start.115
  546.2 5.3 collective-permute-start.106
  575.8 5.1 collective-permute-done.119.refs_1_
  644.1 5.9 collective-permute-start.138
  653.6 8.3 collective-permute-done.135.refs_1_
  672.0 4.6 collective-permute-done.136.refs_0_
  679.9 4.4 collective-permute-start.144
  692.1 4.5 collective-permute-start.150
  710.3 6.0 collective-permute-done.151.refs_1_
  721.9 5.6 collective-permute-done.149.refs_1_
  733.0 5.7 collective-permute-done.155.refs_1_
  744.2 5.7 collective-permute-done.153.refs_1_
  755.5 5.7 collective-permute-done.159.refs_1_
  766.7 5.7 collective-permute-done.157.refs_1_
  777.9 5.7 collective-permute-done.163.refs_1_
  789.2 5.7 collective-permute-done.161.refs_1_
  800.4 5.7 collective-permute-done.167.refs_1_
  811.6 5.7 collective-permute-done.165.refs_1_
  822.9 5.7 collective-permute-done.171.refs_1_
  831.5 8.4 collective-permute-done.169.refs_1_
  842.7 8.4 collective-permute-done.175.refs_1_
  853.9 8.4 collective-permute-done.173.refs_1_
  866.9 6.7 collective-permute-done.179.refs_1_
  874.4 5.0 collective-permute-done.177.refs_1_
  (488 shorter events, 579.9 us)
Async XLA Ops:
  8.9 21.5 %collective-permute-start = (bf16[32,8192]{1,0:T(8,128)(2,1)S(1)}, bf16[32,8192]{1,0:T(8,128)(2,1)S(1)}, u32[]{:S(2)}, u32[]{:S(2)}) collective-permute-start(bf16[32,8192]{1,0:T(8,128)(2,1)S(1)} %get-tuple-element.486), channel_id=1, source_target_pairs={{0,8},{1,9},{2,10},{3,11},{4,12},{5,13},{6,14},{7,15}} | collective-permute-start | bytes 1572872 | tf_op jit(solution)/shard_map/ppermute | solution.py:285
  10.2 20.2 %collective-permute-start.1 = (bf16[32,8192]{1,0:T(8,128)(2,1)S(1)}, bf16[32,8192]{1,0:T(8,128)(2,1)S(1)}, u32[]{:S(2)}, u32[]{:S(2)}) collective-permute-start(bf16[32,8192]{1,0:T(8,128)(2,1)S(1)} %get-tuple-element.487), channel_id=1, source_target_pairs={{24,16},{25,17},{26,18},{27,19},{28,20},{29,21},{30,22},{31,23}} | collective-permute-start | bytes 1572872 | tf_op jit(solution)/shard_map/ppermute | solution.py:285
  20.6 21.1 %collective-permute-start.6 = (bf16[32,8192]{1,0:T(8,128)(2,1)S(1)}, bf16[32,8192]{1,0:T(8,128)(2,1)S(1)}, u32[]{:S(2)}, u32[]{:S(2)}) collective-permute-start(bf16[32,8192]{1,0:T(8,128)(2,1)S(1)} %get-tuple-element.492), channel_id=1, source_target_pairs={{0,8},{8,16},{1,9},{9,17},{2,10},{10,18},{3,11},{11,19},{4,12},{12... | collective-permute-start | bytes 1572872 | tf_op jit(solution)/shard_map/ppermute | solution.py:285
  31.8 21.1 %collective-permute-start.4 = (bf16[32,8192]{1,0:T(8,128)(2,1)S(1)}, bf16[32,8192]{1,0:T(8,128)(2,1)S(1)}, u32[]{:S(2)}, u32[]{:S(2)}) collective-permute-start(bf16[32,8192]{1,0:T(8,128)(2,1)S(1)} %get-tuple-element.494), channel_id=1, source_target_pairs={{0,8},{8,16},{1,9},{9,17},{2,10},{10,18},{3,11},{11,19},{4,12},{12... | collective-permute-start | bytes 1572872 | tf_op jit(solution)/shard_map/ppermute | solution.py:285
  43.0 21.1 %collective-permute-start.10 = (bf16[32,8192]{1,0:T(8,128)(2,1)S(1)}, bf16[32,8192]{1,0:T(8,128)(2,1)S(1)}, u32[]{:S(2)}, u32[]{:S(2)}) collective-permute-start(bf16[32,8192]{1,0:T(8,128)(2,1)S(1)} %get-tuple-element.500), channel_id=1, source_target_pairs={{0,8},{8,16},{16,24},{1,9},{9,17},{17,25},{2,10},{10,18},{18,26},{... | collective-permute-start | bytes 1572872 | tf_op jit(solution)/shard_map/ppermute | solution.py:285
  54.3 21.1 %collective-permute-start.8 = (bf16[32,8192]{1,0:T(8,128)(2,1)S(1)}, bf16[32,8192]{1,0:T(8,128)(2,1)S(1)}, u32[]{:S(2)}, u32[]{:S(2)}) collective-permute-start(bf16[32,8192]{1,0:T(8,128)(2,1)S(1)} %get-tuple-element.502), channel_id=1, source_target_pairs={{0,8},{8,16},{16,24},{1,9},{9,17},{17,25},{2,10},{10,18},{18,26},{... | collective-permute-start | bytes 1572872 | tf_op jit(solution)/shard_map/ppermute | solution.py:285
  66.4 20.2 %collective-permute-start.14 = (bf16[32,8192]{1,0:T(8,128)(2,1)S(1)}, bf16[32,8192]{1,0:T(8,128)(2,1)S(1)}, u32[]{:S(2)}, u32[]{:S(2)}) collective-permute-start(bf16[32,8192]{1,0:T(8,128)(2,1)S(1)} %get-tuple-element.511), channel_id=1, source_target_pairs={{0,8},{8,16},{16,24},{1,9},{9,17},{17,25},{2,10},{10,18},{18,26},{... | collective-permute-start | bytes 1572872 | tf_op jit(solution)/shard_map/ppermute | solution.py:285
  77.6 20.2 %collective-permute-start.12 = (bf16[32,8192]{1,0:T(8,128)(2,1)S(1)}, bf16[32,8192]{1,0:T(8,128)(2,1)S(1)}, u32[]{:S(2)}, u32[]{:S(2)}) collective-permute-start(bf16[32,8192]{1,0:T(8,128)(2,1)S(1)} %get-tuple-element.513), channel_id=1, source_target_pairs={{0,8},{8,16},{16,24},{1,9},{9,17},{17,25},{2,10},{10,18},{18,26},{... | collective-permute-start | bytes 1572872 | tf_op jit(solution)/shard_map/ppermute | solution.py:285
  88.8 20.2 %collective-permute-start.18 = (bf16[32,8192]{1,0:T(8,128)(2,1)S(1)}, bf16[32,8192]{1,0:T(8,128)(2,1)S(1)}, u32[]{:S(2)}, u32[]{:S(2)}) collective-permute-start(bf16[32,8192]{1,0:T(8,128)(2,1)S(1)} %get-tuple-element.525), channel_id=1, source_target_pairs={{0,8},{8,16},{16,24},{1,9},{9,17},{17,25},{2,10},{10,18},{18,26},{... | collective-permute-start | bytes 1572872 | tf_op jit(solution)/shard_map/ppermute | solution.py:285
  100.1 20.2 %collective-permute-start.16 = (bf16[32,8192]{1,0:T(8,128)(2,1)S(1)}, bf16[32,8192]{1,0:T(8,128)(2,1)S(1)}, u32[]{:S(2)}, u32[]{:S(2)}) collective-permute-start(bf16[32,8192]{1,0:T(8,128)(2,1)S(1)} %get-tuple-element.527), channel_id=1, source_target_pairs={{0,8},{8,16},{16,24},{1,9},{9,17},{17,25},{2,10},{10,18},{18,26},{... | collective-permute-start | bytes 1572872 | tf_op jit(solution)/shard_map/ppermute | solution.py:285
  111.3 20.2 %collective-permute-start.22 = (bf16[32,8192]{1,0:T(8,128)(2,1)S(1)}, bf16[32,8192]{1,0:T(8,128)(2,1)S(1)}, u32[]{:S(2)}, u32[]{:S(2)}) collective-permute-start(bf16[32,8192]{1,0:T(8,128)(2,1)S(1)} %get-tuple-element.539), channel_id=1, source_target_pairs={{0,8},{8,16},{16,24},{1,9},{9,17},{17,25},{2,10},{10,18},{18,26},{... | collective-permute-start | bytes 1572872 | tf_op jit(solution)/shard_map/ppermute | solution.py:285
  122.5 20.2 %collective-permute-start.20 = (bf16[32,8192]{1,0:T(8,128)(2,1)S(1)}, bf16[32,8192]{1,0:T(8,128)(2,1)S(1)}, u32[]{:S(2)}, u32[]{:S(2)}) collective-permute-start(bf16[32,8192]{1,0:T(8,128)(2,1)S(1)} %get-tuple-element.541), channel_id=1, source_target_pairs={{0,8},{8,16},{16,24},{1,9},{9,17},{17,25},{2,10},{10,18},{18,26},{... | collective-permute-start | bytes 1572872 | tf_op jit(solution)/shard_map/ppermute | solution.py:285
  133.8 20.2 %collective-permute-start.26 = (bf16[32,8192]{1,0:T(8,128)(2,1)S(1)}, bf16[32,8192]{1,0:T(8,128)(2,1)S(1)}, u32[]{:S(2)}, u32[]{:S(2)}) collective-permute-start(bf16[32,8192]{1,0:T(8,128)(2,1)S(1)} %get-tuple-element.553), channel_id=1, source_target_pairs={{0,8},{8,16},{16,24},{1,9},{9,17},{17,25},{2,10},{10,18},{18,26},{... | collective-permute-start | bytes 1572872 | tf_op jit(solution)/shard_map/ppermute | solution.py:285
  145.0 20.2 %collective-permute-start.24 = (bf16[32,8192]{1,0:T(8,128)(2,1)S(1)}, bf16[32,8192]{1,0:T(8,128)(2,1)S(1)}, u32[]{:S(2)}, u32[]{:S(2)}) collective-permute-start(bf16[32,8192]{1,0:T(8,128)(2,1)S(1)} %get-tuple-element.555), channel_id=1, source_target_pairs={{0,8},{8,16},{16,24},{1,9},{9,17},{17,25},{2,10},{10,18},{18,26},{... | collective-permute-start | bytes 1572872 | tf_op jit(solution)/shard_map/ppermute | solution.py:285
  156.3 20.2 %collective-permute-start.30 = (bf16[32,8192]{1,0:T(8,128)(2,1)S(1)}, bf16[32,8192]{1,0:T(8,128)(2,1)S(1)}, u32[]{:S(2)}, u32[]{:S(2)}) collective-permute-start(bf16[32,8192]{1,0:T(8,128)(2,1)S(1)} %get-tuple-element.567), channel_id=1, source_target_pairs={{0,8},{8,16},{16,24},{1,9},{9,17},{17,25},{2,10},{10,18},{18,26},{... | collective-permute-start | bytes 1572872 | tf_op jit(solution)/shard_map/ppermute | solution.py:285
  167.5 21.9 %collective-permute-start.28 = (bf16[32,8192]{1,0:T(8,128)(2,1)S(1)}, bf16[32,8192]{1,0:T(8,128)(2,1)S(1)}, u32[]{:S(2)}, u32[]{:S(2)}) collective-permute-start(bf16[32,8192]{1,0:T(8,128)(2,1)S(1)} %get-tuple-element.569), channel_id=1, source_target_pairs={{0,8},{8,16},{16,24},{1,9},{9,17},{17,25},{2,10},{10,18},{18,26},{... | collective-permute-start | bytes 1572872 | tf_op jit(solution)/shard_map/ppermute | solution.py:285
  179.4 20.3 %collective-permute-start.38 = (bf16[128,2048]{1,0:T(8,128)(2,1)S(1)}, bf16[128,2048]{1,0:T(8,128)(2,1)S(1)}, u32[]{:S(2)}, u32[]{:S(2)}) collective-permute-start(bf16[128,2048]{1,0:T(8,128)(2,1)S(1)} %get-tuple-element.587), channel_id=1, source_target_pairs={{0,8},{1,9},{2,10},{3,11},{4,12},{5,13},{6,14},{7,15}} | collective-permute-start | bytes 1572872 | tf_op jit(solution)/shard_map/ppermute | solution.py:285
  231.8 24.5 %collective-permute-start.50 = (bf16[128,2048]{1,0:T(8,128)(2,1)}, bf16[128,2048]{1,0:T(8,128)(2,1)S(1)}, u32[]{:S(2)}, u32[]{:S(2)}) collective-permute-start(bf16[128,2048]{1,0:T(8,128)(2,1)} %get-tuple-element.619), channel_id=1, source_target_pairs={{0,8},{8,16},{16,24},{1,9},{9,17},{17,25},{2,10},{10,18},{18,26},{... | collective-permute-start | bytes 1572872 | tf_op jit(solution)/shard_map/ppermute | solution.py:285
  236.6 19.7 %collective-permute-start.51 = (bf16[128,2048]{1,0:T(8,128)(2,1)}, bf16[128,2048]{1,0:T(8,128)(2,1)S(1)}, u32[]{:S(2)}, u32[]{:S(2)}) collective-permute-start(bf16[128,2048]{1,0:T(8,128)(2,1)} %get-tuple-element.620), channel_id=1, source_target_pairs={{24,16},{16,8},{8,0},{25,17},{17,9},{9,1},{26,18},{18,10},{10,2},{... | collective-permute-start | bytes 1572872 | tf_op jit(solution)/shard_map/ppermute | solution.py:285
  273.2 24.7 %collective-permute-start.54 = (bf16[128,2048]{1,0:T(8,128)(2,1)S(1)}, bf16[128,2048]{1,0:T(8,128)(2,1)S(1)}, u32[]{:S(2)}, u32[]{:S(2)}) collective-permute-start(bf16[128,2048]{1,0:T(8,128)(2,1)S(1)} %copy-done.3), channel_id=1, source_target_pairs={{0,8},{8,16},{16,24},{1,9},{9,17},{17,25},{2,10},{10,18},{18,26},{... | collective-permute-start | bytes 1572872 | tf_op jit(solution)/shard_map/ppermute | solution.py:285
  274.5 23.3 %collective-permute-start.55 = (bf16[128,2048]{1,0:T(8,128)(2,1)S(1)}, bf16[128,2048]{1,0:T(8,128)(2,1)S(1)}, u32[]{:S(2)}, u32[]{:S(2)}) collective-permute-start(bf16[128,2048]{1,0:T(8,128)(2,1)S(1)} %copy-done.1), channel_id=1, source_target_pairs={{24,16},{16,8},{8,0},{25,17},{17,9},{9,1},{26,18},{18,10},{10,2},{... | collective-permute-start | bytes 1572872 | tf_op jit(solution)/shard_map/ppermute | solution.py:285
  275.8 30.4 %collective-permute-start.52 = (bf16[128,2048]{1,0:T(8,128)(2,1)S(1)}, bf16[128,2048]{1,0:T(8,128)(2,1)S(1)}, u32[]{:S(2)}, u32[]{:S(2)}) collective-permute-start(bf16[128,2048]{1,0:T(8,128)(2,1)S(1)} %get-tuple-element.632), channel_id=1, source_target_pairs={{0,8},{8,16},{16,24},{1,9},{9,17},{17,25},{2,10},{10,18},{18,26},{... | collective-permute-start | bytes 1572872 | tf_op jit(solution)/shard_map/ppermute | solution.py:285
  280.4 25.8 %collective-permute-start.53 = (bf16[128,2048]{1,0:T(8,128)(2,1)S(1)}, bf16[128,2048]{1,0:T(8,128)(2,1)S(1)}, u32[]{:S(2)}, u32[]{:S(2)}) collective-permute-start(bf16[128,2048]{1,0:T(8,128)(2,1)S(1)} %get-tuple-element.633), channel_id=1, source_target_pairs={{24,16},{16,8},{8,0},{25,17},{17,9},{9,1},{26,18},{18,10},{10,2},{... | collective-permute-start | bytes 1572872 | tf_op jit(solution)/shard_map/ppermute | solution.py:285
  300.6 22.5 %collective-permute-start.58 = (bf16[128,2048]{1,0:T(8,128)(2,1)}, bf16[128,2048]{1,0:T(8,128)(2,1)S(1)}, u32[]{:S(2)}, u32[]{:S(2)}) collective-permute-start(bf16[128,2048]{1,0:T(8,128)(2,1)} %get-tuple-element.644), channel_id=1, source_target_pairs={{0,8},{8,16},{16,24},{1,9},{9,17},{17,25},{2,10},{10,18},{18,26},{... | collective-permute-start | bytes 1572872 | tf_op jit(solution)/shard_map/ppermute | solution.py:285
  305.0 20.5 %collective-permute-start.59 = (bf16[128,2048]{1,0:T(8,128)(2,1)}, bf16[128,2048]{1,0:T(8,128)(2,1)S(1)}, u32[]{:S(2)}, u32[]{:S(2)}) collective-permute-start(bf16[128,2048]{1,0:T(8,128)(2,1)} %get-tuple-element.645), channel_id=1, source_target_pairs={{24,16},{16,8},{8,0},{25,17},{17,9},{9,1},{26,18},{18,10},{10,2},{... | collective-permute-start | bytes 1572872 | tf_op jit(solution)/shard_map/ppermute | solution.py:285
  309.0 24.1 %collective-permute-start.56 = (bf16[128,2048]{1,0:T(8,128)(2,1)}, bf16[128,2048]{1,0:T(8,128)(2,1)S(1)}, u32[]{:S(2)}, u32[]{:S(2)}) collective-permute-start(bf16[128,2048]{1,0:T(8,128)(2,1)} %get-tuple-element.646), channel_id=1, source_target_pairs={{0,8},{8,16},{16,24},{1,9},{9,17},{17,25},{2,10},{10,18},{18,26},{... | collective-permute-start | bytes 1572872 | tf_op jit(solution)/shard_map/ppermute | solution.py:285
  362.1 35.2 %collective-permute-start.70 = (bf16[128,2048]{1,0:T(8,128)(2,1)}, bf16[128,2048]{1,0:T(8,128)(2,1)S(1)}, u32[]{:S(2)}, u32[]{:S(2)}) collective-permute-start(bf16[128,2048]{1,0:T(8,128)(2,1)} %get-tuple-element.689), channel_id=1, source_target_pairs={{0,8},{8,16},{16,24},{1,9},{9,17},{17,25},{2,10},{10,18},{18,26},{... | collective-permute-start | bytes 1572872 | tf_op jit(solution)/shard_map/ppermute | solution.py:285
  364.9 32.4 %collective-permute-start.71 = (bf16[128,2048]{1,0:T(8,128)(2,1)}, bf16[128,2048]{1,0:T(8,128)(2,1)S(1)}, u32[]{:S(2)}, u32[]{:S(2)}) collective-permute-start(bf16[128,2048]{1,0:T(8,128)(2,1)} %get-tuple-element.690), channel_id=1, source_target_pairs={{24,16},{16,8},{8,0},{25,17},{17,9},{9,1},{26,18},{18,10},{10,2},{... | collective-permute-start | bytes 1572872 | tf_op jit(solution)/shard_map/ppermute | solution.py:285
  372.8 33.0 %collective-permute-start.76 = (bf16[128,2048]{1,0:T(8,128)(2,1)}, bf16[128,2048]{1,0:T(8,128)(2,1)S(1)}, u32[]{:S(2)}, u32[]{:S(2)}) collective-permute-start(bf16[128,2048]{1,0:T(8,128)(2,1)} %get-tuple-element.701), channel_id=1, source_target_pairs={{0,8},{8,16},{16,24},{1,9},{9,17},{17,25},{2,10},{10,18},{18,26},{... | collective-permute-start | bytes 1572872 | tf_op jit(solution)/shard_map/ppermute | solution.py:285
  376.1 29.6 %collective-permute-start.77 = (bf16[128,2048]{1,0:T(8,128)(2,1)}, bf16[128,2048]{1,0:T(8,128)(2,1)S(1)}, u32[]{:S(2)}, u32[]{:S(2)}) collective-permute-start(bf16[128,2048]{1,0:T(8,128)(2,1)} %get-tuple-element.702), channel_id=1, source_target_pairs={{24,16},{16,8},{8,0},{25,17},{17,9},{9,1},{26,18},{18,10},{10,2},{... | collective-permute-start | bytes 1572872 | tf_op jit(solution)/shard_map/ppermute | solution.py:285
  456.2 26.8 %collective-permute-start.100 = (bf16[32,8192]{1,0:T(8,128)(2,1)}, bf16[32,8192]{1,0:T(8,128)(2,1)S(1)}, u32[]{:S(2)}, u32[]{:S(2)}) collective-permute-start(bf16[32,8192]{1,0:T(8,128)(2,1)} %get-tuple-element.763), channel_id=1, source_target_pairs={{0,8},{8,16},{16,24},{1,9},{9,17},{17,25},{2,10},{10,18},{18,26},{... | collective-permute-start | bytes 1572872 | tf_op jit(solution)/shard_map/ppermute | solution.py:285
  461.1 21.9 %collective-permute-start.101 = (bf16[32,8192]{1,0:T(8,128)(2,1)}, bf16[32,8192]{1,0:T(8,128)(2,1)S(1)}, u32[]{:S(2)}, u32[]{:S(2)}) collective-permute-start(bf16[32,8192]{1,0:T(8,128)(2,1)} %get-tuple-element.764), channel_id=1, source_target_pairs={{24,16},{16,8},{8,0},{25,17},{17,9},{9,1},{26,18},{18,10},{10,2},{... | collective-permute-start | bytes 1572872 | tf_op jit(solution)/shard_map/ppermute | solution.py:285
  469.3 21.8 %collective-permute-start.98 = (bf16[32,8192]{1,0:T(8,128)(2,1)}, bf16[32,8192]{1,0:T(8,128)(2,1)S(1)}, u32[]{:S(2)}, u32[]{:S(2)}) collective-permute-start(bf16[32,8192]{1,0:T(8,128)(2,1)} %get-tuple-element.765), channel_id=1, source_target_pairs={{0,8},{8,16},{16,24},{1,9},{9,17},{17,25},{2,10},{10,18},{18,26},{... | collective-permute-start | bytes 1572872 | tf_op jit(solution)/shard_map/ppermute | solution.py:285
  485.2 29.9 %collective-permute-start.112 = (f32[2048]{0:T(1024)S(1)}, f32[2048]{0:T(1024)S(1)}, u32[]{:S(2)}, u32[]{:S(2)}) collective-permute-start(f32[2048]{0:T(1024)S(1)} %add.106), channel_id=1, source_target_pairs={{0,4},{2,6},{4,0},{6,2},{1,5},{3,7},{5,1},{7,3},{8,12},{10,14},{12... | collective-permute-start | bytes 24584 | tf_op jit(solution)/shard_map/ppermute | solution.py:252
  485.3 50.3 %collective-permute-start.104 = (bf16[32,8192]{1,0:T(8,128)(2,1)S(1)}, bf16[32,8192]{1,0:T(8,128)(2,1)S(1)}, u32[]{:S(2)}, u32[]{:S(2)}) collective-permute-start(bf16[32,8192]{1,0:T(8,128)(2,1)S(1)} %get-tuple-element.773), channel_id=1, source_target_pairs={{0,8},{8,16},{16,24},{1,9},{9,17},{17,25},{2,10},{10,18},{18,26},{... | collective-permute-start | bytes 1572872 | tf_op jit(solution)/shard_map/ppermute | solution.py:285
  489.7 45.8 %collective-permute-start.105 = (bf16[32,8192]{1,0:T(8,128)(2,1)S(1)}, bf16[32,8192]{1,0:T(8,128)(2,1)S(1)}, u32[]{:S(2)}, u32[]{:S(2)}) collective-permute-start(bf16[32,8192]{1,0:T(8,128)(2,1)S(1)} %get-tuple-element.774), channel_id=1, source_target_pairs={{24,16},{16,8},{8,0},{25,17},{17,9},{9,1},{26,18},{18,10},{10,2},{... | collective-permute-start | bytes 1572872 | tf_op jit(solution)/shard_map/ppermute | solution.py:285
  509.3 34.2 %collective-permute-start.102 = (bf16[32,8192]{1,0:T(8,128)(2,1)S(1)}, bf16[32,8192]{1,0:T(8,128)(2,1)S(1)}, u32[]{:S(2)}, u32[]{:S(2)}) collective-permute-start(bf16[32,8192]{1,0:T(8,128)(2,1)S(1)} %get-tuple-element.775), channel_id=1, source_target_pairs={{0,8},{8,16},{16,24},{1,9},{9,17},{17,25},{2,10},{10,18},{18,26},{... | collective-permute-start | bytes 1572872 | tf_op jit(solution)/shard_map/ppermute | solution.py:285
  513.8 29.7 %collective-permute-start.103 = (bf16[32,8192]{1,0:T(8,128)(2,1)S(1)}, bf16[32,8192]{1,0:T(8,128)(2,1)S(1)}, u32[]{:S(2)}, u32[]{:S(2)}) collective-permute-start(bf16[32,8192]{1,0:T(8,128)(2,1)S(1)} %get-tuple-element.776), channel_id=1, source_target_pairs={{24,16},{16,8},{8,0},{25,17},{17,9},{9,1},{26,18},{18,10},{10,2},{... | collective-permute-start | bytes 1572872 | tf_op jit(solution)/shard_map/ppermute | solution.py:285
  594.9 35.9 %collective-permute-start.120 = (bf16[32,8192]{1,0:T(8,128)(2,1)}, bf16[32,8192]{1,0:T(8,128)(2,1)S(1)}, u32[]{:S(2)}, u32[]{:S(2)}) collective-permute-start(bf16[32,8192]{1,0:T(8,128)(2,1)} %get-tuple-element.820), channel_id=1, source_target_pairs={{0,8},{8,16},{16,24},{1,9},{9,17},{17,25},{2,10},{10,18},{18,26},{... | collective-permute-start | bytes 1572872 | tf_op jit(solution)/shard_map/ppermute | solution.py:285
  598.6 32.1 %collective-permute-start.121 = (bf16[32,8192]{1,0:T(8,128)(2,1)}, bf16[32,8192]{1,0:T(8,128)(2,1)S(1)}, u32[]{:S(2)}, u32[]{:S(2)}) collective-permute-start(bf16[32,8192]{1,0:T(8,128)(2,1)} %get-tuple-element.821), channel_id=1, source_target_pairs={{24,16},{16,8},{8,0},{25,17},{17,9},{9,1},{26,18},{18,10},{10,2},{... | collective-permute-start | bytes 1572872 | tf_op jit(solution)/shard_map/ppermute | solution.py:285
  606.2 33.0 %collective-permute-start.126 = (bf16[32,8192]{1,0:T(8,128)(2,1)}, bf16[32,8192]{1,0:T(8,128)(2,1)S(1)}, u32[]{:S(2)}, u32[]{:S(2)}) collective-permute-start(bf16[32,8192]{1,0:T(8,128)(2,1)} %get-tuple-element.828), channel_id=1, source_target_pairs={{0,8},{8,16},{16,24},{1,9},{9,17},{17,25},{2,10},{10,18},{18,26},{... | collective-permute-start | bytes 1572872 | tf_op jit(solution)/shard_map/ppermute | solution.py:285
  609.7 29.5 %collective-permute-start.127 = (bf16[32,8192]{1,0:T(8,128)(2,1)S(1)}, bf16[32,8192]{1,0:T(8,128)(2,1)S(1)}, u32[]{:S(2)}, u32[]{:S(2)}) collective-permute-start(bf16[32,8192]{1,0:T(8,128)(2,1)S(1)} %get-tuple-element.829), channel_id=1, source_target_pairs={{24,16},{16,8},{8,0},{25,17},{17,9},{9,1},{26,18},{18,10},{10,2},{... | collective-permute-start | bytes 1572872 | tf_op jit(solution)/shard_map/ppermute | solution.py:285
  640.8 21.1 %collective-permute-start.135 = (bf16[32,8192]{1,0:T(8,128)(2,1)S(1)}, bf16[32,8192]{1,0:T(8,128)(2,1)S(1)}, u32[]{:S(2)}, u32[]{:S(2)}) collective-permute-start(bf16[32,8192]{1,0:T(8,128)(2,1)S(1)} %get-tuple-element.849), channel_id=1, source_target_pairs={{16,8},{8,0},{17,9},{9,1},{18,10},{10,2},{19,11},{11,3},{20,12},{1... | collective-permute-start | bytes 1572872 | tf_op jit(solution)/shard_map/ppermute | solution.py:285
  644.1 21.0 %collective-permute-start.138 = (bf16[128,2048]{1,0:T(8,128)(2,1)S(1)}, bf16[128,2048]{1,0:T(8,128)(2,1)S(1)}, u32[]{:S(2)}, u32[]{:S(2)}) collective-permute-start(bf16[128,2048]{1,0:T(8,128)(2,1)S(1)} %get-tuple-element.850), channel_id=1, source_target_pairs={{0,8},{1,9},{2,10},{3,11},{4,12},{5,13},{6,14},{7,15}} | collective-permute-start | bytes 1572872 | tf_op jit(solution)/shard_map/ppermute | solution.py:285
  707.5 20.0 %collective-permute-start.149 = (bf16[128,2048]{1,0:T(8,128)(2,1)S(1)}, bf16[128,2048]{1,0:T(8,128)(2,1)S(1)}, u32[]{:S(2)}, u32[]{:S(2)}) collective-permute-start(bf16[128,2048]{1,0:T(8,128)(2,1)S(1)} %get-tuple-element.886), channel_id=1, source_target_pairs={{24,16},{16,8},{8,0},{25,17},{17,9},{9,1},{26,18},{18,10},{10,2},{... | collective-permute-start | bytes 1572872 | tf_op jit(solution)/shard_map/ppermute | solution.py:285
  830.2 20.9 %collective-permute-start.175 = (bf16[128,2048]{1,0:T(8,128)(2,1)S(1)}, bf16[128,2048]{1,0:T(8,128)(2,1)S(1)}, u32[]{:S(2)}, u32[]{:S(2)}) collective-permute-start(bf16[128,2048]{1,0:T(8,128)(2,1)S(1)} %get-tuple-element.944), channel_id=1, source_target_pairs={{16,8},{8,0},{17,9},{9,1},{18,10},{10,2},{19,11},{11,3},{20,12},{1... | collective-permute-start | bytes 1572872 | tf_op jit(solution)/shard_map/ppermute | solution.py:285
  841.4 20.9 %collective-permute-start.173 = (bf16[128,2048]{1,0:T(8,128)(2,1)S(1)}, bf16[128,2048]{1,0:T(8,128)(2,1)S(1)}, u32[]{:S(2)}, u32[]{:S(2)}) collective-permute-start(bf16[128,2048]{1,0:T(8,128)(2,1)S(1)} %get-tuple-element.946), channel_id=1, source_target_pairs={{16,8},{8,0},{17,9},{9,1},{18,10},{10,2},{19,11},{11,3},{20,12},{1... | collective-permute-start | bytes 1572872 | tf_op jit(solution)/shard_map/ppermute | solution.py:285
  852.6 20.9 %collective-permute-start.179 = (bf16[128,2048]{1,0:T(8,128)(2,1)S(1)}, bf16[128,2048]{1,0:T(8,128)(2,1)S(1)}, u32[]{:S(2)}, u32[]{:S(2)}) collective-permute-start(bf16[128,2048]{1,0:T(8,128)(2,1)S(1)} %get-tuple-element.954), channel_id=1, source_target_pairs={{8,0},{9,1},{10,2},{11,3},{12,4},{13,5},{14,6},{15,7}} | collective-permute-start | bytes 1572872 | tf_op jit(solution)/shard_map/ppermute | solution.py:285
  (150 other events, 2276.3 us)

commit v5 on v0

v5 whole, which is shorter than its diff:
```python
import functools

import jax
import jax.numpy as jnp
from jax import lax
from jax.experimental import pallas as pl
from jax.experimental.pallas import tpu as pltpu
from jax.sharding import PartitionSpec as P

BETA = 0.8
EPS_SQUARE = 1e-30
CHUNKS = 16
LAG = 2
GROUPS = 4
FAR = 2
LANES = 128
VMEM_BYTES = 48 * 1024 * 1024

F32 = jnp.float32
BF16 = jnp.bfloat16
ANY = pl.BlockSpec(memory_space=pl.ANY)


def chunk_count(shapes):
    count = CHUNKS
    while any(rows % (32 * count) for rows, _ in shapes):
        count //= 2
    return count


def step_kernel(plan, place_ref, *refs):
    refs = list(refs)
    gots = [refs.pop(0), refs.pop(0)] if plan["with_got"] else [None, None]
    taken = []
    for part in plan["parts"]:
        taken.append([refs.pop(0) for _ in range(part["operands"])])
    sends = [refs.pop(0), refs.pop(0)] if plan["sending"] else [None, None]
    given = []
    for part in plan["parts"]:
        given.append([refs.pop(0) for _ in range(part["results"])])
    (sems,) = refs

    place, last, count = place_ref[0], plan["last"], plan["count"]
    numbers = [plan["step"] - LAG * place, plan["step"] - LAG * (last - place)]
    positions = [place, last - place]

    def pieces(size, q, width):
        for j in range(q):
            for lane in range(0, width, LANES):
                yield pl.ds(j * size, size), pl.ds(lane, LANES), pl.ds(j * width + lane, LANES)

    for part, ins, outs in zip(plan["parts"], taken, given):
        size, q, width, begin = part["size"], part["q"], part["width"], part["begin"]
        here = [n - begin for n in numbers]
        valids = [(n >= 0) & (n < count) for n in here]
        if part["kind"] == "sum":
            for d in range(2):

                @pl.when(valids[d])
                def _():
                    for at, lanes, full in pieces(size, q, width):
                        value = ins[d][:, full]
                        if plan["with_got"]:
                            value = (gots[d][at, lanes].astype(F32) + value.astype(F32)).astype(BF16)
                        sends[d][at, lanes] = value

            if part["chunk"] is not None:
                total_ref, row_ref, col_ref = outs
                for d, end in ((0, last), (1, 0)):

                    @pl.when(place == end)
                    def _():
                        row_part = jnp.zeros((size, LANES), F32)
                        for at, lanes, full in pieces(size, q, width):
                            total = sends[d][at, lanes]
                            total_ref[:, full] = total
                            wide = total.astype(F32)
                            square = wide * wide + EPS_SQUARE
                            row_part = row_part + square
                            col_part = square[0:8]
                            for r in range(8, size, 8):
                                col_part = col_part + square[r : r + 8]
                            if not part["first"]:
                                col_part = col_part + ins[-1][:, full]
                            col_ref[:, full] = col_part
                        row_ref[...] = row_part

        else:
            out_ref = outs[0]

            def keep(source, d, j):
                row = ((1 - d) * count + jnp.clip(here[d], 0, count - 1)) * size
                return pltpu.make_async_copy(
                    source.at[pl.ds(j * size, size), :],
                    out_ref.at[pl.ds(pl.multiple_of(row, 16), size), pl.ds(j * width, width)],
                    sems.at[d, j],
                )

            for d in range(2):
                if part["chunk"] is not None:
                    total_ref, row_ref, col_ref = ins[:3]

                    @pl.when(valids[d] & (positions[d] == 0))
                    def _():
                        for at, lanes, full in pieces(size, q, width):
                            wide = total_ref[:, full].astype(F32)
                            update = wide * row_ref[...] * col_ref[0:1, full]
                            sends[d][at, lanes] = update.astype(BF16)
                        for j in range(q):
                            keep(sends[d], d, j).start()

                if plan["with_got"]:

                    @pl.when(valids[d] & (positions[d] > 0))
                    def _():
                        for j in range(q):
                            keep(gots[d], d, j).start()
                        if plan["sending"]:
                            for at, lanes, _ in pieces(size, q, width):
                                sends[d][at, lanes] = gots[d][at, lanes]

            for d in range(2):

                @pl.when(valids[d])
                def _():
                    for j in range(q):
                        keep(gots[d] if sends[d] is None else sends[d], d, j).wait()


def run_step(place, s, count, last, gots, parts, message, sending):
    window = pl.BlockSpec(message, lambda i, at: (0, 0))
    operands, in_specs, out_shape, out_specs, aliases = [], [], [], [], {}
    with_got = gots is not None
    if with_got:
        operands += gots
        in_specs += [window, window]
    if sending:
        out_shape += [jax.ShapeDtypeStruct(message, BF16)] * 2
        out_specs += [window, window]
    plans = []
    widest = 1
    for part in parts:
        rows, cols = part["shape"]
        half, size = rows // 2, rows // 2 // count
        q, width = cols // message[1], message[1]
        widest = max(widest, q)
        chunk = part["chunk"]
        block = pl.BlockSpec((size, cols), lambda i, at, k=chunk: (k, 0))
        lanes = pl.BlockSpec((size, LANES), lambda i, at, k=chunk: (k, 0))
        whole = pl.BlockSpec((8, cols), lambda i, at: (0, 0))
        before, results_before = len(operands), len(out_shape)
        if part["kind"] == "sum":
            for d in range(2):

                def from_grad(i, at, d=d, begin=part["begin"]):
                    number = s - begin - LAG * (at[0] if d == 0 else last - at[0])
                    return (d * count + jnp.clip(number, 0, count - 1), 0)

                operands.append(part["grad"])
                in_specs.append(pl.BlockSpec((size, cols), from_grad))
            if chunk is not None:
                if part["state"] is not None:
                    for k in range(3):
                        aliases[len(operands) + 1 + k] = len(out_shape) + k
                    operands += part["state"]
                    in_specs += [ANY, ANY, whole]
                out_shape += [
                    jax.ShapeDtypeStruct((half, cols), BF16),
                    jax.ShapeDtypeStruct((half, LANES), F32),
                    jax.ShapeDtypeStruct((8, cols), F32),
                ]
                out_specs += [block, lanes, whole]
        else:
            if chunk is not None:
                operands += part["scales"]
                in_specs += [block, lanes, whole]
            if part["out"] is not None:
                aliases[len(operands) + 1] = len(out_shape)
                operands.append(part["out"])
                in_specs.append(ANY)
            out_shape.append(jax.ShapeDtypeStruct((rows, cols), BF16))
            out_specs.append(ANY)
        plans.append(
            dict(
                kind=part["kind"],
                begin=part["begin"],
                chunk=chunk,
                first=part.get("state") is None,
                size=size,
                q=q,
                width=width,
                operands=len(operands) - before,
                results=len(out_shape) - results_before,
            )
        )
    plan = dict(
        step=s, count=count, last=last, with_got=with_got, sending=sending, parts=plans
    )
    elements = message[0] * message[1]
    out = pl.pallas_call(
        functools.partial(step_kernel, plan),
        grid_spec=pltpu.PrefetchScalarGridSpec(
            num_scalar_prefetch=1,
            grid=(1,),
            in_specs=in_specs,
            out_specs=out_specs,
            scratch_shapes=[pltpu.SemaphoreType.DMA((2, widest))],
        ),
        out_shape=out_shape,
        input_output_aliases=aliases,
        compiler_params=pltpu.CompilerParams(vmem_limit_bytes=VMEM_BYTES),
        cost_estimate=pl.CostEstimate(
            flops=4 * elements, bytes_accessed=12 * elements, transcendentals=0
        ),
        name="line_step",
    )(place, *operands)
    out = list(out)
    values = [out.pop(0), out.pop(0)] if sending else None
    return values, [[out.pop(0) for _ in range(plan["results"])] for plan in plans]


def make_local(axis_sizes):
    n_dp, n_row, n_col = axis_sizes["dp"], axis_sizes["row"], axis_sizes["col"]
    last = n_dp - 1

    def partner(value, axis, distance):
        n = axis_sizes[axis]
        return lax.ppermute(value, axis, [(i, i ^ distance) for i in range(n)])

    def distances(axis):
        out, d = [], 1
        while d < axis_sizes[axis]:
            out.append(d)
            d *= 2
        return out

    def local(grad_wi, grad_wo, row_wi, col_wi, row_wo, col_wo):
        place = lax.axis_index("dp")
        grads = (grad_wi[0], grad_wo[0])
        prevs = ((row_wi, col_wi), (row_wo, col_wo))
        shapes = [g.shape for g in grads]
        count = chunk_count(shapes)
        here = place[None].astype(jnp.int32)
        at_end = (place == last) | (place == 0)
        width = min(cols for _, cols in shapes)
        message = (shapes[0][0] * shapes[0][1] // (2 * count * width), width)

        kinds = [("sum", 0), ("sum", 1), ("spread", 0), ("spread", 1)]
        messages = len(kinds) * count
        steps = messages + LAG * last

        states = [None, None]
        finished = [0, 0]
        scales = {}
        results = {}
        cell = [None]

        def settle(value):
            value, _ = lax.optimization_barrier((value, cell[0]))
            return value

        def statistics(m):
            rows, cols = shapes[m]
            half = rows // 2
            while finished[m] < count:
                yield [], 1
            total, row_lanes, col_rows = states[m]
            row_part = jnp.sum(row_lanes, axis=1)
            col_part = jnp.sum(col_rows, axis=0)
            levels = max(len(distances("row")), len(distances("col")))
            for level in range(levels):
                row_other = col_other = None
                if level < len(distances("col")):
                    row_other = partner(row_part, "col", distances("col")[level])
                if level < len(distances("row")):
                    col_other = partner(col_part, "row", distances("row")[level])
                yield [], 1
                row_part, col_part, row_other, col_other = settle(
                    (row_part, col_part, row_other, col_other)
                )
                row_part = row_part if row_other is None else row_part + row_other
                col_part = col_part if col_other is None else col_part + col_other
            packed = jnp.concatenate(
                [
                    jnp.where(place == last, row_part, 0.0),
                    jnp.where(place == 0, row_part, 0.0),
                    jnp.where(at_end, col_part, 0.0),
                ]
            )
            far = lax.ppermute(packed, "dp", [(0, last), (last, 0)])
            yield [], FAR
            packed, far = settle((packed, far))

            def factors(sums):
                row_new = BETA * prevs[m][0] + (1.0 - BETA) * (sums[:rows] / (cols * n_col))
                col_new = BETA * prevs[m][1] + (1.0 - BETA) * (sums[rows:] / (rows * n_row))
                return row_new, col_new

            row_new, col_new = factors(packed + far)
            row_scale = lax.rsqrt(jnp.where(place == 0, row_new[half:], row_new[:half]))
            col_scale = lax.rsqrt(col_new)
            energy = None
            for g in range(GROUPS):
                low, high = g * half // GROUPS, (g + 1) * half // GROUPS
                wide = settle(total)[low:high].astype(F32)
                raw = wide * row_scale[low:high, None] * col_scale[None, :]
                part = jnp.sum(raw * raw)
                energy = part if energy is None else energy + part
                if g == GROUPS // 2 - 1:
                    yield [energy], 1
            energy = jnp.broadcast_to(energy, (8, LANES))
            for axis in ("col", "row"):
                for distance in distances(axis):
                    other = partner(energy, axis, distance)
                    yield [], 1
                    energy, other = settle((energy, other))
                    energy = energy + other
            other = lax.ppermute(energy, "dp", [(0, last), (last, 0)])
            yield [], FAR
            energy, other = settle((energy, other))
            energy = (energy + other)[0, 0]
            rms = jnp.sqrt(energy / (rows * n_row * cols * n_col))
            row_final = row_scale / jnp.maximum(1.0, rms)
            scales[m] = [
                total,
                jnp.broadcast_to(row_final[:, None], (half, LANES)),
                jnp.broadcast_to(col_scale[None, :], (8, cols)),
            ]
            yield [scales[m][1], scales[m][2]], count // 2
            sums = packed + far
            for j in range(1, last):
                for pairs in (
                    [[(0, j), (last, last - j)]] if j != last - j else [[(0, j)], [(last, j)]]
                ):
                    got = lax.ppermute(settle(packed), "dp", pairs)
                    yield [], FAR
                    sums = sums + settle(got)
            results[m] = factors(sums)
            yield list(results[m]), steps

        workers = [statistics(0), statistics(1)]
        wakes = [0, 0]
        outs = [None, None]
        inflight = {}
        tied = []
        for s in range(steps):
            before, tied = tied, []
            movers = [p for p in range(n_dp) if 0 <= s - LAG * p < messages]
            parts = []
            for index, (kind, m) in enumerate(kinds):
                begin = index * count
                members = [p for p in movers if begin <= s - LAG * p < begin + count]
                if not members:
                    continue
                part = dict(kind=kind, m=m, begin=begin, shape=shapes[m])
                if kind == "sum":
                    part["chunk"] = s - begin - LAG * last if last in members else None
                    part.update(grad=grads[m], state=states[m])
                else:
                    while m not in scales:
                        wakes[m] = s + next(workers[m])[1]
                    part["chunk"] = s - begin if 0 in members else None
                    part.update(scales=scales[m], out=outs[m])
                parts.append(part)
            gots = inflight.pop(s - LAG, None)
            sending = min(movers) < last
            values, given = run_step(here, s, count, last, gots, parts, message, sending)
            for part, made in zip(parts, given):
                if part["kind"] == "spread":
                    outs[part["m"]] = made[0]
                elif made:
                    states[part["m"]] = made
                    finished[part["m"]] += 1
            if sending:
                tied, _ = lax.optimization_barrier((values, (before, gots)))
                tied = list(tied)
                going = [p for p in movers if p < last]
                inflight[s] = [
                    lax.ppermute(tied[0], "dp", [(p, p + 1) for p in going]),
                    lax.ppermute(tied[1], "dp", [(last - p, last - p - 1) for p in going]),
                ]
                cell[0] = list(tied)
            for m in range(2):
                if s >= wakes[m]:
                    ties, wait = next(workers[m])
                    tied = tied + ties
                    wakes[m] = s + wait
        for m in range(2):
            while m not in results:
                next(workers[m])
        return (outs[0], *results[0], outs[1], *results[1])

    return local


def solution(mesh):
    return jax.shard_map(
        make_local(dict(mesh.shape)),
        mesh=mesh,
        in_specs=(
            P("dp", "row", "col"),
            P("dp", "row", "col"),
            P("row"),
            P("col"),
            P("row"),
            P("col"),
        ),
        out_specs=(P("row", "col"), P("row"), P("col"), P("row", "col"), P("row"), P("col")),
        check_vma=False,
    )
```

time: 1240 us -> 840 us (0.68); the launches traced: 1240 us -> 826 us
  waiting for transfers between devices: 1110 us -> 250 us
  starting transfers between devices: 0.04 us -> 373 us
  Pallas kernels: 0 us -> 174 us
  other arithmetic: 79.8 us -> 13.7 us
  blocking collectives: 32 us -> 0 us
    psum x1 -> x0, waiting for transfers between devices: 1110 us -> none  [local(): lax.psum(terms[0].astype(jnp.bfloat16), 'dp').astype(jnp.float32)]
    ppermute x0 -> x156, starting transfers between devices: none -> 373 us  [the longest x68 237 us: local(): lax.ppermute(tied[0], 'dp', [(p, p + 1) for p in going])]
    ppermute x0 -> x156, waiting for transfers between devices: none -> 250 us  [the longest x68 138 us: local(): lax.ppermute(tied[1], 'dp', [(last - p, last - p - 1) for p in going])]
    pallas_call x0 -> x70, Pallas kernels: none -> 174 us  [run_step(): pl.pallas_call(functools.partial(step_kernel, plan), grid_spec=pltpu.Pref...]
    reduce_sum x4 -> x8, other arithmetic: 46.5 us -> 11 us  [the longest x4 10.5 us: statistics(): part = jnp.sum(raw * raw)]
    convert_element_type x2 -> x0, other arithmetic: 33.2 us -> none  [the longest x1 16.8 us: local(): (raw_wo / jnp.maximum(1.0, jnp.sqrt(energy_wo / (D * FF)))).astype(jnp.bf...]
    psum x3 -> x0, blocking collectives: 32 us -> none  [the longest x1 13.2 us: local(): lax.psum((local_squares[0], local_squares[1]), ('row', 'col'))]
  transfers between devices with their start and end apart: 1 -> 156, of which waited for: 1 -> 80; matrix products, arithmetic and copies ran while one was open for 0% -> 2% of each run, Pallas kernels for 0% -> 21%
where the time goes in v5:
time: 840 us; the launch traced here: 826 us
  starting transfers between devices  373 us (44%)
  waiting for transfers between devices  250 us (30%)
  Pallas kernels  174 us (21%)
  other arithmetic  13.7 us (2%)
  between operations  10.4 us (1%)
    ppermute x68, starting transfers between devices, local(): lax.ppermute(tied[0], 'dp', [(p, p + 1) for p in going])  237 us
    pallas_call x70, Pallas kernels, run_step(): pl.pallas_call(functools.partial(step_kernel, plan), grid_spec=pltpu.Pref...  174 us
    ppermute x68, waiting for transfers between devices, local(): lax.ppermute(tied[1], 'dp', [(last - p, last - p - 1) for p in going])  138 us
    ppermute x68, waiting for transfers between devices, local(): lax.ppermute(tied[0], 'dp', [(p, p + 1) for p in going])  91.7 us
    ppermute x68, starting transfers between devices, local(): lax.ppermute(tied[1], 'dp', [(last - p, last - p - 1) for p in going])  85.9 us
    ppermute x4, starting transfers between devices, statistics(): got = lax.ppermute(settle(packed), 'dp', pairs)  22.4 us
  transfers between devices with their start and end apart: 156, of which 80 were waited for; matrix products, arithmetic and copies ran while one was open for 2% of the time, Pallas kernels for 21%

profile of v5, /device:TPU:0, one launch (start us, length us, event | category | flops | bytes accessed | tf_op | source)
XLA Modules:
  0.0 825.8 jit_solution(11551150422381804940)
XLA Ops:
  2.0 4.9 collective-permute-start.2
  11.0 8.2 collective-permute-done.2.refs_0_
  20.6 4.4 collective-permute-start.6
  25.7 4.7 collective-permute-done.refs_0_
  31.8 4.4 collective-permute-start.4
  37.0 4.7 collective-permute-done.6.refs_0_
  43.1 4.6 collective-permute-start.10
  54.3 4.6 collective-permute-start.8
  66.7 4.2 collective-permute-start.14
  78.0 4.2 collective-permute-start.12
  89.2 4.2 collective-permute-start.18
  100.4 4.2 collective-permute-start.16
  111.7 4.2 collective-permute-start.22
  201.9 4.2 collective-permute-start.38
  213.1 4.2 collective-permute-start.36
  224.7 4.2 collective-permute-start.42
  235.9 4.2 collective-permute-start.40
  259.6 4.3 collective-permute-start.44
  265.3 4.5 collective-permute-start.55
  298.3 4.3 collective-permute-start.58
  313.6 4.6 collective-permute-done.59.refs_1_
  324.9 4.6 collective-permute-done.57.refs_1_
  336.1 4.6 collective-permute-done.63.refs_1_
  399.5 4.4 collective-permute-done.75.refs_1_
  410.7 4.4 collective-permute-done.73.refs_1_
  422.0 4.4 collective-permute-done.79.refs_1_
  463.5 5.2 collective-permute-start.95
  489.4 5.7 collective-permute-start.101
  506.2 4.4 collective-permute-start.96
  543.9 4.2 collective-permute-start.108
  553.8 5.3 collective-permute-start.106
  572.9 5.1 collective-permute-start.113
  605.0 5.1 collective-permute-start.120
  616.1 5.2 collective-permute-start.118
  626.9 5.3 collective-permute-start.124
  639.0 5.1 collective-permute-start.122
  649.5 5.7 collective-permute-start.128
  660.8 5.7 collective-permute-start.126
  672.0 5.7 collective-permute-start.132
  683.3 5.7 collective-permute-start.130
  690.2 4.5 collective-permute-start.138
  697.0 10.4 %collective-permute-start.139 = (f32[6144]{0:T(1024)S(1)}, f32[6144]{0:T(1024)S(1)}, u32[]{:S(2)}, u32[]{:S(2)}) collective-permute-start(f32[6144]{0:T(1024)S(1)} %pad_maximum_fusion.1), channel_id=1, source_target_pairs={{0,16},{24,8},{1,17},{25,9},{2,18},{26,10},{3,19},{27,11},{4,20},{... | collective-permute-start | bytes 73736 | tf_op jit(solution)/shard_map/ppermute | solution.py:335
  714.6 4.4 collective-permute-start.134
  775.7 7.6 collective-permute-done.145.refs_1_
  786.1 8.4 %collective-permute-done.151.refs_1_ = bf16[128,2048]{1,0:T(8,128)(2,1)S(1)} collective-permute-done((bf16[128,2048]{1,0:T(8,128)(2,1)S(1)}, bf16[128,2048]{1,0:T(8,128)(2,1)S(1)}, u32[]{:S(2)}, u32[]{:S(2)}) %collective-permute-start.151) | collective-permute-done | bytes 524320 | tf_op jit(solution)/shard_map/ppermute | solution.py:380
  797.4 8.4 %collective-permute-done.149.refs_1_ = bf16[128,2048]{1,0:T(8,128)(2,1)S(1)} collective-permute-done((bf16[128,2048]{1,0:T(8,128)(2,1)S(1)}, bf16[128,2048]{1,0:T(8,128)(2,1)S(1)}, u32[]{:S(2)}, u32[]{:S(2)}) %collective-permute-start.149) | collective-permute-done | bytes 524320 | tf_op jit(solution)/shard_map/ppermute | solution.py:380
  808.6 8.4 %collective-permute-done.155.refs_1_ = bf16[128,2048]{1,0:T(8,128)(2,1)S(1)} collective-permute-done((bf16[128,2048]{1,0:T(8,128)(2,1)S(1)}, bf16[128,2048]{1,0:T(8,128)(2,1)S(1)}, u32[]{:S(2)}, u32[]{:S(2)}) %collective-permute-start.155) | collective-permute-done | bytes 524320 | tf_op jit(solution)/shard_map/ppermute | solution.py:380
  817.8 6.7 collective-permute-done.153.refs_1_
  (442 shorter events, 564.9 us)
Async XLA Ops:
  8.9 21.5 %collective-permute-start = (bf16[128,2048]{1,0:T(8,128)(2,1)S(1)}, bf16[128,2048]{1,0:T(8,128)(2,1)S(1)}, u32[]{:S(2)}, u32[]{:S(2)}) collective-permute-start(bf16[128,2048]{1,0:T(8,128)(2,1)S(1)} %get-tuple-element.464), channel_id=1, source_target_pairs={{0,8},{1,9},{2,10},{3,11},{4,12},{5,13},{6,14},{7,15}} | collective-permute-start | bytes 1572872 | tf_op jit(solution)/shard_map/ppermute | solution.py:379
  10.3 20.2 %collective-permute-start.1 = (bf16[128,2048]{1,0:T(8,128)(2,1)S(1)}, bf16[128,2048]{1,0:T(8,128)(2,1)S(1)}, u32[]{:S(2)}, u32[]{:S(2)}) collective-permute-start(bf16[128,2048]{1,0:T(8,128)(2,1)S(1)} %get-tuple-element.465), channel_id=1, source_target_pairs={{24,16},{25,17},{26,18},{27,19},{28,20},{29,21},{30,22},{31,23}} | collective-permute-start | bytes 1572872 | tf_op jit(solution)/shard_map/ppermute | solution.py:380
  20.6 21.0 %collective-permute-start.6 = (bf16[128,2048]{1,0:T(8,128)(2,1)S(1)}, bf16[128,2048]{1,0:T(8,128)(2,1)S(1)}, u32[]{:S(2)}, u32[]{:S(2)}) collective-permute-start(bf16[128,2048]{1,0:T(8,128)(2,1)S(1)} %get-tuple-element.470), channel_id=1, source_target_pairs={{0,8},{8,16},{1,9},{9,17},{2,10},{10,18},{3,11},{11,19},{4,12},{12... | collective-permute-start | bytes 1572872 | tf_op jit(solution)/shard_map/ppermute | solution.py:379
  31.8 21.0 %collective-permute-start.4 = (bf16[128,2048]{1,0:T(8,128)(2,1)S(1)}, bf16[128,2048]{1,0:T(8,128)(2,1)S(1)}, u32[]{:S(2)}, u32[]{:S(2)}) collective-permute-start(bf16[128,2048]{1,0:T(8,128)(2,1)S(1)} %get-tuple-element.472), channel_id=1, source_target_pairs={{0,8},{8,16},{1,9},{9,17},{2,10},{10,18},{3,11},{11,19},{4,12},{12... | collective-permute-start | bytes 1572872 | tf_op jit(solution)/shard_map/ppermute | solution.py:379
  43.1 21.0 %collective-permute-start.10 = (bf16[128,2048]{1,0:T(8,128)(2,1)S(1)}, bf16[128,2048]{1,0:T(8,128)(2,1)S(1)}, u32[]{:S(2)}, u32[]{:S(2)}) collective-permute-start(bf16[128,2048]{1,0:T(8,128)(2,1)S(1)} %get-tuple-element.478), channel_id=1, source_target_pairs={{0,8},{8,16},{16,24},{1,9},{9,17},{17,25},{2,10},{10,18},{18,26},{... | collective-permute-start | bytes 1572872 | tf_op jit(solution)/shard_map/ppermute | solution.py:379
  54.3 21.0 %collective-permute-start.8 = (bf16[128,2048]{1,0:T(8,128)(2,1)S(1)}, bf16[128,2048]{1,0:T(8,128)(2,1)S(1)}, u32[]{:S(2)}, u32[]{:S(2)}) collective-permute-start(bf16[128,2048]{1,0:T(8,128)(2,1)S(1)} %get-tuple-element.480), channel_id=1, source_target_pairs={{0,8},{8,16},{16,24},{1,9},{9,17},{17,25},{2,10},{10,18},{18,26},{... | collective-permute-start | bytes 1572872 | tf_op jit(solution)/shard_map/ppermute | solution.py:379
  66.7 19.9 %collective-permute-start.14 = (bf16[128,2048]{1,0:T(8,128)(2,1)S(1)}, bf16[128,2048]{1,0:T(8,128)(2,1)S(1)}, u32[]{:S(2)}, u32[]{:S(2)}) collective-permute-start(bf16[128,2048]{1,0:T(8,128)(2,1)S(1)} %get-tuple-element.489), channel_id=1, source_target_pairs={{0,8},{8,16},{16,24},{1,9},{9,17},{17,25},{2,10},{10,18},{18,26},{... | collective-permute-start | bytes 1572872 | tf_op jit(solution)/shard_map/ppermute | solution.py:379
  78.0 19.9 %collective-permute-start.12 = (bf16[128,2048]{1,0:T(8,128)(2,1)S(1)}, bf16[128,2048]{1,0:T(8,128)(2,1)S(1)}, u32[]{:S(2)}, u32[]{:S(2)}) collective-permute-start(bf16[128,2048]{1,0:T(8,128)(2,1)S(1)} %get-tuple-element.491), channel_id=1, source_target_pairs={{0,8},{8,16},{16,24},{1,9},{9,17},{17,25},{2,10},{10,18},{18,26},{... | collective-permute-start | bytes 1572872 | tf_op jit(solution)/shard_map/ppermute | solution.py:379
  89.2 19.9 %collective-permute-start.18 = (bf16[128,2048]{1,0:T(8,128)(2,1)S(1)}, bf16[128,2048]{1,0:T(8,128)(2,1)S(1)}, u32[]{:S(2)}, u32[]{:S(2)}) collective-permute-start(bf16[128,2048]{1,0:T(8,128)(2,1)S(1)} %get-tuple-element.503), channel_id=1, source_target_pairs={{0,8},{8,16},{16,24},{1,9},{9,17},{17,25},{2,10},{10,18},{18,26},{... | collective-permute-start | bytes 1572872 | tf_op jit(solution)/shard_map/ppermute | solution.py:379
  100.4 19.9 %collective-permute-start.16 = (bf16[128,2048]{1,0:T(8,128)(2,1)S(1)}, bf16[128,2048]{1,0:T(8,128)(2,1)S(1)}, u32[]{:S(2)}, u32[]{:S(2)}) collective-permute-start(bf16[128,2048]{1,0:T(8,128)(2,1)S(1)} %get-tuple-element.505), channel_id=1, source_target_pairs={{0,8},{8,16},{16,24},{1,9},{9,17},{17,25},{2,10},{10,18},{18,26},{... | collective-permute-start | bytes 1572872 | tf_op jit(solution)/shard_map/ppermute | solution.py:379
  111.7 19.9 %collective-permute-start.22 = (bf16[128,2048]{1,0:T(8,128)(2,1)S(1)}, bf16[128,2048]{1,0:T(8,128)(2,1)S(1)}, u32[]{:S(2)}, u32[]{:S(2)}) collective-permute-start(bf16[128,2048]{1,0:T(8,128)(2,1)S(1)} %get-tuple-element.517), channel_id=1, source_target_pairs={{0,8},{8,16},{16,24},{1,9},{9,17},{17,25},{2,10},{10,18},{18,26},{... | collective-permute-start | bytes 1572872 | tf_op jit(solution)/shard_map/ppermute | solution.py:379
  122.9 19.9 %collective-permute-start.20 = (bf16[128,2048]{1,0:T(8,128)(2,1)S(1)}, bf16[128,2048]{1,0:T(8,128)(2,1)S(1)}, u32[]{:S(2)}, u32[]{:S(2)}) collective-permute-start(bf16[128,2048]{1,0:T(8,128)(2,1)S(1)} %get-tuple-element.519), channel_id=1, source_target_pairs={{0,8},{8,16},{16,24},{1,9},{9,17},{17,25},{2,10},{10,18},{18,26},{... | collective-permute-start | bytes 1572872 | tf_op jit(solution)/shard_map/ppermute | solution.py:379
  134.1 19.9 %collective-permute-start.26 = (bf16[128,2048]{1,0:T(8,128)(2,1)S(1)}, bf16[128,2048]{1,0:T(8,128)(2,1)S(1)}, u32[]{:S(2)}, u32[]{:S(2)}) collective-permute-start(bf16[128,2048]{1,0:T(8,128)(2,1)S(1)} %get-tuple-element.531), channel_id=1, source_target_pairs={{0,8},{8,16},{16,24},{1,9},{9,17},{17,25},{2,10},{10,18},{18,26},{... | collective-permute-start | bytes 1572872 | tf_op jit(solution)/shard_map/ppermute | solution.py:379
  145.4 19.9 %collective-permute-start.24 = (bf16[128,2048]{1,0:T(8,128)(2,1)S(1)}, bf16[128,2048]{1,0:T(8,128)(2,1)S(1)}, u32[]{:S(2)}, u32[]{:S(2)}) collective-permute-start(bf16[128,2048]{1,0:T(8,128)(2,1)S(1)} %get-tuple-element.533), channel_id=1, source_target_pairs={{0,8},{8,16},{16,24},{1,9},{9,17},{17,25},{2,10},{10,18},{18,26},{... | collective-permute-start | bytes 1572872 | tf_op jit(solution)/shard_map/ppermute | solution.py:379
  156.6 19.9 %collective-permute-start.30 = (bf16[128,2048]{1,0:T(8,128)(2,1)S(1)}, bf16[128,2048]{1,0:T(8,128)(2,1)S(1)}, u32[]{:S(2)}, u32[]{:S(2)}) collective-permute-start(bf16[128,2048]{1,0:T(8,128)(2,1)S(1)} %get-tuple-element.545), channel_id=1, source_target_pairs={{0,8},{8,16},{16,24},{1,9},{9,17},{17,25},{2,10},{10,18},{18,26},{... | collective-permute-start | bytes 1572872 | tf_op jit(solution)/shard_map/ppermute | solution.py:379
  167.8 19.9 %collective-permute-start.28 = (bf16[128,2048]{1,0:T(8,128)(2,1)S(1)}, bf16[128,2048]{1,0:T(8,128)(2,1)S(1)}, u32[]{:S(2)}, u32[]{:S(2)}) collective-permute-start(bf16[128,2048]{1,0:T(8,128)(2,1)S(1)} %get-tuple-element.547), channel_id=1, source_target_pairs={{0,8},{8,16},{16,24},{1,9},{9,17},{17,25},{2,10},{10,18},{18,26},{... | collective-permute-start | bytes 1572872 | tf_op jit(solution)/shard_map/ppermute | solution.py:379
  179.4 19.5 %collective-permute-start.34 = (bf16[128,2048]{1,0:T(8,128)(2,1)S(1)}, bf16[128,2048]{1,0:T(8,128)(2,1)S(1)}, u32[]{:S(2)}, u32[]{:S(2)}) collective-permute-start(bf16[128,2048]{1,0:T(8,128)(2,1)S(1)} %get-tuple-element.559), channel_id=1, source_target_pairs={{0,8},{8,16},{16,24},{1,9},{9,17},{17,25},{2,10},{10,18},{18,26},{... | collective-permute-start | bytes 1572872 | tf_op jit(solution)/shard_map/ppermute | solution.py:379
  190.6 19.5 %collective-permute-start.32 = (bf16[128,2048]{1,0:T(8,128)(2,1)S(1)}, bf16[128,2048]{1,0:T(8,128)(2,1)S(1)}, u32[]{:S(2)}, u32[]{:S(2)}) collective-permute-start(bf16[128,2048]{1,0:T(8,128)(2,1)S(1)} %get-tuple-element.561), channel_id=1, source_target_pairs={{0,8},{8,16},{16,24},{1,9},{9,17},{17,25},{2,10},{10,18},{18,26},{... | collective-permute-start | bytes 1572872 | tf_op jit(solution)/shard_map/ppermute | solution.py:379
  201.9 19.5 %collective-permute-start.38 = (bf16[128,2048]{1,0:T(8,128)(2,1)S(1)}, bf16[128,2048]{1,0:T(8,128)(2,1)S(1)}, u32[]{:S(2)}, u32[]{:S(2)}) collective-permute-start(bf16[128,2048]{1,0:T(8,128)(2,1)S(1)} %get-tuple-element.573), channel_id=1, source_target_pairs={{0,8},{8,16},{16,24},{1,9},{9,17},{17,25},{2,10},{10,18},{18,26},{... | collective-permute-start | bytes 1572872 | tf_op jit(solution)/shard_map/ppermute | solution.py:379
  213.1 19.5 %collective-permute-start.36 = (bf16[128,2048]{1,0:T(8,128)(2,1)S(1)}, bf16[128,2048]{1,0:T(8,128)(2,1)S(1)}, u32[]{:S(2)}, u32[]{:S(2)}) collective-permute-start(bf16[128,2048]{1,0:T(8,128)(2,1)S(1)} %get-tuple-element.575), channel_id=1, source_target_pairs={{0,8},{8,16},{16,24},{1,9},{9,17},{17,25},{2,10},{10,18},{18,26},{... | collective-permute-start | bytes 1572872 | tf_op jit(solution)/shard_map/ppermute | solution.py:379
  235.9 21.1 %collective-permute-start.40 = (bf16[128,2048]{1,0:T(8,128)(2,1)}, bf16[128,2048]{1,0:T(8,128)(2,1)S(1)}, u32[]{:S(2)}, u32[]{:S(2)}) collective-permute-start(bf16[128,2048]{1,0:T(8,128)(2,1)} %get-tuple-element.589), channel_id=1, source_target_pairs={{0,8},{8,16},{16,24},{1,9},{9,17},{17,25},{2,10},{10,18},{18,26},{... | collective-permute-start | bytes 1572872 | tf_op jit(solution)/shard_map/ppermute | solution.py:379
  259.6 19.9 %collective-permute-start.44 = (bf16[128,2048]{1,0:T(8,128)(2,1)S(1)}, bf16[128,2048]{1,0:T(8,128)(2,1)S(1)}, u32[]{:S(2)}, u32[]{:S(2)}) collective-permute-start(bf16[128,2048]{1,0:T(8,128)(2,1)S(1)} %get-tuple-element.600), channel_id=1, source_target_pairs={{0,8},{8,16},{16,24},{1,9},{9,17},{17,25},{2,10},{10,18},{18,26},{... | collective-permute-start | bytes 1572872 | tf_op jit(solution)/shard_map/ppermute | solution.py:379
  265.3 26.2 %collective-permute-start.55 = (f32[9216]{0:T(1024)S(1)}, f32[9216]{0:T(1024)S(1)}, u32[]{:S(2)}, u32[]{:S(2)}) collective-permute-start(f32[9216]{0:T(1024)S(1)} %pad_maximum_fusion), channel_id=1, source_target_pairs={{0,24},{24,0},{1,25},{25,1},{2,26},{26,2},{3,27},{27,3},{4,28},{28... | collective-permute-start | bytes 110600 | tf_op jit(solution)/shard_map/ppermute | solution.py:290
  275.8 19.9 %collective-permute-start.50 = (bf16[128,2048]{1,0:T(8,128)(2,1)}, bf16[128,2048]{1,0:T(8,128)(2,1)S(1)}, u32[]{:S(2)}, u32[]{:S(2)}) collective-permute-start(bf16[128,2048]{1,0:T(8,128)(2,1)} %get-tuple-element.612), channel_id=1, source_target_pairs={{0,8},{8,16},{16,24},{1,9},{9,17},{17,25},{2,10},{10,18},{18,26},{... | collective-permute-start | bytes 1572872 | tf_op jit(solution)/shard_map/ppermute | solution.py:379
  343.9 36.3 %collective-permute-start.66 = (bf16[128,2048]{1,0:T(8,128)(2,1)}, bf16[128,2048]{1,0:T(8,128)(2,1)S(1)}, u32[]{:S(2)}, u32[]{:S(2)}) collective-permute-start(bf16[128,2048]{1,0:T(8,128)(2,1)} %get-tuple-element.667), channel_id=1, source_target_pairs={{0,8},{8,16},{16,24},{1,9},{9,17},{17,25},{2,10},{10,18},{18,26},{... | collective-permute-start | bytes 1572872 | tf_op jit(solution)/shard_map/ppermute | solution.py:379
  346.6 33.6 %collective-permute-start.67 = (bf16[128,2048]{1,0:T(8,128)(2,1)}, bf16[128,2048]{1,0:T(8,128)(2,1)S(1)}, u32[]{:S(2)}, u32[]{:S(2)}) collective-permute-start(bf16[128,2048]{1,0:T(8,128)(2,1)} %get-tuple-element.668), channel_id=1, source_target_pairs={{24,16},{16,8},{8,0},{25,17},{17,9},{9,1},{26,18},{18,10},{10,2},{... | collective-permute-start | bytes 1572872 | tf_op jit(solution)/shard_map/ppermute | solution.py:380
  354.5 34.0 %collective-permute-start.64 = (bf16[128,2048]{1,0:T(8,128)(2,1)}, bf16[128,2048]{1,0:T(8,128)(2,1)S(1)}, u32[]{:S(2)}, u32[]{:S(2)}) collective-permute-start(bf16[128,2048]{1,0:T(8,128)(2,1)} %get-tuple-element.669), channel_id=1, source_target_pairs={{0,8},{8,16},{16,24},{1,9},{9,17},{17,25},{2,10},{10,18},{18,26},{... | collective-permute-start | bytes 1572872 | tf_op jit(solution)/shard_map/ppermute | solution.py:379
  357.8 30.7 %collective-permute-start.65 = (bf16[128,2048]{1,0:T(8,128)(2,1)}, bf16[128,2048]{1,0:T(8,128)(2,1)S(1)}, u32[]{:S(2)}, u32[]{:S(2)}) collective-permute-start(bf16[128,2048]{1,0:T(8,128)(2,1)} %get-tuple-element.670), channel_id=1, source_target_pairs={{24,16},{16,8},{8,0},{25,17},{17,9},{9,1},{26,18},{18,10},{10,2},{... | collective-permute-start | bytes 1572872 | tf_op jit(solution)/shard_map/ppermute | solution.py:380
  463.5 24.4 %collective-permute-start.95 = (f32[6144]{0:T(1024)S(1)}, f32[6144]{0:T(1024)S(1)}, u32[]{:S(2)}, u32[]{:S(2)}) collective-permute-start(f32[6144]{0:T(1024)S(1)} %pad_maximum_fusion.1), channel_id=1, source_target_pairs={{0,24},{24,0},{1,25},{25,1},{2,26},{26,2},{3,27},{27,3},{4,28},{28... | collective-permute-start | bytes 73736 | tf_op jit(solution)/shard_map/ppermute | solution.py:290
  468.8 20.6 %collective-permute-start.100 = (f32[9216]{0:T(1024)S(1)}, f32[9216]{0:T(1024)S(1)}, u32[]{:S(2)}, u32[]{:S(2)}) collective-permute-start(f32[9216]{0:T(1024)S(1)} %copy-done.9), channel_id=1, source_target_pairs={{0,8},{24,16},{1,9},{25,17},{2,10},{26,18},{3,11},{27,19},{4,12},{... | collective-permute-start | bytes 110600 | tf_op jit(solution)/shard_map/ppermute | solution.py:335
  473.8 25.2 %collective-permute-start.90 = (bf16[128,2048]{1,0:T(8,128)(2,1)}, bf16[128,2048]{1,0:T(8,128)(2,1)S(1)}, u32[]{:S(2)}, u32[]{:S(2)}) collective-permute-start(bf16[128,2048]{1,0:T(8,128)(2,1)} %get-tuple-element.743), channel_id=1, source_target_pairs={{0,8},{8,16},{16,24},{1,9},{9,17},{17,25},{2,10},{10,18},{18,26},{... | collective-permute-start | bytes 1572872 | tf_op jit(solution)/shard_map/ppermute | solution.py:379
  477.6 21.4 %collective-permute-start.91 = (bf16[128,2048]{1,0:T(8,128)(2,1)S(1)}, bf16[128,2048]{1,0:T(8,128)(2,1)S(1)}, u32[]{:S(2)}, u32[]{:S(2)}) collective-permute-start(bf16[128,2048]{1,0:T(8,128)(2,1)S(1)} %get-tuple-element.744), channel_id=1, source_target_pairs={{24,16},{16,8},{8,0},{25,17},{17,9},{9,1},{26,18},{18,10},{10,2},{... | collective-permute-start | bytes 1572872 | tf_op jit(solution)/shard_map/ppermute | solution.py:380
  489.4 22.6 %collective-permute-start.101 = (f32[9216]{0:T(1024)S(1)}, f32[9216]{0:T(1024)S(1)}, u32[]{:S(2)}, u32[]{:S(2)}) collective-permute-start(f32[9216]{0:T(1024)S(1)} %copy-done.9), channel_id=1, source_target_pairs={{0,16},{24,8},{1,17},{25,9},{2,18},{26,10},{3,19},{27,11},{4,20},{... | collective-permute-start | bytes 110600 | tf_op jit(solution)/shard_map/ppermute | solution.py:335
  506.2 20.0 %collective-permute-start.96 = (bf16[128,2048]{1,0:T(8,128)(2,1)S(1)}, bf16[128,2048]{1,0:T(8,128)(2,1)S(1)}, u32[]{:S(2)}, u32[]{:S(2)}) collective-permute-start(bf16[128,2048]{1,0:T(8,128)(2,1)S(1)} %get-tuple-element.768), channel_id=1, source_target_pairs={{0,8},{8,16},{16,24},{1,9},{9,17},{17,25},{2,10},{10,18},{18,26},{... | collective-permute-start | bytes 1572872 | tf_op jit(solution)/shard_map/ppermute | solution.py:379
  543.9 37.5 %collective-permute-start.108 = (bf16[128,2048]{1,0:T(8,128)(2,1)}, bf16[128,2048]{1,0:T(8,128)(2,1)S(1)}, u32[]{:S(2)}, u32[]{:S(2)}) collective-permute-start(bf16[128,2048]{1,0:T(8,128)(2,1)} %get-tuple-element.790), channel_id=1, source_target_pairs={{0,8},{8,16},{16,24},{1,9},{9,17},{17,25},{2,10},{10,18},{18,26},{... | collective-permute-start | bytes 1572872 | tf_op jit(solution)/shard_map/ppermute | solution.py:379
  548.1 33.3 %collective-permute-start.109 = (bf16[128,2048]{1,0:T(8,128)(2,1)}, bf16[128,2048]{1,0:T(8,128)(2,1)S(1)}, u32[]{:S(2)}, u32[]{:S(2)}) collective-permute-start(bf16[128,2048]{1,0:T(8,128)(2,1)} %get-tuple-element.791), channel_id=1, source_target_pairs={{24,16},{16,8},{8,0},{25,17},{17,9},{9,1},{26,18},{18,10},{10,2},{... | collective-permute-start | bytes 1572872 | tf_op jit(solution)/shard_map/ppermute | solution.py:380
  553.8 33.4 %collective-permute-start.106 = (bf16[128,2048]{1,0:T(8,128)(2,1)}, bf16[128,2048]{1,0:T(8,128)(2,1)S(1)}, u32[]{:S(2)}, u32[]{:S(2)}) collective-permute-start(bf16[128,2048]{1,0:T(8,128)(2,1)} %get-tuple-element.792), channel_id=1, source_target_pairs={{0,8},{8,16},{16,24},{1,9},{9,17},{17,25},{2,10},{10,18},{18,26},{... | collective-permute-start | bytes 1572872 | tf_op jit(solution)/shard_map/ppermute | solution.py:379
  559.1 28.1 %collective-permute-start.107 = (bf16[128,2048]{1,0:T(8,128)(2,1)S(1)}, bf16[128,2048]{1,0:T(8,128)(2,1)S(1)}, u32[]{:S(2)}, u32[]{:S(2)}) collective-permute-start(bf16[128,2048]{1,0:T(8,128)(2,1)S(1)} %get-tuple-element.793), channel_id=1, source_target_pairs={{24,16},{16,8},{8,0},{25,17},{17,9},{9,1},{26,18},{18,10},{10,2},{... | collective-permute-start | bytes 1572872 | tf_op jit(solution)/shard_map/ppermute | solution.py:380
  590.2 21.2 %collective-permute-start.114 = (bf16[128,2048]{1,0:T(8,128)(2,1)S(1)}, bf16[128,2048]{1,0:T(8,128)(2,1)S(1)}, u32[]{:S(2)}, u32[]{:S(2)}) collective-permute-start(bf16[128,2048]{1,0:T(8,128)(2,1)S(1)} %get-tuple-element.812), channel_id=1, source_target_pairs={{0,8},{8,16},{16,24},{1,9},{9,17},{17,25},{2,10},{10,18},{18,26},{... | collective-permute-start | bytes 1572872 | tf_op jit(solution)/shard_map/ppermute | solution.py:379
  672.0 35.4 %collective-permute-start.132 = (bf16[128,2048]{1,0:T(8,128)(2,1)S(1)}, bf16[128,2048]{1,0:T(8,128)(2,1)S(1)}, u32[]{:S(2)}, u32[]{:S(2)}) collective-permute-start(bf16[128,2048]{1,0:T(8,128)(2,1)S(1)} %get-tuple-element.855), channel_id=1, source_target_pairs={{0,8},{8,16},{16,24},{1,9},{9,17},{17,25},{2,10},{10,18},{18,26},{... | collective-permute-start | bytes 1572872 | tf_op jit(solution)/shard_map/ppermute | solution.py:379
  677.7 29.8 %collective-permute-start.133 = (bf16[128,2048]{1,0:T(8,128)(2,1)S(1)}, bf16[128,2048]{1,0:T(8,128)(2,1)S(1)}, u32[]{:S(2)}, u32[]{:S(2)}) collective-permute-start(bf16[128,2048]{1,0:T(8,128)(2,1)S(1)} %get-tuple-element.856), channel_id=1, source_target_pairs={{24,16},{16,8},{8,0},{25,17},{17,9},{9,1},{26,18},{18,10},{10,2},{... | collective-permute-start | bytes 1572872 | tf_op jit(solution)/shard_map/ppermute | solution.py:380
  683.3 29.1 %collective-permute-start.130 = (bf16[128,2048]{1,0:T(8,128)(2,1)S(1)}, bf16[128,2048]{1,0:T(8,128)(2,1)S(1)}, u32[]{:S(2)}, u32[]{:S(2)}) collective-permute-start(bf16[128,2048]{1,0:T(8,128)(2,1)S(1)} %get-tuple-element.857), channel_id=1, source_target_pairs={{0,8},{8,16},{16,24},{1,9},{9,17},{17,25},{2,10},{10,18},{18,26},{... | collective-permute-start | bytes 1572872 | tf_op jit(solution)/shard_map/ppermute | solution.py:379
  688.9 23.4 %collective-permute-start.131 = (bf16[128,2048]{1,0:T(8,128)(2,1)S(1)}, bf16[128,2048]{1,0:T(8,128)(2,1)S(1)}, u32[]{:S(2)}, u32[]{:S(2)}) collective-permute-start(bf16[128,2048]{1,0:T(8,128)(2,1)S(1)} %get-tuple-element.858), channel_id=1, source_target_pairs={{24,16},{16,8},{8,0},{25,17},{17,9},{9,1},{26,18},{18,10},{10,2},{... | collective-permute-start | bytes 1572872 | tf_op jit(solution)/shard_map/ppermute | solution.py:380
  697.0 23.3 %collective-permute-start.139 = (f32[6144]{0:T(1024)S(1)}, f32[6144]{0:T(1024)S(1)}, u32[]{:S(2)}, u32[]{:S(2)}) collective-permute-start(f32[6144]{0:T(1024)S(1)} %pad_maximum_fusion.1), channel_id=1, source_target_pairs={{0,16},{24,8},{1,17},{25,9},{2,18},{26,10},{3,19},{27,11},{4,20},{... | collective-permute-start | bytes 73736 | tf_op jit(solution)/shard_map/ppermute | solution.py:335
  714.6 20.0 %collective-permute-start.134 = (bf16[128,2048]{1,0:T(8,128)(2,1)S(1)}, bf16[128,2048]{1,0:T(8,128)(2,1)S(1)}, u32[]{:S(2)}, u32[]{:S(2)}) collective-permute-start(bf16[128,2048]{1,0:T(8,128)(2,1)S(1)} %get-tuple-element.867), channel_id=1, source_target_pairs={{0,8},{8,16},{16,24},{1,9},{9,17},{17,25},{2,10},{10,18},{18,26},{... | collective-permute-start | bytes 1572872 | tf_op jit(solution)/shard_map/ppermute | solution.py:379
  773.6 20.9 %collective-permute-start.151 = (bf16[128,2048]{1,0:T(8,128)(2,1)S(1)}, bf16[128,2048]{1,0:T(8,128)(2,1)S(1)}, u32[]{:S(2)}, u32[]{:S(2)}) collective-permute-start(bf16[128,2048]{1,0:T(8,128)(2,1)S(1)} %get-tuple-element.900), channel_id=1, source_target_pairs={{16,8},{8,0},{17,9},{9,1},{18,10},{10,2},{19,11},{11,3},{20,12},{1... | collective-permute-start | bytes 1572872 | tf_op jit(solution)/shard_map/ppermute | solution.py:380
  784.8 20.9 %collective-permute-start.149 = (bf16[128,2048]{1,0:T(8,128)(2,1)S(1)}, bf16[128,2048]{1,0:T(8,128)(2,1)S(1)}, u32[]{:S(2)}, u32[]{:S(2)}) collective-permute-start(bf16[128,2048]{1,0:T(8,128)(2,1)S(1)} %get-tuple-element.902), channel_id=1, source_target_pairs={{16,8},{8,0},{17,9},{9,1},{18,10},{10,2},{19,11},{11,3},{20,12},{1... | collective-permute-start | bytes 1572872 | tf_op jit(solution)/shard_map/ppermute | solution.py:380
  796.0 20.9 %collective-permute-start.155 = (bf16[128,2048]{1,0:T(8,128)(2,1)S(1)}, bf16[128,2048]{1,0:T(8,128)(2,1)S(1)}, u32[]{:S(2)}, u32[]{:S(2)}) collective-permute-start(bf16[128,2048]{1,0:T(8,128)(2,1)S(1)} %get-tuple-element.910), channel_id=1, source_target_pairs={{8,0},{9,1},{10,2},{11,3},{12,4},{13,5},{14,6},{15,7}} | collective-permute-start | bytes 1572872 | tf_op jit(solution)/shard_map/ppermute | solution.py:380
  (134 other events, 1858.4 us)

commit v6 on v5

--- a/solution.py
+++ b/solution.py
@@ -254,6 +254,7 @@
         scales = {}
         results = {}
         cell = [None]
+        clock = [0]
 
         def settle(value):
             value, _ = lax.optimization_barrier((value, cell[0]))
@@ -274,7 +275,7 @@
                     row_other = partner(row_part, "col", distances("col")[level])
                 if level < len(distances("row")):
                     col_other = partner(col_part, "row", distances("row")[level])
-                yield [], 1
+                yield [row_part, col_part], 1
                 row_part, col_part, row_other, col_other = settle(
                     (row_part, col_part, row_other, col_other)
                 )
@@ -288,7 +289,7 @@
                 ]
             )
             far = lax.ppermute(packed, "dp", [(0, last), (last, 0)])
-            yield [], FAR
+            yield [packed], FAR
             packed, far = settle((packed, far))
 
             def factors(sums):
@@ -307,16 +308,16 @@
                 part = jnp.sum(raw * raw)
                 energy = part if energy is None else energy + part
                 if g == GROUPS // 2 - 1:
-                    yield [energy], 1
+                    yield [energy, row_scale, col_scale], 1
             energy = jnp.broadcast_to(energy, (8, LANES))
             for axis in ("col", "row"):
                 for distance in distances(axis):
                     other = partner(energy, axis, distance)
-                    yield [], 1
+                    yield [energy], 1
                     energy, other = settle((energy, other))
                     energy = energy + other
             other = lax.ppermute(energy, "dp", [(0, last), (last, 0)])
-            yield [], FAR
+            yield [energy], FAR
             energy, other = settle((energy, other))
             energy = (energy + other)[0, 0]
             rms = jnp.sqrt(energy / (rows * n_row * cols * n_col))
@@ -326,14 +327,14 @@
                 jnp.broadcast_to(row_final[:, None], (half, LANES)),
                 jnp.broadcast_to(col_scale[None, :], (8, cols)),
             ]
-            yield [scales[m][1], scales[m][2]], count // 2
+            yield [scales[m][1], scales[m][2]], max(1, 3 * count + 2 + 6 * m - clock[0])
             sums = packed + far
             for j in range(1, last):
                 for pairs in (
                     [[(0, j), (last, last - j)]] if j != last - j else [[(0, j)], [(last, j)]]
                 ):
                     got = lax.ppermute(settle(packed), "dp", pairs)
-                    yield [], FAR
+                    yield [sums], FAR
                     sums = sums + settle(got)
             results[m] = factors(sums)
             yield list(results[m]), steps
@@ -345,6 +346,7 @@
         tied = []
         for s in range(steps):
             before, tied = tied, []
+            clock[0] = s
             movers = [p for p in range(n_dp) if 0 <= s - LAG * p < messages]
             parts = []
             for index, (kind, m) in enumerate(kinds):

time: 840 us -> 836 us (level)
    ppermute x68, waiting for transfers between devices: 138 us -> 114 us  [local(): lax.ppermute(tied[1], 'dp', [(last - p, last - p - 1) for p in going])]
    ppermute x2, waiting for transfers between devices: 6.01 us -> 23.8 us  [statistics(): other = lax.ppermute(energy, 'dp', [(0, last), (last, 0)])]
  transfers between devices with their start and end apart: 156 -> 156, of which waited for: 80 -> 72; matrix products, arithmetic and copies ran while one was open for 2% -> 2% of each run, Pallas kernels for 21% -> 21%
where the time goes in v6:
time: 836 us; the launch traced here: 821 us
  starting transfers between devices  367 us (44%)
  waiting for transfers between devices  252 us (30%)
  Pallas kernels  172 us (21%)
  other arithmetic  16.4 us (2%)
  between operations  10.3 us (1%)
    ppermute x68, starting transfers between devices, local(): lax.ppermute(tied[0], 'dp', [(p, p + 1) for p in going])  230 us
    pallas_call x70, Pallas kernels, run_step(): pl.pallas_call(functools.partial(step_kernel, plan), grid_spec=pltpu.Pref...  172 us
    ppermute x68, waiting for transfers between devices, local(): lax.ppermute(tied[1], 'dp', [(last - p, last - p - 1) for p in going])  114 us
    ppermute x68, waiting for transfers between devices, local(): lax.ppermute(tied[0], 'dp', [(p, p + 1) for p in going])  94.7 us
    ppermute x68, starting transfers between devices, local(): lax.ppermute(tied[1], 'dp', [(last - p, last - p - 1) for p in going])  85.9 us
    ppermute x2, waiting for transfers between devices, statistics(): other = lax.ppermute(energy, 'dp', [(0, last), (last, 0)])  23.8 us
    ppermute x4, starting transfers between devices, statistics(): got = lax.ppermute(settle(packed), 'dp', pairs)  23.1 us
  transfers between devices with their start and end apart: 156, of which 72 were waited for; matrix products, arithmetic and copies ran while one was open for 2% of the time, Pallas kernels for 21%

profile of v6, /device:TPU:0, one launch (start us, length us, event | category | flops | bytes accessed | tf_op | source)
XLA Modules:
  0.0 821.5 jit_solution(1413060089959649395)
XLA Ops:
  2.0 4.9 collective-permute-start.2
  11.0 8.2 %collective-permute-done.2.refs_0_ = bf16[128,2048]{1,0:T(8,128)(2,1)S(1)} collective-permute-done((bf16[128,2048]{1,0:T(8,128)(2,1)S(1)}, bf16[128,2048]{1,0:T(8,128)(2,1)S(1)}, u32[]{:S(2)}, u32[]{:S(2)}) %collective-permute-start.2) | collective-permute-done | bytes 524320 | tf_op jit(solution)/shard_map/ppermute | solution.py:381
  20.6 4.4 collective-permute-start.6
  25.7 4.7 collective-permute-done.refs_0_
  31.8 4.4 collective-permute-start.4
  37.0 4.7 collective-permute-done.6.refs_0_
  43.1 4.6 collective-permute-start.10
  54.3 4.6 collective-permute-start.8
  66.7 4.2 collective-permute-start.14
  78.0 4.2 collective-permute-start.12
  179.4 4.2 collective-permute-start.34
  190.6 4.2 collective-permute-start.32
  201.9 4.2 collective-permute-start.38
  213.1 4.2 collective-permute-start.36
  259.7 4.3 collective-permute-start.46
  265.3 4.5 collective-permute-start.55
  298.6 4.3 collective-permute-start.58
  304.2 4.3 multiply_reduce_fusion.4
  312.4 4.3 collective-permute-start.56
  324.4 4.3 collective-permute-start.64
  333.8 4.3 collective-permute-start.62
  345.9 4.3 collective-permute-start.69
  360.1 4.4 collective-permute-start.71
  364.5 11.5 %collective-permute-done.71 = f32[8,128]{1,0:T(8,128)S(1)} collective-permute-done((f32[8,128]{1,0:T(8,128)S(1)}, f32[8,128]{1,0:T(8,128)S(1)}, u32[]{:S(2)}, u32[]{:S(2)}) %collective-permute-start.71) | collective-permute-done | bytes 4128 | tf_op jit(solution)/shard_map/ppermute | solution.py:319
  457.9 5.4 collective-permute-start.95
  492.3 4.4 collective-permute-start.98
  505.4 4.4 collective-permute-start.96
  517.1 4.4 collective-permute-start.104
  525.1 4.4 collective-permute-start.102
  545.0 4.5 collective-permute-done.103.refs_1_
  558.2 12.4 %collective-permute-done.111 = f32[8,128]{1,0:T(8,128)S(1)} collective-permute-done((f32[8,128]{1,0:T(8,128)S(1)}, f32[8,128]{1,0:T(8,128)S(1)}, u32[]{:S(2)}, u32[]{:S(2)}) %collective-permute-start.111) | collective-permute-done | bytes 4128 | tf_op jit(solution)/shard_map/ppermute | solution.py:319
  588.6 4.4 collective-permute-done.115.refs_1_
  599.9 4.4 collective-permute-done.113.refs_1_
  611.0 4.5 collective-permute-start.120
  633.8 5.9 collective-permute-start.121
  652.7 5.6 collective-permute-start.126
  661.8 4.4 collective-permute-start.132
  690.4 4.7 collective-permute-start.134
  695.1 6.6 collective-permute-done.134
  703.9 4.3 collective-permute-start.135
  709.5 8.1 collective-permute-start.139
  721.0 8.3 %collective-permute-start.142 = (bf16[128,2048]{1,0:T(8,128)(2,1)S(1)}, bf16[128,2048]{1,0:T(8,128)(2,1)S(1)}, u32[]{:S(2)}, u32[]{:S(2)}) collective-permute-start(bf16[128,2048]{1,0:T(8,128)(2,1)S(1)} %get-tuple-element.877), channel_id=1, source_target_pairs={{0,8},{8,16},{16,24},{1,9},{9,17},{17,25},{2,10},{10,18},{18,26},{... | collective-permute-start | bytes 1572872 | tf_op jit(solution)/shard_map/ppermute | solution.py:381
  732.8 4.4 collective-permute-start.140
  771.1 7.9 collective-permute-done.145.refs_1_
  781.9 8.4 %collective-permute-done.151.refs_1_ = bf16[128,2048]{1,0:T(8,128)(2,1)S(1)} collective-permute-done((bf16[128,2048]{1,0:T(8,128)(2,1)S(1)}, bf16[128,2048]{1,0:T(8,128)(2,1)S(1)}, u32[]{:S(2)}, u32[]{:S(2)}) %collective-permute-start.151) | collective-permute-done | bytes 524320 | tf_op jit(solution)/shard_map/ppermute | solution.py:382
  793.1 8.4 %collective-permute-done.149.refs_1_ = bf16[128,2048]{1,0:T(8,128)(2,1)S(1)} collective-permute-done((bf16[128,2048]{1,0:T(8,128)(2,1)S(1)}, bf16[128,2048]{1,0:T(8,128)(2,1)S(1)}, u32[]{:S(2)}, u32[]{:S(2)}) %collective-permute-start.149) | collective-permute-done | bytes 524320 | tf_op jit(solution)/shard_map/ppermute | solution.py:382
  804.3 8.4 %collective-permute-done.155.refs_1_ = bf16[128,2048]{1,0:T(8,128)(2,1)S(1)} collective-permute-done((bf16[128,2048]{1,0:T(8,128)(2,1)S(1)}, bf16[128,2048]{1,0:T(8,128)(2,1)S(1)}, u32[]{:S(2)}, u32[]{:S(2)}) %collective-permute-start.155) | collective-permute-done | bytes 524320 | tf_op jit(solution)/shard_map/ppermute | solution.py:382
  813.6 6.6 collective-permute-done.153.refs_1_
  (433 shorter events, 549.8 us)
Async XLA Ops:
  8.9 21.5 %collective-permute-start = (bf16[128,2048]{1,0:T(8,128)(2,1)S(1)}, bf16[128,2048]{1,0:T(8,128)(2,1)S(1)}, u32[]{:S(2)}, u32[]{:S(2)}) collective-permute-start(bf16[128,2048]{1,0:T(8,128)(2,1)S(1)} %get-tuple-element.464), channel_id=1, source_target_pairs={{0,8},{1,9},{2,10},{3,11},{4,12},{5,13},{6,14},{7,15}} | collective-permute-start | bytes 1572872 | tf_op jit(solution)/shard_map/ppermute | solution.py:381
  10.3 20.2 %collective-permute-start.1 = (bf16[128,2048]{1,0:T(8,128)(2,1)S(1)}, bf16[128,2048]{1,0:T(8,128)(2,1)S(1)}, u32[]{:S(2)}, u32[]{:S(2)}) collective-permute-start(bf16[128,2048]{1,0:T(8,128)(2,1)S(1)} %get-tuple-element.465), channel_id=1, source_target_pairs={{24,16},{25,17},{26,18},{27,19},{28,20},{29,21},{30,22},{31,23}} | collective-permute-start | bytes 1572872 | tf_op jit(solution)/shard_map/ppermute | solution.py:382
  20.6 21.0 %collective-permute-start.6 = (bf16[128,2048]{1,0:T(8,128)(2,1)S(1)}, bf16[128,2048]{1,0:T(8,128)(2,1)S(1)}, u32[]{:S(2)}, u32[]{:S(2)}) collective-permute-start(bf16[128,2048]{1,0:T(8,128)(2,1)S(1)} %get-tuple-element.470), channel_id=1, source_target_pairs={{0,8},{8,16},{1,9},{9,17},{2,10},{10,18},{3,11},{11,19},{4,12},{12... | collective-permute-start | bytes 1572872 | tf_op jit(solution)/shard_map/ppermute | solution.py:381
  31.8 21.0 %collective-permute-start.4 = (bf16[128,2048]{1,0:T(8,128)(2,1)S(1)}, bf16[128,2048]{1,0:T(8,128)(2,1)S(1)}, u32[]{:S(2)}, u32[]{:S(2)}) collective-permute-start(bf16[128,2048]{1,0:T(8,128)(2,1)S(1)} %get-tuple-element.472), channel_id=1, source_target_pairs={{0,8},{8,16},{1,9},{9,17},{2,10},{10,18},{3,11},{11,19},{4,12},{12... | collective-permute-start | bytes 1572872 | tf_op jit(solution)/shard_map/ppermute | solution.py:381
  43.1 21.0 %collective-permute-start.10 = (bf16[128,2048]{1,0:T(8,128)(2,1)S(1)}, bf16[128,2048]{1,0:T(8,128)(2,1)S(1)}, u32[]{:S(2)}, u32[]{:S(2)}) collective-permute-start(bf16[128,2048]{1,0:T(8,128)(2,1)S(1)} %get-tuple-element.478), channel_id=1, source_target_pairs={{0,8},{8,16},{16,24},{1,9},{9,17},{17,25},{2,10},{10,18},{18,26},{... | collective-permute-start | bytes 1572872 | tf_op jit(solution)/shard_map/ppermute | solution.py:381
  54.3 21.0 %collective-permute-start.8 = (bf16[128,2048]{1,0:T(8,128)(2,1)S(1)}, bf16[128,2048]{1,0:T(8,128)(2,1)S(1)}, u32[]{:S(2)}, u32[]{:S(2)}) collective-permute-start(bf16[128,2048]{1,0:T(8,128)(2,1)S(1)} %get-tuple-element.480), channel_id=1, source_target_pairs={{0,8},{8,16},{16,24},{1,9},{9,17},{17,25},{2,10},{10,18},{18,26},{... | collective-permute-start | bytes 1572872 | tf_op jit(solution)/shard_map/ppermute | solution.py:381
  66.7 19.9 %collective-permute-start.14 = (bf16[128,2048]{1,0:T(8,128)(2,1)S(1)}, bf16[128,2048]{1,0:T(8,128)(2,1)S(1)}, u32[]{:S(2)}, u32[]{:S(2)}) collective-permute-start(bf16[128,2048]{1,0:T(8,128)(2,1)S(1)} %get-tuple-element.489), channel_id=1, source_target_pairs={{0,8},{8,16},{16,24},{1,9},{9,17},{17,25},{2,10},{10,18},{18,26},{... | collective-permute-start | bytes 1572872 | tf_op jit(solution)/shard_map/ppermute | solution.py:381
  78.0 19.9 %collective-permute-start.12 = (bf16[128,2048]{1,0:T(8,128)(2,1)S(1)}, bf16[128,2048]{1,0:T(8,128)(2,1)S(1)}, u32[]{:S(2)}, u32[]{:S(2)}) collective-permute-start(bf16[128,2048]{1,0:T(8,128)(2,1)S(1)} %get-tuple-element.491), channel_id=1, source_target_pairs={{0,8},{8,16},{16,24},{1,9},{9,17},{17,25},{2,10},{10,18},{18,26},{... | collective-permute-start | bytes 1572872 | tf_op jit(solution)/shard_map/ppermute | solution.py:381
  89.2 19.9 %collective-permute-start.18 = (bf16[128,2048]{1,0:T(8,128)(2,1)S(1)}, bf16[128,2048]{1,0:T(8,128)(2,1)S(1)}, u32[]{:S(2)}, u32[]{:S(2)}) collective-permute-start(bf16[128,2048]{1,0:T(8,128)(2,1)S(1)} %get-tuple-element.503), channel_id=1, source_target_pairs={{0,8},{8,16},{16,24},{1,9},{9,17},{17,25},{2,10},{10,18},{18,26},{... | collective-permute-start | bytes 1572872 | tf_op jit(solution)/shard_map/ppermute | solution.py:381
  100.4 19.9 %collective-permute-start.16 = (bf16[128,2048]{1,0:T(8,128)(2,1)S(1)}, bf16[128,2048]{1,0:T(8,128)(2,1)S(1)}, u32[]{:S(2)}, u32[]{:S(2)}) collective-permute-start(bf16[128,2048]{1,0:T(8,128)(2,1)S(1)} %get-tuple-element.505), channel_id=1, source_target_pairs={{0,8},{8,16},{16,24},{1,9},{9,17},{17,25},{2,10},{10,18},{18,26},{... | collective-permute-start | bytes 1572872 | tf_op jit(solution)/shard_map/ppermute | solution.py:381
  111.7 19.9 %collective-permute-start.22 = (bf16[128,2048]{1,0:T(8,128)(2,1)S(1)}, bf16[128,2048]{1,0:T(8,128)(2,1)S(1)}, u32[]{:S(2)}, u32[]{:S(2)}) collective-permute-start(bf16[128,2048]{1,0:T(8,128)(2,1)S(1)} %get-tuple-element.517), channel_id=1, source_target_pairs={{0,8},{8,16},{16,24},{1,9},{9,17},{17,25},{2,10},{10,18},{18,26},{... | collective-permute-start | bytes 1572872 | tf_op jit(solution)/shard_map/ppermute | solution.py:381
  122.9 19.9 %collective-permute-start.20 = (bf16[128,2048]{1,0:T(8,128)(2,1)S(1)}, bf16[128,2048]{1,0:T(8,128)(2,1)S(1)}, u32[]{:S(2)}, u32[]{:S(2)}) collective-permute-start(bf16[128,2048]{1,0:T(8,128)(2,1)S(1)} %get-tuple-element.519), channel_id=1, source_target_pairs={{0,8},{8,16},{16,24},{1,9},{9,17},{17,25},{2,10},{10,18},{18,26},{... | collective-permute-start | bytes 1572872 | tf_op jit(solution)/shard_map/ppermute | solution.py:381
  134.1 19.9 %collective-permute-start.26 = (bf16[128,2048]{1,0:T(8,128)(2,1)S(1)}, bf16[128,2048]{1,0:T(8,128)(2,1)S(1)}, u32[]{:S(2)}, u32[]{:S(2)}) collective-permute-start(bf16[128,2048]{1,0:T(8,128)(2,1)S(1)} %get-tuple-element.531), channel_id=1, source_target_pairs={{0,8},{8,16},{16,24},{1,9},{9,17},{17,25},{2,10},{10,18},{18,26},{... | collective-permute-start | bytes 1572872 | tf_op jit(solution)/shard_map/ppermute | solution.py:381
  145.4 19.9 %collective-permute-start.24 = (bf16[128,2048]{1,0:T(8,128)(2,1)S(1)}, bf16[128,2048]{1,0:T(8,128)(2,1)S(1)}, u32[]{:S(2)}, u32[]{:S(2)}) collective-permute-start(bf16[128,2048]{1,0:T(8,128)(2,1)S(1)} %get-tuple-element.533), channel_id=1, source_target_pairs={{0,8},{8,16},{16,24},{1,9},{9,17},{17,25},{2,10},{10,18},{18,26},{... | collective-permute-start | bytes 1572872 | tf_op jit(solution)/shard_map/ppermute | solution.py:381
  156.6 19.9 %collective-permute-start.30 = (bf16[128,2048]{1,0:T(8,128)(2,1)S(1)}, bf16[128,2048]{1,0:T(8,128)(2,1)S(1)}, u32[]{:S(2)}, u32[]{:S(2)}) collective-permute-start(bf16[128,2048]{1,0:T(8,128)(2,1)S(1)} %get-tuple-element.545), channel_id=1, source_target_pairs={{0,8},{8,16},{16,24},{1,9},{9,17},{17,25},{2,10},{10,18},{18,26},{... | collective-permute-start | bytes 1572872 | tf_op jit(solution)/shard_map/ppermute | solution.py:381
  167.8 19.9 %collective-permute-start.28 = (bf16[128,2048]{1,0:T(8,128)(2,1)S(1)}, bf16[128,2048]{1,0:T(8,128)(2,1)S(1)}, u32[]{:S(2)}, u32[]{:S(2)}) collective-permute-start(bf16[128,2048]{1,0:T(8,128)(2,1)S(1)} %get-tuple-element.547), channel_id=1, source_target_pairs={{0,8},{8,16},{16,24},{1,9},{9,17},{17,25},{2,10},{10,18},{18,26},{... | collective-permute-start | bytes 1572872 | tf_op jit(solution)/shard_map/ppermute | solution.py:381
  235.9 21.1 %collective-permute-start.40 = (bf16[128,2048]{1,0:T(8,128)(2,1)}, bf16[128,2048]{1,0:T(8,128)(2,1)S(1)}, u32[]{:S(2)}, u32[]{:S(2)}) collective-permute-start(bf16[128,2048]{1,0:T(8,128)(2,1)} %get-tuple-element.589), channel_id=1, source_target_pairs={{0,8},{8,16},{16,24},{1,9},{9,17},{17,25},{2,10},{10,18},{18,26},{... | collective-permute-start | bytes 1572872 | tf_op jit(solution)/shard_map/ppermute | solution.py:381
  259.7 19.9 %collective-permute-start.46 = (bf16[128,2048]{1,0:T(8,128)(2,1)S(1)}, bf16[128,2048]{1,0:T(8,128)(2,1)S(1)}, u32[]{:S(2)}, u32[]{:S(2)}) collective-permute-start(bf16[128,2048]{1,0:T(8,128)(2,1)S(1)} %get-tuple-element.606), channel_id=1, source_target_pairs={{0,8},{8,16},{16,24},{1,9},{9,17},{17,25},{2,10},{10,18},{18,26},{... | collective-permute-start | bytes 1572872 | tf_op jit(solution)/shard_map/ppermute | solution.py:381
  265.3 26.2 %collective-permute-start.55 = (f32[9216]{0:T(1024)S(1)}, f32[9216]{0:T(1024)S(1)}, u32[]{:S(2)}, u32[]{:S(2)}) collective-permute-start(f32[9216]{0:T(1024)S(1)} %pad_maximum_fusion), channel_id=1, source_target_pairs={{0,24},{24,0},{1,25},{25,1},{2,26},{26,2},{3,27},{27,3},{4,28},{28... | collective-permute-start | bytes 110600 | tf_op jit(solution)/shard_map/ppermute | solution.py:291
  286.6 23.2 %collective-permute-start.51 = (bf16[128,2048]{1,0:T(8,128)(2,1)}, bf16[128,2048]{1,0:T(8,128)(2,1)S(1)}, u32[]{:S(2)}, u32[]{:S(2)}) collective-permute-start(bf16[128,2048]{1,0:T(8,128)(2,1)} %get-tuple-element.623), channel_id=1, source_target_pairs={{0,8},{8,16},{16,24},{1,9},{9,17},{17,25},{2,10},{10,18},{18,26},{... | collective-permute-start | bytes 1572872 | tf_op jit(solution)/shard_map/ppermute | solution.py:381
  298.6 23.1 %collective-permute-start.58 = (bf16[128,2048]{1,0:T(8,128)(2,1)}, bf16[128,2048]{1,0:T(8,128)(2,1)S(1)}, u32[]{:S(2)}, u32[]{:S(2)}) collective-permute-start(bf16[128,2048]{1,0:T(8,128)(2,1)} %get-tuple-element.639), channel_id=1, source_target_pairs={{0,8},{8,16},{16,24},{1,9},{9,17},{17,25},{2,10},{10,18},{18,26},{... | collective-permute-start | bytes 1572872 | tf_op jit(solution)/shard_map/ppermute | solution.py:381
  345.9 31.4 %collective-permute-start.69 = (bf16[128,2048]{1,0:T(8,128)(2,1)S(1)}, bf16[128,2048]{1,0:T(8,128)(2,1)S(1)}, u32[]{:S(2)}, u32[]{:S(2)}) collective-permute-start(bf16[128,2048]{1,0:T(8,128)(2,1)S(1)} %get-tuple-element.674), channel_id=1, source_target_pairs={{0,8},{8,16},{16,24},{1,9},{9,17},{17,25},{2,10},{10,18},{18,26},{... | collective-permute-start | bytes 1572872 | tf_op jit(solution)/shard_map/ppermute | solution.py:381
  350.2 27.1 %collective-permute-start.70 = (bf16[128,2048]{1,0:T(8,128)(2,1)S(1)}, bf16[128,2048]{1,0:T(8,128)(2,1)S(1)}, u32[]{:S(2)}, u32[]{:S(2)}) collective-permute-start(bf16[128,2048]{1,0:T(8,128)(2,1)S(1)} %get-tuple-element.675), channel_id=1, source_target_pairs={{24,16},{16,8},{8,0},{25,17},{17,9},{9,1},{26,18},{18,10},{10,2},{... | collective-permute-start | bytes 1572872 | tf_op jit(solution)/shard_map/ppermute | solution.py:382
  356.9 26.9 %collective-permute-start.67 = (bf16[128,2048]{1,0:T(8,128)(2,1)S(1)}, bf16[128,2048]{1,0:T(8,128)(2,1)S(1)}, u32[]{:S(2)}, u32[]{:S(2)}) collective-permute-start(bf16[128,2048]{1,0:T(8,128)(2,1)S(1)} %get-tuple-element.676), channel_id=1, source_target_pairs={{0,8},{8,16},{16,24},{1,9},{9,17},{17,25},{2,10},{10,18},{18,26},{... | collective-permute-start | bytes 1572872 | tf_op jit(solution)/shard_map/ppermute | solution.py:381
  358.8 24.9 %collective-permute-start.68 = (bf16[128,2048]{1,0:T(8,128)(2,1)S(1)}, bf16[128,2048]{1,0:T(8,128)(2,1)S(1)}, u32[]{:S(2)}, u32[]{:S(2)}) collective-permute-start(bf16[128,2048]{1,0:T(8,128)(2,1)S(1)} %get-tuple-element.677), channel_id=1, source_target_pairs={{24,16},{16,8},{8,0},{25,17},{17,9},{9,1},{26,18},{18,10},{10,2},{... | collective-permute-start | bytes 1572872 | tf_op jit(solution)/shard_map/ppermute | solution.py:382
  457.9 27.1 %collective-permute-start.95 = (f32[6144]{0:T(1024)S(1)}, f32[6144]{0:T(1024)S(1)}, u32[]{:S(2)}, u32[]{:S(2)}) collective-permute-start(f32[6144]{0:T(1024)S(1)} %pad_maximum_fusion.1), channel_id=1, source_target_pairs={{0,24},{24,0},{1,25},{25,1},{2,26},{26,2},{3,27},{27,3},{4,28},{28... | collective-permute-start | bytes 73736 | tf_op jit(solution)/shard_map/ppermute | solution.py:291
  468.4 20.6 %collective-permute-start.93 = (bf16[128,2048]{1,0:T(8,128)(2,1)}, bf16[128,2048]{1,0:T(8,128)(2,1)S(1)}, u32[]{:S(2)}, u32[]{:S(2)}) collective-permute-start(bf16[128,2048]{1,0:T(8,128)(2,1)} %get-tuple-element.752), channel_id=1, source_target_pairs={{0,8},{8,16},{16,24},{1,9},{9,17},{17,25},{2,10},{10,18},{18,26},{... | collective-permute-start | bytes 1572872 | tf_op jit(solution)/shard_map/ppermute | solution.py:381
  479.6 23.6 %collective-permute-start.91 = (bf16[128,2048]{1,0:T(8,128)(2,1)}, bf16[128,2048]{1,0:T(8,128)(2,1)S(1)}, u32[]{:S(2)}, u32[]{:S(2)}) collective-permute-start(bf16[128,2048]{1,0:T(8,128)(2,1)} %get-tuple-element.754), channel_id=1, source_target_pairs={{0,8},{8,16},{16,24},{1,9},{9,17},{17,25},{2,10},{10,18},{18,26},{... | collective-permute-start | bytes 1572872 | tf_op jit(solution)/shard_map/ppermute | solution.py:381
  492.3 22.5 %collective-permute-start.98 = (bf16[128,2048]{1,0:T(8,128)(2,1)}, bf16[128,2048]{1,0:T(8,128)(2,1)S(1)}, u32[]{:S(2)}, u32[]{:S(2)}) collective-permute-start(bf16[128,2048]{1,0:T(8,128)(2,1)} %get-tuple-element.766), channel_id=1, source_target_pairs={{0,8},{8,16},{16,24},{1,9},{9,17},{17,25},{2,10},{10,18},{18,26},{... | collective-permute-start | bytes 1572872 | tf_op jit(solution)/shard_map/ppermute | solution.py:381
  525.1 19.9 %collective-permute-start.102 = (bf16[128,2048]{1,0:T(8,128)(2,1)S(1)}, bf16[128,2048]{1,0:T(8,128)(2,1)S(1)}, u32[]{:S(2)}, u32[]{:S(2)}) collective-permute-start(bf16[128,2048]{1,0:T(8,128)(2,1)S(1)} %get-tuple-element.783), channel_id=1, source_target_pairs={{0,8},{8,16},{16,24},{1,9},{9,17},{17,25},{2,10},{10,18},{18,26},{... | collective-permute-start | bytes 1572872 | tf_op jit(solution)/shard_map/ppermute | solution.py:381
  529.6 19.9 %collective-permute-start.103 = (bf16[128,2048]{1,0:T(8,128)(2,1)S(1)}, bf16[128,2048]{1,0:T(8,128)(2,1)S(1)}, u32[]{:S(2)}, u32[]{:S(2)}) collective-permute-start(bf16[128,2048]{1,0:T(8,128)(2,1)S(1)} %get-tuple-element.784), channel_id=1, source_target_pairs={{24,16},{16,8},{8,0},{25,17},{17,9},{9,1},{26,18},{18,10},{10,2},{... | collective-permute-start | bytes 1572872 | tf_op jit(solution)/shard_map/ppermute | solution.py:382
  540.4 31.3 %collective-permute-start.109 = (bf16[128,2048]{1,0:T(8,128)(2,1)S(1)}, bf16[128,2048]{1,0:T(8,128)(2,1)S(1)}, u32[]{:S(2)}, u32[]{:S(2)}) collective-permute-start(bf16[128,2048]{1,0:T(8,128)(2,1)S(1)} %get-tuple-element.793), channel_id=1, source_target_pairs={{0,8},{8,16},{16,24},{1,9},{9,17},{17,25},{2,10},{10,18},{18,26},{... | collective-permute-start | bytes 1572872 | tf_op jit(solution)/shard_map/ppermute | solution.py:381
  542.2 29.6 %collective-permute-start.110 = (bf16[128,2048]{1,0:T(8,128)(2,1)S(1)}, bf16[128,2048]{1,0:T(8,128)(2,1)S(1)}, u32[]{:S(2)}, u32[]{:S(2)}) collective-permute-start(bf16[128,2048]{1,0:T(8,128)(2,1)S(1)} %get-tuple-element.794), channel_id=1, source_target_pairs={{24,16},{16,8},{8,0},{25,17},{17,9},{9,1},{26,18},{18,10},{10,2},{... | collective-permute-start | bytes 1572872 | tf_op jit(solution)/shard_map/ppermute | solution.py:382
  551.7 25.9 %collective-permute-start.107 = (bf16[128,2048]{1,0:T(8,128)(2,1)S(1)}, bf16[128,2048]{1,0:T(8,128)(2,1)S(1)}, u32[]{:S(2)}, u32[]{:S(2)}) collective-permute-start(bf16[128,2048]{1,0:T(8,128)(2,1)S(1)} %get-tuple-element.795), channel_id=1, source_target_pairs={{0,8},{8,16},{16,24},{1,9},{9,17},{17,25},{2,10},{10,18},{18,26},{... | collective-permute-start | bytes 1572872 | tf_op jit(solution)/shard_map/ppermute | solution.py:381
  553.4 24.2 %collective-permute-start.108 = (bf16[128,2048]{1,0:T(8,128)(2,1)S(1)}, bf16[128,2048]{1,0:T(8,128)(2,1)S(1)}, u32[]{:S(2)}, u32[]{:S(2)}) collective-permute-start(bf16[128,2048]{1,0:T(8,128)(2,1)S(1)} %get-tuple-element.796), channel_id=1, source_target_pairs={{24,16},{16,8},{8,0},{25,17},{17,9},{9,1},{26,18},{18,10},{10,2},{... | collective-permute-start | bytes 1572872 | tf_op jit(solution)/shard_map/ppermute | solution.py:382
  584.3 20.0 %collective-permute-start.113 = (bf16[128,2048]{1,0:T(8,128)(2,1)S(1)}, bf16[128,2048]{1,0:T(8,128)(2,1)S(1)}, u32[]{:S(2)}, u32[]{:S(2)}) collective-permute-start(bf16[128,2048]{1,0:T(8,128)(2,1)S(1)} %get-tuple-element.809), channel_id=1, source_target_pairs={{24,16},{16,8},{8,0},{25,17},{17,9},{9,1},{26,18},{18,10},{10,2},{... | collective-permute-start | bytes 1572872 | tf_op jit(solution)/shard_map/ppermute | solution.py:382
  618.7 21.0 %collective-permute-start.122 = (bf16[128,2048]{1,0:T(8,128)(2,1)S(1)}, bf16[128,2048]{1,0:T(8,128)(2,1)S(1)}, u32[]{:S(2)}, u32[]{:S(2)}) collective-permute-start(bf16[128,2048]{1,0:T(8,128)(2,1)S(1)} %get-tuple-element.830), channel_id=1, source_target_pairs={{0,8},{8,16},{16,24},{1,9},{9,17},{17,25},{2,10},{10,18},{18,26},{... | collective-permute-start | bytes 1572872 | tf_op jit(solution)/shard_map/ppermute | solution.py:381
  661.8 20.0 %collective-permute-start.132 = (bf16[128,2048]{1,0:T(8,128)(2,1)S(1)}, bf16[128,2048]{1,0:T(8,128)(2,1)S(1)}, u32[]{:S(2)}, u32[]{:S(2)}) collective-permute-start(bf16[128,2048]{1,0:T(8,128)(2,1)S(1)} %get-tuple-element.855), channel_id=1, source_target_pairs={{0,8},{8,16},{16,24},{1,9},{9,17},{17,25},{2,10},{10,18},{18,26},{... | collective-permute-start | bytes 1572872 | tf_op jit(solution)/shard_map/ppermute | solution.py:381
  674.8 26.9 %collective-permute-start.130 = (bf16[128,2048]{1,0:T(8,128)(2,1)S(1)}, bf16[128,2048]{1,0:T(8,128)(2,1)S(1)}, u32[]{:S(2)}, u32[]{:S(2)}) collective-permute-start(bf16[128,2048]{1,0:T(8,128)(2,1)S(1)} %get-tuple-element.857), channel_id=1, source_target_pairs={{0,8},{8,16},{16,24},{1,9},{9,17},{17,25},{2,10},{10,18},{18,26},{... | collective-permute-start | bytes 1572872 | tf_op jit(solution)/shard_map/ppermute | solution.py:381
  677.8 23.8 %collective-permute-start.131 = (bf16[128,2048]{1,0:T(8,128)(2,1)S(1)}, bf16[128,2048]{1,0:T(8,128)(2,1)S(1)}, u32[]{:S(2)}, u32[]{:S(2)}) collective-permute-start(bf16[128,2048]{1,0:T(8,128)(2,1)S(1)} %get-tuple-element.858), channel_id=1, source_target_pairs={{24,16},{16,8},{8,0},{25,17},{17,9},{9,1},{26,18},{18,10},{10,2},{... | collective-permute-start | bytes 1572872 | tf_op jit(solution)/shard_map/ppermute | solution.py:382
  686.0 31.5 %collective-permute-start.137 = (bf16[128,2048]{1,0:T(8,128)(2,1)S(1)}, bf16[128,2048]{1,0:T(8,128)(2,1)S(1)}, u32[]{:S(2)}, u32[]{:S(2)}) collective-permute-start(bf16[128,2048]{1,0:T(8,128)(2,1)S(1)} %get-tuple-element.865), channel_id=1, source_target_pairs={{0,8},{8,16},{16,24},{1,9},{9,17},{17,25},{2,10},{10,18},{18,26},{... | collective-permute-start | bytes 1572872 | tf_op jit(solution)/shard_map/ppermute | solution.py:381
  689.1 28.5 %collective-permute-start.138 = (bf16[128,2048]{1,0:T(8,128)(2,1)S(1)}, bf16[128,2048]{1,0:T(8,128)(2,1)S(1)}, u32[]{:S(2)}, u32[]{:S(2)}) collective-permute-start(bf16[128,2048]{1,0:T(8,128)(2,1)S(1)} %get-tuple-element.866), channel_id=1, source_target_pairs={{24,16},{16,8},{8,0},{25,17},{17,9},{9,1},{26,18},{18,10},{10,2},{... | collective-permute-start | bytes 1572872 | tf_op jit(solution)/shard_map/ppermute | solution.py:382
  703.9 26.7 %collective-permute-start.135 = (bf16[128,2048]{1,0:T(8,128)(2,1)S(1)}, bf16[128,2048]{1,0:T(8,128)(2,1)S(1)}, u32[]{:S(2)}, u32[]{:S(2)}) collective-permute-start(bf16[128,2048]{1,0:T(8,128)(2,1)S(1)} %get-tuple-element.869), channel_id=1, source_target_pairs={{0,8},{8,16},{16,24},{1,9},{9,17},{17,25},{2,10},{10,18},{18,26},{... | collective-permute-start | bytes 1572872 | tf_op jit(solution)/shard_map/ppermute | solution.py:381
  708.2 22.5 %collective-permute-start.136 = (bf16[128,2048]{1,0:T(8,128)(2,1)S(1)}, bf16[128,2048]{1,0:T(8,128)(2,1)S(1)}, u32[]{:S(2)}, u32[]{:S(2)}) collective-permute-start(bf16[128,2048]{1,0:T(8,128)(2,1)S(1)} %get-tuple-element.870), channel_id=1, source_target_pairs={{24,16},{16,8},{8,0},{25,17},{17,9},{9,1},{26,18},{18,10},{10,2},{... | collective-permute-start | bytes 1572872 | tf_op jit(solution)/shard_map/ppermute | solution.py:382
  721.0 20.1 %collective-permute-start.142 = (bf16[128,2048]{1,0:T(8,128)(2,1)S(1)}, bf16[128,2048]{1,0:T(8,128)(2,1)S(1)}, u32[]{:S(2)}, u32[]{:S(2)}) collective-permute-start(bf16[128,2048]{1,0:T(8,128)(2,1)S(1)} %get-tuple-element.877), channel_id=1, source_target_pairs={{0,8},{8,16},{16,24},{1,9},{9,17},{17,25},{2,10},{10,18},{18,26},{... | collective-permute-start | bytes 1572872 | tf_op jit(solution)/shard_map/ppermute | solution.py:381
  769.3 20.9 %collective-permute-start.151 = (bf16[128,2048]{1,0:T(8,128)(2,1)S(1)}, bf16[128,2048]{1,0:T(8,128)(2,1)S(1)}, u32[]{:S(2)}, u32[]{:S(2)}) collective-permute-start(bf16[128,2048]{1,0:T(8,128)(2,1)S(1)} %get-tuple-element.900), channel_id=1, source_target_pairs={{16,8},{8,0},{17,9},{9,1},{18,10},{10,2},{19,11},{11,3},{20,12},{1... | collective-permute-start | bytes 1572872 | tf_op jit(solution)/shard_map/ppermute | solution.py:382
  780.6 20.9 %collective-permute-start.149 = (bf16[128,2048]{1,0:T(8,128)(2,1)S(1)}, bf16[128,2048]{1,0:T(8,128)(2,1)S(1)}, u32[]{:S(2)}, u32[]{:S(2)}) collective-permute-start(bf16[128,2048]{1,0:T(8,128)(2,1)S(1)} %get-tuple-element.902), channel_id=1, source_target_pairs={{16,8},{8,0},{17,9},{9,1},{18,10},{10,2},{19,11},{11,3},{20,12},{1... | collective-permute-start | bytes 1572872 | tf_op jit(solution)/shard_map/ppermute | solution.py:382
  791.8 20.9 %collective-permute-start.155 = (bf16[128,2048]{1,0:T(8,128)(2,1)S(1)}, bf16[128,2048]{1,0:T(8,128)(2,1)S(1)}, u32[]{:S(2)}, u32[]{:S(2)}) collective-permute-start(bf16[128,2048]{1,0:T(8,128)(2,1)S(1)} %get-tuple-element.910), channel_id=1, source_target_pairs={{8,0},{9,1},{10,2},{11,3},{12,4},{13,5},{14,6},{15,7}} | collective-permute-start | bytes 1572872 | tf_op jit(solution)/shard_map/ppermute | solution.py:382
  (130 other events, 1858.9 us)

commit v7 on v6

--- a/solution.py
+++ b/solution.py
@@ -253,8 +253,8 @@
         finished = [0, 0]
         scales = {}
         results = {}
+        sums = {}
         cell = [None]
-        clock = [0]
 
         def settle(value):
             value, _ = lax.optimization_barrier((value, cell[0]))
@@ -292,12 +292,7 @@
             yield [packed], FAR
             packed, far = settle((packed, far))
 
-            def factors(sums):
-                row_new = BETA * prevs[m][0] + (1.0 - BETA) * (sums[:rows] / (cols * n_col))
-                col_new = BETA * prevs[m][1] + (1.0 - BETA) * (sums[rows:] / (rows * n_row))
-                return row_new, col_new
-
-            row_new, col_new = factors(packed + far)
+            row_new, col_new = factors(m, packed + far)
             row_scale = lax.rsqrt(jnp.where(place == 0, row_new[half:], row_new[:half]))
             col_scale = lax.rsqrt(col_new)
             energy = None
@@ -307,8 +302,6 @@
                 raw = wide * row_scale[low:high, None] * col_scale[None, :]
                 part = jnp.sum(raw * raw)
                 energy = part if energy is None else energy + part
-                if g == GROUPS // 2 - 1:
-                    yield [energy, row_scale, col_scale], 1
             energy = jnp.broadcast_to(energy, (8, LANES))
             for axis in ("col", "row"):
                 for distance in distances(axis):
@@ -317,7 +310,7 @@
                     energy, other = settle((energy, other))
                     energy = energy + other
             other = lax.ppermute(energy, "dp", [(0, last), (last, 0)])
-            yield [energy], FAR
+            yield [energy], FAR + m
             energy, other = settle((energy, other))
             energy = (energy + other)[0, 0]
             rms = jnp.sqrt(energy / (rows * n_row * cols * n_col))
@@ -327,26 +320,37 @@
                 jnp.broadcast_to(row_final[:, None], (half, LANES)),
                 jnp.broadcast_to(col_scale[None, :], (8, cols)),
             ]
-            yield [scales[m][1], scales[m][2]], max(1, 3 * count + 2 + 6 * m - clock[0])
-            sums = packed + far
+            sums[m] = (packed, far)
+            yield [scales[m][1], scales[m][2]], steps
+
+        def factors(m, total):
+            rows, cols = shapes[m]
+            row_new = BETA * prevs[m][0] + (1.0 - BETA) * (total[:rows] / (cols * n_col))
+            col_new = BETA * prevs[m][1] + (1.0 - BETA) * (total[rows:] / (rows * n_row))
+            return row_new, col_new
+
+        def closing():
+            packed, far = (jnp.concatenate([sums[m][k] for m in range(2)]) for k in range(2))
+            total = packed + far
             for j in range(1, last):
                 for pairs in (
                     [[(0, j), (last, last - j)]] if j != last - j else [[(0, j)], [(last, j)]]
                 ):
                     got = lax.ppermute(settle(packed), "dp", pairs)
-                    yield [sums], FAR
-                    sums = sums + settle(got)
-            results[m] = factors(sums)
-            yield list(results[m]), steps
-
-        workers = [statistics(0), statistics(1)]
-        wakes = [0, 0]
+                    yield [total], FAR
+                    total = total + settle(got)
+            cut = sum(shapes[0])
+            results[0] = factors(0, total[:cut])
+            results[1] = factors(1, total[cut:])
+            yield [*results[0], *results[1]], steps
+
+        workers = [statistics(0), statistics(1), closing()]
+        wakes = [0, 0, messages - 2]
         outs = [None, None]
         inflight = {}
         tied = []
         for s in range(steps):
             before, tied = tied, []
-            clock[0] = s
             movers = [p for p in range(n_dp) if 0 <= s - LAG * p < messages]
             parts = []
             for index, (kind, m) in enumerate(kinds):
@@ -382,14 +386,13 @@
                     lax.ppermute(tied[1], "dp", [(last - p, last - p - 1) for p in going]),
                 ]
                 cell[0] = list(tied)
-            for m in range(2):
-                if s >= wakes[m]:
-                    ties, wait = next(workers[m])
+            for w, worker in enumerate(workers):
+                if s >= wakes[w]:
+                    ties, wait = next(worker)
                     tied = tied + ties
-                    wakes[m] = s + wait
-        for m in range(2):
-            while m not in results:
-                next(workers[m])
+                    wakes[w] = s + wait
+        while not results:
+            next(workers[2])
         return (outs[0], *results[0], outs[1], *results[1])
 
     return local

time: 836 us -> 800 us (0.957)
  starting transfers between devices: 367 us -> 327 us
  waiting for transfers between devices: 252 us -> 263 us
    ppermute x68, waiting for transfers between devices: 114 us -> 150 us  [local(): lax.ppermute(tied[1], 'dp', [(last - p, last - p - 1) for p in going])]
    ppermute x68, starting transfers between devices: 230 us -> 203 us  [local(): lax.ppermute(tied[0], 'dp', [(p, p + 1) for p in going])]
    ppermute x2, waiting for transfers between devices: 23.8 us -> 8.85 us  [statistics(): other = lax.ppermute(energy, 'dp', [(0, last), (last, 0)])]
    ppermute x4 -> x2, starting transfers between devices: 23.1 us -> 12 us  [closing(): got = lax.ppermute(settle(packed), 'dp', pairs)]
  transfers between devices with their start and end apart: 156 -> 154, of which waited for: 72 -> 87; matrix products, arithmetic and copies ran while one was open for 2% -> 2% of each run, Pallas kernels for 21% -> 21%
where the time goes in v7:
time: 800 us; the launch traced here: 786 us
  starting transfers between devices  327 us (41%)
  waiting for transfers between devices  263 us (33%)
  Pallas kernels  170 us (21%)
  other arithmetic  11.9 us (1%)
  between operations  10 us (1%)
    ppermute x68, starting transfers between devices, local(): lax.ppermute(tied[0], 'dp', [(p, p + 1) for p in going])  203 us
    pallas_call x70, Pallas kernels, run_step(): pl.pallas_call(functools.partial(step_kernel, plan), grid_spec=pltpu.Pref...  170 us
    ppermute x68, waiting for transfers between devices, local(): lax.ppermute(tied[1], 'dp', [(last - p, last - p - 1) for p in going])  150 us
    ppermute x68, waiting for transfers between devices, local(): lax.ppermute(tied[0], 'dp', [(p, p + 1) for p in going])  90.5 us
    ppermute x68, starting transfers between devices, local(): lax.ppermute(tied[1], 'dp', [(last - p, last - p - 1) for p in going])  86.1 us
  transfers between devices with their start and end apart: 154, of which 87 were waited for; matrix products, arithmetic and copies ran while one was open for 2% of the time, Pallas kernels for 21%

profile of v7, /device:TPU:0, one launch (start us, length us, event | category | flops | bytes accessed | tf_op | source)
XLA Modules:
  0.0 785.7 jit_solution(4024707436456582519)
XLA Ops:
  2.0 4.9 collective-permute-start.2
  11.0 8.2 %collective-permute-done.2.refs_0_ = bf16[128,2048]{1,0:T(8,128)(2,1)S(1)} collective-permute-done((bf16[128,2048]{1,0:T(8,128)(2,1)S(1)}, bf16[128,2048]{1,0:T(8,128)(2,1)S(1)}, u32[]{:S(2)}, u32[]{:S(2)}) %collective-permute-start.2) | collective-permute-done | bytes 524320 | tf_op jit(solution)/shard_map/ppermute | solution.py:385
  20.6 4.4 collective-permute-start.6
  25.7 4.7 collective-permute-done.refs_0_
  31.8 4.4 collective-permute-start.4
  37.0 4.7 collective-permute-done.6.refs_0_
  43.1 4.6 collective-permute-start.10
  54.3 4.6 collective-permute-start.8
  66.7 4.2 collective-permute-start.14
  201.9 4.2 collective-permute-start.38
  259.7 4.3 collective-permute-start.46
  265.4 4.5 collective-permute-start.55
  301.0 4.3 collective-permute-start.59
  312.9 4.3 collective-permute-start.57
  322.4 4.3 collective-permute-start.65
  334.3 4.3 collective-permute-start.63
  362.3 4.4 collective-permute-done.71.refs_1_
  373.6 4.4 collective-permute-done.69.refs_1_
  384.8 4.4 collective-permute-done.75.refs_1_
  396.0 4.4 collective-permute-done.73.refs_1_
  407.3 4.4 collective-permute-done.79.refs_1_
  464.0 5.0 collective-permute-done.87.refs_1_
  484.9 4.4 collective-permute-start.99
  496.6 4.4 collective-permute-start.97
  505.8 4.4 collective-permute-start.105
  517.5 4.4 collective-permute-start.103
  544.0 4.9 collective-permute-done.111
  556.8 4.4 collective-permute-done.108.refs_1_
  568.1 4.4 collective-permute-done.115.refs_1_
  579.3 4.4 collective-permute-done.113.refs_1_
  590.5 4.4 collective-permute-done.119.refs_1_
  601.8 4.4 collective-permute-done.117.refs_1_
  613.0 4.4 collective-permute-done.121.refs_1_
  624.2 4.4 collective-permute-done.125.refs_1_
  635.5 4.4 collective-permute-done.123.refs_1_
  646.7 4.4 collective-permute-done.129.refs_1_
  657.9 4.4 collective-permute-done.127.refs_1_
  669.2 4.4 collective-permute-done.133.refs_1_
  680.4 4.4 collective-permute-done.131.refs_1_
  691.6 4.4 collective-permute-done.137.refs_1_
  702.9 4.4 collective-permute-done.135.refs_1_
  714.1 4.4 collective-permute-done.142.refs_1_
  725.4 4.4 collective-permute-done.140.refs_1_
  732.6 5.6 collective-permute-start.138
  740.1 6.3 collective-permute-start.143
  757.6 7.2 collective-permute-done.149.refs_1_
  767.6 8.4 %collective-permute-done.153.refs_1_ = bf16[128,2048]{1,0:T(8,128)(2,1)S(1)} collective-permute-done((bf16[128,2048]{1,0:T(8,128)(2,1)S(1)}, bf16[128,2048]{1,0:T(8,128)(2,1)S(1)}, u32[]{:S(2)}, u32[]{:S(2)}) %collective-permute-start.153) | collective-permute-done | bytes 524320 | tf_op jit(solution)/shard_map/ppermute | solution.py:386
  776.8 7.6 collective-permute-done.151.refs_1_
  (421 shorter events, 545.0 us)
Async XLA Ops:
  8.9 21.5 %collective-permute-start = (bf16[128,2048]{1,0:T(8,128)(2,1)S(1)}, bf16[128,2048]{1,0:T(8,128)(2,1)S(1)}, u32[]{:S(2)}, u32[]{:S(2)}) collective-permute-start(bf16[128,2048]{1,0:T(8,128)(2,1)S(1)} %get-tuple-element.458), channel_id=1, source_target_pairs={{0,8},{1,9},{2,10},{3,11},{4,12},{5,13},{6,14},{7,15}} | collective-permute-start | bytes 1572872 | tf_op jit(solution)/shard_map/ppermute | solution.py:385
  10.3 20.2 %collective-permute-start.1 = (bf16[128,2048]{1,0:T(8,128)(2,1)S(1)}, bf16[128,2048]{1,0:T(8,128)(2,1)S(1)}, u32[]{:S(2)}, u32[]{:S(2)}) collective-permute-start(bf16[128,2048]{1,0:T(8,128)(2,1)S(1)} %get-tuple-element.459), channel_id=1, source_target_pairs={{24,16},{25,17},{26,18},{27,19},{28,20},{29,21},{30,22},{31,23}} | collective-permute-start | bytes 1572872 | tf_op jit(solution)/shard_map/ppermute | solution.py:386
  20.6 21.0 %collective-permute-start.6 = (bf16[128,2048]{1,0:T(8,128)(2,1)S(1)}, bf16[128,2048]{1,0:T(8,128)(2,1)S(1)}, u32[]{:S(2)}, u32[]{:S(2)}) collective-permute-start(bf16[128,2048]{1,0:T(8,128)(2,1)S(1)} %get-tuple-element.464), channel_id=1, source_target_pairs={{0,8},{8,16},{1,9},{9,17},{2,10},{10,18},{3,11},{11,19},{4,12},{12... | collective-permute-start | bytes 1572872 | tf_op jit(solution)/shard_map/ppermute | solution.py:385
  31.8 21.0 %collective-permute-start.4 = (bf16[128,2048]{1,0:T(8,128)(2,1)S(1)}, bf16[128,2048]{1,0:T(8,128)(2,1)S(1)}, u32[]{:S(2)}, u32[]{:S(2)}) collective-permute-start(bf16[128,2048]{1,0:T(8,128)(2,1)S(1)} %get-tuple-element.466), channel_id=1, source_target_pairs={{0,8},{8,16},{1,9},{9,17},{2,10},{10,18},{3,11},{11,19},{4,12},{12... | collective-permute-start | bytes 1572872 | tf_op jit(solution)/shard_map/ppermute | solution.py:385
  43.1 21.0 %collective-permute-start.10 = (bf16[128,2048]{1,0:T(8,128)(2,1)S(1)}, bf16[128,2048]{1,0:T(8,128)(2,1)S(1)}, u32[]{:S(2)}, u32[]{:S(2)}) collective-permute-start(bf16[128,2048]{1,0:T(8,128)(2,1)S(1)} %get-tuple-element.472), channel_id=1, source_target_pairs={{0,8},{8,16},{16,24},{1,9},{9,17},{17,25},{2,10},{10,18},{18,26},{... | collective-permute-start | bytes 1572872 | tf_op jit(solution)/shard_map/ppermute | solution.py:385
  54.3 21.0 %collective-permute-start.8 = (bf16[128,2048]{1,0:T(8,128)(2,1)S(1)}, bf16[128,2048]{1,0:T(8,128)(2,1)S(1)}, u32[]{:S(2)}, u32[]{:S(2)}) collective-permute-start(bf16[128,2048]{1,0:T(8,128)(2,1)S(1)} %get-tuple-element.474), channel_id=1, source_target_pairs={{0,8},{8,16},{16,24},{1,9},{9,17},{17,25},{2,10},{10,18},{18,26},{... | collective-permute-start | bytes 1572872 | tf_op jit(solution)/shard_map/ppermute | solution.py:385
  66.7 19.9 %collective-permute-start.14 = (bf16[128,2048]{1,0:T(8,128)(2,1)S(1)}, bf16[128,2048]{1,0:T(8,128)(2,1)S(1)}, u32[]{:S(2)}, u32[]{:S(2)}) collective-permute-start(bf16[128,2048]{1,0:T(8,128)(2,1)S(1)} %get-tuple-element.483), channel_id=1, source_target_pairs={{0,8},{8,16},{16,24},{1,9},{9,17},{17,25},{2,10},{10,18},{18,26},{... | collective-permute-start | bytes 1572872 | tf_op jit(solution)/shard_map/ppermute | solution.py:385
  78.0 19.9 %collective-permute-start.12 = (bf16[128,2048]{1,0:T(8,128)(2,1)S(1)}, bf16[128,2048]{1,0:T(8,128)(2,1)S(1)}, u32[]{:S(2)}, u32[]{:S(2)}) collective-permute-start(bf16[128,2048]{1,0:T(8,128)(2,1)S(1)} %get-tuple-element.485), channel_id=1, source_target_pairs={{0,8},{8,16},{16,24},{1,9},{9,17},{17,25},{2,10},{10,18},{18,26},{... | collective-permute-start | bytes 1572872 | tf_op jit(solution)/shard_map/ppermute | solution.py:385
  89.2 19.9 %collective-permute-start.18 = (bf16[128,2048]{1,0:T(8,128)(2,1)S(1)}, bf16[128,2048]{1,0:T(8,128)(2,1)S(1)}, u32[]{:S(2)}, u32[]{:S(2)}) collective-permute-start(bf16[128,2048]{1,0:T(8,128)(2,1)S(1)} %get-tuple-element.497), channel_id=1, source_target_pairs={{0,8},{8,16},{16,24},{1,9},{9,17},{17,25},{2,10},{10,18},{18,26},{... | collective-permute-start | bytes 1572872 | tf_op jit(solution)/shard_map/ppermute | solution.py:385
  100.4 19.9 %collective-permute-start.16 = (bf16[128,2048]{1,0:T(8,128)(2,1)S(1)}, bf16[128,2048]{1,0:T(8,128)(2,1)S(1)}, u32[]{:S(2)}, u32[]{:S(2)}) collective-permute-start(bf16[128,2048]{1,0:T(8,128)(2,1)S(1)} %get-tuple-element.499), channel_id=1, source_target_pairs={{0,8},{8,16},{16,24},{1,9},{9,17},{17,25},{2,10},{10,18},{18,26},{... | collective-permute-start | bytes 1572872 | tf_op jit(solution)/shard_map/ppermute | solution.py:385
  111.7 19.9 %collective-permute-start.22 = (bf16[128,2048]{1,0:T(8,128)(2,1)S(1)}, bf16[128,2048]{1,0:T(8,128)(2,1)S(1)}, u32[]{:S(2)}, u32[]{:S(2)}) collective-permute-start(bf16[128,2048]{1,0:T(8,128)(2,1)S(1)} %get-tuple-element.511), channel_id=1, source_target_pairs={{0,8},{8,16},{16,24},{1,9},{9,17},{17,25},{2,10},{10,18},{18,26},{... | collective-permute-start | bytes 1572872 | tf_op jit(solution)/shard_map/ppermute | solution.py:385
  122.9 19.9 %collective-permute-start.20 = (bf16[128,2048]{1,0:T(8,128)(2,1)S(1)}, bf16[128,2048]{1,0:T(8,128)(2,1)S(1)}, u32[]{:S(2)}, u32[]{:S(2)}) collective-permute-start(bf16[128,2048]{1,0:T(8,128)(2,1)S(1)} %get-tuple-element.513), channel_id=1, source_target_pairs={{0,8},{8,16},{16,24},{1,9},{9,17},{17,25},{2,10},{10,18},{18,26},{... | collective-permute-start | bytes 1572872 | tf_op jit(solution)/shard_map/ppermute | solution.py:385
  134.1 19.9 %collective-permute-start.26 = (bf16[128,2048]{1,0:T(8,128)(2,1)S(1)}, bf16[128,2048]{1,0:T(8,128)(2,1)S(1)}, u32[]{:S(2)}, u32[]{:S(2)}) collective-permute-start(bf16[128,2048]{1,0:T(8,128)(2,1)S(1)} %get-tuple-element.525), channel_id=1, source_target_pairs={{0,8},{8,16},{16,24},{1,9},{9,17},{17,25},{2,10},{10,18},{18,26},{... | collective-permute-start | bytes 1572872 | tf_op jit(solution)/shard_map/ppermute | solution.py:385
  145.4 19.9 %collective-permute-start.24 = (bf16[128,2048]{1,0:T(8,128)(2,1)S(1)}, bf16[128,2048]{1,0:T(8,128)(2,1)S(1)}, u32[]{:S(2)}, u32[]{:S(2)}) collective-permute-start(bf16[128,2048]{1,0:T(8,128)(2,1)S(1)} %get-tuple-element.527), channel_id=1, source_target_pairs={{0,8},{8,16},{16,24},{1,9},{9,17},{17,25},{2,10},{10,18},{18,26},{... | collective-permute-start | bytes 1572872 | tf_op jit(solution)/shard_map/ppermute | solution.py:385
  156.6 19.9 %collective-permute-start.30 = (bf16[128,2048]{1,0:T(8,128)(2,1)S(1)}, bf16[128,2048]{1,0:T(8,128)(2,1)S(1)}, u32[]{:S(2)}, u32[]{:S(2)}) collective-permute-start(bf16[128,2048]{1,0:T(8,128)(2,1)S(1)} %get-tuple-element.539), channel_id=1, source_target_pairs={{0,8},{8,16},{16,24},{1,9},{9,17},{17,25},{2,10},{10,18},{18,26},{... | collective-permute-start | bytes 1572872 | tf_op jit(solution)/shard_map/ppermute | solution.py:385
  167.8 19.9 %collective-permute-start.28 = (bf16[128,2048]{1,0:T(8,128)(2,1)S(1)}, bf16[128,2048]{1,0:T(8,128)(2,1)S(1)}, u32[]{:S(2)}, u32[]{:S(2)}) collective-permute-start(bf16[128,2048]{1,0:T(8,128)(2,1)S(1)} %get-tuple-element.541), channel_id=1, source_target_pairs={{0,8},{8,16},{16,24},{1,9},{9,17},{17,25},{2,10},{10,18},{18,26},{... | collective-permute-start | bytes 1572872 | tf_op jit(solution)/shard_map/ppermute | solution.py:385
  179.4 19.5 %collective-permute-start.34 = (bf16[128,2048]{1,0:T(8,128)(2,1)S(1)}, bf16[128,2048]{1,0:T(8,128)(2,1)S(1)}, u32[]{:S(2)}, u32[]{:S(2)}) collective-permute-start(bf16[128,2048]{1,0:T(8,128)(2,1)S(1)} %get-tuple-element.553), channel_id=1, source_target_pairs={{0,8},{8,16},{16,24},{1,9},{9,17},{17,25},{2,10},{10,18},{18,26},{... | collective-permute-start | bytes 1572872 | tf_op jit(solution)/shard_map/ppermute | solution.py:385
  190.6 19.5 %collective-permute-start.32 = (bf16[128,2048]{1,0:T(8,128)(2,1)S(1)}, bf16[128,2048]{1,0:T(8,128)(2,1)S(1)}, u32[]{:S(2)}, u32[]{:S(2)}) collective-permute-start(bf16[128,2048]{1,0:T(8,128)(2,1)S(1)} %get-tuple-element.555), channel_id=1, source_target_pairs={{0,8},{8,16},{16,24},{1,9},{9,17},{17,25},{2,10},{10,18},{18,26},{... | collective-permute-start | bytes 1572872 | tf_op jit(solution)/shard_map/ppermute | solution.py:385
  201.9 19.5 %collective-permute-start.38 = (bf16[128,2048]{1,0:T(8,128)(2,1)S(1)}, bf16[128,2048]{1,0:T(8,128)(2,1)S(1)}, u32[]{:S(2)}, u32[]{:S(2)}) collective-permute-start(bf16[128,2048]{1,0:T(8,128)(2,1)S(1)} %get-tuple-element.567), channel_id=1, source_target_pairs={{0,8},{8,16},{16,24},{1,9},{9,17},{17,25},{2,10},{10,18},{18,26},{... | collective-permute-start | bytes 1572872 | tf_op jit(solution)/shard_map/ppermute | solution.py:385
  213.1 19.5 %collective-permute-start.36 = (bf16[128,2048]{1,0:T(8,128)(2,1)S(1)}, bf16[128,2048]{1,0:T(8,128)(2,1)S(1)}, u32[]{:S(2)}, u32[]{:S(2)}) collective-permute-start(bf16[128,2048]{1,0:T(8,128)(2,1)S(1)} %get-tuple-element.569), channel_id=1, source_target_pairs={{0,8},{8,16},{16,24},{1,9},{9,17},{17,25},{2,10},{10,18},{18,26},{... | collective-permute-start | bytes 1572872 | tf_op jit(solution)/shard_map/ppermute | solution.py:385
  224.7 19.3 %collective-permute-start.42 = (bf16[128,2048]{1,0:T(8,128)(2,1)}, bf16[128,2048]{1,0:T(8,128)(2,1)S(1)}, u32[]{:S(2)}, u32[]{:S(2)}) collective-permute-start(bf16[128,2048]{1,0:T(8,128)(2,1)} %get-tuple-element.581), channel_id=1, source_target_pairs={{0,8},{8,16},{16,24},{1,9},{9,17},{17,25},{2,10},{10,18},{18,26},{... | collective-permute-start | bytes 1572872 | tf_op jit(solution)/shard_map/ppermute | solution.py:385
  235.9 21.1 %collective-permute-start.40 = (bf16[128,2048]{1,0:T(8,128)(2,1)}, bf16[128,2048]{1,0:T(8,128)(2,1)S(1)}, u32[]{:S(2)}, u32[]{:S(2)}) collective-permute-start(bf16[128,2048]{1,0:T(8,128)(2,1)} %get-tuple-element.583), channel_id=1, source_target_pairs={{0,8},{8,16},{16,24},{1,9},{9,17},{17,25},{2,10},{10,18},{18,26},{... | collective-permute-start | bytes 1572872 | tf_op jit(solution)/shard_map/ppermute | solution.py:385
  259.7 19.9 %collective-permute-start.46 = (bf16[128,2048]{1,0:T(8,128)(2,1)S(1)}, bf16[128,2048]{1,0:T(8,128)(2,1)S(1)}, u32[]{:S(2)}, u32[]{:S(2)}) collective-permute-start(bf16[128,2048]{1,0:T(8,128)(2,1)S(1)} %get-tuple-element.600), channel_id=1, source_target_pairs={{0,8},{8,16},{16,24},{1,9},{9,17},{17,25},{2,10},{10,18},{18,26},{... | collective-permute-start | bytes 1572872 | tf_op jit(solution)/shard_map/ppermute | solution.py:385
  264.0 19.5 %collective-permute-start.47 = (bf16[128,2048]{1,0:T(8,128)(2,1)S(1)}, bf16[128,2048]{1,0:T(8,128)(2,1)S(1)}, u32[]{:S(2)}, u32[]{:S(2)}) collective-permute-start(bf16[128,2048]{1,0:T(8,128)(2,1)S(1)} %get-tuple-element.601), channel_id=1, source_target_pairs={{24,16},{16,8},{8,0},{25,17},{17,9},{9,1},{26,18},{18,10},{10,2},{... | collective-permute-start | bytes 1572872 | tf_op jit(solution)/shard_map/ppermute | solution.py:386
  265.4 26.3 %collective-permute-start.55 = (f32[9216]{0:T(1024)S(1)}, f32[9216]{0:T(1024)S(1)}, u32[]{:S(2)}, u32[]{:S(2)}) collective-permute-start(f32[9216]{0:T(1024)S(1)} %pad_maximum_fusion), channel_id=1, source_target_pairs={{0,24},{24,0},{1,25},{25,1},{2,26},{26,2},{3,27},{27,3},{4,28},{28... | collective-permute-start | bytes 110600 | tf_op jit(solution)/shard_map/ppermute | solution.py:291
  275.8 22.6 %collective-permute-start.53 = (bf16[128,2048]{1,0:T(8,128)(2,1)}, bf16[128,2048]{1,0:T(8,128)(2,1)S(1)}, u32[]{:S(2)}, u32[]{:S(2)}) collective-permute-start(bf16[128,2048]{1,0:T(8,128)(2,1)} %get-tuple-element.615), channel_id=1, source_target_pairs={{0,8},{8,16},{16,24},{1,9},{9,17},{17,25},{2,10},{10,18},{18,26},{... | collective-permute-start | bytes 1572872 | tf_op jit(solution)/shard_map/ppermute | solution.py:385
  278.2 20.2 %collective-permute-start.54 = (bf16[128,2048]{1,0:T(8,128)(2,1)}, bf16[128,2048]{1,0:T(8,128)(2,1)S(1)}, u32[]{:S(2)}, u32[]{:S(2)}) collective-permute-start(bf16[128,2048]{1,0:T(8,128)(2,1)} %get-tuple-element.616), channel_id=1, source_target_pairs={{24,16},{16,8},{8,0},{25,17},{17,9},{9,1},{26,18},{18,10},{10,2},{... | collective-permute-start | bytes 1572872 | tf_op jit(solution)/shard_map/ppermute | solution.py:386
  286.6 23.7 %collective-permute-start.51 = (bf16[128,2048]{1,0:T(8,128)(2,1)}, bf16[128,2048]{1,0:T(8,128)(2,1)S(1)}, u32[]{:S(2)}, u32[]{:S(2)}) collective-permute-start(bf16[128,2048]{1,0:T(8,128)(2,1)} %get-tuple-element.617), channel_id=1, source_target_pairs={{0,8},{8,16},{16,24},{1,9},{9,17},{17,25},{2,10},{10,18},{18,26},{... | collective-permute-start | bytes 1572872 | tf_op jit(solution)/shard_map/ppermute | solution.py:385
  290.3 20.0 %collective-permute-start.52 = (bf16[128,2048]{1,0:T(8,128)(2,1)}, bf16[128,2048]{1,0:T(8,128)(2,1)S(1)}, u32[]{:S(2)}, u32[]{:S(2)}) collective-permute-start(bf16[128,2048]{1,0:T(8,128)(2,1)} %get-tuple-element.618), channel_id=1, source_target_pairs={{24,16},{16,8},{8,0},{25,17},{17,9},{9,1},{26,18},{18,10},{10,2},{... | collective-permute-start | bytes 1572872 | tf_op jit(solution)/shard_map/ppermute | solution.py:386
  301.0 18.8 %collective-permute-start.59 = (bf16[128,2048]{1,0:T(8,128)(2,1)S(1)}, bf16[128,2048]{1,0:T(8,128)(2,1)S(1)}, u32[]{:S(2)}, u32[]{:S(2)}) collective-permute-start(bf16[128,2048]{1,0:T(8,128)(2,1)S(1)} %get-tuple-element.633), channel_id=1, source_target_pairs={{0,8},{8,16},{16,24},{1,9},{9,17},{17,25},{2,10},{10,18},{18,26},{... | collective-permute-start | bytes 1572872 | tf_op jit(solution)/shard_map/ppermute | solution.py:385
  312.9 18.8 %collective-permute-start.57 = (bf16[128,2048]{1,0:T(8,128)(2,1)S(1)}, bf16[128,2048]{1,0:T(8,128)(2,1)S(1)}, u32[]{:S(2)}, u32[]{:S(2)}) collective-permute-start(bf16[128,2048]{1,0:T(8,128)(2,1)S(1)} %get-tuple-element.637), channel_id=1, source_target_pairs={{0,8},{8,16},{16,24},{1,9},{9,17},{17,25},{2,10},{10,18},{18,26},{... | collective-permute-start | bytes 1572872 | tf_op jit(solution)/shard_map/ppermute | solution.py:385
  322.4 21.7 %collective-permute-start.65 = (bf16[128,2048]{1,0:T(8,128)(2,1)S(1)}, bf16[128,2048]{1,0:T(8,128)(2,1)S(1)}, u32[]{:S(2)}, u32[]{:S(2)}) collective-permute-start(bf16[128,2048]{1,0:T(8,128)(2,1)S(1)} %get-tuple-element.651), channel_id=1, source_target_pairs={{0,8},{8,16},{16,24},{1,9},{9,17},{17,25},{2,10},{10,18},{18,26},{... | collective-permute-start | bytes 1572872 | tf_op jit(solution)/shard_map/ppermute | solution.py:385
  334.3 20.3 %collective-permute-start.63 = (bf16[128,2048]{1,0:T(8,128)(2,1)S(1)}, bf16[128,2048]{1,0:T(8,128)(2,1)S(1)}, u32[]{:S(2)}, u32[]{:S(2)}) collective-permute-start(bf16[128,2048]{1,0:T(8,128)(2,1)S(1)} %get-tuple-element.655), channel_id=1, source_target_pairs={{0,8},{8,16},{16,24},{1,9},{9,17},{17,25},{2,10},{10,18},{18,26},{... | collective-permute-start | bytes 1572872 | tf_op jit(solution)/shard_map/ppermute | solution.py:385
  348.1 18.7 %collective-permute-start.71 = (bf16[128,2048]{1,0:T(8,128)(2,1)S(1)}, bf16[128,2048]{1,0:T(8,128)(2,1)S(1)}, u32[]{:S(2)}, u32[]{:S(2)}) collective-permute-start(bf16[128,2048]{1,0:T(8,128)(2,1)S(1)} %get-tuple-element.668), channel_id=1, source_target_pairs={{24,16},{16,8},{8,0},{25,17},{17,9},{9,1},{26,18},{18,10},{10,2},{... | collective-permute-start | bytes 1572872 | tf_op jit(solution)/shard_map/ppermute | solution.py:386
  448.4 20.5 %collective-permute-start.87 = (bf16[128,2048]{1,0:T(8,128)(2,1)S(1)}, bf16[128,2048]{1,0:T(8,128)(2,1)S(1)}, u32[]{:S(2)}, u32[]{:S(2)}) collective-permute-start(bf16[128,2048]{1,0:T(8,128)(2,1)S(1)} %get-tuple-element.735), channel_id=1, source_target_pairs={{24,16},{16,8},{8,0},{25,17},{17,9},{9,1},{26,18},{18,10},{10,2},{... | collective-permute-start | bytes 1572872 | tf_op jit(solution)/shard_map/ppermute | solution.py:386
  449.8 25.6 %collective-permute-start.95 = (f32[6144]{0:T(1024)S(1)}, f32[6144]{0:T(1024)S(1)}, u32[]{:S(2)}, u32[]{:S(2)}) collective-permute-start(f32[6144]{0:T(1024)S(1)} %pad_maximum_fusion.1), channel_id=1, source_target_pairs={{0,24},{24,0},{1,25},{25,1},{2,26},{26,2},{3,27},{27,3},{4,28},{28... | collective-permute-start | bytes 73736 | tf_op jit(solution)/shard_map/ppermute | solution.py:291
  460.5 22.2 %collective-permute-start.93 = (bf16[128,2048]{1,0:T(8,128)(2,1)}, bf16[128,2048]{1,0:T(8,128)(2,1)S(1)}, u32[]{:S(2)}, u32[]{:S(2)}) collective-permute-start(bf16[128,2048]{1,0:T(8,128)(2,1)} %get-tuple-element.745), channel_id=1, source_target_pairs={{0,8},{8,16},{16,24},{1,9},{9,17},{17,25},{2,10},{10,18},{18,26},{... | collective-permute-start | bytes 1572872 | tf_op jit(solution)/shard_map/ppermute | solution.py:385
  462.5 20.2 %collective-permute-start.94 = (bf16[128,2048]{1,0:T(8,128)(2,1)}, bf16[128,2048]{1,0:T(8,128)(2,1)S(1)}, u32[]{:S(2)}, u32[]{:S(2)}) collective-permute-start(bf16[128,2048]{1,0:T(8,128)(2,1)} %get-tuple-element.746), channel_id=1, source_target_pairs={{24,16},{16,8},{8,0},{25,17},{17,9},{9,1},{26,18},{18,10},{10,2},{... | collective-permute-start | bytes 1572872 | tf_op jit(solution)/shard_map/ppermute | solution.py:386
  472.2 22.2 %collective-permute-start.91 = (bf16[128,2048]{1,0:T(8,128)(2,1)}, bf16[128,2048]{1,0:T(8,128)(2,1)S(1)}, u32[]{:S(2)}, u32[]{:S(2)}) collective-permute-start(bf16[128,2048]{1,0:T(8,128)(2,1)} %get-tuple-element.747), channel_id=1, source_target_pairs={{0,8},{8,16},{16,24},{1,9},{9,17},{17,25},{2,10},{10,18},{18,26},{... | collective-permute-start | bytes 1572872 | tf_op jit(solution)/shard_map/ppermute | solution.py:385
  474.1 20.3 %collective-permute-start.92 = (bf16[128,2048]{1,0:T(8,128)(2,1)S(1)}, bf16[128,2048]{1,0:T(8,128)(2,1)S(1)}, u32[]{:S(2)}, u32[]{:S(2)}) collective-permute-start(bf16[128,2048]{1,0:T(8,128)(2,1)S(1)} %get-tuple-element.748), channel_id=1, source_target_pairs={{24,16},{16,8},{8,0},{25,17},{17,9},{9,1},{26,18},{18,10},{10,2},{... | collective-permute-start | bytes 1572872 | tf_op jit(solution)/shard_map/ppermute | solution.py:386
  484.9 18.7 %collective-permute-start.99 = (bf16[128,2048]{1,0:T(8,128)(2,1)S(1)}, bf16[128,2048]{1,0:T(8,128)(2,1)S(1)}, u32[]{:S(2)}, u32[]{:S(2)}) collective-permute-start(bf16[128,2048]{1,0:T(8,128)(2,1)S(1)} %get-tuple-element.759), channel_id=1, source_target_pairs={{0,8},{8,16},{16,24},{1,9},{9,17},{17,25},{2,10},{10,18},{18,26},{... | collective-permute-start | bytes 1572872 | tf_op jit(solution)/shard_map/ppermute | solution.py:385
  529.0 21.1 %collective-permute-start.109 = (bf16[128,2048]{1,0:T(8,128)(2,1)S(1)}, bf16[128,2048]{1,0:T(8,128)(2,1)S(1)}, u32[]{:S(2)}, u32[]{:S(2)}) collective-permute-start(bf16[128,2048]{1,0:T(8,128)(2,1)S(1)} %get-tuple-element.785), channel_id=1, source_target_pairs={{0,8},{8,16},{16,24},{1,9},{9,17},{17,25},{2,10},{10,18},{18,26},{... | collective-permute-start | bytes 1572872 | tf_op jit(solution)/shard_map/ppermute | solution.py:385
  531.0 19.2 %collective-permute-start.110 = (bf16[128,2048]{1,0:T(8,128)(2,1)S(1)}, bf16[128,2048]{1,0:T(8,128)(2,1)S(1)}, u32[]{:S(2)}, u32[]{:S(2)}) collective-permute-start(bf16[128,2048]{1,0:T(8,128)(2,1)S(1)} %get-tuple-element.786), channel_id=1, source_target_pairs={{24,16},{16,8},{8,0},{25,17},{17,9},{9,1},{26,18},{18,10},{10,2},{... | collective-permute-start | bytes 1572872 | tf_op jit(solution)/shard_map/ppermute | solution.py:386
  720.7 25.7 %collective-permute-start.146 = (bf16[128,2048]{1,0:T(8,128)(2,1)S(1)}, bf16[128,2048]{1,0:T(8,128)(2,1)S(1)}, u32[]{:S(2)}, u32[]{:S(2)}) collective-permute-start(bf16[128,2048]{1,0:T(8,128)(2,1)S(1)} %get-tuple-element.879), channel_id=1, source_target_pairs={{0,8},{8,16},{16,24},{1,9},{9,17},{17,25},{2,10},{10,18},{18,26},{... | collective-permute-start | bytes 1572872 | tf_op jit(solution)/shard_map/ppermute | solution.py:385
  723.1 23.4 %collective-permute-start.147 = (bf16[128,2048]{1,0:T(8,128)(2,1)S(1)}, bf16[128,2048]{1,0:T(8,128)(2,1)S(1)}, u32[]{:S(2)}, u32[]{:S(2)}) collective-permute-start(bf16[128,2048]{1,0:T(8,128)(2,1)S(1)} %get-tuple-element.880), channel_id=1, source_target_pairs={{24,16},{16,8},{8,0},{25,17},{17,9},{9,1},{26,18},{18,10},{10,2},{... | collective-permute-start | bytes 1572872 | tf_op jit(solution)/shard_map/ppermute | solution.py:386
  730.6 18.7 %collective-permute-start.144 = (bf16[128,2048]{1,0:T(8,128)(2,1)S(1)}, bf16[128,2048]{1,0:T(8,128)(2,1)S(1)}, u32[]{:S(2)}, u32[]{:S(2)}) collective-permute-start(bf16[128,2048]{1,0:T(8,128)(2,1)S(1)} %get-tuple-element.881), channel_id=1, source_target_pairs={{8,16},{16,24},{9,17},{17,25},{10,18},{18,26},{11,19},{19,27},{12,... | collective-permute-start | bytes 1572872 | tf_op jit(solution)/shard_map/ppermute | solution.py:385
  731.3 20.9 %collective-permute-start.145 = (bf16[128,2048]{1,0:T(8,128)(2,1)S(1)}, bf16[128,2048]{1,0:T(8,128)(2,1)S(1)}, u32[]{:S(2)}, u32[]{:S(2)}) collective-permute-start(bf16[128,2048]{1,0:T(8,128)(2,1)S(1)} %get-tuple-element.882), channel_id=1, source_target_pairs={{16,8},{8,0},{17,9},{9,1},{18,10},{10,2},{19,11},{11,3},{20,12},{1... | collective-permute-start | bytes 1572872 | tf_op jit(solution)/shard_map/ppermute | solution.py:386
  755.0 21.0 %collective-permute-start.153 = (bf16[128,2048]{1,0:T(8,128)(2,1)S(1)}, bf16[128,2048]{1,0:T(8,128)(2,1)S(1)}, u32[]{:S(2)}, u32[]{:S(2)}) collective-permute-start(bf16[128,2048]{1,0:T(8,128)(2,1)S(1)} %get-tuple-element.894), channel_id=1, source_target_pairs={{8,0},{9,1},{10,2},{11,3},{12,4},{13,5},{14,6},{15,7}} | collective-permute-start | bytes 1572872 | tf_op jit(solution)/shard_map/ppermute | solution.py:386
  (125 other events, 1704.7 us)

commit v8 on v7

--- a/solution.py
+++ b/solution.py
@@ -14,6 +14,7 @@
 GROUPS = 4
 FAR = 2
 LANES = 128
+PIECE = 16384
 VMEM_BYTES = 48 * 1024 * 1024
 
 F32 = jnp.float32
@@ -44,10 +45,16 @@
     numbers = [plan["step"] - LAG * place, plan["step"] - LAG * (last - place)]
     positions = [place, last - place]
 
-    def pieces(size, q, width):
-        for j in range(q):
-            for lane in range(0, width, LANES):
-                yield pl.ds(j * size, size), pl.ds(lane, LANES), pl.ds(j * width + lane, LANES)
+    def each_piece(size, q, width, body, carry=0):
+        step = min(width, max(LANES, PIECE // size // LANES * LANES))
+        across = width // step
+
+        def turn(t, carry):
+            at = pl.ds(pl.multiple_of(t // across * size, 16), size)
+            lanes = pl.ds(pl.multiple_of(t % across * step, LANES), step)
+            return body(at, lanes, pl.ds(pl.multiple_of(t * step, LANES), step), carry)
+
+        return lax.fori_loop(0, q * across, turn, carry)
 
     for part, ins, outs in zip(plan["parts"], taken, given):
         size, q, width, begin = part["size"], part["q"], part["width"], part["begin"]
@@ -58,11 +65,14 @@
 
                 @pl.when(valids[d])
                 def _():
-                    for at, lanes, full in pieces(size, q, width):
+                    def add(at, lanes, full, carry):
                         value = ins[d][:, full]
                         if plan["with_got"]:
                             value = (gots[d][at, lanes].astype(F32) + value.astype(F32)).astype(BF16)
                         sends[d][at, lanes] = value
+                        return carry
+
+                    each_piece(size, q, width, add)
 
             if part["chunk"] is not None:
                 total_ref, row_ref, col_ref = outs
@@ -70,20 +80,24 @@
 
                     @pl.when(place == end)
                     def _():
-                        row_part = jnp.zeros((size, LANES), F32)
-                        for at, lanes, full in pieces(size, q, width):
+                        def measure(at, lanes, full, row_part):
                             total = sends[d][at, lanes]
                             total_ref[:, full] = total
                             wide = total.astype(F32)
                             square = wide * wide + EPS_SQUARE
-                            row_part = row_part + square
+                            for lane in range(0, square.shape[1], LANES):
+                                row_part = row_part + square[:, lane : lane + LANES]
                             col_part = square[0:8]
                             for r in range(8, size, 8):
                                 col_part = col_part + square[r : r + 8]
                             if not part["first"]:
                                 col_part = col_part + ins[-1][:, full]
                             col_ref[:, full] = col_part
-                        row_ref[...] = row_part
+                            return row_part
+
+                        row_ref[...] = each_piece(
+                            size, q, width, measure, jnp.zeros((size, LANES), F32)
+                        )
 
         else:
             out_ref = outs[0]
@@ -102,10 +116,14 @@
 
                     @pl.when(valids[d] & (positions[d] == 0))
                     def _():
-                        for at, lanes, full in pieces(size, q, width):
+                        def scale(at, lanes, full, carry):
                             wide = total_ref[:, full].astype(F32)
-                            update = wide * row_ref[...] * col_ref[0:1, full]
+                            rows = jnp.concatenate([row_ref[...]] * (wide.shape[1] // LANES), axis=1)
+                            update = wide * rows * col_ref[0:1, full]
                             sends[d][at, lanes] = update.astype(BF16)
+                            return carry
+
+                        each_piece(size, q, width, scale)
                         for j in range(q):
                             keep(sends[d], d, j).start()
 
@@ -116,8 +134,11 @@
                         for j in range(q):
                             keep(gots[d], d, j).start()
                         if plan["sending"]:
-                            for at, lanes, _ in pieces(size, q, width):
+                            def forward(at, lanes, full, carry):
                                 sends[d][at, lanes] = gots[d][at, lanes]
+                                return carry
+
+                            each_piece(size, q, width, forward)
 
             for d in range(2):
 

time: 800 us -> 795 us (level); the launches traced: 786 us -> 789 us
  Pallas kernels: 170 us -> 193 us
  waiting for transfers between devices: 263 us -> 244 us
    pallas_call x70, Pallas kernels: 170 us -> 193 us  [run_step(): pl.pallas_call(functools.partial(step_kernel, plan), grid_spec=pltpu.Pref...]
    ppermute x68, waiting for transfers between devices: 90.5 us -> 79.1 us  [local(): lax.ppermute(tied[0], 'dp', [(p, p + 1) for p in going])]
  transfers between devices with their start and end apart: 154 -> 154, of which waited for: 87 -> 80; matrix products, arithmetic and copies ran while one was open for 2% -> 2% of each run, Pallas kernels for 21% -> 24%
where the time goes in v8:
time: 795 us; the launch traced here: 789 us
  starting transfers between devices  328 us (41%)
  waiting for transfers between devices  244 us (31%)
  Pallas kernels  193 us (24%)
  other arithmetic  11.9 us (1%)
  between operations  9.81 us (1%)
    ppermute x68, starting transfers between devices, local(): lax.ppermute(tied[0], 'dp', [(p, p + 1) for p in going])  200 us
    pallas_call x70, Pallas kernels, run_step(): pl.pallas_call(functools.partial(step_kernel, plan), grid_spec=pltpu.Pref...  193 us
    ppermute x68, waiting for transfers between devices, local(): lax.ppermute(tied[1], 'dp', [(last - p, last - p - 1) for p in going])  142 us
    ppermute x68, starting transfers between devices, local(): lax.ppermute(tied[1], 'dp', [(last - p, last - p - 1) for p in going])  85.7 us
    ppermute x68, waiting for transfers between devices, local(): lax.ppermute(tied[0], 'dp', [(p, p + 1) for p in going])  79.1 us
  transfers between devices with their start and end apart: 154, of which 80 were waited for; matrix products, arithmetic and copies ran while one was open for 2% of the time, Pallas kernels for 24%

profile of v8, /device:TPU:0, one launch (start us, length us, event | category | flops | bytes accessed | tf_op | source)
XLA Modules:
  0.0 789.3 jit_solution(6139234744130561183)
XLA Ops:
  2.1 4.8 collective-permute-start.2
  11.1 8.1 %collective-permute-done.2.refs_0_ = bf16[128,2048]{1,0:T(8,128)(2,1)S(1)} collective-permute-done((bf16[128,2048]{1,0:T(8,128)(2,1)S(1)}, bf16[128,2048]{1,0:T(8,128)(2,1)S(1)}, u32[]{:S(2)}, u32[]{:S(2)}) %collective-permute-start.2) | collective-permute-done | bytes 524320 | tf_op jit(solution)/shard_map/ppermute | solution.py:406
  20.7 4.4 collective-permute-start.6
  25.9 4.6 collective-permute-done.refs_0_
  32.0 4.4 collective-permute-start.4
  37.1 4.6 collective-permute-done.6.refs_0_
  43.2 4.7 collective-permute-start.10
  54.4 4.7 collective-permute-start.8
  225.2 4.2 collective-permute-start.42
  266.0 5.3 collective-permute-start.55
  343.0 5.1 collective-permute-start.67
  365.2 4.4 collective-permute-done.71.refs_1_
  369.6 4.3 line_step.102
  376.5 4.3 collective-permute-done.69.refs_1_
  380.8 4.2 line_step.103
  387.7 4.4 collective-permute-done.75.refs_1_
  392.1 4.2 line_step.104
  398.9 4.4 collective-permute-done.73.refs_1_
  403.3 4.2 line_step.105
  414.5 4.5 line_step.106
  426.3 4.6 line_step.107
  452.2 5.5 collective-permute-start.95
  488.7 4.3 collective-permute-start.99
  500.4 4.6 collective-permute-start.97
  509.8 4.3 collective-permute-start.105
  521.5 4.3 collective-permute-start.103
  547.9 5.8 collective-permute-done.111
  560.9 4.2 collective-permute-done.108.refs_1_
  572.0 4.4 collective-permute-done.115.refs_1_
  583.2 4.4 collective-permute-done.113.refs_1_
  594.4 4.4 collective-permute-done.119.refs_1_
  605.7 4.4 collective-permute-done.117.refs_1_
  616.9 4.4 collective-permute-done.121.refs_1_
  628.1 4.4 collective-permute-done.125.refs_1_
  639.4 4.4 collective-permute-done.123.refs_1_
  650.6 4.4 collective-permute-done.129.refs_1_
  661.8 4.4 collective-permute-done.127.refs_1_
  673.1 4.4 collective-permute-done.133.refs_1_
  684.3 4.4 collective-permute-done.131.refs_1_
  695.5 4.4 collective-permute-done.137.refs_1_
  706.8 4.4 collective-permute-done.135.refs_1_
  718.0 4.4 collective-permute-done.142.refs_1_
  729.3 4.4 collective-permute-done.140.refs_1_
  736.5 5.9 collective-permute-start.138
  744.2 6.2 collective-permute-start.143
  761.5 7.3 collective-permute-done.149.refs_1_
  771.6 8.4 %collective-permute-done.153.refs_1_ = bf16[128,2048]{1,0:T(8,128)(2,1)S(1)} collective-permute-done((bf16[128,2048]{1,0:T(8,128)(2,1)S(1)}, bf16[128,2048]{1,0:T(8,128)(2,1)S(1)}, u32[]{:S(2)}, u32[]{:S(2)}) %collective-permute-start.153) | collective-permute-done | bytes 524320 | tf_op jit(solution)/shard_map/ppermute | solution.py:407
  780.8 7.5 collective-permute-done.151.refs_1_
  (421 shorter events, 546.6 us)
Async XLA Ops:
  9.1 21.3 %collective-permute-start = (bf16[128,2048]{1,0:T(8,128)(2,1)S(1)}, bf16[128,2048]{1,0:T(8,128)(2,1)S(1)}, u32[]{:S(2)}, u32[]{:S(2)}) collective-permute-start(bf16[128,2048]{1,0:T(8,128)(2,1)S(1)} %get-tuple-element.458), channel_id=1, source_target_pairs={{0,8},{1,9},{2,10},{3,11},{4,12},{5,13},{6,14},{7,15}} | collective-permute-start | bytes 1572872 | tf_op jit(solution)/shard_map/ppermute | solution.py:406
  10.4 20.0 %collective-permute-start.1 = (bf16[128,2048]{1,0:T(8,128)(2,1)S(1)}, bf16[128,2048]{1,0:T(8,128)(2,1)S(1)}, u32[]{:S(2)}, u32[]{:S(2)}) collective-permute-start(bf16[128,2048]{1,0:T(8,128)(2,1)S(1)} %get-tuple-element.459), channel_id=1, source_target_pairs={{24,16},{25,17},{26,18},{27,19},{28,20},{29,21},{30,22},{31,23}} | collective-permute-start | bytes 1572872 | tf_op jit(solution)/shard_map/ppermute | solution.py:407
  20.7 20.9 %collective-permute-start.6 = (bf16[128,2048]{1,0:T(8,128)(2,1)S(1)}, bf16[128,2048]{1,0:T(8,128)(2,1)S(1)}, u32[]{:S(2)}, u32[]{:S(2)}) collective-permute-start(bf16[128,2048]{1,0:T(8,128)(2,1)S(1)} %get-tuple-element.464), channel_id=1, source_target_pairs={{0,8},{8,16},{1,9},{9,17},{2,10},{10,18},{3,11},{11,19},{4,12},{12... | collective-permute-start | bytes 1572872 | tf_op jit(solution)/shard_map/ppermute | solution.py:406
  32.0 20.9 %collective-permute-start.4 = (bf16[128,2048]{1,0:T(8,128)(2,1)S(1)}, bf16[128,2048]{1,0:T(8,128)(2,1)S(1)}, u32[]{:S(2)}, u32[]{:S(2)}) collective-permute-start(bf16[128,2048]{1,0:T(8,128)(2,1)S(1)} %get-tuple-element.466), channel_id=1, source_target_pairs={{0,8},{8,16},{1,9},{9,17},{2,10},{10,18},{3,11},{11,19},{4,12},{12... | collective-permute-start | bytes 1572872 | tf_op jit(solution)/shard_map/ppermute | solution.py:406
  43.2 20.9 %collective-permute-start.10 = (bf16[128,2048]{1,0:T(8,128)(2,1)S(1)}, bf16[128,2048]{1,0:T(8,128)(2,1)S(1)}, u32[]{:S(2)}, u32[]{:S(2)}) collective-permute-start(bf16[128,2048]{1,0:T(8,128)(2,1)S(1)} %get-tuple-element.472), channel_id=1, source_target_pairs={{0,8},{8,16},{16,24},{1,9},{9,17},{17,25},{2,10},{10,18},{18,26},{... | collective-permute-start | bytes 1572872 | tf_op jit(solution)/shard_map/ppermute | solution.py:406
  54.4 20.9 %collective-permute-start.8 = (bf16[128,2048]{1,0:T(8,128)(2,1)S(1)}, bf16[128,2048]{1,0:T(8,128)(2,1)S(1)}, u32[]{:S(2)}, u32[]{:S(2)}) collective-permute-start(bf16[128,2048]{1,0:T(8,128)(2,1)S(1)} %get-tuple-element.474), channel_id=1, source_target_pairs={{0,8},{8,16},{16,24},{1,9},{9,17},{17,25},{2,10},{10,18},{18,26},{... | collective-permute-start | bytes 1572872 | tf_op jit(solution)/shard_map/ppermute | solution.py:406
  67.1 19.5 %collective-permute-start.14 = (bf16[128,2048]{1,0:T(8,128)(2,1)S(1)}, bf16[128,2048]{1,0:T(8,128)(2,1)S(1)}, u32[]{:S(2)}, u32[]{:S(2)}) collective-permute-start(bf16[128,2048]{1,0:T(8,128)(2,1)S(1)} %get-tuple-element.483), channel_id=1, source_target_pairs={{0,8},{8,16},{16,24},{1,9},{9,17},{17,25},{2,10},{10,18},{18,26},{... | collective-permute-start | bytes 1572872 | tf_op jit(solution)/shard_map/ppermute | solution.py:406
  78.3 19.5 %collective-permute-start.12 = (bf16[128,2048]{1,0:T(8,128)(2,1)S(1)}, bf16[128,2048]{1,0:T(8,128)(2,1)S(1)}, u32[]{:S(2)}, u32[]{:S(2)}) collective-permute-start(bf16[128,2048]{1,0:T(8,128)(2,1)S(1)} %get-tuple-element.485), channel_id=1, source_target_pairs={{0,8},{8,16},{16,24},{1,9},{9,17},{17,25},{2,10},{10,18},{18,26},{... | collective-permute-start | bytes 1572872 | tf_op jit(solution)/shard_map/ppermute | solution.py:406
  89.6 19.5 %collective-permute-start.18 = (bf16[128,2048]{1,0:T(8,128)(2,1)S(1)}, bf16[128,2048]{1,0:T(8,128)(2,1)S(1)}, u32[]{:S(2)}, u32[]{:S(2)}) collective-permute-start(bf16[128,2048]{1,0:T(8,128)(2,1)S(1)} %get-tuple-element.497), channel_id=1, source_target_pairs={{0,8},{8,16},{16,24},{1,9},{9,17},{17,25},{2,10},{10,18},{18,26},{... | collective-permute-start | bytes 1572872 | tf_op jit(solution)/shard_map/ppermute | solution.py:406
  100.8 19.5 %collective-permute-start.16 = (bf16[128,2048]{1,0:T(8,128)(2,1)S(1)}, bf16[128,2048]{1,0:T(8,128)(2,1)S(1)}, u32[]{:S(2)}, u32[]{:S(2)}) collective-permute-start(bf16[128,2048]{1,0:T(8,128)(2,1)S(1)} %get-tuple-element.499), channel_id=1, source_target_pairs={{0,8},{8,16},{16,24},{1,9},{9,17},{17,25},{2,10},{10,18},{18,26},{... | collective-permute-start | bytes 1572872 | tf_op jit(solution)/shard_map/ppermute | solution.py:406
  112.1 19.5 %collective-permute-start.22 = (bf16[128,2048]{1,0:T(8,128)(2,1)S(1)}, bf16[128,2048]{1,0:T(8,128)(2,1)S(1)}, u32[]{:S(2)}, u32[]{:S(2)}) collective-permute-start(bf16[128,2048]{1,0:T(8,128)(2,1)S(1)} %get-tuple-element.511), channel_id=1, source_target_pairs={{0,8},{8,16},{16,24},{1,9},{9,17},{17,25},{2,10},{10,18},{18,26},{... | collective-permute-start | bytes 1572872 | tf_op jit(solution)/shard_map/ppermute | solution.py:406
  123.3 19.5 %collective-permute-start.20 = (bf16[128,2048]{1,0:T(8,128)(2,1)S(1)}, bf16[128,2048]{1,0:T(8,128)(2,1)S(1)}, u32[]{:S(2)}, u32[]{:S(2)}) collective-permute-start(bf16[128,2048]{1,0:T(8,128)(2,1)S(1)} %get-tuple-element.513), channel_id=1, source_target_pairs={{0,8},{8,16},{16,24},{1,9},{9,17},{17,25},{2,10},{10,18},{18,26},{... | collective-permute-start | bytes 1572872 | tf_op jit(solution)/shard_map/ppermute | solution.py:406
  134.5 19.5 %collective-permute-start.26 = (bf16[128,2048]{1,0:T(8,128)(2,1)S(1)}, bf16[128,2048]{1,0:T(8,128)(2,1)S(1)}, u32[]{:S(2)}, u32[]{:S(2)}) collective-permute-start(bf16[128,2048]{1,0:T(8,128)(2,1)S(1)} %get-tuple-element.525), channel_id=1, source_target_pairs={{0,8},{8,16},{16,24},{1,9},{9,17},{17,25},{2,10},{10,18},{18,26},{... | collective-permute-start | bytes 1572872 | tf_op jit(solution)/shard_map/ppermute | solution.py:406
  145.8 19.5 %collective-permute-start.24 = (bf16[128,2048]{1,0:T(8,128)(2,1)S(1)}, bf16[128,2048]{1,0:T(8,128)(2,1)S(1)}, u32[]{:S(2)}, u32[]{:S(2)}) collective-permute-start(bf16[128,2048]{1,0:T(8,128)(2,1)S(1)} %get-tuple-element.527), channel_id=1, source_target_pairs={{0,8},{8,16},{16,24},{1,9},{9,17},{17,25},{2,10},{10,18},{18,26},{... | collective-permute-start | bytes 1572872 | tf_op jit(solution)/shard_map/ppermute | solution.py:406
  157.0 19.5 %collective-permute-start.30 = (bf16[128,2048]{1,0:T(8,128)(2,1)S(1)}, bf16[128,2048]{1,0:T(8,128)(2,1)S(1)}, u32[]{:S(2)}, u32[]{:S(2)}) collective-permute-start(bf16[128,2048]{1,0:T(8,128)(2,1)S(1)} %get-tuple-element.539), channel_id=1, source_target_pairs={{0,8},{8,16},{16,24},{1,9},{9,17},{17,25},{2,10},{10,18},{18,26},{... | collective-permute-start | bytes 1572872 | tf_op jit(solution)/shard_map/ppermute | solution.py:406
  168.2 19.5 %collective-permute-start.28 = (bf16[128,2048]{1,0:T(8,128)(2,1)S(1)}, bf16[128,2048]{1,0:T(8,128)(2,1)S(1)}, u32[]{:S(2)}, u32[]{:S(2)}) collective-permute-start(bf16[128,2048]{1,0:T(8,128)(2,1)S(1)} %get-tuple-element.541), channel_id=1, source_target_pairs={{0,8},{8,16},{16,24},{1,9},{9,17},{17,25},{2,10},{10,18},{18,26},{... | collective-permute-start | bytes 1572872 | tf_op jit(solution)/shard_map/ppermute | solution.py:406
  179.9 19.0 %collective-permute-start.34 = (bf16[128,2048]{1,0:T(8,128)(2,1)S(1)}, bf16[128,2048]{1,0:T(8,128)(2,1)S(1)}, u32[]{:S(2)}, u32[]{:S(2)}) collective-permute-start(bf16[128,2048]{1,0:T(8,128)(2,1)S(1)} %get-tuple-element.553), channel_id=1, source_target_pairs={{0,8},{8,16},{16,24},{1,9},{9,17},{17,25},{2,10},{10,18},{18,26},{... | collective-permute-start | bytes 1572872 | tf_op jit(solution)/shard_map/ppermute | solution.py:406
  191.2 19.0 %collective-permute-start.32 = (bf16[128,2048]{1,0:T(8,128)(2,1)S(1)}, bf16[128,2048]{1,0:T(8,128)(2,1)S(1)}, u32[]{:S(2)}, u32[]{:S(2)}) collective-permute-start(bf16[128,2048]{1,0:T(8,128)(2,1)S(1)} %get-tuple-element.555), channel_id=1, source_target_pairs={{0,8},{8,16},{16,24},{1,9},{9,17},{17,25},{2,10},{10,18},{18,26},{... | collective-permute-start | bytes 1572872 | tf_op jit(solution)/shard_map/ppermute | solution.py:406
  202.4 19.0 %collective-permute-start.38 = (bf16[128,2048]{1,0:T(8,128)(2,1)S(1)}, bf16[128,2048]{1,0:T(8,128)(2,1)S(1)}, u32[]{:S(2)}, u32[]{:S(2)}) collective-permute-start(bf16[128,2048]{1,0:T(8,128)(2,1)S(1)} %get-tuple-element.567), channel_id=1, source_target_pairs={{0,8},{8,16},{16,24},{1,9},{9,17},{17,25},{2,10},{10,18},{18,26},{... | collective-permute-start | bytes 1572872 | tf_op jit(solution)/shard_map/ppermute | solution.py:406
  213.6 19.0 %collective-permute-start.36 = (bf16[128,2048]{1,0:T(8,128)(2,1)S(1)}, bf16[128,2048]{1,0:T(8,128)(2,1)S(1)}, u32[]{:S(2)}, u32[]{:S(2)}) collective-permute-start(bf16[128,2048]{1,0:T(8,128)(2,1)S(1)} %get-tuple-element.569), channel_id=1, source_target_pairs={{0,8},{8,16},{16,24},{1,9},{9,17},{17,25},{2,10},{10,18},{18,26},{... | collective-permute-start | bytes 1572872 | tf_op jit(solution)/shard_map/ppermute | solution.py:406
  225.2 18.8 %collective-permute-start.42 = (bf16[128,2048]{1,0:T(8,128)(2,1)}, bf16[128,2048]{1,0:T(8,128)(2,1)S(1)}, u32[]{:S(2)}, u32[]{:S(2)}) collective-permute-start(bf16[128,2048]{1,0:T(8,128)(2,1)} %get-tuple-element.581), channel_id=1, source_target_pairs={{0,8},{8,16},{16,24},{1,9},{9,17},{17,25},{2,10},{10,18},{18,26},{... | collective-permute-start | bytes 1572872 | tf_op jit(solution)/shard_map/ppermute | solution.py:406
  236.5 20.8 %collective-permute-start.40 = (bf16[128,2048]{1,0:T(8,128)(2,1)}, bf16[128,2048]{1,0:T(8,128)(2,1)S(1)}, u32[]{:S(2)}, u32[]{:S(2)}) collective-permute-start(bf16[128,2048]{1,0:T(8,128)(2,1)} %get-tuple-element.583), channel_id=1, source_target_pairs={{0,8},{8,16},{16,24},{1,9},{9,17},{17,25},{2,10},{10,18},{18,26},{... | collective-permute-start | bytes 1572872 | tf_op jit(solution)/shard_map/ppermute | solution.py:406
  252.1 19.2 %collective-permute-start.48 = (bf16[128,2048]{1,0:T(8,128)(2,1)}, bf16[128,2048]{1,0:T(8,128)(2,1)S(1)}, u32[]{:S(2)}, u32[]{:S(2)}) collective-permute-start(bf16[128,2048]{1,0:T(8,128)(2,1)} %copy-done.1), channel_id=1, source_target_pairs={{0,8},{8,16},{16,24},{1,9},{9,17},{17,25},{2,10},{10,18},{18,26},{... | collective-permute-start | bytes 1572872 | tf_op jit(solution)/shard_map/ppermute | solution.py:406
  260.6 19.7 %collective-permute-start.46 = (bf16[128,2048]{1,0:T(8,128)(2,1)S(1)}, bf16[128,2048]{1,0:T(8,128)(2,1)S(1)}, u32[]{:S(2)}, u32[]{:S(2)}) collective-permute-start(bf16[128,2048]{1,0:T(8,128)(2,1)S(1)} %get-tuple-element.600), channel_id=1, source_target_pairs={{0,8},{8,16},{16,24},{1,9},{9,17},{17,25},{2,10},{10,18},{18,26},{... | collective-permute-start | bytes 1572872 | tf_op jit(solution)/shard_map/ppermute | solution.py:406
  266.0 26.5 %collective-permute-start.55 = (f32[9216]{0:T(1024)S(1)}, f32[9216]{0:T(1024)S(1)}, u32[]{:S(2)}, u32[]{:S(2)}) collective-permute-start(f32[9216]{0:T(1024)S(1)} %pad_maximum_fusion), channel_id=1, source_target_pairs={{0,24},{24,0},{1,25},{25,1},{2,26},{26,2},{3,27},{27,3},{4,28},{28... | collective-permute-start | bytes 110600 | tf_op jit(solution)/shard_map/ppermute | solution.py:312
  276.7 22.6 %collective-permute-start.53 = (bf16[128,2048]{1,0:T(8,128)(2,1)}, bf16[128,2048]{1,0:T(8,128)(2,1)S(1)}, u32[]{:S(2)}, u32[]{:S(2)}) collective-permute-start(bf16[128,2048]{1,0:T(8,128)(2,1)} %get-tuple-element.615), channel_id=1, source_target_pairs={{0,8},{8,16},{16,24},{1,9},{9,17},{17,25},{2,10},{10,18},{18,26},{... | collective-permute-start | bytes 1572872 | tf_op jit(solution)/shard_map/ppermute | solution.py:406
  279.0 20.4 %collective-permute-start.54 = (bf16[128,2048]{1,0:T(8,128)(2,1)}, bf16[128,2048]{1,0:T(8,128)(2,1)S(1)}, u32[]{:S(2)}, u32[]{:S(2)}) collective-permute-start(bf16[128,2048]{1,0:T(8,128)(2,1)} %get-tuple-element.616), channel_id=1, source_target_pairs={{24,16},{16,8},{8,0},{25,17},{17,9},{9,1},{26,18},{18,10},{10,2},{... | collective-permute-start | bytes 1572872 | tf_op jit(solution)/shard_map/ppermute | solution.py:407
  287.0 24.8 %collective-permute-start.51 = (bf16[128,2048]{1,0:T(8,128)(2,1)}, bf16[128,2048]{1,0:T(8,128)(2,1)S(1)}, u32[]{:S(2)}, u32[]{:S(2)}) collective-permute-start(bf16[128,2048]{1,0:T(8,128)(2,1)} %get-tuple-element.617), channel_id=1, source_target_pairs={{0,8},{8,16},{16,24},{1,9},{9,17},{17,25},{2,10},{10,18},{18,26},{... | collective-permute-start | bytes 1572872 | tf_op jit(solution)/shard_map/ppermute | solution.py:406
  291.0 20.8 %collective-permute-start.52 = (bf16[128,2048]{1,0:T(8,128)(2,1)}, bf16[128,2048]{1,0:T(8,128)(2,1)S(1)}, u32[]{:S(2)}, u32[]{:S(2)}) collective-permute-start(bf16[128,2048]{1,0:T(8,128)(2,1)} %get-tuple-element.618), channel_id=1, source_target_pairs={{24,16},{16,8},{8,0},{25,17},{17,9},{9,1},{26,18},{18,10},{10,2},{... | collective-permute-start | bytes 1572872 | tf_op jit(solution)/shard_map/ppermute | solution.py:407
  302.7 19.1 %collective-permute-start.59 = (bf16[128,2048]{1,0:T(8,128)(2,1)S(1)}, bf16[128,2048]{1,0:T(8,128)(2,1)S(1)}, u32[]{:S(2)}, u32[]{:S(2)}) collective-permute-start(bf16[128,2048]{1,0:T(8,128)(2,1)S(1)} %get-tuple-element.633), channel_id=1, source_target_pairs={{0,8},{8,16},{16,24},{1,9},{9,17},{17,25},{2,10},{10,18},{18,26},{... | collective-permute-start | bytes 1572872 | tf_op jit(solution)/shard_map/ppermute | solution.py:406
  315.2 19.1 %collective-permute-start.57 = (bf16[128,2048]{1,0:T(8,128)(2,1)S(1)}, bf16[128,2048]{1,0:T(8,128)(2,1)S(1)}, u32[]{:S(2)}, u32[]{:S(2)}) collective-permute-start(bf16[128,2048]{1,0:T(8,128)(2,1)S(1)} %get-tuple-element.637), channel_id=1, source_target_pairs={{0,8},{8,16},{16,24},{1,9},{9,17},{17,25},{2,10},{10,18},{18,26},{... | collective-permute-start | bytes 1572872 | tf_op jit(solution)/shard_map/ppermute | solution.py:406
  325.2 23.0 %collective-permute-start.65 = (bf16[128,2048]{1,0:T(8,128)(2,1)S(1)}, bf16[128,2048]{1,0:T(8,128)(2,1)S(1)}, u32[]{:S(2)}, u32[]{:S(2)}) collective-permute-start(bf16[128,2048]{1,0:T(8,128)(2,1)S(1)} %get-tuple-element.651), channel_id=1, source_target_pairs={{0,8},{8,16},{16,24},{1,9},{9,17},{17,25},{2,10},{10,18},{18,26},{... | collective-permute-start | bytes 1572872 | tf_op jit(solution)/shard_map/ppermute | solution.py:406
  329.3 18.9 %collective-permute-start.66 = (bf16[128,2048]{1,0:T(8,128)(2,1)S(1)}, bf16[128,2048]{1,0:T(8,128)(2,1)S(1)}, u32[]{:S(2)}, u32[]{:S(2)}) collective-permute-start(bf16[128,2048]{1,0:T(8,128)(2,1)S(1)} %get-tuple-element.652), channel_id=1, source_target_pairs={{24,16},{16,8},{8,0},{25,17},{17,9},{9,1},{26,18},{18,10},{10,2},{... | collective-permute-start | bytes 1572872 | tf_op jit(solution)/shard_map/ppermute | solution.py:407
  337.6 20.2 %collective-permute-start.63 = (bf16[128,2048]{1,0:T(8,128)(2,1)S(1)}, bf16[128,2048]{1,0:T(8,128)(2,1)S(1)}, u32[]{:S(2)}, u32[]{:S(2)}) collective-permute-start(bf16[128,2048]{1,0:T(8,128)(2,1)S(1)} %get-tuple-element.655), channel_id=1, source_target_pairs={{0,8},{8,16},{16,24},{1,9},{9,17},{17,25},{2,10},{10,18},{18,26},{... | collective-permute-start | bytes 1572872 | tf_op jit(solution)/shard_map/ppermute | solution.py:406
  448.4 19.0 %collective-permute-start.86 = (bf16[128,2048]{1,0:T(8,128)(2,1)S(1)}, bf16[128,2048]{1,0:T(8,128)(2,1)S(1)}, u32[]{:S(2)}, u32[]{:S(2)}) collective-permute-start(bf16[128,2048]{1,0:T(8,128)(2,1)S(1)} %get-tuple-element.734), channel_id=1, source_target_pairs={{0,8},{8,16},{16,24},{1,9},{9,17},{17,25},{2,10},{10,18},{18,26},{... | collective-permute-start | bytes 1572872 | tf_op jit(solution)/shard_map/ppermute | solution.py:406
  450.8 20.2 %collective-permute-start.87 = (bf16[128,2048]{1,0:T(8,128)(2,1)S(1)}, bf16[128,2048]{1,0:T(8,128)(2,1)S(1)}, u32[]{:S(2)}, u32[]{:S(2)}) collective-permute-start(bf16[128,2048]{1,0:T(8,128)(2,1)S(1)} %get-tuple-element.735), channel_id=1, source_target_pairs={{24,16},{16,8},{8,0},{25,17},{17,9},{9,1},{26,18},{18,10},{10,2},{... | collective-permute-start | bytes 1572872 | tf_op jit(solution)/shard_map/ppermute | solution.py:407
  452.2 26.9 %collective-permute-start.95 = (f32[6144]{0:T(1024)S(1)}, f32[6144]{0:T(1024)S(1)}, u32[]{:S(2)}, u32[]{:S(2)}) collective-permute-start(f32[6144]{0:T(1024)S(1)} %pad_maximum_fusion.1), channel_id=1, source_target_pairs={{0,24},{24,0},{1,25},{25,1},{2,26},{26,2},{3,27},{27,3},{4,28},{28... | collective-permute-start | bytes 73736 | tf_op jit(solution)/shard_map/ppermute | solution.py:312
  463.0 23.3 %collective-permute-start.93 = (bf16[128,2048]{1,0:T(8,128)(2,1)}, bf16[128,2048]{1,0:T(8,128)(2,1)S(1)}, u32[]{:S(2)}, u32[]{:S(2)}) collective-permute-start(bf16[128,2048]{1,0:T(8,128)(2,1)} %get-tuple-element.745), channel_id=1, source_target_pairs={{0,8},{8,16},{16,24},{1,9},{9,17},{17,25},{2,10},{10,18},{18,26},{... | collective-permute-start | bytes 1572872 | tf_op jit(solution)/shard_map/ppermute | solution.py:406
  466.2 20.2 %collective-permute-start.94 = (bf16[128,2048]{1,0:T(8,128)(2,1)}, bf16[128,2048]{1,0:T(8,128)(2,1)S(1)}, u32[]{:S(2)}, u32[]{:S(2)}) collective-permute-start(bf16[128,2048]{1,0:T(8,128)(2,1)} %get-tuple-element.746), channel_id=1, source_target_pairs={{24,16},{16,8},{8,0},{25,17},{17,9},{9,1},{26,18},{18,10},{10,2},{... | collective-permute-start | bytes 1572872 | tf_op jit(solution)/shard_map/ppermute | solution.py:407
  474.4 23.7 %collective-permute-start.91 = (bf16[128,2048]{1,0:T(8,128)(2,1)}, bf16[128,2048]{1,0:T(8,128)(2,1)S(1)}, u32[]{:S(2)}, u32[]{:S(2)}) collective-permute-start(bf16[128,2048]{1,0:T(8,128)(2,1)} %get-tuple-element.747), channel_id=1, source_target_pairs={{0,8},{8,16},{16,24},{1,9},{9,17},{17,25},{2,10},{10,18},{18,26},{... | collective-permute-start | bytes 1572872 | tf_op jit(solution)/shard_map/ppermute | solution.py:406
  477.8 20.3 %collective-permute-start.92 = (bf16[128,2048]{1,0:T(8,128)(2,1)S(1)}, bf16[128,2048]{1,0:T(8,128)(2,1)S(1)}, u32[]{:S(2)}, u32[]{:S(2)}) collective-permute-start(bf16[128,2048]{1,0:T(8,128)(2,1)S(1)} %get-tuple-element.748), channel_id=1, source_target_pairs={{24,16},{16,8},{8,0},{25,17},{17,9},{9,1},{26,18},{18,10},{10,2},{... | collective-permute-start | bytes 1572872 | tf_op jit(solution)/shard_map/ppermute | solution.py:407
  533.0 21.9 %collective-permute-start.109 = (bf16[128,2048]{1,0:T(8,128)(2,1)S(1)}, bf16[128,2048]{1,0:T(8,128)(2,1)S(1)}, u32[]{:S(2)}, u32[]{:S(2)}) collective-permute-start(bf16[128,2048]{1,0:T(8,128)(2,1)S(1)} %get-tuple-element.785), channel_id=1, source_target_pairs={{0,8},{8,16},{16,24},{1,9},{9,17},{17,25},{2,10},{10,18},{18,26},{... | collective-permute-start | bytes 1572872 | tf_op jit(solution)/shard_map/ppermute | solution.py:406
  534.8 20.1 %collective-permute-start.110 = (bf16[128,2048]{1,0:T(8,128)(2,1)S(1)}, bf16[128,2048]{1,0:T(8,128)(2,1)S(1)}, u32[]{:S(2)}, u32[]{:S(2)}) collective-permute-start(bf16[128,2048]{1,0:T(8,128)(2,1)S(1)} %get-tuple-element.786), channel_id=1, source_target_pairs={{24,16},{16,8},{8,0},{25,17},{17,9},{9,1},{26,18},{18,10},{10,2},{... | collective-permute-start | bytes 1572872 | tf_op jit(solution)/shard_map/ppermute | solution.py:407
  724.8 25.6 %collective-permute-start.146 = (bf16[128,2048]{1,0:T(8,128)(2,1)S(1)}, bf16[128,2048]{1,0:T(8,128)(2,1)S(1)}, u32[]{:S(2)}, u32[]{:S(2)}) collective-permute-start(bf16[128,2048]{1,0:T(8,128)(2,1)S(1)} %get-tuple-element.879), channel_id=1, source_target_pairs={{0,8},{8,16},{16,24},{1,9},{9,17},{17,25},{2,10},{10,18},{18,26},{... | collective-permute-start | bytes 1572872 | tf_op jit(solution)/shard_map/ppermute | solution.py:406
  727.2 23.2 %collective-permute-start.147 = (bf16[128,2048]{1,0:T(8,128)(2,1)S(1)}, bf16[128,2048]{1,0:T(8,128)(2,1)S(1)}, u32[]{:S(2)}, u32[]{:S(2)}) collective-permute-start(bf16[128,2048]{1,0:T(8,128)(2,1)S(1)} %get-tuple-element.880), channel_id=1, source_target_pairs={{24,16},{16,8},{8,0},{25,17},{17,9},{9,1},{26,18},{18,10},{10,2},{... | collective-permute-start | bytes 1572872 | tf_op jit(solution)/shard_map/ppermute | solution.py:407
  734.5 18.8 %collective-permute-start.144 = (bf16[128,2048]{1,0:T(8,128)(2,1)S(1)}, bf16[128,2048]{1,0:T(8,128)(2,1)S(1)}, u32[]{:S(2)}, u32[]{:S(2)}) collective-permute-start(bf16[128,2048]{1,0:T(8,128)(2,1)S(1)} %get-tuple-element.881), channel_id=1, source_target_pairs={{8,16},{16,24},{9,17},{17,25},{10,18},{18,26},{11,19},{19,27},{12,... | collective-permute-start | bytes 1572872 | tf_op jit(solution)/shard_map/ppermute | solution.py:406
  735.2 21.0 %collective-permute-start.145 = (bf16[128,2048]{1,0:T(8,128)(2,1)S(1)}, bf16[128,2048]{1,0:T(8,128)(2,1)S(1)}, u32[]{:S(2)}, u32[]{:S(2)}) collective-permute-start(bf16[128,2048]{1,0:T(8,128)(2,1)S(1)} %get-tuple-element.882), channel_id=1, source_target_pairs={{16,8},{8,0},{17,9},{9,1},{18,10},{10,2},{19,11},{11,3},{20,12},{1... | collective-permute-start | bytes 1572872 | tf_op jit(solution)/shard_map/ppermute | solution.py:407
  758.9 21.1 %collective-permute-start.153 = (bf16[128,2048]{1,0:T(8,128)(2,1)S(1)}, bf16[128,2048]{1,0:T(8,128)(2,1)S(1)}, u32[]{:S(2)}, u32[]{:S(2)}) collective-permute-start(bf16[128,2048]{1,0:T(8,128)(2,1)S(1)} %get-tuple-element.894), channel_id=1, source_target_pairs={{8,0},{9,1},{10,2},{11,3},{12,4},{13,5},{14,6},{15,7}} | collective-permute-start | bytes 1572872 | tf_op jit(solution)/shard_map/ppermute | solution.py:407
  (125 other events, 1698.4 us)

commit v9 on v8

--- a/solution.py
+++ b/solution.py
@@ -61,27 +61,31 @@
         here = [n - begin for n in numbers]
         valids = [(n >= 0) & (n < count) for n in here]
         if part["kind"] == "sum":
+            def add(d, at, lanes, full):
+                value = ins[d][:, full]
+                if plan["with_got"]:
+                    value = (gots[d][at, lanes].astype(F32) + value.astype(F32)).astype(BF16)
+                sends[d][at, lanes] = value
+                return value
+
             for d in range(2):
-
-                @pl.when(valids[d])
+                ending = (place == (last, 0)[d]) & (part["chunk"] is not None)
+
+                @pl.when(valids[d] & jnp.logical_not(ending))
                 def _():
-                    def add(at, lanes, full, carry):
-                        value = ins[d][:, full]
-                        if plan["with_got"]:
-                            value = (gots[d][at, lanes].astype(F32) + value.astype(F32)).astype(BF16)
-                        sends[d][at, lanes] = value
+                    def pass_on(at, lanes, full, carry):
+                        add(d, at, lanes, full)
                         return carry
 
-                    each_piece(size, q, width, add)
-
-            if part["chunk"] is not None:
-                total_ref, row_ref, col_ref = outs
-                for d, end in ((0, last), (1, 0)):
-
-                    @pl.when(place == end)
+                    each_piece(size, q, width, pass_on)
+
+                if part["chunk"] is not None:
+                    total_ref, row_ref, col_ref = outs
+
+                    @pl.when(ending)
                     def _():
                         def measure(at, lanes, full, row_part):
-                            total = sends[d][at, lanes]
+                            total = add(d, at, lanes, full)
                             total_ref[:, full] = total
                             wide = total.astype(F32)
                             square = wide * wide + EPS_SQUARE

time: 795 us -> 795 us (level)
  transfers between devices with their start and end apart: 154 -> 154, of which waited for: 80 -> 84; matrix products, arithmetic and copies ran while one was open for 2% -> 2% of each run, Pallas kernels for 24% -> 23%
where the time goes in v9:
time: 795 us; the launch traced here: 789 us
  starting transfers between devices  332 us (42%)
  waiting for transfers between devices  247 us (31%)
  Pallas kernels  186 us (23%)
  other arithmetic  11.9 us (1%)
  between operations  9.78 us (1%)
    ppermute x68, starting transfers between devices, local(): lax.ppermute(tied[0], 'dp', [(p, p + 1) for p in going])  206 us
    pallas_call x70, Pallas kernels, run_step(): pl.pallas_call(functools.partial(step_kernel, plan), grid_spec=pltpu.Pref...  186 us
    ppermute x68, waiting for transfers between devices, local(): lax.ppermute(tied[1], 'dp', [(last - p, last - p - 1) for p in going])  144 us
    ppermute x68, starting transfers between devices, local(): lax.ppermute(tied[1], 'dp', [(last - p, last - p - 1) for p in going])  85.9 us
    ppermute x68, waiting for transfers between devices, local(): lax.ppermute(tied[0], 'dp', [(p, p + 1) for p in going])  80.7 us
  transfers between devices with their start and end apart: 154, of which 84 were waited for; matrix products, arithmetic and copies ran while one was open for 2% of the time, Pallas kernels for 23%

profile of v9, /device:TPU:0, one launch (start us, length us, event | category | flops | bytes accessed | tf_op | source)
XLA Modules:
  0.0 789.1 jit_solution(9785191315006829475)
XLA Ops:
  2.1 4.8 collective-permute-start.2
  11.1 8.1 %collective-permute-done.2.refs_0_ = bf16[128,2048]{1,0:T(8,128)(2,1)S(1)} collective-permute-done((bf16[128,2048]{1,0:T(8,128)(2,1)S(1)}, bf16[128,2048]{1,0:T(8,128)(2,1)S(1)}, u32[]{:S(2)}, u32[]{:S(2)}) %collective-permute-start.2) | collective-permute-done | bytes 524320 | tf_op jit(solution)/shard_map/ppermute | solution.py:410
  20.7 4.4 collective-permute-start.6
  25.9 4.6 collective-permute-done.refs_0_
  32.0 4.4 collective-permute-start.4
  37.1 4.6 collective-permute-done.6.refs_0_
  43.2 4.7 collective-permute-start.10
  54.4 4.7 collective-permute-start.8
  202.2 4.2 collective-permute-start.38
  213.4 4.2 collective-permute-start.36
  225.0 4.4 collective-permute-start.42
  236.3 4.4 collective-permute-start.40
  260.3 4.3 collective-permute-start.46
  266.0 4.7 collective-permute-start.55
  286.8 4.3 collective-permute-start.51
  302.5 4.3 collective-permute-start.59
  314.9 4.3 collective-permute-start.57
  324.9 4.3 collective-permute-start.65
  337.4 4.3 collective-permute-start.63
  414.5 4.3 line_step.106
  426.5 4.3 line_step.107
  452.8 4.8 collective-permute-start.95
  467.3 4.6 collective-permute-done.87.refs_1_
  488.6 4.3 collective-permute-start.99
  500.5 4.3 collective-permute-start.97
  509.7 4.3 collective-permute-start.105
  521.4 4.3 collective-permute-start.103
  547.8 5.8 collective-permute-done.111
  571.8 4.4 collective-permute-done.115.refs_1_
  583.1 4.4 collective-permute-done.113.refs_1_
  594.3 4.4 collective-permute-done.119.refs_1_
  605.5 4.4 collective-permute-done.117.refs_1_
  616.8 4.4 collective-permute-done.121.refs_1_
  628.0 4.4 collective-permute-done.125.refs_1_
  639.2 4.4 collective-permute-done.123.refs_1_
  650.5 4.4 collective-permute-done.129.refs_1_
  661.7 4.4 collective-permute-done.127.refs_1_
  672.9 4.4 collective-permute-done.133.refs_1_
  684.2 4.4 collective-permute-done.131.refs_1_
  695.4 4.4 collective-permute-done.137.refs_1_
  706.7 4.4 collective-permute-done.135.refs_1_
  717.9 4.4 collective-permute-done.142.refs_1_
  729.1 4.4 collective-permute-done.140.refs_1_
  736.4 5.9 collective-permute-start.138
  744.1 6.2 collective-permute-start.143
  761.4 7.3 collective-permute-done.149.refs_1_
  771.5 8.4 %collective-permute-done.153.refs_1_ = bf16[128,2048]{1,0:T(8,128)(2,1)S(1)} collective-permute-done((bf16[128,2048]{1,0:T(8,128)(2,1)S(1)}, bf16[128,2048]{1,0:T(8,128)(2,1)S(1)}, u32[]{:S(2)}, u32[]{:S(2)}) %collective-permute-start.153) | collective-permute-done | bytes 524320 | tf_op jit(solution)/shard_map/ppermute | solution.py:411
  780.7 7.5 collective-permute-done.151.refs_1_
  (421 shorter events, 548.6 us)
Async XLA Ops:
  9.1 21.3 %collective-permute-start = (bf16[128,2048]{1,0:T(8,128)(2,1)S(1)}, bf16[128,2048]{1,0:T(8,128)(2,1)S(1)}, u32[]{:S(2)}, u32[]{:S(2)}) collective-permute-start(bf16[128,2048]{1,0:T(8,128)(2,1)S(1)} %get-tuple-element.458), channel_id=1, source_target_pairs={{0,8},{1,9},{2,10},{3,11},{4,12},{5,13},{6,14},{7,15}} | collective-permute-start | bytes 1572872 | tf_op jit(solution)/shard_map/ppermute | solution.py:410
  10.4 20.0 %collective-permute-start.1 = (bf16[128,2048]{1,0:T(8,128)(2,1)S(1)}, bf16[128,2048]{1,0:T(8,128)(2,1)S(1)}, u32[]{:S(2)}, u32[]{:S(2)}) collective-permute-start(bf16[128,2048]{1,0:T(8,128)(2,1)S(1)} %get-tuple-element.459), channel_id=1, source_target_pairs={{24,16},{25,17},{26,18},{27,19},{28,20},{29,21},{30,22},{31,23}} | collective-permute-start | bytes 1572872 | tf_op jit(solution)/shard_map/ppermute | solution.py:411
  20.7 20.9 %collective-permute-start.6 = (bf16[128,2048]{1,0:T(8,128)(2,1)S(1)}, bf16[128,2048]{1,0:T(8,128)(2,1)S(1)}, u32[]{:S(2)}, u32[]{:S(2)}) collective-permute-start(bf16[128,2048]{1,0:T(8,128)(2,1)S(1)} %get-tuple-element.464), channel_id=1, source_target_pairs={{0,8},{8,16},{1,9},{9,17},{2,10},{10,18},{3,11},{11,19},{4,12},{12... | collective-permute-start | bytes 1572872 | tf_op jit(solution)/shard_map/ppermute | solution.py:410
  32.0 20.9 %collective-permute-start.4 = (bf16[128,2048]{1,0:T(8,128)(2,1)S(1)}, bf16[128,2048]{1,0:T(8,128)(2,1)S(1)}, u32[]{:S(2)}, u32[]{:S(2)}) collective-permute-start(bf16[128,2048]{1,0:T(8,128)(2,1)S(1)} %get-tuple-element.466), channel_id=1, source_target_pairs={{0,8},{8,16},{1,9},{9,17},{2,10},{10,18},{3,11},{11,19},{4,12},{12... | collective-permute-start | bytes 1572872 | tf_op jit(solution)/shard_map/ppermute | solution.py:410
  43.2 20.9 %collective-permute-start.10 = (bf16[128,2048]{1,0:T(8,128)(2,1)S(1)}, bf16[128,2048]{1,0:T(8,128)(2,1)S(1)}, u32[]{:S(2)}, u32[]{:S(2)}) collective-permute-start(bf16[128,2048]{1,0:T(8,128)(2,1)S(1)} %get-tuple-element.472), channel_id=1, source_target_pairs={{0,8},{8,16},{16,24},{1,9},{9,17},{17,25},{2,10},{10,18},{18,26},{... | collective-permute-start | bytes 1572872 | tf_op jit(solution)/shard_map/ppermute | solution.py:410
  54.4 20.9 %collective-permute-start.8 = (bf16[128,2048]{1,0:T(8,128)(2,1)S(1)}, bf16[128,2048]{1,0:T(8,128)(2,1)S(1)}, u32[]{:S(2)}, u32[]{:S(2)}) collective-permute-start(bf16[128,2048]{1,0:T(8,128)(2,1)S(1)} %get-tuple-element.474), channel_id=1, source_target_pairs={{0,8},{8,16},{16,24},{1,9},{9,17},{17,25},{2,10},{10,18},{18,26},{... | collective-permute-start | bytes 1572872 | tf_op jit(solution)/shard_map/ppermute | solution.py:410
  66.9 19.6 %collective-permute-start.14 = (bf16[128,2048]{1,0:T(8,128)(2,1)S(1)}, bf16[128,2048]{1,0:T(8,128)(2,1)S(1)}, u32[]{:S(2)}, u32[]{:S(2)}) collective-permute-start(bf16[128,2048]{1,0:T(8,128)(2,1)S(1)} %get-tuple-element.483), channel_id=1, source_target_pairs={{0,8},{8,16},{16,24},{1,9},{9,17},{17,25},{2,10},{10,18},{18,26},{... | collective-permute-start | bytes 1572872 | tf_op jit(solution)/shard_map/ppermute | solution.py:410
  78.2 19.7 %collective-permute-start.12 = (bf16[128,2048]{1,0:T(8,128)(2,1)S(1)}, bf16[128,2048]{1,0:T(8,128)(2,1)S(1)}, u32[]{:S(2)}, u32[]{:S(2)}) collective-permute-start(bf16[128,2048]{1,0:T(8,128)(2,1)S(1)} %get-tuple-element.485), channel_id=1, source_target_pairs={{0,8},{8,16},{16,24},{1,9},{9,17},{17,25},{2,10},{10,18},{18,26},{... | collective-permute-start | bytes 1572872 | tf_op jit(solution)/shard_map/ppermute | solution.py:410
  89.4 19.7 %collective-permute-start.18 = (bf16[128,2048]{1,0:T(8,128)(2,1)S(1)}, bf16[128,2048]{1,0:T(8,128)(2,1)S(1)}, u32[]{:S(2)}, u32[]{:S(2)}) collective-permute-start(bf16[128,2048]{1,0:T(8,128)(2,1)S(1)} %get-tuple-element.497), channel_id=1, source_target_pairs={{0,8},{8,16},{16,24},{1,9},{9,17},{17,25},{2,10},{10,18},{18,26},{... | collective-permute-start | bytes 1572872 | tf_op jit(solution)/shard_map/ppermute | solution.py:410
  100.6 19.7 %collective-permute-start.16 = (bf16[128,2048]{1,0:T(8,128)(2,1)S(1)}, bf16[128,2048]{1,0:T(8,128)(2,1)S(1)}, u32[]{:S(2)}, u32[]{:S(2)}) collective-permute-start(bf16[128,2048]{1,0:T(8,128)(2,1)S(1)} %get-tuple-element.499), channel_id=1, source_target_pairs={{0,8},{8,16},{16,24},{1,9},{9,17},{17,25},{2,10},{10,18},{18,26},{... | collective-permute-start | bytes 1572872 | tf_op jit(solution)/shard_map/ppermute | solution.py:410
  111.9 19.7 %collective-permute-start.22 = (bf16[128,2048]{1,0:T(8,128)(2,1)S(1)}, bf16[128,2048]{1,0:T(8,128)(2,1)S(1)}, u32[]{:S(2)}, u32[]{:S(2)}) collective-permute-start(bf16[128,2048]{1,0:T(8,128)(2,1)S(1)} %get-tuple-element.511), channel_id=1, source_target_pairs={{0,8},{8,16},{16,24},{1,9},{9,17},{17,25},{2,10},{10,18},{18,26},{... | collective-permute-start | bytes 1572872 | tf_op jit(solution)/shard_map/ppermute | solution.py:410
  123.1 19.7 %collective-permute-start.20 = (bf16[128,2048]{1,0:T(8,128)(2,1)S(1)}, bf16[128,2048]{1,0:T(8,128)(2,1)S(1)}, u32[]{:S(2)}, u32[]{:S(2)}) collective-permute-start(bf16[128,2048]{1,0:T(8,128)(2,1)S(1)} %get-tuple-element.513), channel_id=1, source_target_pairs={{0,8},{8,16},{16,24},{1,9},{9,17},{17,25},{2,10},{10,18},{18,26},{... | collective-permute-start | bytes 1572872 | tf_op jit(solution)/shard_map/ppermute | solution.py:410
  134.3 19.7 %collective-permute-start.26 = (bf16[128,2048]{1,0:T(8,128)(2,1)S(1)}, bf16[128,2048]{1,0:T(8,128)(2,1)S(1)}, u32[]{:S(2)}, u32[]{:S(2)}) collective-permute-start(bf16[128,2048]{1,0:T(8,128)(2,1)S(1)} %get-tuple-element.525), channel_id=1, source_target_pairs={{0,8},{8,16},{16,24},{1,9},{9,17},{17,25},{2,10},{10,18},{18,26},{... | collective-permute-start | bytes 1572872 | tf_op jit(solution)/shard_map/ppermute | solution.py:410
  145.6 19.7 %collective-permute-start.24 = (bf16[128,2048]{1,0:T(8,128)(2,1)S(1)}, bf16[128,2048]{1,0:T(8,128)(2,1)S(1)}, u32[]{:S(2)}, u32[]{:S(2)}) collective-permute-start(bf16[128,2048]{1,0:T(8,128)(2,1)S(1)} %get-tuple-element.527), channel_id=1, source_target_pairs={{0,8},{8,16},{16,24},{1,9},{9,17},{17,25},{2,10},{10,18},{18,26},{... | collective-permute-start | bytes 1572872 | tf_op jit(solution)/shard_map/ppermute | solution.py:410
  156.8 19.7 %collective-permute-start.30 = (bf16[128,2048]{1,0:T(8,128)(2,1)S(1)}, bf16[128,2048]{1,0:T(8,128)(2,1)S(1)}, u32[]{:S(2)}, u32[]{:S(2)}) collective-permute-start(bf16[128,2048]{1,0:T(8,128)(2,1)S(1)} %get-tuple-element.539), channel_id=1, source_target_pairs={{0,8},{8,16},{16,24},{1,9},{9,17},{17,25},{2,10},{10,18},{18,26},{... | collective-permute-start | bytes 1572872 | tf_op jit(solution)/shard_map/ppermute | solution.py:410
  168.0 19.7 %collective-permute-start.28 = (bf16[128,2048]{1,0:T(8,128)(2,1)S(1)}, bf16[128,2048]{1,0:T(8,128)(2,1)S(1)}, u32[]{:S(2)}, u32[]{:S(2)}) collective-permute-start(bf16[128,2048]{1,0:T(8,128)(2,1)S(1)} %get-tuple-element.541), channel_id=1, source_target_pairs={{0,8},{8,16},{16,24},{1,9},{9,17},{17,25},{2,10},{10,18},{18,26},{... | collective-permute-start | bytes 1572872 | tf_op jit(solution)/shard_map/ppermute | solution.py:410
  179.7 19.2 %collective-permute-start.34 = (bf16[128,2048]{1,0:T(8,128)(2,1)S(1)}, bf16[128,2048]{1,0:T(8,128)(2,1)S(1)}, u32[]{:S(2)}, u32[]{:S(2)}) collective-permute-start(bf16[128,2048]{1,0:T(8,128)(2,1)S(1)} %get-tuple-element.553), channel_id=1, source_target_pairs={{0,8},{8,16},{16,24},{1,9},{9,17},{17,25},{2,10},{10,18},{18,26},{... | collective-permute-start | bytes 1572872 | tf_op jit(solution)/shard_map/ppermute | solution.py:410
  191.0 19.2 %collective-permute-start.32 = (bf16[128,2048]{1,0:T(8,128)(2,1)S(1)}, bf16[128,2048]{1,0:T(8,128)(2,1)S(1)}, u32[]{:S(2)}, u32[]{:S(2)}) collective-permute-start(bf16[128,2048]{1,0:T(8,128)(2,1)S(1)} %get-tuple-element.555), channel_id=1, source_target_pairs={{0,8},{8,16},{16,24},{1,9},{9,17},{17,25},{2,10},{10,18},{18,26},{... | collective-permute-start | bytes 1572872 | tf_op jit(solution)/shard_map/ppermute | solution.py:410
  202.2 19.2 %collective-permute-start.38 = (bf16[128,2048]{1,0:T(8,128)(2,1)S(1)}, bf16[128,2048]{1,0:T(8,128)(2,1)S(1)}, u32[]{:S(2)}, u32[]{:S(2)}) collective-permute-start(bf16[128,2048]{1,0:T(8,128)(2,1)S(1)} %get-tuple-element.567), channel_id=1, source_target_pairs={{0,8},{8,16},{16,24},{1,9},{9,17},{17,25},{2,10},{10,18},{18,26},{... | collective-permute-start | bytes 1572872 | tf_op jit(solution)/shard_map/ppermute | solution.py:410
  213.4 19.2 %collective-permute-start.36 = (bf16[128,2048]{1,0:T(8,128)(2,1)S(1)}, bf16[128,2048]{1,0:T(8,128)(2,1)S(1)}, u32[]{:S(2)}, u32[]{:S(2)}) collective-permute-start(bf16[128,2048]{1,0:T(8,128)(2,1)S(1)} %get-tuple-element.569), channel_id=1, source_target_pairs={{0,8},{8,16},{16,24},{1,9},{9,17},{17,25},{2,10},{10,18},{18,26},{... | collective-permute-start | bytes 1572872 | tf_op jit(solution)/shard_map/ppermute | solution.py:410
  225.0 19.0 %collective-permute-start.42 = (bf16[128,2048]{1,0:T(8,128)(2,1)}, bf16[128,2048]{1,0:T(8,128)(2,1)S(1)}, u32[]{:S(2)}, u32[]{:S(2)}) collective-permute-start(bf16[128,2048]{1,0:T(8,128)(2,1)} %get-tuple-element.581), channel_id=1, source_target_pairs={{0,8},{8,16},{16,24},{1,9},{9,17},{17,25},{2,10},{10,18},{18,26},{... | collective-permute-start | bytes 1572872 | tf_op jit(solution)/shard_map/ppermute | solution.py:410
  236.3 20.9 %collective-permute-start.40 = (bf16[128,2048]{1,0:T(8,128)(2,1)}, bf16[128,2048]{1,0:T(8,128)(2,1)S(1)}, u32[]{:S(2)}, u32[]{:S(2)}) collective-permute-start(bf16[128,2048]{1,0:T(8,128)(2,1)} %get-tuple-element.583), channel_id=1, source_target_pairs={{0,8},{8,16},{16,24},{1,9},{9,17},{17,25},{2,10},{10,18},{18,26},{... | collective-permute-start | bytes 1572872 | tf_op jit(solution)/shard_map/ppermute | solution.py:410
  251.8 19.0 %collective-permute-start.48 = (bf16[128,2048]{1,0:T(8,128)(2,1)}, bf16[128,2048]{1,0:T(8,128)(2,1)S(1)}, u32[]{:S(2)}, u32[]{:S(2)}) collective-permute-start(bf16[128,2048]{1,0:T(8,128)(2,1)} %copy-done.1), channel_id=1, source_target_pairs={{0,8},{8,16},{16,24},{1,9},{9,17},{17,25},{2,10},{10,18},{18,26},{... | collective-permute-start | bytes 1572872 | tf_op jit(solution)/shard_map/ppermute | solution.py:410
  260.3 19.9 %collective-permute-start.46 = (bf16[128,2048]{1,0:T(8,128)(2,1)S(1)}, bf16[128,2048]{1,0:T(8,128)(2,1)S(1)}, u32[]{:S(2)}, u32[]{:S(2)}) collective-permute-start(bf16[128,2048]{1,0:T(8,128)(2,1)S(1)} %get-tuple-element.600), channel_id=1, source_target_pairs={{0,8},{8,16},{16,24},{1,9},{9,17},{17,25},{2,10},{10,18},{18,26},{... | collective-permute-start | bytes 1572872 | tf_op jit(solution)/shard_map/ppermute | solution.py:410
  266.0 26.5 %collective-permute-start.55 = (f32[9216]{0:T(1024)S(1)}, f32[9216]{0:T(1024)S(1)}, u32[]{:S(2)}, u32[]{:S(2)}) collective-permute-start(f32[9216]{0:T(1024)S(1)} %pad_maximum_fusion), channel_id=1, source_target_pairs={{0,24},{24,0},{1,25},{25,1},{2,26},{26,2},{3,27},{27,3},{4,28},{28... | collective-permute-start | bytes 110600 | tf_op jit(solution)/shard_map/ppermute | solution.py:316
  276.4 22.9 %collective-permute-start.53 = (bf16[128,2048]{1,0:T(8,128)(2,1)}, bf16[128,2048]{1,0:T(8,128)(2,1)S(1)}, u32[]{:S(2)}, u32[]{:S(2)}) collective-permute-start(bf16[128,2048]{1,0:T(8,128)(2,1)} %get-tuple-element.615), channel_id=1, source_target_pairs={{0,8},{8,16},{16,24},{1,9},{9,17},{17,25},{2,10},{10,18},{18,26},{... | collective-permute-start | bytes 1572872 | tf_op jit(solution)/shard_map/ppermute | solution.py:410
  279.0 20.4 %collective-permute-start.54 = (bf16[128,2048]{1,0:T(8,128)(2,1)}, bf16[128,2048]{1,0:T(8,128)(2,1)S(1)}, u32[]{:S(2)}, u32[]{:S(2)}) collective-permute-start(bf16[128,2048]{1,0:T(8,128)(2,1)} %get-tuple-element.616), channel_id=1, source_target_pairs={{24,16},{16,8},{8,0},{25,17},{17,9},{9,1},{26,18},{18,10},{10,2},{... | collective-permute-start | bytes 1572872 | tf_op jit(solution)/shard_map/ppermute | solution.py:411
  286.8 25.0 %collective-permute-start.51 = (bf16[128,2048]{1,0:T(8,128)(2,1)}, bf16[128,2048]{1,0:T(8,128)(2,1)S(1)}, u32[]{:S(2)}, u32[]{:S(2)}) collective-permute-start(bf16[128,2048]{1,0:T(8,128)(2,1)} %get-tuple-element.617), channel_id=1, source_target_pairs={{0,8},{8,16},{16,24},{1,9},{9,17},{17,25},{2,10},{10,18},{18,26},{... | collective-permute-start | bytes 1572872 | tf_op jit(solution)/shard_map/ppermute | solution.py:410
  291.0 20.8 %collective-permute-start.52 = (bf16[128,2048]{1,0:T(8,128)(2,1)}, bf16[128,2048]{1,0:T(8,128)(2,1)S(1)}, u32[]{:S(2)}, u32[]{:S(2)}) collective-permute-start(bf16[128,2048]{1,0:T(8,128)(2,1)} %get-tuple-element.618), channel_id=1, source_target_pairs={{24,16},{16,8},{8,0},{25,17},{17,9},{9,1},{26,18},{18,10},{10,2},{... | collective-permute-start | bytes 1572872 | tf_op jit(solution)/shard_map/ppermute | solution.py:411
  302.5 19.4 %collective-permute-start.59 = (bf16[128,2048]{1,0:T(8,128)(2,1)S(1)}, bf16[128,2048]{1,0:T(8,128)(2,1)S(1)}, u32[]{:S(2)}, u32[]{:S(2)}) collective-permute-start(bf16[128,2048]{1,0:T(8,128)(2,1)S(1)} %get-tuple-element.633), channel_id=1, source_target_pairs={{0,8},{8,16},{16,24},{1,9},{9,17},{17,25},{2,10},{10,18},{18,26},{... | collective-permute-start | bytes 1572872 | tf_op jit(solution)/shard_map/ppermute | solution.py:410
  314.9 19.4 %collective-permute-start.57 = (bf16[128,2048]{1,0:T(8,128)(2,1)S(1)}, bf16[128,2048]{1,0:T(8,128)(2,1)S(1)}, u32[]{:S(2)}, u32[]{:S(2)}) collective-permute-start(bf16[128,2048]{1,0:T(8,128)(2,1)S(1)} %get-tuple-element.637), channel_id=1, source_target_pairs={{0,8},{8,16},{16,24},{1,9},{9,17},{17,25},{2,10},{10,18},{18,26},{... | collective-permute-start | bytes 1572872 | tf_op jit(solution)/shard_map/ppermute | solution.py:410
  324.9 22.2 %collective-permute-start.65 = (bf16[128,2048]{1,0:T(8,128)(2,1)S(1)}, bf16[128,2048]{1,0:T(8,128)(2,1)S(1)}, u32[]{:S(2)}, u32[]{:S(2)}) collective-permute-start(bf16[128,2048]{1,0:T(8,128)(2,1)S(1)} %get-tuple-element.651), channel_id=1, source_target_pairs={{0,8},{8,16},{16,24},{1,9},{9,17},{17,25},{2,10},{10,18},{18,26},{... | collective-permute-start | bytes 1572872 | tf_op jit(solution)/shard_map/ppermute | solution.py:410
  337.4 19.5 %collective-permute-start.63 = (bf16[128,2048]{1,0:T(8,128)(2,1)S(1)}, bf16[128,2048]{1,0:T(8,128)(2,1)S(1)}, u32[]{:S(2)}, u32[]{:S(2)}) collective-permute-start(bf16[128,2048]{1,0:T(8,128)(2,1)S(1)} %get-tuple-element.655), channel_id=1, source_target_pairs={{0,8},{8,16},{16,24},{1,9},{9,17},{17,25},{2,10},{10,18},{18,26},{... | collective-permute-start | bytes 1572872 | tf_op jit(solution)/shard_map/ppermute | solution.py:410
  448.4 18.9 %collective-permute-start.86 = (bf16[128,2048]{1,0:T(8,128)(2,1)S(1)}, bf16[128,2048]{1,0:T(8,128)(2,1)S(1)}, u32[]{:S(2)}, u32[]{:S(2)}) collective-permute-start(bf16[128,2048]{1,0:T(8,128)(2,1)S(1)} %get-tuple-element.734), channel_id=1, source_target_pairs={{0,8},{8,16},{16,24},{1,9},{9,17},{17,25},{2,10},{10,18},{18,26},{... | collective-permute-start | bytes 1572872 | tf_op jit(solution)/shard_map/ppermute | solution.py:410
  451.5 20.5 %collective-permute-start.87 = (bf16[128,2048]{1,0:T(8,128)(2,1)S(1)}, bf16[128,2048]{1,0:T(8,128)(2,1)S(1)}, u32[]{:S(2)}, u32[]{:S(2)}) collective-permute-start(bf16[128,2048]{1,0:T(8,128)(2,1)S(1)} %get-tuple-element.735), channel_id=1, source_target_pairs={{24,16},{16,8},{8,0},{25,17},{17,9},{9,1},{26,18},{18,10},{10,2},{... | collective-permute-start | bytes 1572872 | tf_op jit(solution)/shard_map/ppermute | solution.py:411
  452.8 26.1 %collective-permute-start.95 = (f32[6144]{0:T(1024)S(1)}, f32[6144]{0:T(1024)S(1)}, u32[]{:S(2)}, u32[]{:S(2)}) collective-permute-start(f32[6144]{0:T(1024)S(1)} %pad_maximum_fusion.1), channel_id=1, source_target_pairs={{0,24},{24,0},{1,25},{25,1},{2,26},{26,2},{3,27},{27,3},{4,28},{28... | collective-permute-start | bytes 73736 | tf_op jit(solution)/shard_map/ppermute | solution.py:316
  463.7 22.5 %collective-permute-start.93 = (bf16[128,2048]{1,0:T(8,128)(2,1)}, bf16[128,2048]{1,0:T(8,128)(2,1)S(1)}, u32[]{:S(2)}, u32[]{:S(2)}) collective-permute-start(bf16[128,2048]{1,0:T(8,128)(2,1)} %get-tuple-element.745), channel_id=1, source_target_pairs={{0,8},{8,16},{16,24},{1,9},{9,17},{17,25},{2,10},{10,18},{18,26},{... | collective-permute-start | bytes 1572872 | tf_op jit(solution)/shard_map/ppermute | solution.py:410
  466.0 20.2 %collective-permute-start.94 = (bf16[128,2048]{1,0:T(8,128)(2,1)}, bf16[128,2048]{1,0:T(8,128)(2,1)S(1)}, u32[]{:S(2)}, u32[]{:S(2)}) collective-permute-start(bf16[128,2048]{1,0:T(8,128)(2,1)} %get-tuple-element.746), channel_id=1, source_target_pairs={{24,16},{16,8},{8,0},{25,17},{17,9},{9,1},{26,18},{18,10},{10,2},{... | collective-permute-start | bytes 1572872 | tf_op jit(solution)/shard_map/ppermute | solution.py:411
  475.3 22.8 %collective-permute-start.91 = (bf16[128,2048]{1,0:T(8,128)(2,1)}, bf16[128,2048]{1,0:T(8,128)(2,1)S(1)}, u32[]{:S(2)}, u32[]{:S(2)}) collective-permute-start(bf16[128,2048]{1,0:T(8,128)(2,1)} %get-tuple-element.747), channel_id=1, source_target_pairs={{0,8},{8,16},{16,24},{1,9},{9,17},{17,25},{2,10},{10,18},{18,26},{... | collective-permute-start | bytes 1572872 | tf_op jit(solution)/shard_map/ppermute | solution.py:410
  477.6 20.5 %collective-permute-start.92 = (bf16[128,2048]{1,0:T(8,128)(2,1)S(1)}, bf16[128,2048]{1,0:T(8,128)(2,1)S(1)}, u32[]{:S(2)}, u32[]{:S(2)}) collective-permute-start(bf16[128,2048]{1,0:T(8,128)(2,1)S(1)} %get-tuple-element.748), channel_id=1, source_target_pairs={{24,16},{16,8},{8,0},{25,17},{17,9},{9,1},{26,18},{18,10},{10,2},{... | collective-permute-start | bytes 1572872 | tf_op jit(solution)/shard_map/ppermute | solution.py:411
  488.6 18.8 %collective-permute-start.99 = (bf16[128,2048]{1,0:T(8,128)(2,1)S(1)}, bf16[128,2048]{1,0:T(8,128)(2,1)S(1)}, u32[]{:S(2)}, u32[]{:S(2)}) collective-permute-start(bf16[128,2048]{1,0:T(8,128)(2,1)S(1)} %get-tuple-element.759), channel_id=1, source_target_pairs={{0,8},{8,16},{16,24},{1,9},{9,17},{17,25},{2,10},{10,18},{18,26},{... | collective-permute-start | bytes 1572872 | tf_op jit(solution)/shard_map/ppermute | solution.py:410
  532.9 21.9 %collective-permute-start.109 = (bf16[128,2048]{1,0:T(8,128)(2,1)S(1)}, bf16[128,2048]{1,0:T(8,128)(2,1)S(1)}, u32[]{:S(2)}, u32[]{:S(2)}) collective-permute-start(bf16[128,2048]{1,0:T(8,128)(2,1)S(1)} %get-tuple-element.785), channel_id=1, source_target_pairs={{0,8},{8,16},{16,24},{1,9},{9,17},{17,25},{2,10},{10,18},{18,26},{... | collective-permute-start | bytes 1572872 | tf_op jit(solution)/shard_map/ppermute | solution.py:410
  534.7 20.1 %collective-permute-start.110 = (bf16[128,2048]{1,0:T(8,128)(2,1)S(1)}, bf16[128,2048]{1,0:T(8,128)(2,1)S(1)}, u32[]{:S(2)}, u32[]{:S(2)}) collective-permute-start(bf16[128,2048]{1,0:T(8,128)(2,1)S(1)} %get-tuple-element.786), channel_id=1, source_target_pairs={{24,16},{16,8},{8,0},{25,17},{17,9},{9,1},{26,18},{18,10},{10,2},{... | collective-permute-start | bytes 1572872 | tf_op jit(solution)/shard_map/ppermute | solution.py:411
  724.7 25.6 %collective-permute-start.146 = (bf16[128,2048]{1,0:T(8,128)(2,1)S(1)}, bf16[128,2048]{1,0:T(8,128)(2,1)S(1)}, u32[]{:S(2)}, u32[]{:S(2)}) collective-permute-start(bf16[128,2048]{1,0:T(8,128)(2,1)S(1)} %get-tuple-element.879), channel_id=1, source_target_pairs={{0,8},{8,16},{16,24},{1,9},{9,17},{17,25},{2,10},{10,18},{18,26},{... | collective-permute-start | bytes 1572872 | tf_op jit(solution)/shard_map/ppermute | solution.py:410
  727.1 23.2 %collective-permute-start.147 = (bf16[128,2048]{1,0:T(8,128)(2,1)S(1)}, bf16[128,2048]{1,0:T(8,128)(2,1)S(1)}, u32[]{:S(2)}, u32[]{:S(2)}) collective-permute-start(bf16[128,2048]{1,0:T(8,128)(2,1)S(1)} %get-tuple-element.880), channel_id=1, source_target_pairs={{24,16},{16,8},{8,0},{25,17},{17,9},{9,1},{26,18},{18,10},{10,2},{... | collective-permute-start | bytes 1572872 | tf_op jit(solution)/shard_map/ppermute | solution.py:411
  734.4 18.8 %collective-permute-start.144 = (bf16[128,2048]{1,0:T(8,128)(2,1)S(1)}, bf16[128,2048]{1,0:T(8,128)(2,1)S(1)}, u32[]{:S(2)}, u32[]{:S(2)}) collective-permute-start(bf16[128,2048]{1,0:T(8,128)(2,1)S(1)} %get-tuple-element.881), channel_id=1, source_target_pairs={{8,16},{16,24},{9,17},{17,25},{10,18},{18,26},{11,19},{19,27},{12,... | collective-permute-start | bytes 1572872 | tf_op jit(solution)/shard_map/ppermute | solution.py:410
  735.1 21.0 %collective-permute-start.145 = (bf16[128,2048]{1,0:T(8,128)(2,1)S(1)}, bf16[128,2048]{1,0:T(8,128)(2,1)S(1)}, u32[]{:S(2)}, u32[]{:S(2)}) collective-permute-start(bf16[128,2048]{1,0:T(8,128)(2,1)S(1)} %get-tuple-element.882), channel_id=1, source_target_pairs={{16,8},{8,0},{17,9},{9,1},{18,10},{10,2},{19,11},{11,3},{20,12},{1... | collective-permute-start | bytes 1572872 | tf_op jit(solution)/shard_map/ppermute | solution.py:411
  758.8 21.1 %collective-permute-start.153 = (bf16[128,2048]{1,0:T(8,128)(2,1)S(1)}, bf16[128,2048]{1,0:T(8,128)(2,1)S(1)}, u32[]{:S(2)}, u32[]{:S(2)}) collective-permute-start(bf16[128,2048]{1,0:T(8,128)(2,1)S(1)} %get-tuple-element.894), channel_id=1, source_target_pairs={{8,0},{9,1},{10,2},{11,3},{12,4},{13,5},{14,6},{15,7}} | collective-permute-start | bytes 1572872 | tf_op jit(solution)/shard_map/ppermute | solution.py:411
  (125 other events, 1698.8 us)

commit v10 on v9

--- a/solution.py
+++ b/solution.py
@@ -11,7 +11,7 @@
 EPS_SQUARE = 1e-30
 CHUNKS = 16
 LAG = 2
-GROUPS = 4
+GROUPS = 1
 FAR = 2
 LANES = 128
 PIECE = 16384

time: 795 us -> 804 us (1.011); the launches traced: 789 us -> 790 us
  transfers between devices with their start and end apart: 154 -> 154, of which waited for: 84 -> 85; matrix products, arithmetic and copies ran while one was open for 2% -> 3% of each run, Pallas kernels for 23% -> 23%
where the time goes in v10:
time: 804 us; the launch traced here: 790 us
  starting transfers between devices  331 us (41%)
  waiting for transfers between devices  248 us (31%)
  Pallas kernels  183 us (23%)
  other arithmetic  17.5 us (2%)
    ppermute x68, starting transfers between devices, local(): lax.ppermute(tied[0], 'dp', [(p, p + 1) for p in going])  206 us
    pallas_call x70, Pallas kernels, run_step(): pl.pallas_call(functools.partial(step_kernel, plan), grid_spec=pltpu.Pref...  183 us
    ppermute x68, waiting for transfers between devices, local(): lax.ppermute(tied[1], 'dp', [(last - p, last - p - 1) for p in going])  146 us
    ppermute x68, starting transfers between devices, local(): lax.ppermute(tied[1], 'dp', [(last - p, last - p - 1) for p in going])  85.6 us
    ppermute x68, waiting for transfers between devices, local(): lax.ppermute(tied[0], 'dp', [(p, p + 1) for p in going])  80.7 us
  transfers between devices with their start and end apart: 154, of which 85 were waited for; matrix products, arithmetic and copies ran while one was open for 3% of the time, Pallas kernels for 23%

profile of v10, /device:TPU:0, one launch (start us, length us, event | category | flops | bytes accessed | tf_op | source)
XLA Modules:
  0.0 789.7 jit_solution(232051681666395340)
XLA Ops:
  2.1 4.8 collective-permute-start.2
  11.1 8.1 %collective-permute-done.2.refs_0_ = bf16[128,2048]{1,0:T(8,128)(2,1)S(1)} collective-permute-done((bf16[128,2048]{1,0:T(8,128)(2,1)S(1)}, bf16[128,2048]{1,0:T(8,128)(2,1)S(1)}, u32[]{:S(2)}, u32[]{:S(2)}) %collective-permute-start.2) | collective-permute-done | bytes 524320 | tf_op jit(solution)/shard_map/ppermute | solution.py:410
  20.7 4.4 collective-permute-start.6
  25.9 4.6 collective-permute-done.refs_0_
  32.0 4.4 collective-permute-start.4
  37.1 4.6 collective-permute-done.6.refs_0_
  43.2 4.7 collective-permute-start.10
  54.4 4.7 collective-permute-start.8
  225.0 4.4 collective-permute-start.42
  236.3 4.4 collective-permute-start.40
  260.3 4.3 collective-permute-start.46
  266.0 4.7 collective-permute-start.55
  292.8 6.4 multiply_reduce_fusion.1
  303.0 4.3 collective-permute-start.59
  315.5 4.3 collective-permute-start.57
  325.5 4.3 collective-permute-start.65
  337.9 4.3 collective-permute-start.63
  415.0 4.2 line_step.106
  427.0 4.3 line_step.107
  453.4 4.6 collective-permute-start.95
  467.6 5.0 collective-permute-done.87.refs_1_
  479.5 6.7 multiply_reduce_fusion
  489.1 4.3 collective-permute-start.99
  500.8 4.3 collective-permute-start.97
  510.0 4.3 collective-permute-start.105
  521.7 4.3 collective-permute-start.103
  548.1 5.6 collective-permute-done.111
  561.0 4.4 collective-permute-done.108.refs_1_
  572.1 4.4 collective-permute-done.115.refs_1_
  583.4 4.4 collective-permute-done.113.refs_1_
  594.6 4.4 collective-permute-done.119.refs_1_
  605.9 4.4 collective-permute-done.117.refs_1_
  617.1 4.4 collective-permute-done.121.refs_1_
  628.3 4.4 collective-permute-done.125.refs_1_
  639.6 4.4 collective-permute-done.123.refs_1_
  650.8 4.4 collective-permute-done.129.refs_1_
  662.0 4.4 collective-permute-done.127.refs_1_
  673.3 4.4 collective-permute-done.133.refs_1_
  684.5 4.4 collective-permute-done.131.refs_1_
  695.7 4.4 collective-permute-done.137.refs_1_
  707.0 4.4 collective-permute-done.135.refs_1_
  718.2 4.4 collective-permute-done.142.refs_1_
  729.4 4.4 collective-permute-done.140.refs_1_
  736.7 5.9 collective-permute-start.138
  744.4 6.2 collective-permute-start.143
  761.6 7.4 collective-permute-done.149.refs_1_
  771.8 8.4 %collective-permute-done.153.refs_1_ = bf16[128,2048]{1,0:T(8,128)(2,1)S(1)} collective-permute-done((bf16[128,2048]{1,0:T(8,128)(2,1)S(1)}, bf16[128,2048]{1,0:T(8,128)(2,1)S(1)}, u32[]{:S(2)}, u32[]{:S(2)}) %collective-permute-start.153) | collective-permute-done | bytes 524320 | tf_op jit(solution)/shard_map/ppermute | solution.py:411
  781.1 7.4 collective-permute-done.151.refs_1_
  (418 shorter events, 549.3 us)
Async XLA Ops:
  9.1 21.3 %collective-permute-start = (bf16[128,2048]{1,0:T(8,128)(2,1)S(1)}, bf16[128,2048]{1,0:T(8,128)(2,1)S(1)}, u32[]{:S(2)}, u32[]{:S(2)}) collective-permute-start(bf16[128,2048]{1,0:T(8,128)(2,1)S(1)} %get-tuple-element.458), channel_id=1, source_target_pairs={{0,8},{1,9},{2,10},{3,11},{4,12},{5,13},{6,14},{7,15}} | collective-permute-start | bytes 1572872 | tf_op jit(solution)/shard_map/ppermute | solution.py:410
  10.4 20.0 %collective-permute-start.1 = (bf16[128,2048]{1,0:T(8,128)(2,1)S(1)}, bf16[128,2048]{1,0:T(8,128)(2,1)S(1)}, u32[]{:S(2)}, u32[]{:S(2)}) collective-permute-start(bf16[128,2048]{1,0:T(8,128)(2,1)S(1)} %get-tuple-element.459), channel_id=1, source_target_pairs={{24,16},{25,17},{26,18},{27,19},{28,20},{29,21},{30,22},{31,23}} | collective-permute-start | bytes 1572872 | tf_op jit(solution)/shard_map/ppermute | solution.py:411
  20.7 20.9 %collective-permute-start.6 = (bf16[128,2048]{1,0:T(8,128)(2,1)S(1)}, bf16[128,2048]{1,0:T(8,128)(2,1)S(1)}, u32[]{:S(2)}, u32[]{:S(2)}) collective-permute-start(bf16[128,2048]{1,0:T(8,128)(2,1)S(1)} %get-tuple-element.464), channel_id=1, source_target_pairs={{0,8},{8,16},{1,9},{9,17},{2,10},{10,18},{3,11},{11,19},{4,12},{12... | collective-permute-start | bytes 1572872 | tf_op jit(solution)/shard_map/ppermute | solution.py:410
  32.0 20.9 %collective-permute-start.4 = (bf16[128,2048]{1,0:T(8,128)(2,1)S(1)}, bf16[128,2048]{1,0:T(8,128)(2,1)S(1)}, u32[]{:S(2)}, u32[]{:S(2)}) collective-permute-start(bf16[128,2048]{1,0:T(8,128)(2,1)S(1)} %get-tuple-element.466), channel_id=1, source_target_pairs={{0,8},{8,16},{1,9},{9,17},{2,10},{10,18},{3,11},{11,19},{4,12},{12... | collective-permute-start | bytes 1572872 | tf_op jit(solution)/shard_map/ppermute | solution.py:410
  43.2 20.9 %collective-permute-start.10 = (bf16[128,2048]{1,0:T(8,128)(2,1)S(1)}, bf16[128,2048]{1,0:T(8,128)(2,1)S(1)}, u32[]{:S(2)}, u32[]{:S(2)}) collective-permute-start(bf16[128,2048]{1,0:T(8,128)(2,1)S(1)} %get-tuple-element.472), channel_id=1, source_target_pairs={{0,8},{8,16},{16,24},{1,9},{9,17},{17,25},{2,10},{10,18},{18,26},{... | collective-permute-start | bytes 1572872 | tf_op jit(solution)/shard_map/ppermute | solution.py:410
  54.4 20.9 %collective-permute-start.8 = (bf16[128,2048]{1,0:T(8,128)(2,1)S(1)}, bf16[128,2048]{1,0:T(8,128)(2,1)S(1)}, u32[]{:S(2)}, u32[]{:S(2)}) collective-permute-start(bf16[128,2048]{1,0:T(8,128)(2,1)S(1)} %get-tuple-element.474), channel_id=1, source_target_pairs={{0,8},{8,16},{16,24},{1,9},{9,17},{17,25},{2,10},{10,18},{18,26},{... | collective-permute-start | bytes 1572872 | tf_op jit(solution)/shard_map/ppermute | solution.py:410
  66.9 19.6 %collective-permute-start.14 = (bf16[128,2048]{1,0:T(8,128)(2,1)S(1)}, bf16[128,2048]{1,0:T(8,128)(2,1)S(1)}, u32[]{:S(2)}, u32[]{:S(2)}) collective-permute-start(bf16[128,2048]{1,0:T(8,128)(2,1)S(1)} %get-tuple-element.483), channel_id=1, source_target_pairs={{0,8},{8,16},{16,24},{1,9},{9,17},{17,25},{2,10},{10,18},{18,26},{... | collective-permute-start | bytes 1572872 | tf_op jit(solution)/shard_map/ppermute | solution.py:410
  78.2 19.7 %collective-permute-start.12 = (bf16[128,2048]{1,0:T(8,128)(2,1)S(1)}, bf16[128,2048]{1,0:T(8,128)(2,1)S(1)}, u32[]{:S(2)}, u32[]{:S(2)}) collective-permute-start(bf16[128,2048]{1,0:T(8,128)(2,1)S(1)} %get-tuple-element.485), channel_id=1, source_target_pairs={{0,8},{8,16},{16,24},{1,9},{9,17},{17,25},{2,10},{10,18},{18,26},{... | collective-permute-start | bytes 1572872 | tf_op jit(solution)/shard_map/ppermute | solution.py:410
  89.4 19.7 %collective-permute-start.18 = (bf16[128,2048]{1,0:T(8,128)(2,1)S(1)}, bf16[128,2048]{1,0:T(8,128)(2,1)S(1)}, u32[]{:S(2)}, u32[]{:S(2)}) collective-permute-start(bf16[128,2048]{1,0:T(8,128)(2,1)S(1)} %get-tuple-element.497), channel_id=1, source_target_pairs={{0,8},{8,16},{16,24},{1,9},{9,17},{17,25},{2,10},{10,18},{18,26},{... | collective-permute-start | bytes 1572872 | tf_op jit(solution)/shard_map/ppermute | solution.py:410
  100.6 19.7 %collective-permute-start.16 = (bf16[128,2048]{1,0:T(8,128)(2,1)S(1)}, bf16[128,2048]{1,0:T(8,128)(2,1)S(1)}, u32[]{:S(2)}, u32[]{:S(2)}) collective-permute-start(bf16[128,2048]{1,0:T(8,128)(2,1)S(1)} %get-tuple-element.499), channel_id=1, source_target_pairs={{0,8},{8,16},{16,24},{1,9},{9,17},{17,25},{2,10},{10,18},{18,26},{... | collective-permute-start | bytes 1572872 | tf_op jit(solution)/shard_map/ppermute | solution.py:410
  111.9 19.7 %collective-permute-start.22 = (bf16[128,2048]{1,0:T(8,128)(2,1)S(1)}, bf16[128,2048]{1,0:T(8,128)(2,1)S(1)}, u32[]{:S(2)}, u32[]{:S(2)}) collective-permute-start(bf16[128,2048]{1,0:T(8,128)(2,1)S(1)} %get-tuple-element.511), channel_id=1, source_target_pairs={{0,8},{8,16},{16,24},{1,9},{9,17},{17,25},{2,10},{10,18},{18,26},{... | collective-permute-start | bytes 1572872 | tf_op jit(solution)/shard_map/ppermute | solution.py:410
  123.1 19.7 %collective-permute-start.20 = (bf16[128,2048]{1,0:T(8,128)(2,1)S(1)}, bf16[128,2048]{1,0:T(8,128)(2,1)S(1)}, u32[]{:S(2)}, u32[]{:S(2)}) collective-permute-start(bf16[128,2048]{1,0:T(8,128)(2,1)S(1)} %get-tuple-element.513), channel_id=1, source_target_pairs={{0,8},{8,16},{16,24},{1,9},{9,17},{17,25},{2,10},{10,18},{18,26},{... | collective-permute-start | bytes 1572872 | tf_op jit(solution)/shard_map/ppermute | solution.py:410
  134.3 19.7 %collective-permute-start.26 = (bf16[128,2048]{1,0:T(8,128)(2,1)S(1)}, bf16[128,2048]{1,0:T(8,128)(2,1)S(1)}, u32[]{:S(2)}, u32[]{:S(2)}) collective-permute-start(bf16[128,2048]{1,0:T(8,128)(2,1)S(1)} %get-tuple-element.525), channel_id=1, source_target_pairs={{0,8},{8,16},{16,24},{1,9},{9,17},{17,25},{2,10},{10,18},{18,26},{... | collective-permute-start | bytes 1572872 | tf_op jit(solution)/shard_map/ppermute | solution.py:410
  145.6 19.7 %collective-permute-start.24 = (bf16[128,2048]{1,0:T(8,128)(2,1)S(1)}, bf16[128,2048]{1,0:T(8,128)(2,1)S(1)}, u32[]{:S(2)}, u32[]{:S(2)}) collective-permute-start(bf16[128,2048]{1,0:T(8,128)(2,1)S(1)} %get-tuple-element.527), channel_id=1, source_target_pairs={{0,8},{8,16},{16,24},{1,9},{9,17},{17,25},{2,10},{10,18},{18,26},{... | collective-permute-start | bytes 1572872 | tf_op jit(solution)/shard_map/ppermute | solution.py:410
  156.8 19.7 %collective-permute-start.30 = (bf16[128,2048]{1,0:T(8,128)(2,1)S(1)}, bf16[128,2048]{1,0:T(8,128)(2,1)S(1)}, u32[]{:S(2)}, u32[]{:S(2)}) collective-permute-start(bf16[128,2048]{1,0:T(8,128)(2,1)S(1)} %get-tuple-element.539), channel_id=1, source_target_pairs={{0,8},{8,16},{16,24},{1,9},{9,17},{17,25},{2,10},{10,18},{18,26},{... | collective-permute-start | bytes 1572872 | tf_op jit(solution)/shard_map/ppermute | solution.py:410
  168.0 19.7 %collective-permute-start.28 = (bf16[128,2048]{1,0:T(8,128)(2,1)S(1)}, bf16[128,2048]{1,0:T(8,128)(2,1)S(1)}, u32[]{:S(2)}, u32[]{:S(2)}) collective-permute-start(bf16[128,2048]{1,0:T(8,128)(2,1)S(1)} %get-tuple-element.541), channel_id=1, source_target_pairs={{0,8},{8,16},{16,24},{1,9},{9,17},{17,25},{2,10},{10,18},{18,26},{... | collective-permute-start | bytes 1572872 | tf_op jit(solution)/shard_map/ppermute | solution.py:410
  179.7 19.2 %collective-permute-start.34 = (bf16[128,2048]{1,0:T(8,128)(2,1)S(1)}, bf16[128,2048]{1,0:T(8,128)(2,1)S(1)}, u32[]{:S(2)}, u32[]{:S(2)}) collective-permute-start(bf16[128,2048]{1,0:T(8,128)(2,1)S(1)} %get-tuple-element.553), channel_id=1, source_target_pairs={{0,8},{8,16},{16,24},{1,9},{9,17},{17,25},{2,10},{10,18},{18,26},{... | collective-permute-start | bytes 1572872 | tf_op jit(solution)/shard_map/ppermute | solution.py:410
  191.0 19.2 %collective-permute-start.32 = (bf16[128,2048]{1,0:T(8,128)(2,1)S(1)}, bf16[128,2048]{1,0:T(8,128)(2,1)S(1)}, u32[]{:S(2)}, u32[]{:S(2)}) collective-permute-start(bf16[128,2048]{1,0:T(8,128)(2,1)S(1)} %get-tuple-element.555), channel_id=1, source_target_pairs={{0,8},{8,16},{16,24},{1,9},{9,17},{17,25},{2,10},{10,18},{18,26},{... | collective-permute-start | bytes 1572872 | tf_op jit(solution)/shard_map/ppermute | solution.py:410
  202.2 19.2 %collective-permute-start.38 = (bf16[128,2048]{1,0:T(8,128)(2,1)S(1)}, bf16[128,2048]{1,0:T(8,128)(2,1)S(1)}, u32[]{:S(2)}, u32[]{:S(2)}) collective-permute-start(bf16[128,2048]{1,0:T(8,128)(2,1)S(1)} %get-tuple-element.567), channel_id=1, source_target_pairs={{0,8},{8,16},{16,24},{1,9},{9,17},{17,25},{2,10},{10,18},{18,26},{... | collective-permute-start | bytes 1572872 | tf_op jit(solution)/shard_map/ppermute | solution.py:410
  213.4 19.2 %collective-permute-start.36 = (bf16[128,2048]{1,0:T(8,128)(2,1)S(1)}, bf16[128,2048]{1,0:T(8,128)(2,1)S(1)}, u32[]{:S(2)}, u32[]{:S(2)}) collective-permute-start(bf16[128,2048]{1,0:T(8,128)(2,1)S(1)} %get-tuple-element.569), channel_id=1, source_target_pairs={{0,8},{8,16},{16,24},{1,9},{9,17},{17,25},{2,10},{10,18},{18,26},{... | collective-permute-start | bytes 1572872 | tf_op jit(solution)/shard_map/ppermute | solution.py:410
  225.0 19.0 %collective-permute-start.42 = (bf16[128,2048]{1,0:T(8,128)(2,1)}, bf16[128,2048]{1,0:T(8,128)(2,1)S(1)}, u32[]{:S(2)}, u32[]{:S(2)}) collective-permute-start(bf16[128,2048]{1,0:T(8,128)(2,1)} %get-tuple-element.581), channel_id=1, source_target_pairs={{0,8},{8,16},{16,24},{1,9},{9,17},{17,25},{2,10},{10,18},{18,26},{... | collective-permute-start | bytes 1572872 | tf_op jit(solution)/shard_map/ppermute | solution.py:410
  236.3 20.9 %collective-permute-start.40 = (bf16[128,2048]{1,0:T(8,128)(2,1)}, bf16[128,2048]{1,0:T(8,128)(2,1)S(1)}, u32[]{:S(2)}, u32[]{:S(2)}) collective-permute-start(bf16[128,2048]{1,0:T(8,128)(2,1)} %get-tuple-element.583), channel_id=1, source_target_pairs={{0,8},{8,16},{16,24},{1,9},{9,17},{17,25},{2,10},{10,18},{18,26},{... | collective-permute-start | bytes 1572872 | tf_op jit(solution)/shard_map/ppermute | solution.py:410
  251.8 19.0 %collective-permute-start.48 = (bf16[128,2048]{1,0:T(8,128)(2,1)}, bf16[128,2048]{1,0:T(8,128)(2,1)S(1)}, u32[]{:S(2)}, u32[]{:S(2)}) collective-permute-start(bf16[128,2048]{1,0:T(8,128)(2,1)} %copy-done.1), channel_id=1, source_target_pairs={{0,8},{8,16},{16,24},{1,9},{9,17},{17,25},{2,10},{10,18},{18,26},{... | collective-permute-start | bytes 1572872 | tf_op jit(solution)/shard_map/ppermute | solution.py:410
  260.3 19.6 %collective-permute-start.46 = (bf16[128,2048]{1,0:T(8,128)(2,1)S(1)}, bf16[128,2048]{1,0:T(8,128)(2,1)S(1)}, u32[]{:S(2)}, u32[]{:S(2)}) collective-permute-start(bf16[128,2048]{1,0:T(8,128)(2,1)S(1)} %get-tuple-element.600), channel_id=1, source_target_pairs={{0,8},{8,16},{16,24},{1,9},{9,17},{17,25},{2,10},{10,18},{18,26},{... | collective-permute-start | bytes 1572872 | tf_op jit(solution)/shard_map/ppermute | solution.py:410
  264.7 19.0 %collective-permute-start.47 = (bf16[128,2048]{1,0:T(8,128)(2,1)S(1)}, bf16[128,2048]{1,0:T(8,128)(2,1)S(1)}, u32[]{:S(2)}, u32[]{:S(2)}) collective-permute-start(bf16[128,2048]{1,0:T(8,128)(2,1)S(1)} %get-tuple-element.601), channel_id=1, source_target_pairs={{24,16},{16,8},{8,0},{25,17},{17,9},{9,1},{26,18},{18,10},{10,2},{... | collective-permute-start | bytes 1572872 | tf_op jit(solution)/shard_map/ppermute | solution.py:411
  266.0 26.1 %collective-permute-start.55 = (f32[9216]{0:T(1024)S(1)}, f32[9216]{0:T(1024)S(1)}, u32[]{:S(2)}, u32[]{:S(2)}) collective-permute-start(f32[9216]{0:T(1024)S(1)} %pad_maximum_fusion), channel_id=1, source_target_pairs={{0,24},{24,0},{1,25},{25,1},{2,26},{26,2},{3,27},{27,3},{4,28},{28... | collective-permute-start | bytes 110600 | tf_op jit(solution)/shard_map/ppermute | solution.py:316
  276.1 23.2 %collective-permute-start.53 = (bf16[128,2048]{1,0:T(8,128)(2,1)S(1)}, bf16[128,2048]{1,0:T(8,128)(2,1)S(1)}, u32[]{:S(2)}, u32[]{:S(2)}) collective-permute-start(bf16[128,2048]{1,0:T(8,128)(2,1)S(1)} %get-tuple-element.615), channel_id=1, source_target_pairs={{0,8},{8,16},{16,24},{1,9},{9,17},{17,25},{2,10},{10,18},{18,26},{... | collective-permute-start | bytes 1572872 | tf_op jit(solution)/shard_map/ppermute | solution.py:410
  278.6 20.7 %collective-permute-start.54 = (bf16[128,2048]{1,0:T(8,128)(2,1)S(1)}, bf16[128,2048]{1,0:T(8,128)(2,1)S(1)}, u32[]{:S(2)}, u32[]{:S(2)}) collective-permute-start(bf16[128,2048]{1,0:T(8,128)(2,1)S(1)} %get-tuple-element.616), channel_id=1, source_target_pairs={{24,16},{16,8},{8,0},{25,17},{17,9},{9,1},{26,18},{18,10},{10,2},{... | collective-permute-start | bytes 1572872 | tf_op jit(solution)/shard_map/ppermute | solution.py:411
  286.9 25.4 %collective-permute-start.51 = (bf16[128,2048]{1,0:T(8,128)(2,1)S(1)}, bf16[128,2048]{1,0:T(8,128)(2,1)S(1)}, u32[]{:S(2)}, u32[]{:S(2)}) collective-permute-start(bf16[128,2048]{1,0:T(8,128)(2,1)S(1)} %get-tuple-element.617), channel_id=1, source_target_pairs={{0,8},{8,16},{16,24},{1,9},{9,17},{17,25},{2,10},{10,18},{18,26},{... | collective-permute-start | bytes 1572872 | tf_op jit(solution)/shard_map/ppermute | solution.py:410
  290.6 21.7 %collective-permute-start.52 = (bf16[128,2048]{1,0:T(8,128)(2,1)S(1)}, bf16[128,2048]{1,0:T(8,128)(2,1)S(1)}, u32[]{:S(2)}, u32[]{:S(2)}) collective-permute-start(bf16[128,2048]{1,0:T(8,128)(2,1)S(1)} %get-tuple-element.618), channel_id=1, source_target_pairs={{24,16},{16,8},{8,0},{25,17},{17,9},{9,1},{26,18},{18,10},{10,2},{... | collective-permute-start | bytes 1572872 | tf_op jit(solution)/shard_map/ppermute | solution.py:411
  303.0 19.4 %collective-permute-start.59 = (bf16[128,2048]{1,0:T(8,128)(2,1)S(1)}, bf16[128,2048]{1,0:T(8,128)(2,1)S(1)}, u32[]{:S(2)}, u32[]{:S(2)}) collective-permute-start(bf16[128,2048]{1,0:T(8,128)(2,1)S(1)} %get-tuple-element.633), channel_id=1, source_target_pairs={{0,8},{8,16},{16,24},{1,9},{9,17},{17,25},{2,10},{10,18},{18,26},{... | collective-permute-start | bytes 1572872 | tf_op jit(solution)/shard_map/ppermute | solution.py:410
  315.5 19.4 %collective-permute-start.57 = (bf16[128,2048]{1,0:T(8,128)(2,1)S(1)}, bf16[128,2048]{1,0:T(8,128)(2,1)S(1)}, u32[]{:S(2)}, u32[]{:S(2)}) collective-permute-start(bf16[128,2048]{1,0:T(8,128)(2,1)S(1)} %get-tuple-element.637), channel_id=1, source_target_pairs={{0,8},{8,16},{16,24},{1,9},{9,17},{17,25},{2,10},{10,18},{18,26},{... | collective-permute-start | bytes 1572872 | tf_op jit(solution)/shard_map/ppermute | solution.py:410
  325.5 22.2 %collective-permute-start.65 = (bf16[128,2048]{1,0:T(8,128)(2,1)S(1)}, bf16[128,2048]{1,0:T(8,128)(2,1)S(1)}, u32[]{:S(2)}, u32[]{:S(2)}) collective-permute-start(bf16[128,2048]{1,0:T(8,128)(2,1)S(1)} %get-tuple-element.651), channel_id=1, source_target_pairs={{0,8},{8,16},{16,24},{1,9},{9,17},{17,25},{2,10},{10,18},{18,26},{... | collective-permute-start | bytes 1572872 | tf_op jit(solution)/shard_map/ppermute | solution.py:410
  337.9 19.5 %collective-permute-start.63 = (bf16[128,2048]{1,0:T(8,128)(2,1)S(1)}, bf16[128,2048]{1,0:T(8,128)(2,1)S(1)}, u32[]{:S(2)}, u32[]{:S(2)}) collective-permute-start(bf16[128,2048]{1,0:T(8,128)(2,1)S(1)} %get-tuple-element.655), channel_id=1, source_target_pairs={{0,8},{8,16},{16,24},{1,9},{9,17},{17,25},{2,10},{10,18},{18,26},{... | collective-permute-start | bytes 1572872 | tf_op jit(solution)/shard_map/ppermute | solution.py:410
  449.0 18.6 %collective-permute-start.86 = (bf16[128,2048]{1,0:T(8,128)(2,1)S(1)}, bf16[128,2048]{1,0:T(8,128)(2,1)S(1)}, u32[]{:S(2)}, u32[]{:S(2)}) collective-permute-start(bf16[128,2048]{1,0:T(8,128)(2,1)S(1)} %get-tuple-element.734), channel_id=1, source_target_pairs={{0,8},{8,16},{16,24},{1,9},{9,17},{17,25},{2,10},{10,18},{18,26},{... | collective-permute-start | bytes 1572872 | tf_op jit(solution)/shard_map/ppermute | solution.py:410
  452.1 20.5 %collective-permute-start.87 = (bf16[128,2048]{1,0:T(8,128)(2,1)S(1)}, bf16[128,2048]{1,0:T(8,128)(2,1)S(1)}, u32[]{:S(2)}, u32[]{:S(2)}) collective-permute-start(bf16[128,2048]{1,0:T(8,128)(2,1)S(1)} %get-tuple-element.735), channel_id=1, source_target_pairs={{24,16},{16,8},{8,0},{25,17},{17,9},{9,1},{26,18},{18,10},{10,2},{... | collective-permute-start | bytes 1572872 | tf_op jit(solution)/shard_map/ppermute | solution.py:411
  453.4 25.4 %collective-permute-start.95 = (f32[6144]{0:T(1024)S(1)}, f32[6144]{0:T(1024)S(1)}, u32[]{:S(2)}, u32[]{:S(2)}) collective-permute-start(f32[6144]{0:T(1024)S(1)} %pad_maximum_fusion.1), channel_id=1, source_target_pairs={{0,24},{24,0},{1,25},{25,1},{2,26},{26,2},{3,27},{27,3},{4,28},{28... | collective-permute-start | bytes 73736 | tf_op jit(solution)/shard_map/ppermute | solution.py:316
  463.1 23.0 %collective-permute-start.93 = (bf16[128,2048]{1,0:T(8,128)(2,1)S(1)}, bf16[128,2048]{1,0:T(8,128)(2,1)S(1)}, u32[]{:S(2)}, u32[]{:S(2)}) collective-permute-start(bf16[128,2048]{1,0:T(8,128)(2,1)S(1)} %get-tuple-element.745), channel_id=1, source_target_pairs={{0,8},{8,16},{16,24},{1,9},{9,17},{17,25},{2,10},{10,18},{18,26},{... | collective-permute-start | bytes 1572872 | tf_op jit(solution)/shard_map/ppermute | solution.py:410
  465.9 20.3 %collective-permute-start.94 = (bf16[128,2048]{1,0:T(8,128)(2,1)S(1)}, bf16[128,2048]{1,0:T(8,128)(2,1)S(1)}, u32[]{:S(2)}, u32[]{:S(2)}) collective-permute-start(bf16[128,2048]{1,0:T(8,128)(2,1)S(1)} %get-tuple-element.746), channel_id=1, source_target_pairs={{24,16},{16,8},{8,0},{25,17},{17,9},{9,1},{26,18},{18,10},{10,2},{... | collective-permute-start | bytes 1572872 | tf_op jit(solution)/shard_map/ppermute | solution.py:411
  475.0 23.4 %collective-permute-start.91 = (bf16[128,2048]{1,0:T(8,128)(2,1)S(1)}, bf16[128,2048]{1,0:T(8,128)(2,1)S(1)}, u32[]{:S(2)}, u32[]{:S(2)}) collective-permute-start(bf16[128,2048]{1,0:T(8,128)(2,1)S(1)} %get-tuple-element.747), channel_id=1, source_target_pairs={{0,8},{8,16},{16,24},{1,9},{9,17},{17,25},{2,10},{10,18},{18,26},{... | collective-permute-start | bytes 1572872 | tf_op jit(solution)/shard_map/ppermute | solution.py:410
  477.5 21.0 %collective-permute-start.92 = (bf16[128,2048]{1,0:T(8,128)(2,1)S(1)}, bf16[128,2048]{1,0:T(8,128)(2,1)S(1)}, u32[]{:S(2)}, u32[]{:S(2)}) collective-permute-start(bf16[128,2048]{1,0:T(8,128)(2,1)S(1)} %get-tuple-element.748), channel_id=1, source_target_pairs={{24,16},{16,8},{8,0},{25,17},{17,9},{9,1},{26,18},{18,10},{10,2},{... | collective-permute-start | bytes 1572872 | tf_op jit(solution)/shard_map/ppermute | solution.py:411
  533.2 21.7 %collective-permute-start.109 = (bf16[128,2048]{1,0:T(8,128)(2,1)S(1)}, bf16[128,2048]{1,0:T(8,128)(2,1)S(1)}, u32[]{:S(2)}, u32[]{:S(2)}) collective-permute-start(bf16[128,2048]{1,0:T(8,128)(2,1)S(1)} %get-tuple-element.785), channel_id=1, source_target_pairs={{0,8},{8,16},{16,24},{1,9},{9,17},{17,25},{2,10},{10,18},{18,26},{... | collective-permute-start | bytes 1572872 | tf_op jit(solution)/shard_map/ppermute | solution.py:410
  535.0 19.9 %collective-permute-start.110 = (bf16[128,2048]{1,0:T(8,128)(2,1)S(1)}, bf16[128,2048]{1,0:T(8,128)(2,1)S(1)}, u32[]{:S(2)}, u32[]{:S(2)}) collective-permute-start(bf16[128,2048]{1,0:T(8,128)(2,1)S(1)} %get-tuple-element.786), channel_id=1, source_target_pairs={{24,16},{16,8},{8,0},{25,17},{17,9},{9,1},{26,18},{18,10},{10,2},{... | collective-permute-start | bytes 1572872 | tf_op jit(solution)/shard_map/ppermute | solution.py:411
  725.0 25.6 %collective-permute-start.146 = (bf16[128,2048]{1,0:T(8,128)(2,1)S(1)}, bf16[128,2048]{1,0:T(8,128)(2,1)S(1)}, u32[]{:S(2)}, u32[]{:S(2)}) collective-permute-start(bf16[128,2048]{1,0:T(8,128)(2,1)S(1)} %get-tuple-element.879), channel_id=1, source_target_pairs={{0,8},{8,16},{16,24},{1,9},{9,17},{17,25},{2,10},{10,18},{18,26},{... | collective-permute-start | bytes 1572872 | tf_op jit(solution)/shard_map/ppermute | solution.py:410
  727.4 23.2 %collective-permute-start.147 = (bf16[128,2048]{1,0:T(8,128)(2,1)S(1)}, bf16[128,2048]{1,0:T(8,128)(2,1)S(1)}, u32[]{:S(2)}, u32[]{:S(2)}) collective-permute-start(bf16[128,2048]{1,0:T(8,128)(2,1)S(1)} %get-tuple-element.880), channel_id=1, source_target_pairs={{24,16},{16,8},{8,0},{25,17},{17,9},{9,1},{26,18},{18,10},{10,2},{... | collective-permute-start | bytes 1572872 | tf_op jit(solution)/shard_map/ppermute | solution.py:411
  734.7 18.8 %collective-permute-start.144 = (bf16[128,2048]{1,0:T(8,128)(2,1)S(1)}, bf16[128,2048]{1,0:T(8,128)(2,1)S(1)}, u32[]{:S(2)}, u32[]{:S(2)}) collective-permute-start(bf16[128,2048]{1,0:T(8,128)(2,1)S(1)} %get-tuple-element.881), channel_id=1, source_target_pairs={{8,16},{16,24},{9,17},{17,25},{10,18},{18,26},{11,19},{19,27},{12,... | collective-permute-start | bytes 1572872 | tf_op jit(solution)/shard_map/ppermute | solution.py:410
  735.4 21.0 %collective-permute-start.145 = (bf16[128,2048]{1,0:T(8,128)(2,1)S(1)}, bf16[128,2048]{1,0:T(8,128)(2,1)S(1)}, u32[]{:S(2)}, u32[]{:S(2)}) collective-permute-start(bf16[128,2048]{1,0:T(8,128)(2,1)S(1)} %get-tuple-element.882), channel_id=1, source_target_pairs={{16,8},{8,0},{17,9},{9,1},{18,10},{10,2},{19,11},{11,3},{20,12},{1... | collective-permute-start | bytes 1572872 | tf_op jit(solution)/shard_map/ppermute | solution.py:411
  759.1 21.1 %collective-permute-start.153 = (bf16[128,2048]{1,0:T(8,128)(2,1)S(1)}, bf16[128,2048]{1,0:T(8,128)(2,1)S(1)}, u32[]{:S(2)}, u32[]{:S(2)}) collective-permute-start(bf16[128,2048]{1,0:T(8,128)(2,1)S(1)} %get-tuple-element.894), channel_id=1, source_target_pairs={{8,0},{9,1},{10,2},{11,3},{12,4},{13,5},{14,6},{15,7}} | collective-permute-start | bytes 1572872 | tf_op jit(solution)/shard_map/ppermute | solution.py:411
  (125 other events, 1768.5 us)
